TPU v7x, 256 devices: a whole 4x4x8 slice. The times are simulated.
256 devices in a mesh: seq: 32 (over z, x_lo, core), head: 8 (over y, x_hi).
Axes of the slice: x: 4 (x_hi: 2, x_lo: 2; x = x_hi * 2 + x_lo), y: 4, z: 8, core: 2. Of those that a mesh axis runs over, the one named last changes fastest.
Arguments:
- latent: bfloat16 [4, 32, 64, 3072], P(None, 'seq', 'head'), may hold values from -6 to 6
- w_qkv: bfloat16 [3072, 3, 3072], P(None, None, 'head'), may hold values from -1 to 1
- q_gain: float32 [128], replicated, may hold values from 0.5 to 10
- k_gain: float32 [128], replicated, may hold values from 0.5 to 10
- w_out: bfloat16 [3072, 3072], P('head'), may hold values from -0.109375 to 0.109375
- neighbours: int32 [32, 9], replicated, may hold values from -1 to 31, as said below
- tile_owner: int32 [32], replicated, may hold values from 0 to 31, as said below
Outputs:
- mixed: bfloat16 [32, 256, 3072], P('seq', None, 'head')
Inputs may be any that keep to these rules, and one draw needn't show every extreme that they name: `neighbours`: row t lists, in increasing order and followed by -1s, the tiles of the grid whose tile row differs from t's by at most one and whose tile column lies in a block of three consecutive tile columns that holds t's column; t itself is always listed. `tile_owner`: every index of seq owns exactly one tile.
All inputs are finite; a program needn't handle non-finite values.
Results may differ from a plain program's by a relative error of at most 0.017.
Values may be sent and summed in bfloat16 or wider, within the bound.
No kernel may reach another device: no remote copies, remote signals or barrier semaphores. Data moves between devices by JAX's collectives and lax.ppermute only.
A program may use at most 64 MiB of HBM per device.

v0:
```python
import jax
import jax.numpy as jnp
from jax import lax
from jax.sharding import PartitionSpec as P

D = 3072
HEAD_DIM = 128
FRAMES = 4
TILE = 8
TILE_COLS = 8
TILES_DEV = 1
TILE_TOKENS = 256


epsilon = 1e-06


def head_norm(values, gain, heads_here):
    shaped = values.reshape(values.shape[:-1] + (heads_here, HEAD_DIM))
    scaled = shaped * lax.rsqrt(jnp.mean(shaped * shaped, axis=-1, keepdims=True) + epsilon) * gain
    return scaled.reshape(values.shape)


def local(latent, w_qkv, q_gain, k_gain, w_out, neighbours, tile_owner):
    seq_count = lax.axis_size("seq")
    position = lax.axis_index("seq")
    tile_rows = seq_count // TILE
    local_width = w_qkv.shape[2]
    heads_here = local_width // HEAD_DIM
    weight_flat = w_qkv.reshape(D, 3 * local_width)
    shard_piece = lax.all_gather(latent, "head", axis=2, tiled=True)
    flattened = shard_piece.reshape(-1, D)
    result = jnp.dot(flattened, weight_flat, preferred_element_type=jnp.float32)
    projected = result.reshape(shard_piece.shape[:3] + (3 * local_width,))[:, 0]
    queries = head_norm(projected[..., :local_width], q_gain, heads_here).astype(jnp.bfloat16)
    key_rows = head_norm(projected[..., local_width : 2 * local_width], k_gain, heads_here).astype(
        jnp.bfloat16
    )
    values = projected[..., 2 * local_width :].astype(jnp.bfloat16)
    owner_grid = tile_owner.reshape(tile_rows, TILE_COLS)
    devices = jnp.arange(seq_count, dtype=jnp.int32)
    owned_mask = (owner_grid[None] == devices[:, None, None]).astype(jnp.int32)
    present = jnp.sum(owned_mask, axis=2)
    column_of = jnp.sum(owned_mask * jnp.arange(TILE_COLS, dtype=jnp.int32)[None, None, :], axis=2)
    rank_within = jnp.cumsum(present, axis=1) - 1
    chosen = present[:, None, :] * (
        rank_within[:, None, :] == jnp.arange(TILES_DEV, dtype=jnp.int32)[None, :, None]
    ).astype(jnp.int32)
    tile_row = jnp.sum(chosen * jnp.arange(tile_rows, dtype=jnp.int32)[None, None, :], axis=2)
    tile_col = jnp.sum(chosen * column_of[:, None, :], axis=2)
    tile_ident = tile_row * TILE_COLS + tile_col
    window_lists = neighbours[tile_ident]
    listed_cols = jnp.where(window_lists >= 0, window_lists % TILE_COLS, TILE_COLS)
    block_start = jnp.minimum(jnp.min(listed_cols, axis=2), TILE_COLS - 3)
    source_row = position // TILE
    nearby = jnp.abs(tile_row - source_row) <= 1
    own_row = tile_row[position]
    own_col = tile_col[position]
    own_start = block_start[position]
    own_lists = window_lists[position]
    key_tiles = (
        devices[None, :, None] // TILE * TILE_COLS
        + own_start[:, None, None]
        + jnp.arange(3 * TILE, dtype=jnp.int32)[None, None, :] // TILE
    )
    allowed = jnp.any(key_tiles[..., None] == own_lists[:, None, None, :], axis=-1)
    allowed = jnp.broadcast_to(
        allowed[:, :, None, :], (TILES_DEV, seq_count, FRAMES, 3 * TILE)
    ).reshape(TILES_DEV, -1)
    bundle = jnp.concatenate([queries, key_rows, values], axis=-1)
    block_cols = (block_start * TILE).reshape(-1)

    def one_block(column_start):
        return lax.dynamic_slice_in_dim(bundle, column_start, 3 * TILE, 1)

    blocks = jax.vmap(one_block)(block_cols)
    blocks = blocks.reshape((seq_count, TILES_DEV) + blocks.shape[1:])
    arrived = lax.all_to_all(
        jnp.where(nearby[:, :, None, None, None], blocks, jnp.zeros_like(blocks)),
        "seq",
        split_axis=0,
        concat_axis=0,
        tiled=True,
    )
    rows_here = lax.dynamic_slice_in_dim(arrived[:, 0], own_row[0] * TILE, TILE, 0)
    offset = (own_col[0] - own_start[0]) * TILE
    query_piece = lax.dynamic_slice_in_dim(rows_here[..., :local_width], offset, TILE, 2)
    query_tiles = [jnp.transpose(query_piece, (1, 0, 2, 3)).reshape(TILE_TOKENS, local_width)]
    key_part = arrived[..., local_width : 2 * local_width]
    value_part = arrived[..., 2 * local_width :]
    query_stack = jnp.stack(query_tiles)
    key_stack = jnp.transpose(key_part, (1, 0, 2, 3, 4)).reshape(TILES_DEV, -1, local_width)
    value_stack = jnp.transpose(value_part, (1, 0, 2, 3, 4)).reshape(TILES_DEV, -1, local_width)
    score_scale = HEAD_DIM ** (-0.5)

    def to_heads(stacked):
        return jnp.moveaxis(stacked.reshape(stacked.shape[:2] + (heads_here, HEAD_DIM)), 2, 0)

    def attend(operands):
        head_queries, head_keys, head_values = operands
        scores = (
            jnp.einsum("tqd,tkd->tqk", head_queries, head_keys, preferred_element_type=jnp.float32)
            * score_scale
        )
        scores = jnp.where(allowed[:, None, :], scores, -jnp.inf)
        row_max = jnp.max(scores, axis=-1, keepdims=True)
        weights = jnp.exp(scores - row_max)
        probabilities = (weights / jnp.sum(weights, axis=-1, keepdims=True)).astype(jnp.bfloat16)
        return jnp.einsum(
            "tqk,tkd->tqd", probabilities, head_values, preferred_element_type=jnp.float32
        ).astype(jnp.bfloat16)

    attended = lax.map(attend, (to_heads(query_stack), to_heads(key_stack), to_heads(value_stack)))
    attended = jnp.moveaxis(attended, 0, 2).reshape(TILES_DEV * TILE_TOKENS, local_width)
    mixed_rows = lax.psum_scatter(
        lax.dot_general(
            w_out, attended, (((0,), (1,)), ((), ())), preferred_element_type=jnp.float32
        ).astype(jnp.bfloat16),
        "head",
        scatter_dimension=0,
        tiled=True,
    ).astype(jnp.float32)
    return jnp.transpose(mixed_rows).reshape(TILES_DEV, TILE_TOKENS, -1).astype(jnp.bfloat16)


def solution(mesh):
    placed = (
        P(None, "seq", "head", None),
        P(None, None, "head"),
        P(),
        P(),
        P("head", None),
        P(),
        P(),
    )
    return jax.shard_map(
        local, mesh=mesh, in_specs=placed, out_specs=P("seq", None, "head"), check_vma=False
    )
```

profile of v0, /device:TPU:2, one launch (start us, length us, event | category | flops | bytes accessed | tf_op | source)
XLA Modules:
  0.0 410.8 jit_solution(7722512245327893640)
XLA Ops:
  6.5 0.7 all-gather.2.cloned.1.call-update
  7.3 0.7 eq.53
  8.0 0.1 convert_reduce_fusion
  8.1 0.8 copy.89
  8.9 10.3 %copy.83 = bf16[3072,3,384]{0,2,1:T(8,128)(2,1)} copy(bf16[3072,3,384]{2,0,1:T(8,128)(2,1)} %param.10) | data formatting | bytes 14155776 | tf_op args[1]
  19.3 0.5 copy-done.3
  19.8 0.6 gather_fusion
  20.3 0.1 fusion.21
  20.5 46.1 %all-gather.2.cloned.1.call-done = bf16[4,1,64,3072]{3,2,0,1:T(8,128)(2,1)} async-done(((bf16[4,1,8,3072]{3,2,0,1:T(8,128)(2,1)}), bf16[4,1,64,3072]{3,2,0,1:T(8,128)(2,1)}) %all-gather.2.cloned.1.call-update) | async-done | bytes 1572880 | tf_op jit(solution)/shard_map/all_gather | solution.py:31
  66.6 5.7 %fusion.17 = f32[4,64,1152]{2,1,0:T(8,128)S(1)} fusion(bf16[3072,1152,1]{0,1,2:T(8,128)(2,1)} %bitcast.96, bf16[4,1,64,3072]{3,2,0,1:T(8,128)(2,1)} %all-gather.2.cloned.1.call-done), kind=kOutput, calls=%fused_computation.25 | convolution fusion | flops 1811939328 | bytes 9830400 | tf_op jit(solution)/shard_map/dot_general | solution.py:33
  72.3 0.7 slice.41
  73.0 1.0 slice_multiply_fusion.1
  74.0 1.9 mul.150
  76.0 2.1 reduce_sum.67
  78.0 0.9 add_rsqrt_fusion.1
  78.9 1.1 mul.151
  80.1 2.0 mul.152
  82.1 1.9 mul.159
  84.0 2.0 reduce_sum.68
  86.1 0.9 add_rsqrt_fusion
  87.0 1.1 mul.160
  88.1 2.0 mul.161
  90.1 1.2 multiply_convert_fusion.1
  91.3 1.0 pad_maximum_fusion
  92.3 0.5 copy.90
  92.8 9.1 %gather_fusion.1 = bf16[32,4,24,1152]{3,1,2,0:T(4,128)(2,1)} fusion(bf16[4,64,1152]{2,0,1:T(4,128)(2,1)S(1)} %copy.90, s32[32]{0:T(128)S(1)} %fusion.30), kind=kCustom, calls=%fused_computation.1 | custom fusion | bytes 14156160 | tf_op jit(solution)/shard_map/vmap()/gather | solution.py:74
  101.9 8.9 %fusion.15 = bf16[32,1,4,24,1152]{4,2,3,1,0:T(4,128)(2,1)} fusion(bf16[32,4,24,1152]{3,1,2,0:T(4,128)(2,1)} %gather_fusion.1, pred[32]{0:T(512)(128)(4,1)S(1)} %abs_compare_fusion), kind=kLoop, calls=%fused_computation.21 | loop fusion | flops 3538944 | bytes 14155808 | tf_op jit(solution)/shard_map/jit(_where)/select_n | solution.py:79
  110.8 8.8 %all-to-all-start = ((bf16[32,1,4,24,1152]{4,2,3,1,0:T(4,128)(2,1)}), bf16[32,1,4,24,1152]{4,2,3,1,0:T(4,128)(2,1)}, u32[]{:S(2)}, u32[]{:S(2)}) async-start(bf16[32,1,4,24,1152]{4,2,3,1,0:T(4,128)(2,1)} %fusion.15), calls=%async_computation | async-start | bytes 14155776 | tf_op jit(solution)/shard_map/all_to_all | solution.py:78
  119.7 0.6 dynamic-slice.11
  120.9 0.6 dynamic-slice.12
  121.5 0.6 dynamic-slice.10
  123.4 0.7 fusion.24
  124.0 0.6 fusion.26
  124.9 0.1 copy.99
  124.9 150.1 %all-to-all-done = bf16[32,1,4,24,1152]{4,2,3,1,0:T(4,128)(2,1)} async-done(((bf16[32,1,4,24,1152]{4,2,3,1,0:T(4,128)(2,1)}), bf16[32,1,4,24,1152]{4,2,3,1,0:T(4,128)(2,1)}, u32[]{:S(2)}, u32[]{:S(2)}) %all-to-all-start) | async-done | bytes 7077920 | tf_op jit(solution)/shard_map/all_to_all | solution.py:78
  275.1 5.5 %fusion.32 = (bf16[32,1,4,24,384]{4,2,3,1,0:T(4,128)(2,1)S(1)}, bf16[32,1,4,24,384]{4,2,3,1,0:T(4,128)(2,1)}) fusion(bf16[32,1,4,24,1152]{4,2,3,1,0:T(4,128)(2,1)} %all-to-all-done), kind=kLoop, calls=%fused_computation.78 | loop fusion | bytes 9437184 | tf_op jit(solution)/shard_map/slice | solution.py:90
  280.5 1.7 copy.95
  282.3 2.1 constant_dynamic-slice_fusion
  284.4 0.2 copy.111
  284.8 7.0 %reshape_reshape_transpose.7 = bf16[1,3072,3,128]{3,2,1,0:T(4,128)(2,1)} reshape(bf16[32,1,4,24,384]{4,3,2,0,1:T(8,128)(2,1)} %copy.95) | data formatting | bytes 4718592 | tf_op jit(solution)/shard_map/reshape;reshape;transpose | solution.py:97
  291.9 3.8 copy.98
  295.7 1.8 copy.94
  297.4 7.0 %reshape_reshape_transpose.6 = bf16[1,3072,3,128]{3,2,1,0:T(4,128)(2,1)} reshape(bf16[32,1,4,24,384]{4,3,2,0,1:T(8,128)(2,1)} %copy.94) | data formatting | bytes 4718592 | tf_op jit(solution)/shard_map/reshape;reshape;transpose | solution.py:97
  304.5 3.6 copy.97
  308.1 13.8 %while.11 = (s32[]{:T(128)}, bf16[3,1,256,128]{2,3,0,1:T(8,128)(2,1)S(1)}, bf16[3,1,256,128]{3,2,1,0:T(8,128)(2,1)S(1)}, bf16[3,1,3072,128]{3,2,1,0:T(8,128)(2,1...) while((s32[]{:T(128)}, ...), condition=%wide.region_12.13_spmd.clone, body=%wide.region_9.12_spmd.clone.sunk | while | flops 408976896 | bytes 11422557 | solution.py:113
  308.1 0.1 broadcast_in_dim.77
  308.2 1.8 fusion.41
  310.0 0.6 fusion.42
  310.6 1.9 fusion.43
  312.5 0.1 copy.113
  312.7 0.1 broadcast_in_dim.77
  312.8 1.8 fusion.41
  314.6 0.6 fusion.42
  315.2 1.9 fusion.43
  317.1 0.1 copy.113
  317.3 0.1 broadcast_in_dim.77
  317.4 1.8 fusion.41
  319.2 0.6 fusion.42
  319.8 1.9 fusion.43
  321.7 0.1 copy.113
  321.9 2.2 fusion.16
  324.0 2.6 copy.103
  326.7 75.5 %reduce-scatter.4.cloned.1.call-done = bf16[384,256]{1,0:T(8,128)(2,1)} async-done(((bf16[3072,256]{1,0:T(8,128)(2,1)}), bf16[384,256]{1,0:T(8,128)(2,1)}) %reduce-scatter.4.cloned.1.call-update) | async-done | bytes 196624
  402.2 1.7 copy.104
  (47 shorter events, 0.7 us)
Async XLA Ops:
  6.5 315.3 %copy-start = (bf16[384,3072]{1,0:T(8,128)(2,1)S(1)}, bf16[384,3072]{1,0:T(8,128)(2,1)}, u32[]{:S(2)}) copy-start(bf16[384,3072]{1,0:T(8,128)(2,1)} %param.13) | copy-start | bytes 7077892
  6.5 60.1 %all-gather.2.cloned.1.call-start = ((), (), s32[]{:S(2)}) async-start(), calls=%async_computation.2 | async-start | bytes 1769472 | tf_op jit(solution)/shard_map/all_gather | solution.py:31
  8.9 11.6 %copy-start.7 = (f32[128]{0:T(128)S(1)}, f32[128]{0:T(128)}, u32[]{:S(2)}) copy-start(f32[128]{0:T(128)} %param.12) | copy-start | bytes 1540
  8.9 11.6 %copy-start.8 = (f32[128]{0:T(128)S(1)}, f32[128]{0:T(128)}, u32[]{:S(2)}) copy-start(f32[128]{0:T(128)} %param.11) | copy-start | bytes 1540
  19.2 0.5 copy-start.3
  19.2 47.4 %copy-start.5 = (s32[32]{0:T(128)}, s32[32]{0:T(128)S(1)}, u32[]{:S(2)}) copy-start(s32[32]{0:T(128)S(1)} %get-tuple-element.89) | copy-start | bytes 388
  20.3 46.3 %copy-start.2 = (s32[32,9]{1,0:T(8,128)}, s32[32,9]{1,0:T(8,128)S(1)}, u32[]{:S(2)}) copy-start(s32[32,9]{1,0:T(8,128)S(1)} %gather_fusion) | copy-start | bytes 3460
  20.5 46.2 %copy-start.9 = (s32[32]{0:T(128)}, s32[32]{0:T(128)S(1)}, u32[]{:S(2)}) copy-start(s32[32]{0:T(128)S(1)} %fusion.21) | copy-start | bytes 388
  110.8 8.9 %copy-start.6 = (s32[32]{0:T(128)S(1)}, s32[32]{0:T(128)}, u32[]{:S(2)}) copy-start(s32[32]{0:T(128)} %copy-done.5) | copy-start | bytes 388
  110.8 10.1 %copy-start.4 = (s32[32]{0:T(128)S(1)}, s32[32]{0:T(128)}, u32[]{:S(2)}) copy-start(s32[32]{0:T(128)} %copy-done.3) | copy-start | bytes 388
  110.8 10.7 %copy-start.10 = (s32[32]{0:T(128)S(1)}, s32[32]{0:T(128)}, u32[]{:S(2)}) copy-start(s32[32]{0:T(128)} %copy-done.9) | copy-start | bytes 388
  110.8 164.3 %all-to-all-start = ((bf16[32,1,4,24,1152]{4,2,3,1,0:T(4,128)(2,1)}), bf16[32,1,4,24,1152]{4,2,3,1,0:T(4,128)(2,1)}, u32[]{:S(2)}, u32[]{:S(2)}) async-start(bf16[32,1,4,24,1152]{4,2,3,1,0:T(4,128)(2,1)} %fusion.15), calls=%async_computation | async-start | bytes 14155776 | tf_op jit(solution)/shard_map/all_to_all | solution.py:78
  119.6 282.6 %reduce-scatter.4.cloned.1.call-start = ((), (), s32[]{:S(2)}) async-start(), calls=%async_computation.3 | async-start | bytes 1769472
  291.9 3.8 copy-start.1
Sparse Core Ops, SparseCore 0:
  10.0 56.5 all-gather.1
  326.8 75.3 reduce-scatter.3
where the time goes:
time: 413 us; the launch traced here: 411 us
  waiting for transfers between devices  272 us (66%)
  local copies, waits for them, and re-layouts  73.9 us (18%)
  other arithmetic  20.9 us (5%)
  matrix products  19.1 us (5%)
  between operations  15.5 us (4%)
  starting transfers between devices  8.85 us (2%)
    all_to_all x1, waiting for transfers between devices, local(): lax.all_to_all(jnp.where(nearby[:, :, None, None, None], blocks, jnp.zero...  150 us
    unnamed x3, waiting for transfers between devices  76.3 us
    all_gather x1, waiting for transfers between devices, local(): shard_piece = lax.all_gather(latent, 'head', axis=2, tiled=True)  46.1 us
    unnamed x31, local copies, waits for them, and re-layouts  23.7 us
    another operation x3, local copies, waits for them, and re-layouts, to_heads(): stacked.reshape(stacked.shape[:2] + (heads_here, HEAD_DIM))  14.1 us
    gather x1, local copies, waits for them, and re-layouts, one_block(): return lax.dynamic_slice_in_dim(bundle, column_start, 3 * TILE, 1)  9.11 us
    select_n x1, other arithmetic, local(): jnp.where(nearby[:, :, None, None, None], blocks, jnp.zeros_like(blocks))  8.88 us
    all_to_all x1, starting transfers between devices, local(): lax.all_to_all(jnp.where(nearby[:, :, None, None, None], blocks, jnp.zero...  8.81 us
  transfers between devices with their start and end apart: 3, of which 3 were waited for; matrix products, arithmetic and copies ran while one was open for 4% of the time, Pallas kernels for 0%

commit v1 on v0

v1 whole, which is shorter than its diff:
```python
import functools

import jax
import jax.numpy as jnp
from jax import lax
from jax.experimental import pallas as pl
from jax.experimental.pallas import tpu as pltpu
from jax.sharding import PartitionSpec as P

D = 3072
HEAD_DIM = 128
FRAMES = 4
TILE = 8
TILE_COLS = 8
TILES = 32
TILE_TOKENS = 256
N_HEAD = 8
PLANE = 4
PLANES = 8
PIECE = FRAMES * TILE
WIDTH = 384
HEADS_HERE = 3
SLOTS = 6
WINDOW = 3 * PIECE
KEYS = SLOTS * WINDOW
SCORE_SCALE = HEAD_DIM ** (-0.5) * 1.4426950408889634

epsilon = 1e-06
VMEM_LIMIT = 40 * 1024 * 1024


def params():
    return pltpu.CompilerParams(vmem_limit_bytes=VMEM_LIMIT)


def project_kernel(place, *refs):
    pieces, (w_ref, gain_ref, q_ref, kv_ref, rows) = refs[:N_HEAD], refs[N_HEAD:]
    step = pl.program_id(0)

    @pl.when(step == 0)
    def _():
        for k in range(N_HEAD):
            start = pl.multiple_of(place[k] * PIECE, PIECE)
            rows[pl.ds(start, PIECE), :] = pieces[k][...]

    result = jnp.dot(rows[...], w_ref[...], preferred_element_type=jnp.float32)

    def normed(gain):
        heads = []
        for h in range(HEADS_HERE):
            part = result[:, h * HEAD_DIM : (h + 1) * HEAD_DIM]
            mean = jnp.mean(part * part, axis=-1, keepdims=True)
            heads.append((part * lax.rsqrt(mean + epsilon) * gain).astype(jnp.bfloat16))
        return jnp.concatenate(heads, axis=1)

    @pl.when(step == 0)
    def _():
        q_ref[...] = normed(gain_ref[0:1, :])

    @pl.when(step == 1)
    def _():
        kv_ref[...] = normed(gain_ref[1:2, :])

    @pl.when(step == 2)
    def _():
        kv_ref[...] = result.astype(jnp.bfloat16)


def project(place, pieces, weight, gains):
    tokens = N_HEAD * PIECE
    grid_spec = pltpu.PrefetchScalarGridSpec(
        num_scalar_prefetch=1,
        grid=(3,),
        in_specs=[pl.BlockSpec((PIECE, D), lambda p, s: (0, 0))] * N_HEAD
        + [
            pl.BlockSpec((D, WIDTH), lambda p, s: (0, p)),
            pl.BlockSpec((2, HEAD_DIM), lambda p, s: (0, 0)),
        ],
        out_specs=[
            pl.BlockSpec((tokens, WIDTH), lambda p, s: (0, 0)),
            pl.BlockSpec((tokens, WIDTH), lambda p, s: (0, jnp.maximum(p - 1, 0))),
        ],
        scratch_shapes=[pltpu.VMEM((tokens, D), jnp.bfloat16)],
    )
    return pl.pallas_call(
        project_kernel,
        grid_spec=grid_spec,
        out_shape=[
            jax.ShapeDtypeStruct((tokens, WIDTH), jnp.bfloat16),
            jax.ShapeDtypeStruct((tokens, 2 * WIDTH), jnp.bfloat16),
        ],
        compiler_params=params(),
        cost_estimate=pl.CostEstimate(
            flops=2 * tokens * D * 3 * WIDTH, bytes_accessed=10_000_000, transcendentals=0
        ),
        name="project",
    )(place, *pieces, weight, gains)


def attend_kernel(starts, *refs):
    queries, slots = refs[:PLANE], refs[PLANE : PLANE + SLOTS]
    bias_ref = refs[PLANE + SLOTS]
    outs = refs[PLANE + SLOTS + 1 : 2 * PLANE + SLOTS + 1]
    level_ref = refs[2 * PLANE + SLOTS + 1]
    lanes = lax.broadcasted_iota(jnp.int32, (PLANE * PIECE, HEAD_DIM), 1)
    level_ref[...] = jnp.zeros_like(level_ref)

    def column(c, carry):
        here = pl.ds(pl.multiple_of(c * PIECE, PIECE), PIECE)
        window = pl.ds(pl.multiple_of(starts[c] * PIECE, PIECE), WINDOW)
        bias = bias_ref[c]
        levels = level_ref[...]
        for h in range(HEADS_HERE):
            head = slice(h * HEAD_DIM, (h + 1) * HEAD_DIM)
            value_head = slice(WIDTH + h * HEAD_DIM, WIDTH + (h + 1) * HEAD_DIM)
            q = jnp.concatenate([ref[here, head] for ref in queries], axis=0)
            keys = jnp.concatenate([ref[window, head] for ref in slots], axis=0)
            values = jnp.concatenate([ref[window, value_head] for ref in slots], axis=0)
            scores = lax.dot_general(
                q, keys, (((1,), (1,)), ((), ())), preferred_element_type=jnp.float32
            )
            scores = scores * SCORE_SCALE + bias
            top = jnp.max(scores, axis=-1, keepdims=True)
            weights = jnp.exp2(scores - top)
            total = jnp.sum(weights, axis=-1, keepdims=True)
            mixed = jnp.dot(
                weights.astype(jnp.bfloat16), values, preferred_element_type=jnp.float32
            )
            mixed = (mixed / total).astype(jnp.bfloat16)
            for k in range(PLANE):
                outs[k][here, head] = mixed[k * PIECE : (k + 1) * PIECE]
            levels = jnp.where(lanes == HEADS_HERE * c + h, top + jnp.log2(total), levels)
        level_ref[...] = levels
        return carry

    lax.fori_loop(0, TILE_COLS, column, 0)


def attend(starts, queries, slots, bias):
    tokens = TILE_COLS * PIECE
    whole = pl.BlockSpec(memory_space=pltpu.VMEM)
    return pl.pallas_call(
        attend_kernel,
        in_specs=[pl.BlockSpec(memory_space=pltpu.SMEM)] + [whole] * (PLANE + SLOTS + 1),
        out_specs=[whole] * (PLANE + 1),
        out_shape=[jax.ShapeDtypeStruct((tokens, WIDTH), jnp.bfloat16)] * PLANE
        + [jax.ShapeDtypeStruct((PLANE * PIECE, HEAD_DIM), jnp.float32)],
        compiler_params=params(),
        cost_estimate=pl.CostEstimate(
            flops=4 * PLANE * tokens * KEYS * WIDTH, bytes_accessed=5_000_000, transcendentals=2_000_000
        ),
        name="attend",
    )(starts, *queries, *slots, bias)


def join_kernel(place, *refs):
    shares, levels = refs[:PLANE], refs[PLANE : 2 * PLANE]
    w_ref = refs[2 * PLANE]
    outs = refs[2 * PLANE + 1 : 2 * PLANE + 1 + N_HEAD]
    joined = refs[-1]
    level = [ref[...] for ref in levels]
    top = functools.reduce(jnp.maximum, level)
    weight = [jnp.exp2(value - top) for value in level]
    scale = 1.0 / functools.reduce(jnp.add, weight)
    weight = [value * scale for value in weight]
    for c in range(TILE_COLS):
        rows = slice(c * PIECE, (c + 1) * PIECE)
        for h in range(HEADS_HERE):
            head = slice(h * HEAD_DIM, (h + 1) * HEAD_DIM)
            lane = HEADS_HERE * c + h
            total = None
            for k in range(PLANE):
                term = weight[k][:, lane : lane + 1] * shares[k][rows, head].astype(jnp.float32)
                total = term if total is None else total + term
            joined[rows, head] = total.astype(jnp.bfloat16)
    attended = joined[...]
    for k in range(N_HEAD):
        columns = pl.ds(pl.multiple_of(place[k] * WIDTH, WIDTH), WIDTH)
        outs[k][...] = jnp.dot(
            attended, w_ref[:, columns], preferred_element_type=jnp.float32
        ).astype(jnp.bfloat16)


def join(place, shares, levels, w_out):
    tokens = TILE_COLS * PIECE
    whole = pl.BlockSpec(memory_space=pltpu.VMEM)
    return pl.pallas_call(
        join_kernel,
        in_specs=[pl.BlockSpec(memory_space=pltpu.SMEM)] + [whole] * (2 * PLANE + 1),
        out_specs=[whole] * N_HEAD,
        out_shape=[jax.ShapeDtypeStruct((tokens, WIDTH), jnp.bfloat16)] * N_HEAD,
        scratch_shapes=[pltpu.VMEM((tokens, WIDTH), jnp.bfloat16)],
        compiler_params=params(),
        cost_estimate=pl.CostEstimate(
            flops=2 * tokens * WIDTH * D, bytes_accessed=5_000_000, transcendentals=0
        ),
        name="join",
    )(place, *shares, *levels, w_out)


def total_kernel(picks, *refs):
    terms, (out_ref, rows) = refs[:N_HEAD], refs[N_HEAD:]
    total = terms[0][...].astype(jnp.float32)
    for ref in terms[1:]:
        total = total + ref[...].astype(jnp.float32)
    rows[...] = total.astype(jnp.bfloat16)

    def copy(d, carry):
        start = pl.multiple_of(picks[d] * PIECE, PIECE)
        to = pl.multiple_of(d * PIECE, PIECE)
        out_ref[pl.ds(to, PIECE), :] = rows[pl.ds(start, PIECE), :]
        return carry

    lax.fori_loop(0, TILES, copy, 0)


def add_terms(picks, terms):
    tokens = TILE_COLS * PIECE
    whole = pl.BlockSpec(memory_space=pltpu.VMEM)
    return pl.pallas_call(
        total_kernel,
        in_specs=[pl.BlockSpec(memory_space=pltpu.SMEM)] + [whole] * N_HEAD,
        out_specs=whole,
        out_shape=jax.ShapeDtypeStruct((TILES * PIECE, WIDTH), jnp.bfloat16),
        scratch_shapes=[pltpu.VMEM((tokens, WIDTH), jnp.bfloat16)],
        compiler_params=params(),
        cost_estimate=pl.CostEstimate(flops=800_000, bytes_accessed=3_000_000, transcendentals=0),
        name="add_terms",
    )(picks, *terms)


def tile_kernel(row, arrived, out_ref):
    base = row[0] * (TILE * PIECE)
    pieces = [
        arrived[pl.ds(pl.multiple_of(base + j * PIECE, PIECE), PIECE), :].astype(jnp.float32)
        for j in range(TILE)
    ]
    parts = [
        pieces[j][f * TILE : (f + 1) * TILE] for f in range(FRAMES) for j in range(TILE)
    ]
    out_ref[...] = jnp.concatenate(parts, axis=0).astype(jnp.bfloat16)


def to_tile(row, arrived):
    whole = pl.BlockSpec(memory_space=pltpu.VMEM)
    return pl.pallas_call(
        tile_kernel,
        in_specs=[pl.BlockSpec(memory_space=pltpu.SMEM), whole],
        out_specs=whole,
        out_shape=jax.ShapeDtypeStruct((TILE_TOKENS, WIDTH), jnp.bfloat16),
        compiler_params=params(),
        cost_estimate=pl.CostEstimate(flops=100_000, bytes_accessed=1_000_000, transcendentals=0),
        name="to_tile",
    )(row, arrived)


def head_swap(array, k):
    return lax.ppermute(array, "head", [(h, h ^ k) for h in range(N_HEAD)])


def plane_swap(array, k):
    return lax.ppermute(array, "seq", [(s, s ^ k) for s in range(PLANE * PLANES)])


def shift(array, d):
    pairs = [
        (z * PLANE + i, (z + d) * PLANE + i)
        for z in range(PLANES)
        if 0 <= z + d < PLANES
        for i in range(PLANE)
    ]
    return lax.ppermute(array, "seq", pairs)


def local(latent, w_qkv, q_gain, k_gain, w_out, neighbours, tile_owner):
    position = lax.axis_index("seq")
    group = lax.axis_index("head")
    plane = position // PLANE
    odd = plane % 2
    tile_row = position // TILE
    place = jnp.bitwise_xor(group, jnp.arange(N_HEAD, dtype=jnp.int32))

    piece = latent.reshape(PIECE, D)
    pieces = [piece] + [head_swap(piece, k) for k in range(1, N_HEAD)]
    gains = jnp.stack([q_gain, k_gain])
    queries, keys = project(place, pieces, w_qkv.reshape(D, 3 * WIDTH), gains)

    all_queries = [queries] + [plane_swap(queries, k) for k in range(1, PLANE)]
    below_1, above_1 = shift(keys, 1), shift(keys, -1)
    below_2, above_2 = shift(below_1, 1), shift(above_1, -1)
    far = plane_swap(jnp.where(odd == 1, above_2, below_2), PLANE)
    slots = [keys, below_1, above_1, below_2, above_2, far]

    lists = lax.dynamic_slice_in_dim(neighbours, tile_row * TILE_COLS, TILE_COLS, 0)
    columns = jnp.where(lists >= 0, lists % TILE_COLS, TILE_COLS)
    starts = jnp.minimum(jnp.min(columns, axis=1), TILE_COLS - 3)
    slot_plane = plane + jnp.stack(
        [jnp.int32(0), jnp.int32(-1), jnp.int32(1), jnp.int32(-2), jnp.int32(2), 3 - 6 * odd]
    )
    inside = (slot_plane >= 0) & (slot_plane < PLANES)
    key_tile = (slot_plane // 2)[None, :, None] * TILE_COLS + (
        starts[:, None, None] + jnp.arange(3, dtype=jnp.int32)[None, None, :]
    )
    allowed = jnp.any(key_tile[..., None] == lists[:, None, None, :], axis=-1) & inside[None, :, None]
    bias = jnp.where(allowed, 0.0, -jnp.inf).astype(jnp.float32)
    bias = jnp.broadcast_to(bias[..., None], (TILE_COLS, SLOTS, 3, PIECE)).reshape(TILE_COLS, 1, KEYS)

    *shares, level = attend(starts, all_queries, slots, bias)
    levels = [level[k * PIECE : (k + 1) * PIECE] for k in range(PLANE)]
    shares = [shares[0]] + [plane_swap(shares[k], k) for k in range(1, PLANE)]
    levels = [levels[0]] + [plane_swap(levels[k], k) for k in range(1, PLANE)]

    terms = join(place, shares, levels, w_out)
    terms = [terms[0]] + [head_swap(terms[k], k) for k in range(1, N_HEAD)]

    numbers = jnp.arange(TILES, dtype=jnp.int32)
    owned = tile_owner[None, :] == numbers[:, None]
    tile_of = jnp.sum(jnp.where(owned, numbers[None, :], 0), axis=1)
    sent = add_terms(tile_of % TILE_COLS, terms)
    arrived = lax.all_to_all(
        sent.reshape(TILES, PIECE, WIDTH), "seq", split_axis=0, concat_axis=0, tiled=True
    )
    own_row = (tile_of[position] // TILE_COLS).reshape(1)
    return to_tile(own_row, arrived.reshape(TILES * PIECE, WIDTH)).reshape(1, TILE_TOKENS, WIDTH)


def solution(mesh):
    placed = (
        P(None, "seq", "head", None),
        P(None, None, "head"),
        P(),
        P(),
        P("head", None),
        P(),
        P(),
    )
    return jax.shard_map(
        local, mesh=mesh, in_specs=placed, out_specs=P("seq", None, "head"), check_vma=False
    )
```

time: 413 us -> 186 us (0.45)
  waiting for transfers between devices: 272 us -> 67.7 us
  starting transfers between devices: 8.85 us -> 59.6 us
  local copies, waits for them, and re-layouts: 73.9 us -> 32.9 us
  Pallas kernels: 0 us -> 19.7 us
  matrix products: 19.1 us -> 0 us
  other arithmetic: 20.9 us -> 2.32 us
  between operations: 15.5 us -> 2.86 us
    all_to_all x1, waiting for transfers between devices: 150 us -> 20.1 us  [local(): lax.all_to_all(sent.reshape(TILES, PIECE, WIDTH), 'seq', split_axis=0, co...]
    unnamed x3 -> x0, waiting for transfers between devices: 76.3 us -> none
    ppermute x0 -> x28, starting transfers between devices: none -> 50.3 us  [the longest x14 31 us: head_swap(): return lax.ppermute(array, 'head', [(h, h ^ k) for h in range(N_HEAD)])]
    ppermute x0 -> x28, waiting for transfers between devices: none -> 47.6 us  [the longest x14 20.2 us: head_swap(): return lax.ppermute(array, 'head', [(h, h ^ k) for h in range(N_HEAD)])]
    all_gather x1 -> x0, waiting for transfers between devices: 46.1 us -> none  [local(): shard_piece = lax.all_gather(latent, 'head', axis=2, tiled=True)]
    pallas_call x0 -> x5, Pallas kernels: none -> 19.7 us  [the longest x1 9.93 us: attend(): pl.pallas_call(attend_kernel, in_specs=[pl.BlockSpec(memory_space=pltpu.S...]
    dot_general x8 -> x0, matrix products: 19.1 us -> none  [the longest x3 5.82 us: attend(): jnp.einsum('tqk,tkd->tqd', probabilities, head_values, preferred_element_...]
    another operation x6 -> x1, local copies, waits for them, and re-layouts: 15.9 us -> 0.08 us  [local(): jnp.stack([jnp.int32(0), jnp.int32(-1), jnp.int32(1), jnp.int32(-2), jnp....]
  transfers between devices with their start and end apart: 3 -> 29, of which waited for: 3 -> 12; matrix products, arithmetic and copies ran while one was open for 4% -> 12% of each run, Pallas kernels for 0% -> 0%
where the time goes in v1:
time: 186 us; the launch traced here: 185 us
  waiting for transfers between devices  67.7 us (36%)
  starting transfers between devices  59.6 us (32%)
  local copies, waits for them, and re-layouts  32.9 us (18%)
  Pallas kernels  19.7 us (11%)
  between operations  2.86 us (2%)
  other arithmetic  2.32 us (1%)
    ppermute x14, starting transfers between devices, head_swap(): return lax.ppermute(array, 'head', [(h, h ^ k) for h in range(N_HEAD)])  31 us
    unnamed x33, local copies, waits for them, and re-layouts  21.7 us
    ppermute x14, waiting for transfers between devices, head_swap(): return lax.ppermute(array, 'head', [(h, h ^ k) for h in range(N_HEAD)])  20.2 us
    all_to_all x1, waiting for transfers between devices, local(): lax.all_to_all(sent.reshape(TILES, PIECE, WIDTH), 'seq', split_axis=0, co...  20.1 us
    ppermute x10, waiting for transfers between devices, plane_swap(): lax.ppermute(array, 'seq', [(s, s ^ k) for s in range(PLANE * PLANES)])  15.8 us
    ppermute x4, waiting for transfers between devices, shift(): return lax.ppermute(array, 'seq', pairs)  11.6 us
    ppermute x4, starting transfers between devices, shift(): return lax.ppermute(array, 'seq', pairs)  10.8 us
    reshape x1, local copies, waits for them, and re-layouts, local(): queries, keys = project(place, pieces, w_qkv.reshape(D, 3 * WIDTH), gains)  10 us
  transfers between devices with their start and end apart: 29, of which 12 were waited for; matrix products, arithmetic and copies ran while one was open for 12% of the time, Pallas kernels for 0%

profile of v1, /device:TPU:2, one launch (start us, length us, event | category | flops | bytes accessed | tf_op | source)
XLA Modules:
  0.0 185.0 jit_solution(5714600239531827586)
XLA Ops:
  0.0 2.1 %collective-permute-start = (bf16[32,3072]{1,0:T(8,128)(2,1)}, bf16[32,3072]{1,0:T(8,128)(2,1)S(1)}, u32[]{:S(2)}, u32[]{:S(2)}) collective-permute-start(bf16[32,3072]{1,0:T(8,128)(2,1)} %bitcast.11), channel_id=1, source_target_pairs={{0,1},{1,0},{2,3},{3,2},{4,5},{5,4},{6,7},{7,6},{8,9},{9,8},{10,11... | collective-permute-start | bytes 589832 | tf_op jit(solution)/shard_map/ppermute | solution.py:258
  2.1 1.6 collective-permute-start.1
  3.7 1.3 collective-permute-start.2
  5.0 3.2 %collective-permute-start.3 = (bf16[32,3072]{1,0:T(8,128)(2,1)}, bf16[32,3072]{1,0:T(8,128)(2,1)S(1)}, u32[]{:S(2)}, u32[]{:S(2)}) collective-permute-start(bf16[32,3072]{1,0:T(8,128)(2,1)} %bitcast.14), channel_id=1, source_target_pairs={{0,4},{1,5},{2,6},{3,7},{4,0},{5,1},{6,2},{7,3},{8,12},{9,13},{10,... | collective-permute-start | bytes 589832 | tf_op jit(solution)/shard_map/ppermute | solution.py:258
  8.2 1.9 %collective-permute-start.4 = (bf16[32,3072]{1,0:T(8,128)(2,1)}, bf16[32,3072]{1,0:T(8,128)(2,1)S(1)}, u32[]{:S(2)}, u32[]{:S(2)}) collective-permute-start(bf16[32,3072]{1,0:T(8,128)(2,1)} %bitcast.15), channel_id=1, source_target_pairs={{0,5},{1,4},{2,7},{3,6},{4,1},{5,0},{6,3},{7,2},{8,13},{9,12},{10,... | collective-permute-start | bytes 589832 | tf_op jit(solution)/shard_map/ppermute | solution.py:258
  10.1 10.3 %copy.14 = bf16[3072,3,384]{0,2,1:T(8,128)(2,1)} copy(bf16[3072,3,384]{2,0,1:T(8,128)(2,1)} %param.8) | data formatting | bytes 14155776 | tf_op args[1]
  20.4 10.0 %copy.15.refs_8_ = bf16[3072,1152]{1,0:T(8,128)(2,1)} copy(bf16[3072,1152]{0,1:T(8,128)(2,1)} %bitcast.19) | data formatting | bytes 14155776 | tf_op jit(solution)/shard_map/reshape | solution.py:286
  30.5 3.1 %collective-permute-start.5 = (bf16[32,3072]{1,0:T(8,128)(2,1)S(1)}, bf16[32,3072]{1,0:T(8,128)(2,1)S(1)}, u32[]{:S(2)}, u32[]{:S(2)}) collective-permute-start(bf16[32,3072]{1,0:T(8,128)(2,1)S(1)} %bitcast.16), channel_id=1, source_target_pairs={{0,6},{1,7},{2,4},{3,5},{4,2},{5,3},{6,0},{7,1},{8,14},{9,15},{10,... | collective-permute-start | bytes 589832 | tf_op jit(solution)/shard_map/ppermute | solution.py:258
  33.6 1.1 collective-permute-start.6
  34.8 6.2 %collective-permute-done.5.refs_6_ = bf16[32,3072]{1,0:T(8,128)(2,1)S(1)} collective-permute-done((bf16[32,3072]{1,0:T(8,128)(2,1)S(1)}, bf16[32,3072]{1,0:T(8,128)(2,1)S(1)}, u32[]{:S(2)}, u32[]{:S(2)}) %collective-permute-start.5) | collective-permute-done | bytes 196640 | tf_op jit(solution)/shard_map/ppermute | solution.py:258
  41.0 1.9 %collective-permute-done.6.refs_7_ = bf16[32,3072]{1,0:T(8,128)(2,1)S(1)} collective-permute-done((bf16[32,3072]{1,0:T(8,128)(2,1)S(1)}, bf16[32,3072]{1,0:T(8,128)(2,1)S(1)}, u32[]{:S(2)}, u32[]{:S(2)}) %collective-permute-start.6) | collective-permute-done | bytes 196640 | tf_op jit(solution)/shard_map/ppermute | solution.py:258
  42.9 3.0 %copy-done = bf16[3072,1152]{1,0:T(8,128)(2,1)S(1)} copy-done((bf16[3072,1152]{1,0:T(8,128)(2,1)S(1)}, bf16[3072,1152]{1,0:T(8,128)(2,1)}, u32[]{:S(2)}) %copy-start) | copy-done | bytes 7077912
  45.9 4.9 %project.1 = (bf16[256,384]{1,0:T(8,128)(2,1)S(1)}, bf16[256,768]{1,0:T(8,128)(2,1)S(1)}) custom-call(s32[8]{0:T(128)S(1)} %iota_xor_fusion.place, bf16[32,3072]{1,0:T(8,128)(2,1)S(1)} %bitcast.18, bf16[32,3072]{1,0:T(8,128)(2,1)S(1)} %collective-permute-done.refs_1_, bf16[32,3072]{1,0:T(8,128)(2,1)S(1)} %collective-permute-done.1.refs_2_, ...), custom_call_target="tpu_custom_call" | custom-call | flops 1811939328 | bytes 10000000 | tf_op jit(solution)/shard_map/project/pallas_call | solution.py:85
  50.8 0.7 copy-done.9
  51.5 3.8 %collective-permute-start.10 = (bf16[256,768]{1,0:T(8,128)(2,1)S(1)}, bf16[256,768]{1,0:T(8,128)(2,1)S(1)}, u32[]{:S(2)}, u32[]{:S(2)}) collective-permute-start(bf16[256,768]{1,0:T(8,128)(2,1)S(1)} %get-tuple-element.21.refs_4_), channel_id=1, source_target_pairs={{0,32},{8,40},{16,48},{24,56},{32,64},{40,72},{48,80},{56,88},{64,... | collective-permute-start | bytes 1179656 | tf_op jit(solution)/shard_map/ppermute | solution.py:272
  55.3 1.3 collective-permute-start.11
  56.6 0.7 copy-done.3
  57.4 3.4 %collective-permute-done.10.refs_5_ = bf16[256,768]{1,0:T(8,128)(2,1)S(1)} collective-permute-done((bf16[256,768]{1,0:T(8,128)(2,1)S(1)}, bf16[256,768]{1,0:T(8,128)(2,1)S(1)}, u32[]{:S(2)}, u32[]{:S(2)}) %collective-permute-start.10) | collective-permute-done | bytes 393248 | tf_op jit(solution)/shard_map/ppermute | solution.py:272
  60.8 4.4 %collective-permute-start.12 = (bf16[256,768]{1,0:T(8,128)(2,1)S(1)}, bf16[256,768]{1,0:T(8,128)(2,1)S(1)}, u32[]{:S(2)}, u32[]{:S(2)}) collective-permute-start(bf16[256,768]{1,0:T(8,128)(2,1)S(1)} %collective-permute-done.10.refs_5_), channel_id=1, source_target_pairs={{0,32},{8,40},{16,48},{24,56},{32,64},{40,72},{48,80},{56,88},{64,... | collective-permute-start | bytes 1179656 | tf_op jit(solution)/shard_map/ppermute | solution.py:272
  65.2 0.8 copy-done.5
  66.0 1.3 collective-permute-start.13
  67.3 0.7 copy-done.7
  68.1 2.4 %collective-permute-done.12.refs_7_ = bf16[256,768]{1,0:T(8,128)(2,1)S(1)} collective-permute-done((bf16[256,768]{1,0:T(8,128)(2,1)S(1)}, bf16[256,768]{1,0:T(8,128)(2,1)S(1)}, u32[]{:S(2)}, u32[]{:S(2)}) %collective-permute-start.12) | collective-permute-done | bytes 393248 | tf_op jit(solution)/shard_map/ppermute | solution.py:272
  70.5 5.8 %collective-permute-done.13.refs_8_ = bf16[256,768]{1,0:T(8,128)(2,1)S(1)} collective-permute-done((bf16[256,768]{1,0:T(8,128)(2,1)S(1)}, bf16[256,768]{1,0:T(8,128)(2,1)S(1)}, u32[]{:S(2)}, u32[]{:S(2)}) %collective-permute-start.13) | collective-permute-done | bytes 393248 | tf_op jit(solution)/shard_map/ppermute | solution.py:272
  76.3 0.8 broadcast_select_fusion
  77.1 1.8 collective-permute-start.14
  79.0 0.5 compare_reduce_fusion
  79.6 1.5 collective-permute-start.8
  81.1 0.3 collective-permute-start.9
  81.5 0.1 copy.17
  81.6 0.1 broadcast_in_dim.41
  81.7 0.1 reshape.150.refs_10_
  81.9 0.7 copy-done.11
  82.6 5.1 %collective-permute-done.8.refs_2_ = bf16[256,384]{1,0:T(8,128)(2,1)} collective-permute-done((bf16[256,384]{1,0:T(8,128)(2,1)}, bf16[256,384]{1,0:T(8,128)(2,1)}, u32[]{:S(2)}, u32[]{:S(2)}) %collective-permute-start.8) | collective-permute-done | bytes 196640 | tf_op jit(solution)/shard_map/ppermute | solution.py:262
  87.7 3.3 %collective-permute-done.9.refs_3_ = bf16[256,384]{1,0:T(8,128)(2,1)} collective-permute-done((bf16[256,384]{1,0:T(8,128)(2,1)}, bf16[256,384]{1,0:T(8,128)(2,1)}, u32[]{:S(2)}, u32[]{:S(2)}) %collective-permute-start.9) | collective-permute-done | bytes 196640 | tf_op jit(solution)/shard_map/ppermute | solution.py:262
  90.9 1.0 copy-done.4
  91.9 1.0 copy-done.6
  92.9 1.0 copy-done.8
  93.9 0.9 copy-done.10
  94.9 0.9 copy-done.12
  95.8 9.9 %attend.1 = (bf16[256,384]{1,0:T(8,128)(2,1)S(1)}, bf16[256,384]{1,0:T(8,128)(2,1)S(1)}, bf16[256,384]{1,0:T(8,128)(2,1)S(1)}, bf16[256,384]{1,0:T(8,128)(2,1)S(1)}, f32[128,128]{1,0:T(8,128)S(1)}) custom-call(s32[8]{0:T(128)S(1)} %broadcast_minimum_fusion.starts, bf16[256,384]{1,0:T(8,128)(2,1)S(1)} %copy-done.10, bf16[256,384]{1,0:T(8,128)(2,1)S(1)} %copy-done.12, ...), custom_call_target="tpu_custom_call" | custom-call | flops 905969664 | bytes 5000000 | tf_op jit(solution)/shard_map/attend/pallas_call | solution.py:142
  105.7 0.4 collective-permute-start.15
  106.1 1.4 collective-permute-start.16
  107.5 0.1 collective-permute-start.17
  107.7 0.6 collective-permute-start.18
  108.3 1.4 collective-permute-start.19
  109.7 0.8 collective-permute-start.20
  110.5 7.4 %collective-permute-done.19.refs_6_ = f32[32,128]{1,0:T(8,128)S(1)} collective-permute-done((f32[32,128]{1,0:T(8,128)S(1)}, f32[32,128]{1,0:T(8,128)S(1)}, u32[]{:S(2)}, u32[]{:S(2)}) %collective-permute-start.19) | collective-permute-done | bytes 16416 | tf_op jit(solution)/shard_map/ppermute | solution.py:262
  117.9 2.2 %join.1 = (bf16[256,384]{1,0:T(8,128)(2,1)S(1)}, bf16[256,384]{1,0:T(8,128)(2,1)S(1)}, bf16[256,384]{1,0:T(8,128)(2,1)S(1)}, bf16[256,384]{1,0:T(8,128)(2,1)S(1)...) custom-call(s32[8]{0:T(128)S(1)} %iota_xor_fusion.place, ...), custom_call_target="tpu_custom_call" | custom-call | flops 603979776 | bytes 5000000 | tf_op jit(solution)/shard_map/join/pallas_call | solution.py:187
  120.1 1.5 collective-permute-start.21
  121.6 0.8 select_reduce_fusion
  122.4 3.7 %collective-permute-start.23 = (bf16[256,384]{1,0:T(8,128)(2,1)S(1)}, bf16[256,384]{1,0:T(8,128)(2,1)S(1)}, u32[]{:S(2)}, u32[]{:S(2)}) collective-permute-start(bf16[256,384]{1,0:T(8,128)(2,1)S(1)} %get-tuple-element.30), channel_id=1, source_target_pairs={{0,3},{1,2},{2,1},{3,0},{4,7},{5,6},{6,5},{7,4},{8,11},{9,10},{10,... | collective-permute-start | bytes 589832 | tf_op jit(solution)/shard_map/ppermute | solution.py:258
  126.1 1.9 %collective-permute-start.24 = (bf16[256,384]{1,0:T(8,128)(2,1)S(1)}, bf16[256,384]{1,0:T(8,128)(2,1)S(1)}, u32[]{:S(2)}, u32[]{:S(2)}) collective-permute-start(bf16[256,384]{1,0:T(8,128)(2,1)S(1)} %get-tuple-element.31), channel_id=1, source_target_pairs={{0,4},{1,5},{2,6},{3,7},{4,0},{5,1},{6,2},{7,3},{8,12},{9,13},{10,... | collective-permute-start | bytes 589832 | tf_op jit(solution)/shard_map/ppermute | solution.py:258
  128.0 2.4 %collective-permute-start.25 = (bf16[256,384]{1,0:T(8,128)(2,1)S(1)}, bf16[256,384]{1,0:T(8,128)(2,1)S(1)}, u32[]{:S(2)}, u32[]{:S(2)}) collective-permute-start(bf16[256,384]{1,0:T(8,128)(2,1)S(1)} %get-tuple-element.32), channel_id=1, source_target_pairs={{0,5},{1,4},{2,7},{3,6},{4,1},{5,0},{6,3},{7,2},{8,13},{9,12},{10,... | collective-permute-start | bytes 589832 | tf_op jit(solution)/shard_map/ppermute | solution.py:258
  130.4 2.5 %collective-permute-start.26 = (bf16[256,384]{1,0:T(8,128)(2,1)S(1)}, bf16[256,384]{1,0:T(8,128)(2,1)S(1)}, u32[]{:S(2)}, u32[]{:S(2)}) collective-permute-start(bf16[256,384]{1,0:T(8,128)(2,1)S(1)} %get-tuple-element.33), channel_id=1, source_target_pairs={{0,6},{1,7},{2,4},{3,5},{4,2},{5,3},{6,0},{7,1},{8,14},{9,15},{10,... | collective-permute-start | bytes 589832 | tf_op jit(solution)/shard_map/ppermute | solution.py:258
  133.0 4.3 %collective-permute-done.22.refs_2_ = bf16[256,384]{1,0:T(8,128)(2,1)S(1)} collective-permute-done((bf16[256,384]{1,0:T(8,128)(2,1)S(1)}, bf16[256,384]{1,0:T(8,128)(2,1)S(1)}, u32[]{:S(2)}, u32[]{:S(2)}) %collective-permute-start.22) | collective-permute-done | bytes 196640 | tf_op jit(solution)/shard_map/ppermute | solution.py:258
  137.3 4.7 %collective-permute-start.27 = (bf16[256,384]{1,0:T(8,128)(2,1)S(1)}, bf16[256,384]{1,0:T(8,128)(2,1)S(1)}, u32[]{:S(2)}, u32[]{:S(2)}) collective-permute-start(bf16[256,384]{1,0:T(8,128)(2,1)S(1)} %get-tuple-element.34), channel_id=1, source_target_pairs={{0,7},{1,6},{2,5},{3,4},{4,3},{5,2},{6,1},{7,0},{8,15},{9,14},{10,... | collective-permute-start | bytes 589832 | tf_op jit(solution)/shard_map/ppermute | solution.py:258
  142.0 2.9 %collective-permute-done.24.refs_4_ = bf16[256,384]{1,0:T(8,128)(2,1)S(1)} collective-permute-done((bf16[256,384]{1,0:T(8,128)(2,1)S(1)}, bf16[256,384]{1,0:T(8,128)(2,1)S(1)}, u32[]{:S(2)}, u32[]{:S(2)}) %collective-permute-start.24) | collective-permute-done | bytes 196640 | tf_op jit(solution)/shard_map/ppermute | solution.py:258
  144.9 4.9 %collective-permute-done.26.refs_6_ = bf16[256,384]{1,0:T(8,128)(2,1)S(1)} collective-permute-done((bf16[256,384]{1,0:T(8,128)(2,1)S(1)}, bf16[256,384]{1,0:T(8,128)(2,1)S(1)}, u32[]{:S(2)}, u32[]{:S(2)}) %collective-permute-start.26) | collective-permute-done | bytes 196640 | tf_op jit(solution)/shard_map/ppermute | solution.py:258
  149.8 1.9 %add_terms.1 = bf16[1024,384]{1,0:T(8,128)(2,1)} custom-call(s32[32]{0:T(128)S(1)} %and_select_fusion.2.picks, bf16[256,384]{1,0:T(8,128)(2,1)S(1)} %get-tuple-element.27.refs_0_, bf16[256,384]{1,0:T(8,128)(2,1)S(1)} %collective-permute-done.21.refs_1_, bf16[256,384]{1,0:T(8,128)(2,1)S(1)} %collective-permute-done.22.refs_2_, ...), custom_call_target="tpu_custom_call" | custom-call | flops 800000 | bytes 3000000 | tf_op jit(solution)/shard_map/add_terms/pallas_call | solution.py:220
  151.7 9.3 %all-to-all-start = ((bf16[32,32,384]{2,1,0:T(8,128)(2,1)}), bf16[32,32,384]{2,1,0:T(8,128)(2,1)S(1)}, u32[]{:S(2)}, u32[]{:S(2)}) async-start(bf16[32,32,384]{2,1,0:T(8,128)(2,1)} %bitcast.7), calls=%async_computation | async-start | bytes 1572864 | tf_op jit(solution)/shard_map/all_to_all | solution.py:320
  161.0 0.6 dynamic_slice.6
  164.2 20.1 %all-to-all-done = bf16[32,32,384]{2,1,0:T(8,128)(2,1)S(1)} async-done(((bf16[32,32,384]{2,1,0:T(8,128)(2,1)}), bf16[32,32,384]{2,1,0:T(8,128)(2,1)S(1)}, u32[]{:S(2)}, u32[]{:S(2)}) %all-to-all-start) | async-done | bytes 786464 | tf_op jit(solution)/shard_map/all_to_all | solution.py:320
  184.3 0.7 to_tile.1
  (53 shorter events, 0.6 us)
Async XLA Ops:
  0.0 30.5 %collective-permute-start = (bf16[32,3072]{1,0:T(8,128)(2,1)}, bf16[32,3072]{1,0:T(8,128)(2,1)S(1)}, u32[]{:S(2)}, u32[]{:S(2)}) collective-permute-start(bf16[32,3072]{1,0:T(8,128)(2,1)} %bitcast.11), channel_id=1, source_target_pairs={{0,1},{1,0},{2,3},{3,2},{4,5},{5,4},{6,7},{7,6},{8,9},{9,8},{10,11... | collective-permute-start | bytes 589832 | tf_op jit(solution)/shard_map/ppermute | solution.py:258
  2.1 31.5 %collective-permute-start.1 = (bf16[32,3072]{1,0:T(8,128)(2,1)}, bf16[32,3072]{1,0:T(8,128)(2,1)S(1)}, u32[]{:S(2)}, u32[]{:S(2)}) collective-permute-start(bf16[32,3072]{1,0:T(8,128)(2,1)} %bitcast.12), channel_id=1, source_target_pairs={{0,2},{1,3},{2,0},{3,1},{4,6},{5,7},{6,4},{7,5},{8,10},{9,11},{10,... | collective-permute-start | bytes 589832 | tf_op jit(solution)/shard_map/ppermute | solution.py:258
  3.7 31.1 %collective-permute-start.2 = (bf16[32,3072]{1,0:T(8,128)(2,1)}, bf16[32,3072]{1,0:T(8,128)(2,1)S(1)}, u32[]{:S(2)}, u32[]{:S(2)}) collective-permute-start(bf16[32,3072]{1,0:T(8,128)(2,1)} %bitcast.13), channel_id=1, source_target_pairs={{0,3},{1,2},{2,1},{3,0},{4,7},{5,6},{6,5},{7,4},{8,11},{9,10},{10,... | collective-permute-start | bytes 589832 | tf_op jit(solution)/shard_map/ppermute | solution.py:258
  5.0 29.8 %collective-permute-start.3 = (bf16[32,3072]{1,0:T(8,128)(2,1)}, bf16[32,3072]{1,0:T(8,128)(2,1)S(1)}, u32[]{:S(2)}, u32[]{:S(2)}) collective-permute-start(bf16[32,3072]{1,0:T(8,128)(2,1)} %bitcast.14), channel_id=1, source_target_pairs={{0,4},{1,5},{2,6},{3,7},{4,0},{5,1},{6,2},{7,3},{8,12},{9,13},{10,... | collective-permute-start | bytes 589832 | tf_op jit(solution)/shard_map/ppermute | solution.py:258
  8.2 26.6 %collective-permute-start.4 = (bf16[32,3072]{1,0:T(8,128)(2,1)}, bf16[32,3072]{1,0:T(8,128)(2,1)S(1)}, u32[]{:S(2)}, u32[]{:S(2)}) collective-permute-start(bf16[32,3072]{1,0:T(8,128)(2,1)} %bitcast.15), channel_id=1, source_target_pairs={{0,5},{1,4},{2,7},{3,6},{4,1},{5,0},{6,3},{7,2},{8,13},{9,12},{10,... | collective-permute-start | bytes 589832 | tf_op jit(solution)/shard_map/ppermute | solution.py:258
  20.3 10.1 %copy-start.14 = (f32[128]{0:T(128)S(1)}, f32[128]{0:T(128)}, u32[]{:S(2)}) copy-start(f32[128]{0:T(128)} %param.10) | copy-start | bytes 1540
  20.3 10.1 %copy-start.15 = (f32[128]{0:T(128)S(1)}, f32[128]{0:T(128)}, u32[]{:S(2)}) copy-start(f32[128]{0:T(128)} %param.9) | copy-start | bytes 1540
  20.4 10.2 %copy-start.2 = (bf16[4,1,8,3072]{3,2,1,0:T(8,128)(2,1)S(1)}, bf16[4,1,8,3072]{3,2,1,0:T(8,128)(2,1)}, u32[]{:S(2)}) copy-start(bf16[4,1,8,3072]{3,2,1,0:T(8,128)(2,1)} %param.7) | copy-start | bytes 589828
  20.4 14.3 %copy-start.13 = (s32[32,9]{0,1:T(8,128)S(1)}, s32[32,9]{0,1:T(8,128)}, u32[]{:S(2)}) copy-start(s32[32,9]{0,1:T(8,128)} %param.12) | copy-start | bytes 3460
  30.5 10.5 %collective-permute-start.5 = (bf16[32,3072]{1,0:T(8,128)(2,1)S(1)}, bf16[32,3072]{1,0:T(8,128)(2,1)S(1)}, u32[]{:S(2)}, u32[]{:S(2)}) collective-permute-start(bf16[32,3072]{1,0:T(8,128)(2,1)S(1)} %bitcast.16), channel_id=1, source_target_pairs={{0,6},{1,7},{2,4},{3,5},{4,2},{5,3},{6,0},{7,1},{8,14},{9,15},{10,... | collective-permute-start | bytes 589832 | tf_op jit(solution)/shard_map/ppermute | solution.py:258
  33.6 9.3 %collective-permute-start.6 = (bf16[32,3072]{1,0:T(8,128)(2,1)S(1)}, bf16[32,3072]{1,0:T(8,128)(2,1)S(1)}, u32[]{:S(2)}, u32[]{:S(2)}) collective-permute-start(bf16[32,3072]{1,0:T(8,128)(2,1)S(1)} %bitcast.17), channel_id=1, source_target_pairs={{0,7},{1,6},{2,5},{3,4},{4,3},{5,2},{6,1},{7,0},{8,15},{9,14},{10,... | collective-permute-start | bytes 589832 | tf_op jit(solution)/shard_map/ppermute | solution.py:258
  42.9 3.0 %copy-start = (bf16[3072,1152]{1,0:T(8,128)(2,1)S(1)}, bf16[3072,1152]{1,0:T(8,128)(2,1)}, u32[]{:S(2)}) copy-start(bf16[3072,1152]{1,0:T(8,128)(2,1)} %copy.15.refs_8_) | copy-start | bytes 21233668
  45.9 72.0 %copy-start.1 = (bf16[384,3072]{1,0:T(8,128)(2,1)S(1)}, bf16[384,3072]{1,0:T(8,128)(2,1)}, u32[]{:S(2)}) copy-start(bf16[384,3072]{1,0:T(8,128)(2,1)} %refs_8_.1) | copy-start | bytes 7077892
  50.8 0.7 copy-start.9
  51.5 9.3 %collective-permute-start.10 = (bf16[256,768]{1,0:T(8,128)(2,1)S(1)}, bf16[256,768]{1,0:T(8,128)(2,1)S(1)}, u32[]{:S(2)}, u32[]{:S(2)}) collective-permute-start(bf16[256,768]{1,0:T(8,128)(2,1)S(1)} %get-tuple-element.21.refs_4_), channel_id=1, source_target_pairs={{0,32},{8,40},{16,48},{24,56},{32,64},{40,72},{48,80},{56,88},{64,... | collective-permute-start | bytes 1179656 | tf_op jit(solution)/shard_map/ppermute | solution.py:272
  55.3 10.7 %collective-permute-start.11 = (bf16[256,768]{1,0:T(8,128)(2,1)S(1)}, bf16[256,768]{1,0:T(8,128)(2,1)S(1)}, u32[]{:S(2)}, u32[]{:S(2)}) collective-permute-start(bf16[256,768]{1,0:T(8,128)(2,1)S(1)} %get-tuple-element.21.refs_4_), channel_id=1, source_target_pairs={{32,0},{40,8},{48,16},{56,24},{64,32},{72,40},{80,48},{88,56},{96,... | collective-permute-start | bytes 1179656 | tf_op jit(solution)/shard_map/ppermute | solution.py:272
  56.6 0.7 copy-start.3
  60.8 9.7 %collective-permute-start.12 = (bf16[256,768]{1,0:T(8,128)(2,1)S(1)}, bf16[256,768]{1,0:T(8,128)(2,1)S(1)}, u32[]{:S(2)}, u32[]{:S(2)}) collective-permute-start(bf16[256,768]{1,0:T(8,128)(2,1)S(1)} %collective-permute-done.10.refs_5_), channel_id=1, source_target_pairs={{0,32},{8,40},{16,48},{24,56},{32,64},{40,72},{48,80},{56,88},{64,... | collective-permute-start | bytes 1179656 | tf_op jit(solution)/shard_map/ppermute | solution.py:272
  65.2 0.8 copy-start.5
  66.0 10.3 %collective-permute-start.13 = (bf16[256,768]{1,0:T(8,128)(2,1)S(1)}, bf16[256,768]{1,0:T(8,128)(2,1)S(1)}, u32[]{:S(2)}, u32[]{:S(2)}) collective-permute-start(bf16[256,768]{1,0:T(8,128)(2,1)S(1)} %collective-permute-done.11.refs_6_), channel_id=1, source_target_pairs={{32,0},{40,8},{48,16},{56,24},{64,32},{72,40},{80,48},{88,56},{96,... | collective-permute-start | bytes 1179656 | tf_op jit(solution)/shard_map/ppermute | solution.py:272
  67.3 0.7 copy-start.7
  77.1 13.8 %collective-permute-start.14 = (bf16[256,768]{1,0:T(8,128)(2,1)}, bf16[256,768]{1,0:T(8,128)(2,1)}, u32[]{:S(2)}, u32[]{:S(2)}) collective-permute-start(bf16[256,768]{1,0:T(8,128)(2,1)} %broadcast_select_fusion), channel_id=1, source_target_pairs={{0,32},{8,40},{16,48},{24,56},{32,0},{40,8},{48,16},{56,24},{64,96... | collective-permute-start | bytes 1179656 | tf_op jit(solution)/shard_map/ppermute | solution.py:262
  79.5 2.4 %collective-permute-start.7 = (bf16[256,384]{1,0:T(8,128)(2,1)}, bf16[256,384]{1,0:T(8,128)(2,1)S(1)}, u32[]{:S(2)}, u32[]{:S(2)}) collective-permute-start(bf16[256,384]{1,0:T(8,128)(2,1)} %copy-done.9), channel_id=1, source_target_pairs={{0,8},{8,0},{16,24},{24,16},{32,40},{40,32},{48,56},{56,48},{64,72... | collective-permute-start | bytes 589832 | tf_op jit(solution)/shard_map/ppermute | solution.py:262
  79.6 8.1 %collective-permute-start.8 = (bf16[256,384]{1,0:T(8,128)(2,1)}, bf16[256,384]{1,0:T(8,128)(2,1)}, u32[]{:S(2)}, u32[]{:S(2)}) collective-permute-start(bf16[256,384]{1,0:T(8,128)(2,1)} %copy-done.9), channel_id=1, source_target_pairs={{0,16},{8,24},{16,0},{24,8},{32,48},{40,56},{48,32},{56,40},{64,80... | collective-permute-start | bytes 589832 | tf_op jit(solution)/shard_map/ppermute | solution.py:262
  81.1 9.9 %collective-permute-start.9 = (bf16[256,384]{1,0:T(8,128)(2,1)}, bf16[256,384]{1,0:T(8,128)(2,1)}, u32[]{:S(2)}, u32[]{:S(2)}) collective-permute-start(bf16[256,384]{1,0:T(8,128)(2,1)} %copy-done.9), channel_id=1, source_target_pairs={{0,24},{8,16},{16,8},{24,0},{32,56},{40,48},{48,40},{56,32},{64,88... | collective-permute-start | bytes 589832 | tf_op jit(solution)/shard_map/ppermute | solution.py:262
  81.9 0.7 copy-start.11
  90.9 1.0 copy-start.4
  91.9 1.0 copy-start.6
  92.9 1.0 copy-start.8
  93.9 0.9 copy-start.10
  94.9 0.9 copy-start.12
  105.7 12.2 %collective-permute-start.15 = (bf16[256,384]{1,0:T(8,128)(2,1)S(1)}, bf16[256,384]{1,0:T(8,128)(2,1)S(1)}, u32[]{:S(2)}, u32[]{:S(2)}) collective-permute-start(bf16[256,384]{1,0:T(8,128)(2,1)S(1)} %get-tuple-element.23), channel_id=1, source_target_pairs={{0,8},{8,0},{16,24},{24,16},{32,40},{40,32},{48,56},{56,48},{64,72... | collective-permute-start | bytes 589832 | tf_op jit(solution)/shard_map/ppermute | solution.py:262
  106.1 11.8 %collective-permute-start.16 = (bf16[256,384]{1,0:T(8,128)(2,1)S(1)}, bf16[256,384]{1,0:T(8,128)(2,1)S(1)}, u32[]{:S(2)}, u32[]{:S(2)}) collective-permute-start(bf16[256,384]{1,0:T(8,128)(2,1)S(1)} %get-tuple-element.24), channel_id=1, source_target_pairs={{0,16},{8,24},{16,0},{24,8},{32,48},{40,56},{48,32},{56,40},{64,80... | collective-permute-start | bytes 589832 | tf_op jit(solution)/shard_map/ppermute | solution.py:262
  107.5 10.3 %collective-permute-start.17 = (bf16[256,384]{1,0:T(8,128)(2,1)S(1)}, bf16[256,384]{1,0:T(8,128)(2,1)S(1)}, u32[]{:S(2)}, u32[]{:S(2)}) collective-permute-start(bf16[256,384]{1,0:T(8,128)(2,1)S(1)} %get-tuple-element.25), channel_id=1, source_target_pairs={{0,24},{8,16},{16,8},{24,0},{32,56},{40,48},{48,40},{56,32},{64,88... | collective-permute-start | bytes 589832 | tf_op jit(solution)/shard_map/ppermute | solution.py:262
  107.7 2.0 %collective-permute-start.18 = (f32[32,128]{1,0:T(8,128)S(1)}, f32[32,128]{1,0:T(8,128)S(1)}, u32[]{:S(2)}, u32[]{:S(2)}) collective-permute-start(f32[32,128]{1,0:T(8,128)S(1)} %get-tuple-element.39), channel_id=1, source_target_pairs={{0,8},{8,0},{16,24},{24,16},{32,40},{40,32},{48,56},{56,48},{64,72... | collective-permute-start | bytes 49160 | tf_op jit(solution)/shard_map/ppermute | solution.py:262
  108.3 9.6 %collective-permute-start.19 = (f32[32,128]{1,0:T(8,128)S(1)}, f32[32,128]{1,0:T(8,128)S(1)}, u32[]{:S(2)}, u32[]{:S(2)}) collective-permute-start(f32[32,128]{1,0:T(8,128)S(1)} %get-tuple-element.38), channel_id=1, source_target_pairs={{0,16},{8,24},{16,0},{24,8},{32,48},{40,56},{48,32},{56,40},{64,80... | collective-permute-start | bytes 49160 | tf_op jit(solution)/shard_map/ppermute | solution.py:262
  109.7 8.2 %collective-permute-start.20 = (f32[32,128]{1,0:T(8,128)S(1)}, f32[32,128]{1,0:T(8,128)S(1)}, u32[]{:S(2)}, u32[]{:S(2)}) collective-permute-start(f32[32,128]{1,0:T(8,128)S(1)} %get-tuple-element.37), channel_id=1, source_target_pairs={{0,24},{8,16},{16,8},{24,0},{32,56},{40,48},{48,40},{56,32},{64,88... | collective-permute-start | bytes 49160 | tf_op jit(solution)/shard_map/ppermute | solution.py:262
  120.1 10.3 %collective-permute-start.21 = (bf16[256,384]{1,0:T(8,128)(2,1)S(1)}, bf16[256,384]{1,0:T(8,128)(2,1)S(1)}, u32[]{:S(2)}, u32[]{:S(2)}) collective-permute-start(bf16[256,384]{1,0:T(8,128)(2,1)S(1)} %get-tuple-element.28), channel_id=1, source_target_pairs={{0,1},{1,0},{2,3},{3,2},{4,5},{5,4},{6,7},{7,6},{8,9},{9,8},{10,11... | collective-permute-start | bytes 589832 | tf_op jit(solution)/shard_map/ppermute | solution.py:258
  121.6 15.7 %collective-permute-start.22 = (bf16[256,384]{1,0:T(8,128)(2,1)S(1)}, bf16[256,384]{1,0:T(8,128)(2,1)S(1)}, u32[]{:S(2)}, u32[]{:S(2)}) collective-permute-start(bf16[256,384]{1,0:T(8,128)(2,1)S(1)} %get-tuple-element.29), channel_id=1, source_target_pairs={{0,2},{1,3},{2,0},{3,1},{4,6},{5,7},{6,4},{7,5},{8,10},{9,11},{10,... | collective-permute-start | bytes 589832 | tf_op jit(solution)/shard_map/ppermute | solution.py:258
  122.4 19.6 %collective-permute-start.23 = (bf16[256,384]{1,0:T(8,128)(2,1)S(1)}, bf16[256,384]{1,0:T(8,128)(2,1)S(1)}, u32[]{:S(2)}, u32[]{:S(2)}) collective-permute-start(bf16[256,384]{1,0:T(8,128)(2,1)S(1)} %get-tuple-element.30), channel_id=1, source_target_pairs={{0,3},{1,2},{2,1},{3,0},{4,7},{5,6},{6,5},{7,4},{8,11},{9,10},{10,... | collective-permute-start | bytes 589832 | tf_op jit(solution)/shard_map/ppermute | solution.py:258
  126.1 18.8 %collective-permute-start.24 = (bf16[256,384]{1,0:T(8,128)(2,1)S(1)}, bf16[256,384]{1,0:T(8,128)(2,1)S(1)}, u32[]{:S(2)}, u32[]{:S(2)}) collective-permute-start(bf16[256,384]{1,0:T(8,128)(2,1)S(1)} %get-tuple-element.31), channel_id=1, source_target_pairs={{0,4},{1,5},{2,6},{3,7},{4,0},{5,1},{6,2},{7,3},{8,12},{9,13},{10,... | collective-permute-start | bytes 589832 | tf_op jit(solution)/shard_map/ppermute | solution.py:258
  128.0 16.9 %collective-permute-start.25 = (bf16[256,384]{1,0:T(8,128)(2,1)S(1)}, bf16[256,384]{1,0:T(8,128)(2,1)S(1)}, u32[]{:S(2)}, u32[]{:S(2)}) collective-permute-start(bf16[256,384]{1,0:T(8,128)(2,1)S(1)} %get-tuple-element.32), channel_id=1, source_target_pairs={{0,5},{1,4},{2,7},{3,6},{4,1},{5,0},{6,3},{7,2},{8,13},{9,12},{10,... | collective-permute-start | bytes 589832 | tf_op jit(solution)/shard_map/ppermute | solution.py:258
  130.4 19.3 %collective-permute-start.26 = (bf16[256,384]{1,0:T(8,128)(2,1)S(1)}, bf16[256,384]{1,0:T(8,128)(2,1)S(1)}, u32[]{:S(2)}, u32[]{:S(2)}) collective-permute-start(bf16[256,384]{1,0:T(8,128)(2,1)S(1)} %get-tuple-element.33), channel_id=1, source_target_pairs={{0,6},{1,7},{2,4},{3,5},{4,2},{5,3},{6,0},{7,1},{8,14},{9,15},{10,... | collective-permute-start | bytes 589832 | tf_op jit(solution)/shard_map/ppermute | solution.py:258
  137.3 12.5 %collective-permute-start.27 = (bf16[256,384]{1,0:T(8,128)(2,1)S(1)}, bf16[256,384]{1,0:T(8,128)(2,1)S(1)}, u32[]{:S(2)}, u32[]{:S(2)}) collective-permute-start(bf16[256,384]{1,0:T(8,128)(2,1)S(1)} %get-tuple-element.34), channel_id=1, source_target_pairs={{0,7},{1,6},{2,5},{3,4},{4,3},{5,2},{6,1},{7,0},{8,15},{9,14},{10,... | collective-permute-start | bytes 589832 | tf_op jit(solution)/shard_map/ppermute | solution.py:258
  151.7 32.6 %all-to-all-start = ((bf16[32,32,384]{2,1,0:T(8,128)(2,1)}), bf16[32,32,384]{2,1,0:T(8,128)(2,1)S(1)}, u32[]{:S(2)}, u32[]{:S(2)}) async-start(bf16[32,32,384]{2,1,0:T(8,128)(2,1)} %bitcast.7), calls=%async_computation | async-start | bytes 1572864 | tf_op jit(solution)/shard_map/all_to_all | solution.py:320

commit v2 on v1

v2 whole, which is shorter than its diff:
```python
import functools

import jax
import jax.numpy as jnp
from jax import lax
from jax.experimental import pallas as pl
from jax.experimental.pallas import tpu as pltpu
from jax.sharding import PartitionSpec as P

D = 3072
HEAD_DIM = 128
FRAMES = 4
TILE = 8
TILE_COLS = 8
TILES = 32
TILE_TOKENS = 256
N_HEAD = 8
PLANE = 4
PLANES = 8
PIECE = FRAMES * TILE
PAIR = 2 * TILE
WIDTH = 384
HEADS_HERE = 3
SLOTS = 6
WINDOW = 3 * PIECE
SCORE_SCALE = HEAD_DIM ** (-0.5) * 1.4426950408889634

LOADS = 4

epsilon = 1e-06
LOWEST = -1e30


def params(mib):
    return pltpu.CompilerParams(vmem_limit_bytes=mib * 1024 * 1024)


def plan_kernel(ids, neighbours, tile_owner, starts, flags, tile_of, first, half):
    position = ids[0]
    tile_row = position // TILE
    odd = (position // PLANE) % 2
    for c in range(TILE_COLS):
        tile = tile_row * TILE_COLS + c
        start = jnp.int32(TILE_COLS - 3)
        for n in range(9):
            listed = neighbours[tile, n]
            start = jnp.where(listed >= 0, jnp.minimum(start, listed % TILE_COLS), start)
        starts[c] = start
        for n in range(9):
            flags[c, n] = 0
        for n in range(9):
            listed = neighbours[tile, n]

            @pl.when(listed >= 0)
            def _():
                step = listed // TILE_COLS - tile_row
                kind = jnp.where(step == 0, 0, jnp.where((step > 0) == (odd == 1), 1, 2))
                flags[c, kind * 3 + listed % TILE_COLS - start] = 1

    for t in range(TILES):
        tile_of[tile_owner[t]] = t
    first[0] = tile_of[position] // (2 * TILE_COLS)
    half[0] = tile_row % 2


def plan(ids, neighbours, tile_owner):
    scalars = pl.BlockSpec(memory_space=pltpu.SMEM)
    shapes = [(TILE_COLS,), (TILE_COLS, 9), (TILES,), (1,), (1,)]
    return pl.pallas_call(
        plan_kernel,
        in_specs=[scalars] * 3,
        out_specs=[scalars] * len(shapes),
        out_shape=[jax.ShapeDtypeStruct(shape, jnp.int32) for shape in shapes],
        compiler_params=params(8),
        cost_estimate=pl.CostEstimate(flops=0, bytes_accessed=8_000_000, transcendentals=0),
        name="plan",
    )(ids, neighbours, tile_owner)


def normed(result, gain):
    heads = []
    for h in range(HEADS_HERE):
        part = result[:, h * HEAD_DIM : (h + 1) * HEAD_DIM]
        mean = jnp.mean(part * part, axis=-1, keepdims=True)
        heads.append((part * lax.rsqrt(mean + epsilon) * gain).astype(jnp.bfloat16))
    return jnp.concatenate(heads, axis=1)


def gather_rows(ids, pieces, rows):
    for k, piece in enumerate(pieces):
        start = pl.multiple_of((ids[1] ^ k) * PIECE, PIECE)
        rows[pl.ds(start, PIECE), :] = piece[...]


def load_kernel(w_ref, out_ref, sems):
    rows = D // LOADS
    copies = []
    for n in range(3):
        for e in range(LOADS):
            part = pl.ds(e * rows, rows)
            copies.append(
                pltpu.make_async_copy(w_ref.at[n, part], out_ref.at[n, part], sems.at[n, e])
            )
    for copy in copies:
        copy.start()
    for copy in copies:
        copy.wait()


def load_weight(weight):
    return pl.pallas_call(
        load_kernel,
        in_specs=[pl.BlockSpec(memory_space=pltpu.HBM)],
        out_specs=pl.BlockSpec(memory_space=pltpu.VMEM),
        out_shape=jax.ShapeDtypeStruct(weight.shape, weight.dtype),
        scratch_shapes=[pltpu.SemaphoreType.DMA((3, LOADS))],
        compiler_params=params(8),
        cost_estimate=pl.CostEstimate(flops=0, bytes_accessed=7_100_000, transcendentals=0),
        name="load_weight",
    )(weight)


def queries_kernel(ids, *refs):
    pieces, (w_ref, gain_ref, out_ref, rows_ref) = refs[:N_HEAD], refs[N_HEAD:]
    gather_rows(ids, pieces, rows_ref)
    result = jnp.dot(rows_ref[...], w_ref[0], preferred_element_type=jnp.float32)
    out_ref[...] = normed(result, gain_ref[...])


def project_queries(ids, pieces, weight, gain):
    tokens = N_HEAD * PIECE
    whole = pl.BlockSpec(memory_space=pltpu.VMEM)
    return pl.pallas_call(
        queries_kernel,
        in_specs=[pl.BlockSpec(memory_space=pltpu.SMEM)] + [whole] * (N_HEAD + 2),
        out_specs=[whole] * 2,
        out_shape=[
            jax.ShapeDtypeStruct((tokens, WIDTH), jnp.bfloat16),
            jax.ShapeDtypeStruct((tokens, D), jnp.bfloat16),
        ],
        compiler_params=params(16),
        cost_estimate=pl.CostEstimate(
            flops=2 * tokens * D * WIDTH, bytes_accessed=4_000_000, transcendentals=0
        ),
        name="project_queries",
    )(ids, *pieces, weight, gain)


def keys_kernel(rows_ref, w_ref, gain_ref, out_ref):
    rows = rows_ref[...]
    keys = jnp.dot(rows, w_ref[1], preferred_element_type=jnp.float32)
    out_ref[:, :WIDTH] = normed(keys, gain_ref[...])
    values = jnp.dot(rows, w_ref[2], preferred_element_type=jnp.float32)
    out_ref[:, WIDTH:] = values.astype(jnp.bfloat16)


def project_keys(rows, weight, gain):
    tokens = N_HEAD * PIECE
    whole = pl.BlockSpec(memory_space=pltpu.VMEM)
    return pl.pallas_call(
        keys_kernel,
        in_specs=[whole] * 3,
        out_specs=whole,
        out_shape=jax.ShapeDtypeStruct((tokens, 2 * WIDTH), jnp.bfloat16),
        compiler_params=params(16),
        cost_estimate=pl.CostEstimate(
            flops=2 * tokens * D * 2 * WIDTH, bytes_accessed=6_000_000, transcendentals=0
        ),
        name="project_keys",
    )(rows, weight, gain)


def attend_kernel(kinds, last, starts, flags, *refs):
    count = len(kinds)
    refs = list(refs)
    take = lambda n: [refs.pop(0) for _ in range(n)]
    queries, slots = take(PLANE), take(count)
    before = take(PLANE + 1) if last else None
    outs = take(PLANE) if last else take(PLANE + 1)
    piece_of = lax.broadcasted_iota(jnp.int32, (1, count * WINDOW), 1) // PIECE
    ones = jnp.ones((count * WINDOW, HEAD_DIM), jnp.bfloat16)
    level_ref = refs.pop(0) if last else outs[PLANE]
    level_ref[...] = jnp.zeros_like(level_ref)
    for c in range(TILE_COLS):
        here = slice(c * PIECE, (c + 1) * PIECE)
        window = pl.ds(pl.multiple_of(starts[c] * PIECE, PIECE), WINDOW)
        bias = jnp.full((1, count * WINDOW), -jnp.inf, jnp.float32)
        for n in range(3 * count):
            bias = jnp.where((piece_of == n) & (flags[c, kinds[n // 3] * 3 + n % 3] > 0), 0.0, bias)
        for h in range(HEADS_HERE):
            head = slice(h * HEAD_DIM, (h + 1) * HEAD_DIM)
            value_head = slice(WIDTH + h * HEAD_DIM, WIDTH + (h + 1) * HEAD_DIM)
            lane = slice(HEADS_HERE * c + h, HEADS_HERE * c + h + 1)
            q = jnp.concatenate([ref[here, head] for ref in queries], axis=0)
            k = jnp.concatenate([slot[window, head] for slot in slots], axis=0)
            v = jnp.concatenate([slot[window, value_head] for slot in slots], axis=0)
            scores = lax.dot_general(
                q, k, (((1,), (1,)), ((), ())), preferred_element_type=jnp.float32
            )
            scores = scores * SCORE_SCALE + bias
            top = jnp.maximum(jnp.max(scores, axis=-1, keepdims=True), LOWEST)
            weights = jnp.exp2(scores - top).astype(jnp.bfloat16)
            both = jnp.dot(
                weights, jnp.concatenate([v, ones], axis=1), preferred_element_type=jnp.float32
            )
            mixed, total = both[:, :HEAD_DIM], both[:, HEAD_DIM:]
            if last:
                other = before[PLANE][:, lane]
                mixed_before = jnp.concatenate([ref[here, head] for ref in before[:PLANE]], axis=0)
                high = jnp.maximum(top, other)
                share = jnp.exp2(other - high)
                mine = jnp.exp2(top - high)
                whole = mine * total + share
                mixed = (mixed * mine + mixed_before.astype(jnp.float32) * share) / whole
                level = high + jnp.log2(whole)
            else:
                mixed = mixed / total
                level = top + jnp.log2(total)
            mixed = mixed.astype(jnp.bfloat16)
            for n in range(PLANE):
                outs[n][here, head] = mixed[n * PIECE : (n + 1) * PIECE]
            level_ref[:, lane] = level[:, lane]
    if last:
        tail = slice(TILE_COLS * PIECE, (TILE_COLS + 1) * PIECE)
        rest = level_ref[...]
        for part in range(3):
            rounded = rest.astype(jnp.bfloat16)
            rest = rest - rounded.astype(jnp.float32)
            for n in range(PLANE):
                outs[n][tail, part * HEAD_DIM : (part + 1) * HEAD_DIM] = rounded[
                    n * PIECE : (n + 1) * PIECE
                ]


def attend(starts, flags, queries, slots, before=()):
    tokens = TILE_COLS * PIECE
    count = len(slots)
    last = bool(before)
    kinds = (1, 2, 2) if last else (0, 0, 1)
    whole = pl.BlockSpec(memory_space=pltpu.VMEM)
    scalars = pl.BlockSpec(memory_space=pltpu.SMEM)
    operands = [*queries, *slots, *before]
    levels = (PLANE * PIECE, HEAD_DIM)
    if last:
        out_shape = [jax.ShapeDtypeStruct((tokens + PIECE, WIDTH), jnp.bfloat16)] * PLANE
    else:
        out_shape = [jax.ShapeDtypeStruct((tokens, WIDTH), jnp.bfloat16)] * PLANE
        out_shape.append(jax.ShapeDtypeStruct(levels, jnp.float32))
    scratch = [pltpu.VMEM(levels, jnp.float32)] if last else []
    return pl.pallas_call(
        functools.partial(attend_kernel, kinds, last),
        in_specs=[scalars] * 2 + [whole] * len(operands),
        out_specs=[whole] * len(out_shape),
        out_shape=out_shape,
        scratch_shapes=scratch,
        compiler_params=params(16),
        cost_estimate=pl.CostEstimate(
            flops=4 * PLANE * tokens * count * WINDOW * WIDTH,
            bytes_accessed=4_000_000,
            transcendentals=1_000_000,
        ),
        name="attend",
    )(starts, flags, *operands)


def join_kernel(ids, *refs):
    shares, w_ref = refs[:PLANE], refs[PLANE]
    outs, joined = refs[PLANE + 1 : PLANE + 1 + N_HEAD], refs[-1]
    tail = slice(TILE_COLS * PIECE, (TILE_COLS + 1) * PIECE)
    level = []
    for ref in shares:
        parts = [
            ref[tail, n * HEAD_DIM : (n + 1) * HEAD_DIM].astype(jnp.float32) for n in range(3)
        ]
        level.append(parts[0] + (parts[1] + parts[2]))
    top = functools.reduce(jnp.maximum, level)
    weight = [jnp.exp2(value - top) for value in level]
    scale = 1.0 / functools.reduce(jnp.add, weight)
    weight = [value * scale for value in weight]
    for c in range(TILE_COLS):
        rows = slice(c * PIECE, (c + 1) * PIECE)
        for h in range(HEADS_HERE):
            head = slice(h * HEAD_DIM, (h + 1) * HEAD_DIM)
            lane = HEADS_HERE * c + h
            total = None
            for k in range(PLANE):
                term = weight[k][:, lane : lane + 1] * shares[k][rows, head].astype(jnp.float32)
                total = term if total is None else total + term
            joined[rows, head] = total.astype(jnp.bfloat16)
    attended = joined[...]
    for k in range(N_HEAD):
        columns = pl.ds(pl.multiple_of((ids[1] ^ k) * WIDTH, WIDTH), WIDTH)
        outs[k][...] = jnp.dot(
            attended, w_ref[:, columns], preferred_element_type=jnp.float32
        ).astype(jnp.bfloat16)


def join(ids, shares, w_out):
    tokens = TILE_COLS * PIECE
    whole = pl.BlockSpec(memory_space=pltpu.VMEM)
    return pl.pallas_call(
        join_kernel,
        in_specs=[pl.BlockSpec(memory_space=pltpu.SMEM)] + [whole] * (PLANE + 1),
        out_specs=[whole] * N_HEAD,
        out_shape=[jax.ShapeDtypeStruct((tokens, WIDTH), jnp.bfloat16)] * N_HEAD,
        scratch_shapes=[pltpu.VMEM((tokens, WIDTH), jnp.bfloat16)],
        compiler_params=params(16),
        cost_estimate=pl.CostEstimate(
            flops=2 * tokens * WIDTH * D, bytes_accessed=5_000_000, transcendentals=0
        ),
        name="join",
    )(ids, *shares, w_out)


def add_kernel(side, *refs):
    terms, (kept_ref, given_ref, rows) = refs[:N_HEAD], refs[N_HEAD:]
    total = terms[0][...].astype(jnp.float32)
    for ref in terms[1:]:
        total = total + ref[...].astype(jnp.float32)
    rows[...] = total.astype(jnp.bfloat16)
    for c in range(TILE_COLS):
        to = slice(c * PAIR, (c + 1) * PAIR)
        for ref, which in ((kept_ref, side[0]), (given_ref, 1 - side[0])):
            start = pl.multiple_of(c * PIECE + which * PAIR, PAIR)
            ref[to, :] = rows[pl.ds(start, PAIR), :]


def add_terms(side, terms):
    whole = pl.BlockSpec(memory_space=pltpu.VMEM)
    return pl.pallas_call(
        add_kernel,
        in_specs=[pl.BlockSpec(memory_space=pltpu.SMEM)] + [whole] * N_HEAD,
        out_specs=[whole] * 2,
        out_shape=[jax.ShapeDtypeStruct((TILE_COLS * PAIR, WIDTH), jnp.bfloat16)] * 2,
        scratch_shapes=[pltpu.VMEM((TILE_COLS * PIECE, WIDTH), jnp.bfloat16)],
        compiler_params=params(8),
        cost_estimate=pl.CostEstimate(flops=800_000, bytes_accessed=2_000_000, transcendentals=0),
        name="add_terms",
    )(side, *terms)


def order_kernel(side, tile_of, kept_ref, got_ref, out_ref, rows):
    size = TILE_COLS * PAIR
    for ref, which in ((kept_ref, side[0]), (got_ref, 1 - side[0])):
        rows[pl.ds(pl.multiple_of(which * size, size), size), :] = ref[...]
    for d in range(TILES):
        start = pl.multiple_of((tile_of[d] % (2 * TILE_COLS)) * PAIR, PAIR)
        out_ref[d * PAIR : (d + 1) * PAIR, :] = rows[pl.ds(start, PAIR), :]


def order(side, tile_of, kept, got):
    whole = pl.BlockSpec(memory_space=pltpu.VMEM)
    scalars = pl.BlockSpec(memory_space=pltpu.SMEM)
    return pl.pallas_call(
        order_kernel,
        in_specs=[scalars, scalars, whole, whole],
        out_specs=whole,
        out_shape=jax.ShapeDtypeStruct((TILES * PAIR, WIDTH), jnp.bfloat16),
        scratch_shapes=[pltpu.VMEM((2 * TILE_COLS * PAIR, WIDTH), jnp.bfloat16)],
        compiler_params=params(8),
        cost_estimate=pl.CostEstimate(flops=100_000, bytes_accessed=800_000, transcendentals=0),
        name="order",
    )(side, tile_of, kept, got)


def tile_kernel(first, arrived, out_ref):
    base = first[0] * (2 * TILE * PAIR)
    pieces = [
        arrived[pl.ds(pl.multiple_of(base + n * PAIR, PAIR), PAIR), :].astype(jnp.float32)
        for n in range(2 * TILE)
    ]
    parts = [
        pieces[(f // 2) * TILE + j][(f % 2) * TILE : (f % 2 + 1) * TILE]
        for f in range(FRAMES)
        for j in range(TILE)
    ]
    out_ref[...] = jnp.concatenate(parts, axis=0).astype(jnp.bfloat16)


def to_tile(first, arrived):
    whole = pl.BlockSpec(memory_space=pltpu.VMEM)
    return pl.pallas_call(
        tile_kernel,
        in_specs=[pl.BlockSpec(memory_space=pltpu.SMEM), whole],
        out_specs=whole,
        out_shape=jax.ShapeDtypeStruct((TILE_TOKENS, WIDTH), jnp.bfloat16),
        compiler_params=params(8),
        cost_estimate=pl.CostEstimate(flops=100_000, bytes_accessed=800_000, transcendentals=0),
        name="to_tile",
    )(first, arrived)


def head_swap(array, k):
    return lax.ppermute(array, "head", [(h, h ^ k) for h in range(N_HEAD)])


def plane_swap(array, k):
    return lax.ppermute(array, "seq", [(s, s ^ k) for s in range(PLANE * PLANES)])


def mate_swap(array):
    return plane_swap(array, PLANE)


def edge_swap(array):
    pairs = []
    for z in range(1, PLANES - 1, 2):
        for i in range(PLANE):
            pairs += [(z * PLANE + i, (z + 1) * PLANE + i), ((z + 1) * PLANE + i, z * PLANE + i)]
    return lax.ppermute(array, "seq", pairs)


def local(latent, w_qkv, q_gain, k_gain, w_out, neighbours, tile_owner):
    ids = jnp.stack([lax.axis_index("seq"), lax.axis_index("head")]).astype(jnp.int32)
    weight = load_weight(jnp.transpose(w_qkv, (1, 0, 2)))
    q_gain, k_gain = q_gain.reshape(1, HEAD_DIM), k_gain.reshape(1, HEAD_DIM)
    starts, flags, tile_of, first, half = plan(ids, neighbours, tile_owner)

    pieces = [latent.reshape(PIECE, D)]
    pieces += [head_swap(pieces[0], k) for k in range(1, N_HEAD)]

    queries, rows = project_queries(ids, pieces, weight, q_gain)
    all_queries = [queries] + [plane_swap(queries, k) for k in range(1, PLANE)]
    own = project_keys(rows, weight, k_gain)
    mate, edge = mate_swap(own), edge_swap(own)
    mate, edge, *all_queries = lax.optimization_barrier((mate, edge, *all_queries))
    far_1, edge_2 = mate_swap(edge), edge_swap(mate)
    far_2 = mate_swap(edge_2)
    near = attend(starts, flags, all_queries, [own, mate, edge])
    shares = attend(starts, flags, all_queries, [edge_2, far_1, far_2], near)
    shares = [shares[0]] + [plane_swap(shares[k], k) for k in range(1, PLANE)]

    terms = join(ids, shares, w_out)
    terms = [terms[0]] + [head_swap(terms[k], k) for k in range(1, N_HEAD)]

    kept, given = add_terms(half, terms)
    sent = order(half, tile_of, kept, plane_swap(given, TILE))
    arrived = lax.all_to_all(
        sent.reshape(TILES, PAIR, WIDTH), "seq", split_axis=0, concat_axis=0, tiled=True
    )
    return to_tile(first, arrived.reshape(TILES * PAIR, WIDTH)).reshape(1, TILE_TOKENS, WIDTH)


def solution(mesh):
    placed = (
        P(None, "seq", "head", None),
        P(None, None, "head"),
        P(),
        P(),
        P("head", None),
        P(),
        P(),
    )
    return jax.shard_map(
        local, mesh=mesh, in_specs=placed, out_specs=P("seq", None, "head"), check_vma=False
    )
```

time: 186 us -> 157 us (0.84)
  waiting for transfers between devices: 67.7 us -> 33.8 us
  local copies, waits for them, and re-layouts: 32.9 us -> 7.51 us
  blocking collectives: 0 us -> 21.4 us
  starting transfers between devices: 59.6 us -> 69.4 us
  Pallas kernels: 19.7 us -> 22.9 us
  between operations: 2.86 us -> 0.17 us
  other arithmetic: 2.32 us -> 0.08 us
    all_to_all x0 -> x1, blocking collectives: none -> 21.4 us  [local(): lax.all_to_all(sent.reshape(TILES, PAIR, WIDTH), 'seq', split_axis=0, con...]
    all_to_all x1 -> x0, waiting for transfers between devices: 20.1 us -> none  [local(): lax.all_to_all(sent.reshape(TILES, PIECE, WIDTH), 'seq', split_axis=0, co...]
    ppermute x10, starting transfers between devices: 8.51 us -> 26.9 us  [plane_swap(): lax.ppermute(array, 'seq', [(s, s ^ k) for s in range(PLANE * PLANES)])]
    unnamed x33 -> x23, local copies, waits for them, and re-layouts: 21.7 us -> 7.51 us
    ppermute x4 -> x2, waiting for transfers between devices: 11.6 us -> 0.01 us  [edge_swap(): return lax.ppermute(array, 'seq', pairs)]
    reshape x2 -> x0, local copies, waits for them, and re-layouts: 10.2 us -> none  [the longest x1 10 us: local(): queries, keys = project(place, pieces, w_qkv.reshape(D, 3 * WIDTH), gains)]
    all_to_all x1 -> x0, starting transfers between devices: 9.27 us -> none  [local(): lax.all_to_all(sent.reshape(TILES, PIECE, WIDTH), 'seq', split_axis=0, co...]
    ppermute x14, starting transfers between devices: 31 us -> 39.7 us  [head_swap(): return lax.ppermute(array, 'head', [(h, h ^ k) for h in range(N_HEAD)])]
  transfers between devices with their start and end apart: 29 -> 26, of which waited for: 12 -> 11; matrix products, arithmetic and copies ran while one was open for 12% -> 1% of each run, Pallas kernels for 0% -> 5%
where the time goes in v2:
time: 157 us; the launch traced here: 155 us
  starting transfers between devices  69.4 us (44%)
  waiting for transfers between devices  33.8 us (22%)
  Pallas kernels  22.9 us (15%)
  blocking collectives  21.4 us (14%)
  local copies, waits for them, and re-layouts  7.51 us (5%)
    ppermute x14, starting transfers between devices, head_swap(): return lax.ppermute(array, 'head', [(h, h ^ k) for h in range(N_HEAD)])  39.7 us
    ppermute x10, starting transfers between devices, plane_swap(): lax.ppermute(array, 'seq', [(s, s ^ k) for s in range(PLANE * PLANES)])  26.9 us
    ppermute x10, waiting for transfers between devices, plane_swap(): lax.ppermute(array, 'seq', [(s, s ^ k) for s in range(PLANE * PLANES)])  21.6 us
    all_to_all x1, blocking collectives, local(): lax.all_to_all(sent.reshape(TILES, PAIR, WIDTH), 'seq', split_axis=0, con...  21.4 us
    ppermute x14, waiting for transfers between devices, head_swap(): return lax.ppermute(array, 'head', [(h, h ^ k) for h in range(N_HEAD)])  12.2 us
    pallas_call x2, Pallas kernels, attend(): pl.pallas_call(functools.partial(attend_kernel, kinds, last), in_specs=[s...  9.07 us
    unnamed x23, local copies, waits for them, and re-layouts  7.51 us
  transfers between devices with their start and end apart: 26, of which 11 were waited for; matrix products, arithmetic and copies ran while one was open for 1% of the time, Pallas kernels for 5%

profile of v2, /device:TPU:2, one launch (start us, length us, event | category | flops | bytes accessed | tf_op | source)
XLA Modules:
  0.0 155.3 jit_solution(5486108021485902088)
XLA Ops:
  0.0 2.1 %collective-permute-start = (bf16[32,3072]{1,0:T(8,128)(2,1)}, bf16[32,3072]{1,0:T(8,128)(2,1)S(1)}, u32[]{:S(2)}, u32[]{:S(2)}) collective-permute-start(bf16[32,3072]{1,0:T(8,128)(2,1)} %bitcast.12), channel_id=1, source_target_pairs={{0,1},{1,0},{2,3},{3,2},{4,5},{5,4},{6,7},{7,6},{8,9},{9,8},{10,11... | collective-permute-start | bytes 589832 | tf_op jit(solution)/shard_map/ppermute | solution.py:394
  2.1 1.6 %collective-permute-start.1 = (bf16[32,3072]{1,0:T(8,128)(2,1)}, bf16[32,3072]{1,0:T(8,128)(2,1)S(1)}, u32[]{:S(2)}, u32[]{:S(2)}) collective-permute-start(bf16[32,3072]{1,0:T(8,128)(2,1)} %bitcast.13), channel_id=1, source_target_pairs={{0,2},{1,3},{2,0},{3,1},{4,6},{5,7},{6,4},{7,5},{8,10},{9,11},{10,... | collective-permute-start | bytes 589832 | tf_op jit(solution)/shard_map/ppermute | solution.py:394
  3.7 1.3 collective-permute-start.2
  5.0 3.2 %collective-permute-start.3 = (bf16[32,3072]{1,0:T(8,128)(2,1)}, bf16[32,3072]{1,0:T(8,128)(2,1)S(1)}, u32[]{:S(2)}, u32[]{:S(2)}) collective-permute-start(bf16[32,3072]{1,0:T(8,128)(2,1)} %bitcast.15), channel_id=1, source_target_pairs={{0,4},{1,5},{2,6},{3,7},{4,0},{5,1},{6,2},{7,3},{8,12},{9,13},{10,... | collective-permute-start | bytes 589832 | tf_op jit(solution)/shard_map/ppermute | solution.py:394
  8.2 1.9 %collective-permute-start.4 = (bf16[32,3072]{1,0:T(8,128)(2,1)}, bf16[32,3072]{1,0:T(8,128)(2,1)S(1)}, u32[]{:S(2)}, u32[]{:S(2)}) collective-permute-start(bf16[32,3072]{1,0:T(8,128)(2,1)} %bitcast.16), channel_id=1, source_target_pairs={{0,5},{1,4},{2,7},{3,6},{4,1},{5,0},{6,3},{7,2},{8,13},{9,12},{10,... | collective-permute-start | bytes 589832 | tf_op jit(solution)/shard_map/ppermute | solution.py:394
  10.1 3.0 %collective-permute-start.5 = (bf16[32,3072]{1,0:T(8,128)(2,1)}, bf16[32,3072]{1,0:T(8,128)(2,1)S(1)}, u32[]{:S(2)}, u32[]{:S(2)}) collective-permute-start(bf16[32,3072]{1,0:T(8,128)(2,1)} %bitcast.17), channel_id=1, source_target_pairs={{0,6},{1,7},{2,4},{3,5},{4,2},{5,3},{6,0},{7,1},{8,14},{9,15},{10,... | collective-permute-start | bytes 589832 | tf_op jit(solution)/shard_map/ppermute | solution.py:394
  13.1 3.8 %collective-permute-done.1.refs_2_ = bf16[32,3072]{1,0:T(8,128)(2,1)S(1)} collective-permute-done((bf16[32,3072]{1,0:T(8,128)(2,1)}, bf16[32,3072]{1,0:T(8,128)(2,1)S(1)}, u32[]{:S(2)}, u32[]{:S(2)}) %collective-permute-start.1) | collective-permute-done | bytes 196640 | tf_op jit(solution)/shard_map/ppermute | solution.py:394
  16.9 5.3 %collective-permute-start.6 = (bf16[32,3072]{1,0:T(8,128)(2,1)}, bf16[32,3072]{1,0:T(8,128)(2,1)S(1)}, u32[]{:S(2)}, u32[]{:S(2)}) collective-permute-start(bf16[32,3072]{1,0:T(8,128)(2,1)} %bitcast.18), channel_id=1, source_target_pairs={{0,7},{1,6},{2,5},{3,4},{4,3},{5,2},{6,1},{7,0},{8,15},{9,14},{10,... | collective-permute-start | bytes 589832 | tf_op jit(solution)/shard_map/ppermute | solution.py:394
  22.2 3.0 %copy-done = bf16[3072,3,384]{2,0,1:T(8,128)(2,1)S(1)} copy-done((bf16[3072,3,384]{2,0,1:T(8,128)(2,1)S(1)}, bf16[3072,3,384]{2,0,1:T(8,128)(2,1)}, u32[]{:S(2)}) %copy-start) | copy-done | bytes 7077912
  25.2 1.6 %load_weight.1.refs_8_.w_ref = bf16[3,3072,384]{2,1,0:T(8,128)(2,1)S(1)} custom-call(bf16[3,3072,384]{2,1,0:T(8,128)(2,1)S(1)} %bitcast.9), custom_call_target="tpu_custom_call" | custom-call | bytes 7100000 | tf_op jit(solution)/shard_map/load_weight/pallas_call | solution.py:111
  26.8 0.0 copy-start.9
  26.8 0.1 pad_add_fusion.ids
  26.9 0.0 collective-permute-done.2.refs_3_
  26.9 0.0 collective-permute-done.3.refs_4_
  26.9 1.9 %collective-permute-done.5.refs_6_ = bf16[32,3072]{1,0:T(8,128)(2,1)S(1)} collective-permute-done((bf16[32,3072]{1,0:T(8,128)(2,1)}, bf16[32,3072]{1,0:T(8,128)(2,1)S(1)}, u32[]{:S(2)}, u32[]{:S(2)}) %collective-permute-start.5) | collective-permute-done | bytes 196640 | tf_op jit(solution)/shard_map/ppermute | solution.py:394
  28.8 0.0 collective-permute-done.6.refs_7_
  28.8 1.7 %project_queries.1 = (bf16[256,384]{1,0:T(8,128)(2,1)S(1)}, bf16[256,3072]{1,0:T(8,128)(2,1)S(1)}) custom-call(s32[2]{0:T(128)S(1)} %pad_add_fusion.ids, bf16[32,3072]{1,0:T(8,128)(2,1)S(1)} %bitcast.19, bf16[32,3072]{1,0:T(8,128)(2,1)S(1)} %collective-permute-done.refs_1_, bf16[32,3072]{1,0:T(8,128)(2,1)S(1)} %collective-permute-done.1.refs_2_, ...), custom_call_target="tpu_custom_call" | custom-call | flops 603979776 | bytes 4000000 | tf_op jit(solution)/shard_map/project_queries/pallas_call | solution.py:133
  30.5 0.0 copy-start.1
  30.6 1.8 %project_keys.1.refs_4_ = bf16[256,768]{1,0:T(8,128)(2,1)S(1)} custom-call(bf16[256,3072]{1,0:T(8,128)(2,1)S(1)} %get-tuple-element.42.rows_ref, bf16[3,3072,384]{2,1,0:T(8,128)(2,1)S(1)} %load_weight.1.refs_8_.w_ref, f32[1,128]{1,0:T(1,128)S(1)} %bitcast.21), custom_call_target="tpu_custom_call" | custom-call | flops 1207959552 | bytes 6000000 | tf_op jit(solution)/shard_map/project_keys/pallas_call | solution.py:160
  32.4 2.0 %collective-permute-start.7 = (bf16[256,768]{1,0:T(8,128)(2,1)S(1)}, bf16[256,768]{1,0:T(8,128)(2,1)S(1)}, u32[]{:S(2)}, u32[]{:S(2)}) collective-permute-start(bf16[256,768]{1,0:T(8,128)(2,1)S(1)} %project_keys.1.refs_4_), channel_id=1, source_target_pairs={{0,32},{8,40},{16,48},{24,56},{32,0},{40,8},{48,16},{56,24},{64,96... | collective-permute-start | bytes 1179656 | tf_op jit(solution)/shard_map/ppermute | solution.py:398
  34.4 1.4 collective-permute-start.8
  35.8 1.9 %collective-permute-start.10 = (bf16[256,384]{1,0:T(8,128)(2,1)S(1)}, bf16[256,384]{1,0:T(8,128)(2,1)S(1)}, u32[]{:S(2)}, u32[]{:S(2)}) collective-permute-start(bf16[256,384]{1,0:T(8,128)(2,1)S(1)} %get-tuple-element.44.refs_0_), channel_id=1, source_target_pairs={{0,16},{8,24},{16,0},{24,8},{32,48},{40,56},{48,32},{56,40},{64,80... | collective-permute-start | bytes 589832 | tf_op jit(solution)/shard_map/ppermute | solution.py:398
  37.7 0.0 collective-permute-start.11
  37.7 0.3 collective-permute-start.9
  38.0 4.6 %collective-permute-done.10.refs_2_ = bf16[256,384]{1,0:T(8,128)(2,1)S(1)} collective-permute-done((bf16[256,384]{1,0:T(8,128)(2,1)S(1)}, bf16[256,384]{1,0:T(8,128)(2,1)S(1)}, u32[]{:S(2)}, u32[]{:S(2)}) %collective-permute-start.10) | collective-permute-done | bytes 196640 | tf_op jit(solution)/shard_map/ppermute | solution.py:398
  42.6 2.4 %collective-permute-done.11.refs_3_ = bf16[256,384]{1,0:T(8,128)(2,1)S(1)} collective-permute-done((bf16[256,384]{1,0:T(8,128)(2,1)S(1)}, bf16[256,384]{1,0:T(8,128)(2,1)S(1)}, u32[]{:S(2)}, u32[]{:S(2)}) %collective-permute-start.11) | collective-permute-done | bytes 196640 | tf_op jit(solution)/shard_map/ppermute | solution.py:398
  44.9 0.0 collective-permute-done.9.refs_1_
  44.9 0.0 collective-permute-done.7.refs_5_
  44.9 0.0 collective-permute-done.8.refs_6_
  44.9 1.4 collective-permute-start.12
  46.4 0.7 copy-done.2
  47.1 4.9 %collective-permute-start.13 = (bf16[256,768]{1,0:T(8,128)(2,1)}, bf16[256,768]{1,0:T(8,128)(2,1)}, u32[]{:S(2)}, u32[]{:S(2)}) collective-permute-start(bf16[256,768]{1,0:T(8,128)(2,1)} %collective-permute-done.8.refs_6_), channel_id=1, source_target_pairs={{0,32},{8,40},{16,48},{24,56},{32,0},{40,8},{48,16},{56,24},{64,96... | collective-permute-start | bytes 1179656 | tf_op jit(solution)/shard_map/ppermute | solution.py:398
  52.1 10.9 %collective-permute-start.14 = (bf16[256,768]{1,0:T(8,128)(2,1)}, bf16[256,768]{1,0:T(8,128)(2,1)}, u32[]{:S(2)}, u32[]{:S(2)}) collective-permute-start(bf16[256,768]{1,0:T(8,128)(2,1)} %collective-permute-done.12.refs_4_), channel_id=1, source_target_pairs={{0,32},{8,40},{16,48},{24,56},{32,0},{40,8},{48,16},{56,24},{64,96... | collective-permute-start | bytes 1179656 | tf_op jit(solution)/shard_map/ppermute | solution.py:398
  63.0 0.8 copy.8.neighbours
  63.7 0.7 copy-done.6
  64.4 0.7 copy-done.10
  65.0 2.7 %plan.1 = (s32[8]{0:T(128)S(1)}, s32[8,9]{1,0:T(8,128)S(1)}, s32[32]{0:T(128)S(1)}, s32[1]{0:T(128)}, s32[1]{0:T(128)}) custom-call(s32[2]{0:T(128)S(1)} %copy-done.6, s32[32,9]{1,0:T(8,128)S(1)} %copy.8.neighbours, s32[32]{0:T(128)S(1)} %copy-done.10), custom_call_target="tpu_custom_call" | custom-call | bytes 8000000 | tf_op jit(solution)/shard_map/plan/pallas_call | solution.py:69
  67.7 1.0 copy-done.3
  68.7 3.4 %attend.2 = (bf16[256,384]{1,0:T(8,128)(2,1)S(1)}, bf16[256,384]{1,0:T(8,128)(2,1)S(1)}, bf16[256,384]{1,0:T(8,128)(2,1)S(1)}, bf16[256,384]{1,0:T(8,128)(2,1)S(1)}, f32[128,128]{1,0:T(8,128)S(1)}) custom-call(s32[8]{0:T(128)S(1)} %get-tuple-element.40.starts, s32[8,9]{1,0:T(8,128)S(1)} %get-tuple-element.41.flags, ...), custom_call_target="tpu_custom_call" | custom-call | flops 452984832 | bytes 4000000 | tf_op jit(solution)/shard_map/attend/pallas_call | solution.py:250
  72.1 0.2 collective-permute-done.14.refs_6_
  72.4 5.7 %attend.3 = (bf16[288,384]{1,0:T(8,128)(2,1)S(1)}, bf16[288,384]{1,0:T(8,128)(2,1)S(1)}, bf16[288,384]{1,0:T(8,128)(2,1)S(1)}, bf16[288,384]{1,0:T(8,128)(2,1)S(1)}) custom-call(s32[8]{0:T(128)S(1)} %get-tuple-element.40.starts, s32[8,9]{1,0:T(8,128)S(1)} %get-tuple-element.41.flags, bf16[256,384]{1,0:T(8,128)(2,1)S(1)} %get-tuple-element.44.refs_0_, ...), custom_call_target="tpu_custom_call" | custom-call | flops 452984832 | bytes 4000000 | tf_op jit(solution)/shard_map/attend/pallas_call | solution.py:250
  78.0 0.1 collective-permute-start.15
  78.1 1.2 collective-permute-start.16
  79.3 0.7 collective-permute-start.17
  80.0 6.5 %collective-permute-done.16.refs_2_ = bf16[288,384]{1,0:T(8,128)(2,1)S(1)} collective-permute-done((bf16[288,384]{1,0:T(8,128)(2,1)S(1)}, bf16[288,384]{1,0:T(8,128)(2,1)S(1)}, u32[]{:S(2)}, u32[]{:S(2)}) %collective-permute-start.16) | collective-permute-done | bytes 221216 | tf_op jit(solution)/shard_map/ppermute | solution.py:398
  86.5 3.8 %collective-permute-done.17.refs_3_ = bf16[288,384]{1,0:T(8,128)(2,1)S(1)} collective-permute-done((bf16[288,384]{1,0:T(8,128)(2,1)S(1)}, bf16[288,384]{1,0:T(8,128)(2,1)S(1)}, u32[]{:S(2)}, u32[]{:S(2)}) %collective-permute-start.17) | collective-permute-done | bytes 221216 | tf_op jit(solution)/shard_map/ppermute | solution.py:398
  90.3 0.7 copy-done.7
  90.9 2.2 %join.1 = (bf16[256,384]{1,0:T(8,128)(2,1)S(1)}, bf16[256,384]{1,0:T(8,128)(2,1)S(1)}, bf16[256,384]{1,0:T(8,128)(2,1)S(1)}, bf16[256,384]{1,0:T(8,128)(2,1)S(1)...) custom-call(s32[2]{0:T(128)S(1)} %copy-done.7, ...), custom_call_target="tpu_custom_call" | custom-call | flops 603979776 | bytes 5000000 | tf_op jit(solution)/shard_map/join/pallas_call | solution.py:301
  93.1 0.5 collective-permute-start.18
  93.6 1.2 collective-permute-start.19
  94.9 3.4 %collective-permute-start.20 = (bf16[256,384]{1,0:T(8,128)(2,1)S(1)}, bf16[256,384]{1,0:T(8,128)(2,1)S(1)}, u32[]{:S(2)}, u32[]{:S(2)}) collective-permute-start(bf16[256,384]{1,0:T(8,128)(2,1)S(1)} %get-tuple-element.62), channel_id=1, source_target_pairs={{0,3},{1,2},{2,1},{3,0},{4,7},{5,6},{6,5},{7,4},{8,11},{9,10},{10,... | collective-permute-start | bytes 589832 | tf_op jit(solution)/shard_map/ppermute | solution.py:394
  98.2 2.4 %collective-permute-start.21 = (bf16[256,384]{1,0:T(8,128)(2,1)S(1)}, bf16[256,384]{1,0:T(8,128)(2,1)S(1)}, u32[]{:S(2)}, u32[]{:S(2)}) collective-permute-start(bf16[256,384]{1,0:T(8,128)(2,1)S(1)} %get-tuple-element.63), channel_id=1, source_target_pairs={{0,4},{1,5},{2,6},{3,7},{4,0},{5,1},{6,2},{7,3},{8,12},{9,13},{10,... | collective-permute-start | bytes 589832 | tf_op jit(solution)/shard_map/ppermute | solution.py:394
  100.6 1.0 collective-permute-start.22
  101.6 0.8 collective-permute-done.18.refs_1_
  102.5 2.9 %collective-permute-start.23 = (bf16[256,384]{1,0:T(8,128)(2,1)S(1)}, bf16[256,384]{1,0:T(8,128)(2,1)S(1)}, u32[]{:S(2)}, u32[]{:S(2)}) collective-permute-start(bf16[256,384]{1,0:T(8,128)(2,1)S(1)} %get-tuple-element.65), channel_id=1, source_target_pairs={{0,6},{1,7},{2,4},{3,5},{4,2},{5,3},{6,0},{7,1},{8,14},{9,15},{10,... | collective-permute-start | bytes 589832 | tf_op jit(solution)/shard_map/ppermute | solution.py:394
  105.3 9.9 %collective-permute-start.24 = (bf16[256,384]{1,0:T(8,128)(2,1)S(1)}, bf16[256,384]{1,0:T(8,128)(2,1)S(1)}, u32[]{:S(2)}, u32[]{:S(2)}) collective-permute-start(bf16[256,384]{1,0:T(8,128)(2,1)S(1)} %get-tuple-element.66), channel_id=1, source_target_pairs={{0,7},{1,6},{2,5},{3,4},{4,3},{5,2},{6,1},{7,0},{8,15},{9,14},{10,... | collective-permute-start | bytes 589832 | tf_op jit(solution)/shard_map/ppermute | solution.py:394
  115.2 2.0 %collective-permute-done.21.refs_4_ = bf16[256,384]{1,0:T(8,128)(2,1)S(1)} collective-permute-done((bf16[256,384]{1,0:T(8,128)(2,1)S(1)}, bf16[256,384]{1,0:T(8,128)(2,1)S(1)}, u32[]{:S(2)}, u32[]{:S(2)}) %collective-permute-start.21) | collective-permute-done | bytes 196640 | tf_op jit(solution)/shard_map/ppermute | solution.py:394
  117.2 3.7 %collective-permute-done.23.refs_6_ = bf16[256,384]{1,0:T(8,128)(2,1)S(1)} collective-permute-done((bf16[256,384]{1,0:T(8,128)(2,1)S(1)}, bf16[256,384]{1,0:T(8,128)(2,1)S(1)}, u32[]{:S(2)}, u32[]{:S(2)}) %collective-permute-start.23) | collective-permute-done | bytes 196640 | tf_op jit(solution)/shard_map/ppermute | solution.py:394
  120.9 1.0 add_terms.1
  122.0 5.0 %collective-permute-start.25 = (bf16[128,384]{1,0:T(8,128)(2,1)S(1)}, bf16[128,384]{1,0:T(8,128)(2,1)S(1)}, u32[]{:S(2)}, u32[]{:S(2)}) collective-permute-start(bf16[128,384]{1,0:T(8,128)(2,1)S(1)} %get-tuple-element.68), channel_id=1, source_target_pairs={{0,64},{8,72},{16,80},{24,88},{32,96},{40,104},{48,112},{56,120},{... | collective-permute-start | bytes 294920 | tf_op jit(solution)/shard_map/ppermute | solution.py:398
  127.0 4.2 %collective-permute-done.25.got_ref = bf16[128,384]{1,0:T(8,128)(2,1)S(1)} collective-permute-done((bf16[128,384]{1,0:T(8,128)(2,1)S(1)}, bf16[128,384]{1,0:T(8,128)(2,1)S(1)}, u32[]{:S(2)}, u32[]{:S(2)}) %collective-permute-start.25) | collective-permute-done | bytes 98336 | tf_op jit(solution)/shard_map/ppermute | solution.py:398
  131.1 1.4 order.1
  132.5 21.4 %all_to_all.5 = bf16[32,16,384]{2,1,0:T(8,128)(2,1)S(1)} all-to-all(bf16[32,16,384]{2,1,0:T(8,128)(2,1)S(1)} %bitcast.10), channel_id=1, replica_groups=mesh['seq'=32,'head'=8] {'seq'}, dimensions={0} | all-to-all | bytes 786432 | tf_op jit(solution)/shard_map/all_to_all | solution.py:438
  153.9 1.4 to_tile.1
  (23 shorter events, 0.0 us)
Async XLA Ops:
  0.0 10.1 %collective-permute-start = (bf16[32,3072]{1,0:T(8,128)(2,1)}, bf16[32,3072]{1,0:T(8,128)(2,1)S(1)}, u32[]{:S(2)}, u32[]{:S(2)}) collective-permute-start(bf16[32,3072]{1,0:T(8,128)(2,1)} %bitcast.12), channel_id=1, source_target_pairs={{0,1},{1,0},{2,3},{3,2},{4,5},{5,4},{6,7},{7,6},{8,9},{9,8},{10,11... | collective-permute-start | bytes 589832 | tf_op jit(solution)/shard_map/ppermute | solution.py:394
  2.1 14.8 %collective-permute-start.1 = (bf16[32,3072]{1,0:T(8,128)(2,1)}, bf16[32,3072]{1,0:T(8,128)(2,1)S(1)}, u32[]{:S(2)}, u32[]{:S(2)}) collective-permute-start(bf16[32,3072]{1,0:T(8,128)(2,1)} %bitcast.13), channel_id=1, source_target_pairs={{0,2},{1,3},{2,0},{3,1},{4,6},{5,7},{6,4},{7,5},{8,10},{9,11},{10,... | collective-permute-start | bytes 589832 | tf_op jit(solution)/shard_map/ppermute | solution.py:394
  3.7 23.2 %collective-permute-start.2 = (bf16[32,3072]{1,0:T(8,128)(2,1)}, bf16[32,3072]{1,0:T(8,128)(2,1)S(1)}, u32[]{:S(2)}, u32[]{:S(2)}) collective-permute-start(bf16[32,3072]{1,0:T(8,128)(2,1)} %bitcast.14), channel_id=1, source_target_pairs={{0,3},{1,2},{2,1},{3,0},{4,7},{5,6},{6,5},{7,4},{8,11},{9,10},{10,... | collective-permute-start | bytes 589832 | tf_op jit(solution)/shard_map/ppermute | solution.py:394
  5.0 21.9 %collective-permute-start.3 = (bf16[32,3072]{1,0:T(8,128)(2,1)}, bf16[32,3072]{1,0:T(8,128)(2,1)S(1)}, u32[]{:S(2)}, u32[]{:S(2)}) collective-permute-start(bf16[32,3072]{1,0:T(8,128)(2,1)} %bitcast.15), channel_id=1, source_target_pairs={{0,4},{1,5},{2,6},{3,7},{4,0},{5,1},{6,2},{7,3},{8,12},{9,13},{10,... | collective-permute-start | bytes 589832 | tf_op jit(solution)/shard_map/ppermute | solution.py:394
  8.2 18.7 %collective-permute-start.4 = (bf16[32,3072]{1,0:T(8,128)(2,1)}, bf16[32,3072]{1,0:T(8,128)(2,1)S(1)}, u32[]{:S(2)}, u32[]{:S(2)}) collective-permute-start(bf16[32,3072]{1,0:T(8,128)(2,1)} %bitcast.16), channel_id=1, source_target_pairs={{0,5},{1,4},{2,7},{3,6},{4,1},{5,0},{6,3},{7,2},{8,13},{9,12},{10,... | collective-permute-start | bytes 589832 | tf_op jit(solution)/shard_map/ppermute | solution.py:394
  10.1 18.7 %collective-permute-start.5 = (bf16[32,3072]{1,0:T(8,128)(2,1)}, bf16[32,3072]{1,0:T(8,128)(2,1)S(1)}, u32[]{:S(2)}, u32[]{:S(2)}) collective-permute-start(bf16[32,3072]{1,0:T(8,128)(2,1)} %bitcast.17), channel_id=1, source_target_pairs={{0,6},{1,7},{2,4},{3,5},{4,2},{5,3},{6,0},{7,1},{8,14},{9,15},{10,... | collective-permute-start | bytes 589832 | tf_op jit(solution)/shard_map/ppermute | solution.py:394
  16.9 11.9 %collective-permute-start.6 = (bf16[32,3072]{1,0:T(8,128)(2,1)}, bf16[32,3072]{1,0:T(8,128)(2,1)S(1)}, u32[]{:S(2)}, u32[]{:S(2)}) collective-permute-start(bf16[32,3072]{1,0:T(8,128)(2,1)} %bitcast.18), channel_id=1, source_target_pairs={{0,7},{1,6},{2,5},{3,4},{4,3},{5,2},{6,1},{7,0},{8,15},{9,14},{10,... | collective-permute-start | bytes 589832 | tf_op jit(solution)/shard_map/ppermute | solution.py:394
  22.2 3.0 %copy-start = (bf16[3072,3,384]{2,0,1:T(8,128)(2,1)S(1)}, bf16[3072,3,384]{2,0,1:T(8,128)(2,1)}, u32[]{:S(2)}) copy-start(bf16[3072,3,384]{2,0,1:T(8,128)(2,1)} %param.8) | copy-start | bytes 21233668
  25.2 3.5 %copy-start.4 = (bf16[4,1,8,3072]{3,2,1,0:T(8,128)(2,1)S(1)}, bf16[4,1,8,3072]{3,2,1,0:T(8,128)(2,1)}, u32[]{:S(2)}) copy-start(bf16[4,1,8,3072]{3,2,1,0:T(8,128)(2,1)} %param.7) | copy-start | bytes 589828
  25.2 3.6 %copy-start.8 = (f32[128]{0:T(128)S(1)}, f32[128]{0:T(128)}, u32[]{:S(2)}) copy-start(f32[128]{0:T(128)} %param.9) | copy-start | bytes 1540
  26.8 3.7 %copy-start.9 = (f32[128]{0:T(128)S(1)}, f32[128]{0:T(128)}, u32[]{:S(2)}) copy-start(f32[128]{0:T(128)} %param.10) | copy-start | bytes 1540
  26.9 1.9 %copy-start.5 = (s32[2]{0:T(128)}, s32[2]{0:T(128)S(1)}, u32[]{:S(2)}) copy-start(s32[2]{0:T(128)S(1)} %pad_add_fusion.ids) | copy-start | bytes 28
  30.5 59.7 %copy-start.1 = (bf16[384,3072]{1,0:T(8,128)(2,1)S(1)}, bf16[384,3072]{1,0:T(8,128)(2,1)}, u32[]{:S(2)}) copy-start(bf16[384,3072]{1,0:T(8,128)(2,1)} %refs_4_.1) | copy-start | bytes 7077892
  32.4 12.5 %collective-permute-start.7 = (bf16[256,768]{1,0:T(8,128)(2,1)S(1)}, bf16[256,768]{1,0:T(8,128)(2,1)S(1)}, u32[]{:S(2)}, u32[]{:S(2)}) collective-permute-start(bf16[256,768]{1,0:T(8,128)(2,1)S(1)} %project_keys.1.refs_4_), channel_id=1, source_target_pairs={{0,32},{8,40},{16,48},{24,56},{32,0},{40,8},{48,16},{56,24},{64,96... | collective-permute-start | bytes 1179656 | tf_op jit(solution)/shard_map/ppermute | solution.py:398
  34.4 10.5 %collective-permute-start.8 = (bf16[256,768]{1,0:T(8,128)(2,1)S(1)}, bf16[256,768]{1,0:T(8,128)(2,1)}, u32[]{:S(2)}, u32[]{:S(2)}) collective-permute-start(bf16[256,768]{1,0:T(8,128)(2,1)S(1)} %project_keys.1.refs_4_), channel_id=1, source_target_pairs={{32,64},{64,32},{40,72},{72,40},{48,80},{80,48},{56,88},{88,56},{9... | collective-permute-start | bytes 1179656 | tf_op jit(solution)/shard_map/ppermute | solution.py:410
  35.8 6.7 %collective-permute-start.10 = (bf16[256,384]{1,0:T(8,128)(2,1)S(1)}, bf16[256,384]{1,0:T(8,128)(2,1)S(1)}, u32[]{:S(2)}, u32[]{:S(2)}) collective-permute-start(bf16[256,384]{1,0:T(8,128)(2,1)S(1)} %get-tuple-element.44.refs_0_), channel_id=1, source_target_pairs={{0,16},{8,24},{16,0},{24,8},{32,48},{40,56},{48,32},{56,40},{64,80... | collective-permute-start | bytes 589832 | tf_op jit(solution)/shard_map/ppermute | solution.py:398
  37.7 7.2 %collective-permute-start.11 = (bf16[256,384]{1,0:T(8,128)(2,1)S(1)}, bf16[256,384]{1,0:T(8,128)(2,1)S(1)}, u32[]{:S(2)}, u32[]{:S(2)}) collective-permute-start(bf16[256,384]{1,0:T(8,128)(2,1)S(1)} %get-tuple-element.44.refs_0_), channel_id=1, source_target_pairs={{0,24},{8,16},{16,8},{24,0},{32,56},{40,48},{48,40},{56,32},{64,88... | collective-permute-start | bytes 589832 | tf_op jit(solution)/shard_map/ppermute | solution.py:398
  37.7 7.2 %collective-permute-start.9 = (bf16[256,384]{1,0:T(8,128)(2,1)S(1)}, bf16[256,384]{1,0:T(8,128)(2,1)S(1)}, u32[]{:S(2)}, u32[]{:S(2)}) collective-permute-start(bf16[256,384]{1,0:T(8,128)(2,1)S(1)} %get-tuple-element.44.refs_0_), channel_id=1, source_target_pairs={{0,8},{8,0},{16,24},{24,16},{32,40},{40,32},{48,56},{56,48},{64,72... | collective-permute-start | bytes 589832 | tf_op jit(solution)/shard_map/ppermute | solution.py:398
  44.9 7.1 %collective-permute-start.12 = (bf16[256,768]{1,0:T(8,128)(2,1)S(1)}, bf16[256,768]{1,0:T(8,128)(2,1)}, u32[]{:S(2)}, u32[]{:S(2)}) collective-permute-start(bf16[256,768]{1,0:T(8,128)(2,1)S(1)} %collective-permute-done.7.refs_5_), channel_id=1, source_target_pairs={{32,64},{64,32},{40,72},{72,40},{48,80},{80,48},{56,88},{88,56},{9... | collective-permute-start | bytes 1179656 | tf_op jit(solution)/shard_map/ppermute | solution.py:410
  46.4 0.8 copy-start.2
  47.1 25.0 %collective-permute-start.13 = (bf16[256,768]{1,0:T(8,128)(2,1)}, bf16[256,768]{1,0:T(8,128)(2,1)}, u32[]{:S(2)}, u32[]{:S(2)}) collective-permute-start(bf16[256,768]{1,0:T(8,128)(2,1)} %collective-permute-done.8.refs_6_), channel_id=1, source_target_pairs={{0,32},{8,40},{16,48},{24,56},{32,0},{40,8},{48,16},{56,24},{64,96... | collective-permute-start | bytes 1179656 | tf_op jit(solution)/shard_map/ppermute | solution.py:398
  52.1 20.3 %collective-permute-start.14 = (bf16[256,768]{1,0:T(8,128)(2,1)}, bf16[256,768]{1,0:T(8,128)(2,1)}, u32[]{:S(2)}, u32[]{:S(2)}) collective-permute-start(bf16[256,768]{1,0:T(8,128)(2,1)} %collective-permute-done.12.refs_4_), channel_id=1, source_target_pairs={{0,32},{8,40},{16,48},{24,56},{32,0},{40,8},{48,16},{56,24},{64,96... | collective-permute-start | bytes 1179656 | tf_op jit(solution)/shard_map/ppermute | solution.py:398
  63.7 0.7 copy-start.6
  64.4 0.7 copy-start.10
  67.7 1.0 copy-start.3
  78.0 2.0 %collective-permute-start.15 = (bf16[288,384]{1,0:T(8,128)(2,1)S(1)}, bf16[288,384]{1,0:T(8,128)(2,1)S(1)}, u32[]{:S(2)}, u32[]{:S(2)}) collective-permute-start(bf16[288,384]{1,0:T(8,128)(2,1)S(1)} %get-tuple-element.56), channel_id=1, source_target_pairs={{0,8},{8,0},{16,24},{24,16},{32,40},{40,32},{48,56},{56,48},{64,72... | collective-permute-start | bytes 663560 | tf_op jit(solution)/shard_map/ppermute | solution.py:398
  78.1 8.3 %collective-permute-start.16 = (bf16[288,384]{1,0:T(8,128)(2,1)S(1)}, bf16[288,384]{1,0:T(8,128)(2,1)S(1)}, u32[]{:S(2)}, u32[]{:S(2)}) collective-permute-start(bf16[288,384]{1,0:T(8,128)(2,1)S(1)} %get-tuple-element.57), channel_id=1, source_target_pairs={{0,16},{8,24},{16,0},{24,8},{32,48},{40,56},{48,32},{56,40},{64,80... | collective-permute-start | bytes 663560 | tf_op jit(solution)/shard_map/ppermute | solution.py:398
  79.3 11.0 %collective-permute-start.17 = (bf16[288,384]{1,0:T(8,128)(2,1)S(1)}, bf16[288,384]{1,0:T(8,128)(2,1)S(1)}, u32[]{:S(2)}, u32[]{:S(2)}) collective-permute-start(bf16[288,384]{1,0:T(8,128)(2,1)S(1)} %get-tuple-element.58), channel_id=1, source_target_pairs={{0,24},{8,16},{16,8},{24,0},{32,56},{40,48},{48,40},{56,32},{64,88... | collective-permute-start | bytes 663560 | tf_op jit(solution)/shard_map/ppermute | solution.py:398
  90.3 0.7 copy-start.7
  93.1 9.3 %collective-permute-start.18 = (bf16[256,384]{1,0:T(8,128)(2,1)S(1)}, bf16[256,384]{1,0:T(8,128)(2,1)S(1)}, u32[]{:S(2)}, u32[]{:S(2)}) collective-permute-start(bf16[256,384]{1,0:T(8,128)(2,1)S(1)} %get-tuple-element.60), channel_id=1, source_target_pairs={{0,1},{1,0},{2,3},{3,2},{4,5},{5,4},{6,7},{7,6},{8,9},{9,8},{10,11... | collective-permute-start | bytes 589832 | tf_op jit(solution)/shard_map/ppermute | solution.py:394
  93.6 11.7 %collective-permute-start.19 = (bf16[256,384]{1,0:T(8,128)(2,1)S(1)}, bf16[256,384]{1,0:T(8,128)(2,1)S(1)}, u32[]{:S(2)}, u32[]{:S(2)}) collective-permute-start(bf16[256,384]{1,0:T(8,128)(2,1)S(1)} %get-tuple-element.61), channel_id=1, source_target_pairs={{0,2},{1,3},{2,0},{3,1},{4,6},{5,7},{6,4},{7,5},{8,10},{9,11},{10,... | collective-permute-start | bytes 589832 | tf_op jit(solution)/shard_map/ppermute | solution.py:394
  94.9 20.4 %collective-permute-start.20 = (bf16[256,384]{1,0:T(8,128)(2,1)S(1)}, bf16[256,384]{1,0:T(8,128)(2,1)S(1)}, u32[]{:S(2)}, u32[]{:S(2)}) collective-permute-start(bf16[256,384]{1,0:T(8,128)(2,1)S(1)} %get-tuple-element.62), channel_id=1, source_target_pairs={{0,3},{1,2},{2,1},{3,0},{4,7},{5,6},{6,5},{7,4},{8,11},{9,10},{10,... | collective-permute-start | bytes 589832 | tf_op jit(solution)/shard_map/ppermute | solution.py:394
  98.2 19.0 %collective-permute-start.21 = (bf16[256,384]{1,0:T(8,128)(2,1)S(1)}, bf16[256,384]{1,0:T(8,128)(2,1)S(1)}, u32[]{:S(2)}, u32[]{:S(2)}) collective-permute-start(bf16[256,384]{1,0:T(8,128)(2,1)S(1)} %get-tuple-element.63), channel_id=1, source_target_pairs={{0,4},{1,5},{2,6},{3,7},{4,0},{5,1},{6,2},{7,3},{8,12},{9,13},{10,... | collective-permute-start | bytes 589832 | tf_op jit(solution)/shard_map/ppermute | solution.py:394
  100.6 16.6 %collective-permute-start.22 = (bf16[256,384]{1,0:T(8,128)(2,1)S(1)}, bf16[256,384]{1,0:T(8,128)(2,1)S(1)}, u32[]{:S(2)}, u32[]{:S(2)}) collective-permute-start(bf16[256,384]{1,0:T(8,128)(2,1)S(1)} %get-tuple-element.64), channel_id=1, source_target_pairs={{0,5},{1,4},{2,7},{3,6},{4,1},{5,0},{6,3},{7,2},{8,13},{9,12},{10,... | collective-permute-start | bytes 589832 | tf_op jit(solution)/shard_map/ppermute | solution.py:394
  102.5 18.5 %collective-permute-start.23 = (bf16[256,384]{1,0:T(8,128)(2,1)S(1)}, bf16[256,384]{1,0:T(8,128)(2,1)S(1)}, u32[]{:S(2)}, u32[]{:S(2)}) collective-permute-start(bf16[256,384]{1,0:T(8,128)(2,1)S(1)} %get-tuple-element.65), channel_id=1, source_target_pairs={{0,6},{1,7},{2,4},{3,5},{4,2},{5,3},{6,0},{7,1},{8,14},{9,15},{10,... | collective-permute-start | bytes 589832 | tf_op jit(solution)/shard_map/ppermute | solution.py:394
  105.3 15.6 %collective-permute-start.24 = (bf16[256,384]{1,0:T(8,128)(2,1)S(1)}, bf16[256,384]{1,0:T(8,128)(2,1)S(1)}, u32[]{:S(2)}, u32[]{:S(2)}) collective-permute-start(bf16[256,384]{1,0:T(8,128)(2,1)S(1)} %get-tuple-element.66), channel_id=1, source_target_pairs={{0,7},{1,6},{2,5},{3,4},{4,3},{5,2},{6,1},{7,0},{8,15},{9,14},{10,... | collective-permute-start | bytes 589832 | tf_op jit(solution)/shard_map/ppermute | solution.py:394
  122.0 9.1 %collective-permute-start.25 = (bf16[128,384]{1,0:T(8,128)(2,1)S(1)}, bf16[128,384]{1,0:T(8,128)(2,1)S(1)}, u32[]{:S(2)}, u32[]{:S(2)}) collective-permute-start(bf16[128,384]{1,0:T(8,128)(2,1)S(1)} %get-tuple-element.68), channel_id=1, source_target_pairs={{0,64},{8,72},{16,80},{24,88},{32,96},{40,104},{48,112},{56,120},{... | collective-permute-start | bytes 294920 | tf_op jit(solution)/shard_map/ppermute | solution.py:398

commit v3 on v2

--- a/solution.py
+++ b/solution.py
@@ -27,6 +27,9 @@
 
 LOADS = 4
 
+RELAYED = (4, 5)
+DIRECT = (0, 1, 2, 7, 6, 3)
+
 epsilon = 1e-06
 LOWEST = -1e30
 
@@ -41,15 +44,12 @@
     odd = (position // PLANE) % 2
     for c in range(TILE_COLS):
         tile = tile_row * TILE_COLS + c
-        start = jnp.int32(TILE_COLS - 3)
-        for n in range(9):
-            listed = neighbours[tile, n]
-            start = jnp.where(listed >= 0, jnp.minimum(start, listed % TILE_COLS), start)
+        start = jnp.minimum(neighbours[0, tile] % TILE_COLS, TILE_COLS - 3)
         starts[c] = start
         for n in range(9):
             flags[c, n] = 0
         for n in range(9):
-            listed = neighbours[tile, n]
+            listed = neighbours[n, tile]
 
             @pl.when(listed >= 0)
             def _():
@@ -168,6 +168,57 @@
         ),
         name="project_keys",
     )(rows, weight, gain)
+
+
+TAIL = slice(TILE_COLS * PIECE, (TILE_COLS + 1) * PIECE)
+
+
+def store_level(ref, level):
+    for n in range(3):
+        rounded = level.astype(jnp.bfloat16)
+        level = level - rounded.astype(jnp.float32)
+        ref[TAIL, n * HEAD_DIM : (n + 1) * HEAD_DIM] = rounded
+
+
+def load_level(ref):
+    parts = [ref[TAIL, n * HEAD_DIM : (n + 1) * HEAD_DIM].astype(jnp.float32) for n in range(3)]
+    return parts[0] + (parts[1] + parts[2])
+
+
+def merge(shares, out_ref):
+    levels = [load_level(ref) for ref in shares]
+    top = functools.reduce(jnp.maximum, levels)
+    weights = [jnp.exp2(level - top) for level in levels]
+    total = functools.reduce(jnp.add, weights)
+    weights = [weight / total for weight in weights]
+    for c in range(TILE_COLS):
+        rows = slice(c * PIECE, (c + 1) * PIECE)
+        for h in range(HEADS_HERE):
+            head = slice(h * HEAD_DIM, (h + 1) * HEAD_DIM)
+            lane = HEADS_HERE * c + h
+            mixed = None
+            for weight, ref in zip(weights, shares):
+                term = weight[:, lane : lane + 1] * ref[rows, head].astype(jnp.float32)
+                mixed = term if mixed is None else mixed + term
+            out_ref[rows, head] = mixed.astype(jnp.bfloat16)
+    return top + jnp.log2(total)
+
+
+def merge_kernel(first_ref, second_ref, out_ref):
+    store_level(out_ref, merge([first_ref, second_ref], out_ref))
+
+
+def merge_shares(first, second):
+    whole = pl.BlockSpec(memory_space=pltpu.VMEM)
+    return pl.pallas_call(
+        merge_kernel,
+        in_specs=[whole] * 2,
+        out_specs=whole,
+        out_shape=jax.ShapeDtypeStruct(first.shape, first.dtype),
+        compiler_params=params(8),
+        cost_estimate=pl.CostEstimate(flops=500_000, bytes_accessed=1_000_000, transcendentals=0),
+        name="merge_shares",
+    )(first, second)
 
 
 def attend_kernel(kinds, last, starts, flags, *refs):
@@ -221,22 +272,14 @@
                 outs[n][here, head] = mixed[n * PIECE : (n + 1) * PIECE]
             level_ref[:, lane] = level[:, lane]
     if last:
-        tail = slice(TILE_COLS * PIECE, (TILE_COLS + 1) * PIECE)
-        rest = level_ref[...]
-        for part in range(3):
-            rounded = rest.astype(jnp.bfloat16)
-            rest = rest - rounded.astype(jnp.float32)
-            for n in range(PLANE):
-                outs[n][tail, part * HEAD_DIM : (part + 1) * HEAD_DIM] = rounded[
-                    n * PIECE : (n + 1) * PIECE
-                ]
-
-
-def attend(starts, flags, queries, slots, before=()):
+        for n in range(PLANE):
+            store_level(outs[n], level_ref[n * PIECE : (n + 1) * PIECE])
+
+
+def attend(starts, flags, queries, slots, kinds, before=()):
     tokens = TILE_COLS * PIECE
     count = len(slots)
     last = bool(before)
-    kinds = (1, 2, 2) if last else (0, 0, 1)
     whole = pl.BlockSpec(memory_space=pltpu.VMEM)
     scalars = pl.BlockSpec(memory_space=pltpu.SMEM)
     operands = [*queries, *slots, *before]
@@ -263,36 +306,18 @@
     )(starts, flags, *operands)
 
 
+def term(ids, k, attended, w_ref, out_ref):
+    columns = pl.ds(pl.multiple_of((ids[1] ^ k) * WIDTH, WIDTH), WIDTH)
+    out_ref[...] = jnp.dot(
+        attended, w_ref[:, columns], preferred_element_type=jnp.float32
+    ).astype(jnp.bfloat16)
+
+
 def join_kernel(ids, *refs):
-    shares, w_ref = refs[:PLANE], refs[PLANE]
-    outs, joined = refs[PLANE + 1 : PLANE + 1 + N_HEAD], refs[-1]
-    tail = slice(TILE_COLS * PIECE, (TILE_COLS + 1) * PIECE)
-    level = []
-    for ref in shares:
-        parts = [
-            ref[tail, n * HEAD_DIM : (n + 1) * HEAD_DIM].astype(jnp.float32) for n in range(3)
-        ]
-        level.append(parts[0] + (parts[1] + parts[2]))
-    top = functools.reduce(jnp.maximum, level)
-    weight = [jnp.exp2(value - top) for value in level]
-    scale = 1.0 / functools.reduce(jnp.add, weight)
-    weight = [value * scale for value in weight]
-    for c in range(TILE_COLS):
-        rows = slice(c * PIECE, (c + 1) * PIECE)
-        for h in range(HEADS_HERE):
-            head = slice(h * HEAD_DIM, (h + 1) * HEAD_DIM)
-            lane = HEADS_HERE * c + h
-            total = None
-            for k in range(PLANE):
-                term = weight[k][:, lane : lane + 1] * shares[k][rows, head].astype(jnp.float32)
-                total = term if total is None else total + term
-            joined[rows, head] = total.astype(jnp.bfloat16)
-    attended = joined[...]
-    for k in range(N_HEAD):
-        columns = pl.ds(pl.multiple_of((ids[1] ^ k) * WIDTH, WIDTH), WIDTH)
-        outs[k][...] = jnp.dot(
-            attended, w_ref[:, columns], preferred_element_type=jnp.float32
-        ).astype(jnp.bfloat16)
+    *shares, w_ref, joined = refs[: -len(RELAYED)]
+    merge(shares, joined)
+    for k, out_ref in zip(RELAYED, refs[-len(RELAYED) :]):
+        term(ids, k, joined[...], w_ref, out_ref)
 
 
 def join(ids, shares, w_out):
@@ -300,20 +325,39 @@
     whole = pl.BlockSpec(memory_space=pltpu.VMEM)
     return pl.pallas_call(
         join_kernel,
-        in_specs=[pl.BlockSpec(memory_space=pltpu.SMEM)] + [whole] * (PLANE + 1),
-        out_specs=[whole] * N_HEAD,
-        out_shape=[jax.ShapeDtypeStruct((tokens, WIDTH), jnp.bfloat16)] * N_HEAD,
-        scratch_shapes=[pltpu.VMEM((tokens, WIDTH), jnp.bfloat16)],
+        in_specs=[pl.BlockSpec(memory_space=pltpu.SMEM)] + [whole] * (len(shares) + 1),
+        out_specs=[whole] * (1 + len(RELAYED)),
+        out_shape=[jax.ShapeDtypeStruct((tokens, WIDTH), jnp.bfloat16)] * (1 + len(RELAYED)),
         compiler_params=params(16),
         cost_estimate=pl.CostEstimate(
-            flops=2 * tokens * WIDTH * D, bytes_accessed=5_000_000, transcendentals=0
+            flops=2 * tokens * WIDTH * WIDTH * len(RELAYED), bytes_accessed=3_000_000, transcendentals=0
         ),
         name="join",
     )(ids, *shares, w_out)
 
 
+def terms_kernel(ids, joined, w_ref, *outs):
+    for k, out_ref in zip(DIRECT, outs):
+        term(ids, k, joined[...], w_ref, out_ref)
+
+
+def direct_terms(ids, joined, w_out):
+    whole = pl.BlockSpec(memory_space=pltpu.VMEM)
+    return pl.pallas_call(
+        terms_kernel,
+        in_specs=[pl.BlockSpec(memory_space=pltpu.SMEM)] + [whole] * 2,
+        out_specs=[whole] * len(DIRECT),
+        out_shape=[jax.ShapeDtypeStruct(joined.shape, jnp.bfloat16)] * len(DIRECT),
+        compiler_params=params(16),
+        cost_estimate=pl.CostEstimate(
+            flops=2 * joined.size * WIDTH * len(DIRECT), bytes_accessed=4_000_000, transcendentals=0
+        ),
+        name="direct_terms",
+    )(ids, joined, w_out)
+
+
 def add_kernel(side, *refs):
-    terms, (kept_ref, given_ref, rows) = refs[:N_HEAD], refs[N_HEAD:]
+    *terms, kept_ref, given_ref, rows = refs
     total = terms[0][...].astype(jnp.float32)
     for ref in terms[1:]:
         total = total + ref[...].astype(jnp.float32)
@@ -329,7 +373,7 @@
     whole = pl.BlockSpec(memory_space=pltpu.VMEM)
     return pl.pallas_call(
         add_kernel,
-        in_specs=[pl.BlockSpec(memory_space=pltpu.SMEM)] + [whole] * N_HEAD,
+        in_specs=[pl.BlockSpec(memory_space=pltpu.SMEM)] + [whole] * len(terms),
         out_specs=[whole] * 2,
         out_shape=[jax.ShapeDtypeStruct((TILE_COLS * PAIR, WIDTH), jnp.bfloat16)] * 2,
         scratch_shapes=[pltpu.VMEM((TILE_COLS * PIECE, WIDTH), jnp.bfloat16)],
@@ -414,10 +458,15 @@
     ids = jnp.stack([lax.axis_index("seq"), lax.axis_index("head")]).astype(jnp.int32)
     weight = load_weight(jnp.transpose(w_qkv, (1, 0, 2)))
     q_gain, k_gain = q_gain.reshape(1, HEAD_DIM), k_gain.reshape(1, HEAD_DIM)
-    starts, flags, tile_of, first, half = plan(ids, neighbours, tile_owner)
-
-    pieces = [latent.reshape(PIECE, D)]
-    pieces += [head_swap(pieces[0], k) for k in range(1, N_HEAD)]
+    starts, flags, tile_of, first, half = plan(ids, neighbours.T, tile_owner)
+
+    pieces = [latent.reshape(PIECE, D)] * N_HEAD
+    for k in (1, 2, 3, 6, 7):
+        pieces[k] = head_swap(pieces[0], k)
+    pieces[4], pieces[5] = head_swap(pieces[6], 2), head_swap(pieces[3], 6)
+
+    tables = (starts, flags, tile_of, first, half)
+    (starts, flags, tile_of, first, half), pieces = lax.optimization_barrier((tables, pieces))
 
     queries, rows = project_queries(ids, pieces, weight, q_gain)
     all_queries = [queries] + [plane_swap(queries, k) for k in range(1, PLANE)]
@@ -426,12 +475,17 @@
     mate, edge, *all_queries = lax.optimization_barrier((mate, edge, *all_queries))
     far_1, edge_2 = mate_swap(edge), edge_swap(mate)
     far_2 = mate_swap(edge_2)
-    near = attend(starts, flags, all_queries, [own, mate, edge])
-    shares = attend(starts, flags, all_queries, [edge_2, far_1, far_2], near)
-    shares = [shares[0]] + [plane_swap(shares[k], k) for k in range(1, PLANE)]
-
-    terms = join(ids, shares, w_out)
-    terms = [terms[0]] + [head_swap(terms[k], k) for k in range(1, N_HEAD)]
+    near = attend(starts, flags, all_queries, [own, mate, edge], (0, 0, 1))
+    shares = attend(starts, flags, all_queries, [edge_2, far_1, far_2], (1, 2, 2), near)
+    from_core, for_chip = plane_swap(shares[1], 1), plane_swap(shares[3], 1)
+    from_chip = plane_swap(merge_shares(shares[2], for_chip), 2)
+
+    joined, *relayed = join(ids, [shares[0], from_core, from_chip], w_out)
+    passed = {6: head_swap(relayed[0], 2), 3: head_swap(relayed[1], 6)}
+    terms = dict(zip(DIRECT, direct_terms(ids, joined, w_out)))
+    for k in (6, 3):
+        terms[k] = (terms[k].astype(jnp.float32) + passed[k].astype(jnp.float32)).astype(jnp.bfloat16)
+    terms = [terms[0]] + [head_swap(terms[k], k) for k in DIRECT[1:]]
 
     kept, given = add_terms(half, terms)
     sent = order(half, tile_of, kept, plane_swap(given, TILE))

time: 157 us -> 136 us (0.87)
  starting transfers between devices: 69.4 us -> 51.7 us
  local copies, waits for them, and re-layouts: 7.51 us -> 3.04 us
  blocking collectives: 21.4 us -> 23.3 us
    ppermute x14, starting transfers between devices: 39.7 us -> 23 us  [head_swap(): return lax.ppermute(array, 'head', [(h, h ^ k) for h in range(N_HEAD)])]
    unnamed x23 -> x14, local copies, waits for them, and re-layouts: 7.51 us -> 3.04 us
    ppermute x10, waiting for transfers between devices: 21.6 us -> 24.8 us  [plane_swap(): lax.ppermute(array, 'seq', [(s, s ^ k) for s in range(PLANE * PLANES)])]
    ppermute x14, waiting for transfers between devices: 12.2 us -> 9.98 us  [head_swap(): return lax.ppermute(array, 'head', [(h, h ^ k) for h in range(N_HEAD)])]
    all_to_all x1, blocking collectives: 21.4 us -> 23.3 us  [local(): lax.all_to_all(sent.reshape(TILES, PAIR, WIDTH), 'seq', split_axis=0, con...]
    pallas_call x0 -> x2, Pallas kernels: none -> 1.74 us  [the longest x1 1.42 us: direct_terms(): pl.pallas_call(terms_kernel, in_specs=[pl.BlockSpec(memory_space=pltpu.SM...]
  transfers between devices with their start and end apart: 26 -> 26, of which waited for: 11 -> 10; matrix products, arithmetic and copies ran while one was open for 1% -> 0% of each run, Pallas kernels for 5% -> 6%
where the time goes in v3:
time: 136 us; the launch traced here: 135 us
  starting transfers between devices  51.7 us (38%)
  waiting for transfers between devices  34.8 us (26%)
  blocking collectives  23.3 us (17%)
  Pallas kernels  22.2 us (16%)
  local copies, waits for them, and re-layouts  3.04 us (2%)
    ppermute x10, starting transfers between devices, plane_swap(): lax.ppermute(array, 'seq', [(s, s ^ k) for s in range(PLANE * PLANES)])  27.3 us
    ppermute x10, waiting for transfers between devices, plane_swap(): lax.ppermute(array, 'seq', [(s, s ^ k) for s in range(PLANE * PLANES)])  24.8 us
    all_to_all x1, blocking collectives, local(): lax.all_to_all(sent.reshape(TILES, PAIR, WIDTH), 'seq', split_axis=0, con...  23.3 us
    ppermute x14, starting transfers between devices, head_swap(): return lax.ppermute(array, 'head', [(h, h ^ k) for h in range(N_HEAD)])  23 us
    ppermute x14, waiting for transfers between devices, head_swap(): return lax.ppermute(array, 'head', [(h, h ^ k) for h in range(N_HEAD)])  9.98 us
    pallas_call x2, Pallas kernels, attend(): pl.pallas_call(functools.partial(attend_kernel, kinds, last), in_specs=[s...  8.13 us
    unnamed x14, local copies, waits for them, and re-layouts  3.04 us
  transfers between devices with their start and end apart: 26, of which 10 were waited for; matrix products, arithmetic and copies ran while one was open for 0% of the time, Pallas kernels for 6%

profile of v3, /device:TPU:2, one launch (start us, length us, event | category | flops | bytes accessed | tf_op | source)
XLA Modules:
  0.0 135.4 jit_solution(10148580967210899857)
XLA Ops:
  0.0 3.0 %collective-permute-start.3 = (bf16[32,3072]{1,0:T(8,128)(2,1)}, bf16[32,3072]{1,0:T(8,128)(2,1)S(1)}, u32[]{:S(2)}, u32[]{:S(2)}) collective-permute-start(bf16[32,3072]{1,0:T(8,128)(2,1)} %bitcast.13), channel_id=1, source_target_pairs={{0,6},{1,7},{2,4},{3,5},{4,2},{5,3},{6,0},{7,1},{8,14},{9,15},{10,... | collective-permute-start | bytes 589832 | tf_op jit(solution)/shard_map/ppermute | solution.py:438
  3.0 1.7 %collective-permute-start.2 = (bf16[32,3072]{1,0:T(8,128)(2,1)}, bf16[32,3072]{1,0:T(8,128)(2,1)S(1)}, u32[]{:S(2)}, u32[]{:S(2)}) collective-permute-start(bf16[32,3072]{1,0:T(8,128)(2,1)} %bitcast.14), channel_id=1, source_target_pairs={{0,3},{1,2},{2,1},{3,0},{4,7},{5,6},{6,5},{7,4},{8,11},{9,10},{10,... | collective-permute-start | bytes 589832 | tf_op jit(solution)/shard_map/ppermute | solution.py:438
  4.7 1.9 %collective-permute-start.6 = (bf16[32,3072]{1,0:T(8,128)(2,1)}, bf16[32,3072]{1,0:T(8,128)(2,1)S(1)}, u32[]{:S(2)}, u32[]{:S(2)}) collective-permute-start(bf16[32,3072]{1,0:T(8,128)(2,1)} %bitcast.15), channel_id=1, source_target_pairs={{0,7},{1,6},{2,5},{3,4},{4,3},{5,2},{6,1},{7,0},{8,15},{9,14},{10,... | collective-permute-start | bytes 589832 | tf_op jit(solution)/shard_map/ppermute | solution.py:438
  6.6 0.5 collective-permute-start.1
  7.1 2.1 %collective-permute-start = (bf16[32,3072]{1,0:T(8,128)(2,1)}, bf16[32,3072]{1,0:T(8,128)(2,1)S(1)}, u32[]{:S(2)}, u32[]{:S(2)}) collective-permute-start(bf16[32,3072]{1,0:T(8,128)(2,1)} %bitcast.17), channel_id=1, source_target_pairs={{0,1},{1,0},{2,3},{3,2},{4,5},{5,4},{6,7},{7,6},{8,9},{9,8},{10,11... | collective-permute-start | bytes 589832 | tf_op jit(solution)/shard_map/ppermute | solution.py:438
  9.2 0.0 collective-permute-done.3.refs_6_
  9.2 1.6 %collective-permute-start.4 = (bf16[32,3072]{1,0:T(8,128)(2,1)S(1)}, bf16[32,3072]{1,0:T(8,128)(2,1)S(1)}, u32[]{:S(2)}, u32[]{:S(2)}) collective-permute-start(bf16[32,3072]{1,0:T(8,128)(2,1)S(1)} %collective-permute-done.3.refs_6_), channel_id=1, source_target_pairs={{0,2},{1,3},{2,0},{3,1},{4,6},{5,7},{6,4},{7,5},{8,10},{9,11},{10,... | collective-permute-start | bytes 589832 | tf_op jit(solution)/shard_map/ppermute | solution.py:438
  10.8 2.7 %collective-permute-done.2.refs_3_ = bf16[32,3072]{1,0:T(8,128)(2,1)S(1)} collective-permute-done((bf16[32,3072]{1,0:T(8,128)(2,1)}, bf16[32,3072]{1,0:T(8,128)(2,1)S(1)}, u32[]{:S(2)}, u32[]{:S(2)}) %collective-permute-start.2) | collective-permute-done | bytes 196640 | tf_op jit(solution)/shard_map/ppermute | solution.py:438
  13.5 0.0 collective-permute-start.5
  13.5 3.0 %copy-done.1 = bf16[3072,3,384]{2,0,1:T(8,128)(2,1)S(1)} copy-done((bf16[3072,3,384]{2,0,1:T(8,128)(2,1)S(1)}, bf16[3072,3,384]{2,0,1:T(8,128)(2,1)}, u32[]{:S(2)}) %copy-start.1) | copy-done | bytes 7077912
  16.5 1.6 %load_weight.1.refs_8_.w_ref = bf16[3,3072,384]{2,1,0:T(8,128)(2,1)S(1)} custom-call(bf16[3,3072,384]{2,1,0:T(8,128)(2,1)S(1)} %bitcast.10), custom_call_target="tpu_custom_call" | custom-call | bytes 7100000 | tf_op jit(solution)/shard_map/load_weight/pallas_call | solution.py:111
  18.1 0.0 copy-start.5
  18.1 0.1 pad_add_fusion.ids
  18.2 2.3 %plan.1 = (s32[8]{0:T(128)S(1)}, s32[8,9]{1,0:T(8,128)S(1)}, s32[32]{0:T(128)S(1)}, s32[1]{0:T(128)}, s32[1]{0:T(128)}) custom-call(s32[2]{0:T(128)S(1)} %pad_add_fusion.ids, s32[9,32]{1,0:T(8,128)S(1)} %bitcast.19, s32[32]{0:T(128)S(1)} %copy-done.6), custom_call_target="tpu_custom_call" | custom-call | bytes 8000000 | tf_op jit(solution)/shard_map/plan/pallas_call | solution.py:69
  20.5 0.0 collective-permute-done.6.refs_7_
  20.5 0.0 collective-permute-done.1.refs_2_
  20.5 0.0 collective-permute-done.refs_1_
  20.5 1.7 %project_queries.1 = (bf16[256,384]{1,0:T(8,128)(2,1)S(1)}, bf16[256,3072]{1,0:T(8,128)(2,1)S(1)}) custom-call(s32[2]{0:T(128)S(1)} %pad_add_fusion.ids, bf16[32,3072]{1,0:T(8,128)(2,1)S(1)} %bitcast.18, bf16[32,3072]{1,0:T(8,128)(2,1)S(1)} %collective-permute-done.refs_1_, bf16[32,3072]{1,0:T(8,128)(2,1)S(1)} %collective-permute-done.1.refs_2_, ...), custom_call_target="tpu_custom_call" | custom-call | flops 603979776 | bytes 4000000 | tf_op jit(solution)/shard_map/project_queries/pallas_call | solution.py:133
  22.3 0.0 copy-start
  22.3 1.8 %project_keys.1.refs_4_ = bf16[256,768]{1,0:T(8,128)(2,1)S(1)} custom-call(bf16[256,3072]{1,0:T(8,128)(2,1)S(1)} %get-tuple-element.69.rows_ref, bf16[3,3072,384]{2,1,0:T(8,128)(2,1)S(1)} %load_weight.1.refs_8_.w_ref, f32[1,128]{1,0:T(1,128)S(1)} %bitcast.21), custom_call_target="tpu_custom_call" | custom-call | flops 1207959552 | bytes 6000000 | tf_op jit(solution)/shard_map/project_keys/pallas_call | solution.py:160
  24.1 0.7 collective-permute-start.8
  24.8 5.1 %collective-permute-start.7 = (bf16[256,768]{1,0:T(8,128)(2,1)S(1)}, bf16[256,768]{1,0:T(8,128)(2,1)S(1)}, u32[]{:S(2)}, u32[]{:S(2)}) collective-permute-start(bf16[256,768]{1,0:T(8,128)(2,1)S(1)} %project_keys.1.refs_4_), channel_id=1, source_target_pairs={{0,32},{8,40},{16,48},{24,56},{32,0},{40,8},{48,16},{56,24},{64,96... | collective-permute-start | bytes 1179656 | tf_op jit(solution)/shard_map/ppermute | solution.py:442
  30.0 1.0 collective-permute-start.10
  30.9 0.9 collective-permute-start.9
  31.8 5.3 %collective-permute-done.11.refs_3_ = bf16[256,384]{1,0:T(8,128)(2,1)S(1)} collective-permute-done((bf16[256,384]{1,0:T(8,128)(2,1)S(1)}, bf16[256,384]{1,0:T(8,128)(2,1)S(1)}, u32[]{:S(2)}, u32[]{:S(2)}) %collective-permute-start.11) | collective-permute-done | bytes 196640 | tf_op jit(solution)/shard_map/ppermute | solution.py:442
  37.1 3.4 %collective-permute-done.10.refs_2_ = bf16[256,384]{1,0:T(8,128)(2,1)S(1)} collective-permute-done((bf16[256,384]{1,0:T(8,128)(2,1)S(1)}, bf16[256,384]{1,0:T(8,128)(2,1)S(1)}, u32[]{:S(2)}, u32[]{:S(2)}) %collective-permute-start.10) | collective-permute-done | bytes 196640 | tf_op jit(solution)/shard_map/ppermute | solution.py:442
  40.5 0.7 collective-permute-start.12
  41.2 6.4 %collective-permute-start.13 = (bf16[256,768]{1,0:T(8,128)(2,1)S(1)}, bf16[256,768]{1,0:T(8,128)(2,1)S(1)}, u32[]{:S(2)}, u32[]{:S(2)}) collective-permute-start(bf16[256,768]{1,0:T(8,128)(2,1)S(1)} %collective-permute-done.8.refs_6_), channel_id=1, source_target_pairs={{0,32},{8,40},{16,48},{24,56},{32,0},{40,8},{48,16},{56,24},{64,96... | collective-permute-start | bytes 1179656 | tf_op jit(solution)/shard_map/ppermute | solution.py:442
  47.6 0.0 collective-permute-done.12.refs_4_
  47.6 9.4 %collective-permute-start.14 = (bf16[256,768]{1,0:T(8,128)(2,1)S(1)}, bf16[256,768]{1,0:T(8,128)(2,1)S(1)}, u32[]{:S(2)}, u32[]{:S(2)}) collective-permute-start(bf16[256,768]{1,0:T(8,128)(2,1)S(1)} %collective-permute-done.12.refs_4_), channel_id=1, source_target_pairs={{0,32},{8,40},{16,48},{24,56},{32,0},{40,8},{48,16},{56,24},{64,96... | collective-permute-start | bytes 1179656 | tf_op jit(solution)/shard_map/ppermute | solution.py:442
  57.0 3.1 %attend.2 = (bf16[256,384]{1,0:T(8,128)(2,1)S(1)}, bf16[256,384]{1,0:T(8,128)(2,1)S(1)}, bf16[256,384]{1,0:T(8,128)(2,1)S(1)}, bf16[256,384]{1,0:T(8,128)(2,1)S(1)}, f32[128,128]{1,0:T(8,128)S(1)}) custom-call(s32[8]{0:T(128)S(1)} %get-tuple-element.59.starts, s32[8,9]{1,0:T(8,128)S(1)} %get-tuple-element.60.flags, ...), custom_call_target="tpu_custom_call" | custom-call | flops 452984832 | bytes 4000000 | tf_op jit(solution)/shard_map/attend/pallas_call | solution.py:293
  60.0 0.0 collective-permute-done.13.refs_5_
  60.0 5.9 %collective-permute-done.14.refs_6_ = bf16[256,768]{1,0:T(8,128)(2,1)S(1)} collective-permute-done((bf16[256,768]{1,0:T(8,128)(2,1)S(1)}, bf16[256,768]{1,0:T(8,128)(2,1)S(1)}, u32[]{:S(2)}, u32[]{:S(2)}) %collective-permute-start.14) | collective-permute-done | bytes 393248 | tf_op jit(solution)/shard_map/ppermute | solution.py:442
  66.0 5.1 %attend.3 = (bf16[288,384]{1,0:T(8,128)(2,1)S(1)}, bf16[288,384]{1,0:T(8,128)(2,1)S(1)}, bf16[288,384]{1,0:T(8,128)(2,1)S(1)}, bf16[288,384]{1,0:T(8,128)(2,1)S(1)}) custom-call(s32[8]{0:T(128)S(1)} %get-tuple-element.59.starts, s32[8,9]{1,0:T(8,128)S(1)} %get-tuple-element.60.flags, bf16[256,384]{1,0:T(8,128)(2,1)S(1)} %get-tuple-element.71.refs_0_, ...), custom_call_target="tpu_custom_call" | custom-call | flops 452984832 | bytes 4000000 | tf_op jit(solution)/shard_map/attend/pallas_call | solution.py:293
  71.1 0.1 collective-permute-start.16
  71.2 0.5 collective-permute-start.15
  71.7 1.0 collective-permute-done.16.second_ref
  72.6 0.3 merge_shares.1
  73.0 1.0 collective-permute-start.17
  74.0 6.5 %collective-permute-done.17.refs_2_ = bf16[288,384]{1,0:T(8,128)(2,1)S(1)} collective-permute-done((bf16[288,384]{1,0:T(8,128)(2,1)S(1)}, bf16[288,384]{1,0:T(8,128)(2,1)S(1)}, u32[]{:S(2)}, u32[]{:S(2)}) %collective-permute-start.17) | collective-permute-done | bytes 221216 | tf_op jit(solution)/shard_map/ppermute | solution.py:442
  80.5 1.4 %join.1 = (bf16[256,384]{1,0:T(8,128)(2,1)S(1)}, bf16[256,384]{1,0:T(8,128)(2,1)S(1)}, bf16[256,384]{1,0:T(8,128)(2,1)S(1)}) custom-call(s32[2]{0:T(128)S(1)} %pad_add_fusion.ids, bf16[288,384]{1,0:T(8,128)(2,1)S(1)} %get-tuple-element.82.refs_0_, bf16[288,384]{1,0:T(8,128)(2,1)S(1)} %collective-permute-done.15.refs_1_, ...), custom_call_target="tpu_custom_call" | custom-call | flops 150994944 | bytes 3000000 | tf_op jit(solution)/shard_map/join/pallas_call | solution.py:326
  81.9 0.6 collective-permute-start.21
  82.5 2.6 %collective-permute-start.23 = (bf16[256,384]{1,0:T(8,128)(2,1)S(1)}, bf16[256,384]{1,0:T(8,128)(2,1)S(1)}, u32[]{:S(2)}, u32[]{:S(2)}) collective-permute-start(bf16[256,384]{1,0:T(8,128)(2,1)S(1)} %get-tuple-element.94), channel_id=1, source_target_pairs={{0,6},{1,7},{2,4},{3,5},{4,2},{5,3},{6,0},{7,1},{8,14},{9,15},{10,... | collective-permute-start | bytes 589832 | tf_op jit(solution)/shard_map/ppermute | solution.py:438
  85.2 1.4 %direct_terms.1 = (bf16[256,384]{1,0:T(8,128)(2,1)S(1)}, bf16[256,384]{1,0:T(8,128)(2,1)S(1)}, bf16[256,384]{1,0:T(8,128)(2,1)S(1)}, bf16[256,384]{1,0:T(8,128)(...) custom-call(s32[2]{0:T(128)S(1)} %pad_add_fusion.ids, ...), custom_call_target="tpu_custom_call" | custom-call | flops 452984832 | bytes 4000000 | tf_op jit(solution)/shard_map/direct_terms/pallas_call | solution.py:346
  86.6 2.4 %collective-permute-start.18 = (bf16[256,384]{1,0:T(8,128)(2,1)S(1)}, bf16[256,384]{1,0:T(8,128)(2,1)S(1)}, u32[]{:S(2)}, u32[]{:S(2)}) collective-permute-start(bf16[256,384]{1,0:T(8,128)(2,1)S(1)} %get-tuple-element.88), channel_id=1, source_target_pairs={{0,1},{1,0},{2,3},{3,2},{4,5},{5,4},{6,7},{7,6},{8,9},{9,8},{10,11... | collective-permute-start | bytes 589832 | tf_op jit(solution)/shard_map/ppermute | solution.py:438
  88.9 1.3 collective-permute-start.19
  90.3 1.3 collective-permute-start.20
  91.6 0.0 collective-permute-done.21
  91.6 0.1 add_convert_fusion.1
  91.6 2.7 %collective-permute-start.22 = (bf16[256,384]{1,0:T(8,128)(2,1)S(1)}, bf16[256,384]{1,0:T(8,128)(2,1)S(1)}, u32[]{:S(2)}, u32[]{:S(2)}) collective-permute-start(bf16[256,384]{1,0:T(8,128)(2,1)S(1)} %add_convert_fusion.1), channel_id=1, source_target_pairs={{0,6},{1,7},{2,4},{3,5},{4,2},{5,3},{6,0},{7,1},{8,14},{9,15},{10,... | collective-permute-start | bytes 589832 | tf_op jit(solution)/shard_map/ppermute | solution.py:438
  94.3 0.0 collective-permute-done.23
  94.3 0.1 add_convert_fusion
  94.4 1.3 collective-permute-start.24
  95.7 0.0 collective-permute-done.18.refs_1_
  95.7 0.0 collective-permute-done.19.refs_2_
  95.7 5.4 %collective-permute-done.20.refs_3_ = bf16[256,384]{1,0:T(8,128)(2,1)S(1)} collective-permute-done((bf16[256,384]{1,0:T(8,128)(2,1)S(1)}, bf16[256,384]{1,0:T(8,128)(2,1)S(1)}, u32[]{:S(2)}, u32[]{:S(2)}) %collective-permute-start.20) | collective-permute-done | bytes 196640 | tf_op jit(solution)/shard_map/ppermute | solution.py:438
  101.1 1.0 collective-permute-done.22.refs_4_
  102.1 0.8 collective-permute-done.24.refs_5_
  102.9 0.9 add_terms.1
  103.8 2.9 %collective-permute-start.25 = (bf16[128,384]{1,0:T(8,128)(2,1)S(1)}, bf16[128,384]{1,0:T(8,128)(2,1)S(1)}, u32[]{:S(2)}, u32[]{:S(2)}) collective-permute-start(bf16[128,384]{1,0:T(8,128)(2,1)S(1)} %get-tuple-element.96), channel_id=1, source_target_pairs={{0,64},{8,72},{16,80},{24,88},{32,96},{40,104},{48,112},{56,120},{... | collective-permute-start | bytes 294920 | tf_op jit(solution)/shard_map/ppermute | solution.py:442
  106.7 2.7 %collective-permute-done.25.got_ref = bf16[128,384]{1,0:T(8,128)(2,1)S(1)} collective-permute-done((bf16[128,384]{1,0:T(8,128)(2,1)S(1)}, bf16[128,384]{1,0:T(8,128)(2,1)S(1)}, u32[]{:S(2)}, u32[]{:S(2)}) %collective-permute-start.25) | collective-permute-done | bytes 98336 | tf_op jit(solution)/shard_map/ppermute | solution.py:442
  109.4 1.3 order.1
  110.8 23.3 %all_to_all.5 = bf16[32,16,384]{2,1,0:T(8,128)(2,1)S(1)} all-to-all(bf16[32,16,384]{2,1,0:T(8,128)(2,1)S(1)} %bitcast.11), channel_id=1, replica_groups=mesh['seq'=32,'head'=8] {'seq'}, dimensions={0} | all-to-all | bytes 786432 | tf_op jit(solution)/shard_map/all_to_all | solution.py:492
  134.0 1.3 to_tile.1
  (18 shorter events, 0.0 us)
Async XLA Ops:
  0.0 9.2 %collective-permute-start.3 = (bf16[32,3072]{1,0:T(8,128)(2,1)}, bf16[32,3072]{1,0:T(8,128)(2,1)S(1)}, u32[]{:S(2)}, u32[]{:S(2)}) collective-permute-start(bf16[32,3072]{1,0:T(8,128)(2,1)} %bitcast.13), channel_id=1, source_target_pairs={{0,6},{1,7},{2,4},{3,5},{4,2},{5,3},{6,0},{7,1},{8,14},{9,15},{10,... | collective-permute-start | bytes 589832 | tf_op jit(solution)/shard_map/ppermute | solution.py:438
  3.0 10.5 %collective-permute-start.2 = (bf16[32,3072]{1,0:T(8,128)(2,1)}, bf16[32,3072]{1,0:T(8,128)(2,1)S(1)}, u32[]{:S(2)}, u32[]{:S(2)}) collective-permute-start(bf16[32,3072]{1,0:T(8,128)(2,1)} %bitcast.14), channel_id=1, source_target_pairs={{0,3},{1,2},{2,1},{3,0},{4,7},{5,6},{6,5},{7,4},{8,11},{9,10},{10,... | collective-permute-start | bytes 589832 | tf_op jit(solution)/shard_map/ppermute | solution.py:438
  4.7 15.8 %collective-permute-start.6 = (bf16[32,3072]{1,0:T(8,128)(2,1)}, bf16[32,3072]{1,0:T(8,128)(2,1)S(1)}, u32[]{:S(2)}, u32[]{:S(2)}) collective-permute-start(bf16[32,3072]{1,0:T(8,128)(2,1)} %bitcast.15), channel_id=1, source_target_pairs={{0,7},{1,6},{2,5},{3,4},{4,3},{5,2},{6,1},{7,0},{8,15},{9,14},{10,... | collective-permute-start | bytes 589832 | tf_op jit(solution)/shard_map/ppermute | solution.py:438
  6.6 13.9 %collective-permute-start.1 = (bf16[32,3072]{1,0:T(8,128)(2,1)}, bf16[32,3072]{1,0:T(8,128)(2,1)S(1)}, u32[]{:S(2)}, u32[]{:S(2)}) collective-permute-start(bf16[32,3072]{1,0:T(8,128)(2,1)} %bitcast.16), channel_id=1, source_target_pairs={{0,2},{1,3},{2,0},{3,1},{4,6},{5,7},{6,4},{7,5},{8,10},{9,11},{10,... | collective-permute-start | bytes 589832 | tf_op jit(solution)/shard_map/ppermute | solution.py:438
  7.1 13.4 %collective-permute-start = (bf16[32,3072]{1,0:T(8,128)(2,1)}, bf16[32,3072]{1,0:T(8,128)(2,1)S(1)}, u32[]{:S(2)}, u32[]{:S(2)}) collective-permute-start(bf16[32,3072]{1,0:T(8,128)(2,1)} %bitcast.17), channel_id=1, source_target_pairs={{0,1},{1,0},{2,3},{3,2},{4,5},{5,4},{6,7},{7,6},{8,9},{9,8},{10,11... | collective-permute-start | bytes 589832 | tf_op jit(solution)/shard_map/ppermute | solution.py:438
  9.2 11.3 %collective-permute-start.4 = (bf16[32,3072]{1,0:T(8,128)(2,1)S(1)}, bf16[32,3072]{1,0:T(8,128)(2,1)S(1)}, u32[]{:S(2)}, u32[]{:S(2)}) collective-permute-start(bf16[32,3072]{1,0:T(8,128)(2,1)S(1)} %collective-permute-done.3.refs_6_), channel_id=1, source_target_pairs={{0,2},{1,3},{2,0},{3,1},{4,6},{5,7},{6,4},{7,5},{8,10},{9,11},{10,... | collective-permute-start | bytes 589832 | tf_op jit(solution)/shard_map/ppermute | solution.py:438
  13.5 7.0 %collective-permute-start.5 = (bf16[32,3072]{1,0:T(8,128)(2,1)S(1)}, bf16[32,3072]{1,0:T(8,128)(2,1)S(1)}, u32[]{:S(2)}, u32[]{:S(2)}) collective-permute-start(bf16[32,3072]{1,0:T(8,128)(2,1)S(1)} %collective-permute-done.2.refs_3_), channel_id=1, source_target_pairs={{0,6},{1,7},{2,4},{3,5},{4,2},{5,3},{6,0},{7,1},{8,14},{9,15},{10,... | collective-permute-start | bytes 589832 | tf_op jit(solution)/shard_map/ppermute | solution.py:438
  13.5 3.0 %copy-start.1 = (bf16[3072,3,384]{2,0,1:T(8,128)(2,1)S(1)}, bf16[3072,3,384]{2,0,1:T(8,128)(2,1)}, u32[]{:S(2)}) copy-start(bf16[3072,3,384]{2,0,1:T(8,128)(2,1)} %param.8) | copy-start | bytes 21233668
  16.5 1.7 %copy-start.3 = (s32[32,9]{0,1:T(8,128)S(1)}, s32[32,9]{0,1:T(8,128)}, u32[]{:S(2)}) copy-start(s32[32,9]{0,1:T(8,128)} %param.12) | copy-start | bytes 3460
  16.5 1.7 %copy-start.6 = (s32[32]{0:T(128)S(1)}, s32[32]{0:T(128)}, u32[]{:S(2)}) copy-start(s32[32]{0:T(128)} %tile_owner.1) | copy-start | bytes 388
  16.5 4.0 %copy-start.2 = (bf16[4,1,8,3072]{3,2,1,0:T(8,128)(2,1)S(1)}, bf16[4,1,8,3072]{3,2,1,0:T(8,128)(2,1)}, u32[]{:S(2)}) copy-start(bf16[4,1,8,3072]{3,2,1,0:T(8,128)(2,1)} %param.7) | copy-start | bytes 589828
  16.5 4.0 %copy-start.4 = (f32[128]{0:T(128)S(1)}, f32[128]{0:T(128)}, u32[]{:S(2)}) copy-start(f32[128]{0:T(128)} %param.9) | copy-start | bytes 1540
  18.1 4.2 %copy-start.5 = (f32[128]{0:T(128)S(1)}, f32[128]{0:T(128)}, u32[]{:S(2)}) copy-start(f32[128]{0:T(128)} %param.10) | copy-start | bytes 1540
  22.3 58.2 %copy-start = (bf16[384,3072]{1,0:T(8,128)(2,1)S(1)}, bf16[384,3072]{1,0:T(8,128)(2,1)}, u32[]{:S(2)}) copy-start(bf16[384,3072]{1,0:T(8,128)(2,1)} %w_ref.1) | copy-start | bytes 7077892
  24.1 16.4 %collective-permute-start.8 = (bf16[256,768]{1,0:T(8,128)(2,1)S(1)}, bf16[256,768]{1,0:T(8,128)(2,1)S(1)}, u32[]{:S(2)}, u32[]{:S(2)}) collective-permute-start(bf16[256,768]{1,0:T(8,128)(2,1)S(1)} %project_keys.1.refs_4_), channel_id=1, source_target_pairs={{32,64},{64,32},{40,72},{72,40},{48,80},{80,48},{56,88},{88,56},{9... | collective-permute-start | bytes 1179656 | tf_op jit(solution)/shard_map/ppermute | solution.py:454
  24.8 15.7 %collective-permute-start.7 = (bf16[256,768]{1,0:T(8,128)(2,1)S(1)}, bf16[256,768]{1,0:T(8,128)(2,1)S(1)}, u32[]{:S(2)}, u32[]{:S(2)}) collective-permute-start(bf16[256,768]{1,0:T(8,128)(2,1)S(1)} %project_keys.1.refs_4_), channel_id=1, source_target_pairs={{0,32},{8,40},{16,48},{24,56},{32,0},{40,8},{48,16},{56,24},{64,96... | collective-permute-start | bytes 1179656 | tf_op jit(solution)/shard_map/ppermute | solution.py:442
  30.0 7.1 %collective-permute-start.11 = (bf16[256,384]{1,0:T(8,128)(2,1)S(1)}, bf16[256,384]{1,0:T(8,128)(2,1)S(1)}, u32[]{:S(2)}, u32[]{:S(2)}) collective-permute-start(bf16[256,384]{1,0:T(8,128)(2,1)S(1)} %get-tuple-element.71.refs_0_), channel_id=1, source_target_pairs={{0,24},{8,16},{16,8},{24,0},{32,56},{40,48},{48,40},{56,32},{64,88... | collective-permute-start | bytes 589832 | tf_op jit(solution)/shard_map/ppermute | solution.py:442
  30.0 10.5 %collective-permute-start.10 = (bf16[256,384]{1,0:T(8,128)(2,1)S(1)}, bf16[256,384]{1,0:T(8,128)(2,1)S(1)}, u32[]{:S(2)}, u32[]{:S(2)}) collective-permute-start(bf16[256,384]{1,0:T(8,128)(2,1)S(1)} %get-tuple-element.71.refs_0_), channel_id=1, source_target_pairs={{0,16},{8,24},{16,0},{24,8},{32,48},{40,56},{48,32},{56,40},{64,80... | collective-permute-start | bytes 589832 | tf_op jit(solution)/shard_map/ppermute | solution.py:442
  30.9 9.6 %collective-permute-start.9 = (bf16[256,384]{1,0:T(8,128)(2,1)S(1)}, bf16[256,384]{1,0:T(8,128)(2,1)S(1)}, u32[]{:S(2)}, u32[]{:S(2)}) collective-permute-start(bf16[256,384]{1,0:T(8,128)(2,1)S(1)} %get-tuple-element.71.refs_0_), channel_id=1, source_target_pairs={{0,8},{8,0},{16,24},{24,16},{32,40},{40,32},{48,56},{56,48},{64,72... | collective-permute-start | bytes 589832 | tf_op jit(solution)/shard_map/ppermute | solution.py:442
  40.5 7.1 %collective-permute-start.12 = (bf16[256,768]{1,0:T(8,128)(2,1)S(1)}, bf16[256,768]{1,0:T(8,128)(2,1)S(1)}, u32[]{:S(2)}, u32[]{:S(2)}) collective-permute-start(bf16[256,768]{1,0:T(8,128)(2,1)S(1)} %collective-permute-done.7.refs_5_), channel_id=1, source_target_pairs={{32,64},{64,32},{40,72},{72,40},{48,80},{80,48},{56,88},{88,56},{9... | collective-permute-start | bytes 1179656 | tf_op jit(solution)/shard_map/ppermute | solution.py:454
  41.2 18.8 %collective-permute-start.13 = (bf16[256,768]{1,0:T(8,128)(2,1)S(1)}, bf16[256,768]{1,0:T(8,128)(2,1)S(1)}, u32[]{:S(2)}, u32[]{:S(2)}) collective-permute-start(bf16[256,768]{1,0:T(8,128)(2,1)S(1)} %collective-permute-done.8.refs_6_), channel_id=1, source_target_pairs={{0,32},{8,40},{16,48},{24,56},{32,0},{40,8},{48,16},{56,24},{64,96... | collective-permute-start | bytes 1179656 | tf_op jit(solution)/shard_map/ppermute | solution.py:442
  47.6 18.4 %collective-permute-start.14 = (bf16[256,768]{1,0:T(8,128)(2,1)S(1)}, bf16[256,768]{1,0:T(8,128)(2,1)S(1)}, u32[]{:S(2)}, u32[]{:S(2)}) collective-permute-start(bf16[256,768]{1,0:T(8,128)(2,1)S(1)} %collective-permute-done.12.refs_4_), channel_id=1, source_target_pairs={{0,32},{8,40},{16,48},{24,56},{32,0},{40,8},{48,16},{56,24},{64,96... | collective-permute-start | bytes 1179656 | tf_op jit(solution)/shard_map/ppermute | solution.py:442
  71.1 1.6 %collective-permute-start.16 = (bf16[288,384]{1,0:T(8,128)(2,1)S(1)}, bf16[288,384]{1,0:T(8,128)(2,1)S(1)}, u32[]{:S(2)}, u32[]{:S(2)}) collective-permute-start(bf16[288,384]{1,0:T(8,128)(2,1)S(1)} %get-tuple-element.85), channel_id=1, source_target_pairs={{0,8},{8,0},{16,24},{24,16},{32,40},{40,32},{48,56},{56,48},{64,72... | collective-permute-start | bytes 663560 | tf_op jit(solution)/shard_map/ppermute | solution.py:442
  71.2 2.8 %collective-permute-start.15 = (bf16[288,384]{1,0:T(8,128)(2,1)S(1)}, bf16[288,384]{1,0:T(8,128)(2,1)S(1)}, u32[]{:S(2)}, u32[]{:S(2)}) collective-permute-start(bf16[288,384]{1,0:T(8,128)(2,1)S(1)} %get-tuple-element.83), channel_id=1, source_target_pairs={{0,8},{8,0},{16,24},{24,16},{32,40},{40,32},{48,56},{56,48},{64,72... | collective-permute-start | bytes 663560 | tf_op jit(solution)/shard_map/ppermute | solution.py:442
  73.0 7.6 %collective-permute-start.17 = (bf16[288,384]{1,0:T(8,128)(2,1)S(1)}, bf16[288,384]{1,0:T(8,128)(2,1)S(1)}, u32[]{:S(2)}, u32[]{:S(2)}) collective-permute-start(bf16[288,384]{1,0:T(8,128)(2,1)S(1)} %merge_shares.1), channel_id=1, source_target_pairs={{0,16},{8,24},{16,0},{24,8},{32,48},{40,56},{48,32},{56,40},{64,80... | collective-permute-start | bytes 663560 | tf_op jit(solution)/shard_map/ppermute | solution.py:442
  81.9 9.7 %collective-permute-start.21 = (bf16[256,384]{1,0:T(8,128)(2,1)S(1)}, bf16[256,384]{1,0:T(8,128)(2,1)S(1)}, u32[]{:S(2)}, u32[]{:S(2)}) collective-permute-start(bf16[256,384]{1,0:T(8,128)(2,1)S(1)} %get-tuple-element.92), channel_id=1, source_target_pairs={{0,2},{1,3},{2,0},{3,1},{4,6},{5,7},{6,4},{7,5},{8,10},{9,11},{10,... | collective-permute-start | bytes 589832 | tf_op jit(solution)/shard_map/ppermute | solution.py:438
  82.5 11.8 %collective-permute-start.23 = (bf16[256,384]{1,0:T(8,128)(2,1)S(1)}, bf16[256,384]{1,0:T(8,128)(2,1)S(1)}, u32[]{:S(2)}, u32[]{:S(2)}) collective-permute-start(bf16[256,384]{1,0:T(8,128)(2,1)S(1)} %get-tuple-element.94), channel_id=1, source_target_pairs={{0,6},{1,7},{2,4},{3,5},{4,2},{5,3},{6,0},{7,1},{8,14},{9,15},{10,... | collective-permute-start | bytes 589832 | tf_op jit(solution)/shard_map/ppermute | solution.py:438
  86.6 9.1 %collective-permute-start.18 = (bf16[256,384]{1,0:T(8,128)(2,1)S(1)}, bf16[256,384]{1,0:T(8,128)(2,1)S(1)}, u32[]{:S(2)}, u32[]{:S(2)}) collective-permute-start(bf16[256,384]{1,0:T(8,128)(2,1)S(1)} %get-tuple-element.88), channel_id=1, source_target_pairs={{0,1},{1,0},{2,3},{3,2},{4,5},{5,4},{6,7},{7,6},{8,9},{9,8},{10,11... | collective-permute-start | bytes 589832 | tf_op jit(solution)/shard_map/ppermute | solution.py:438
  88.9 6.8 %collective-permute-start.19 = (bf16[256,384]{1,0:T(8,128)(2,1)S(1)}, bf16[256,384]{1,0:T(8,128)(2,1)S(1)}, u32[]{:S(2)}, u32[]{:S(2)}) collective-permute-start(bf16[256,384]{1,0:T(8,128)(2,1)S(1)} %get-tuple-element.89), channel_id=1, source_target_pairs={{0,2},{1,3},{2,0},{3,1},{4,6},{5,7},{6,4},{7,5},{8,10},{9,11},{10,... | collective-permute-start | bytes 589832 | tf_op jit(solution)/shard_map/ppermute | solution.py:438
  90.3 10.8 %collective-permute-start.20 = (bf16[256,384]{1,0:T(8,128)(2,1)S(1)}, bf16[256,384]{1,0:T(8,128)(2,1)S(1)}, u32[]{:S(2)}, u32[]{:S(2)}) collective-permute-start(bf16[256,384]{1,0:T(8,128)(2,1)S(1)} %get-tuple-element.90), channel_id=1, source_target_pairs={{0,7},{1,6},{2,5},{3,4},{4,3},{5,2},{6,1},{7,0},{8,15},{9,14},{10,... | collective-permute-start | bytes 589832 | tf_op jit(solution)/shard_map/ppermute | solution.py:438
  91.6 10.5 %collective-permute-start.22 = (bf16[256,384]{1,0:T(8,128)(2,1)S(1)}, bf16[256,384]{1,0:T(8,128)(2,1)S(1)}, u32[]{:S(2)}, u32[]{:S(2)}) collective-permute-start(bf16[256,384]{1,0:T(8,128)(2,1)S(1)} %add_convert_fusion.1), channel_id=1, source_target_pairs={{0,6},{1,7},{2,4},{3,5},{4,2},{5,3},{6,0},{7,1},{8,14},{9,15},{10,... | collective-permute-start | bytes 589832 | tf_op jit(solution)/shard_map/ppermute | solution.py:438
  94.4 8.5 %collective-permute-start.24 = (bf16[256,384]{1,0:T(8,128)(2,1)S(1)}, bf16[256,384]{1,0:T(8,128)(2,1)S(1)}, u32[]{:S(2)}, u32[]{:S(2)}) collective-permute-start(bf16[256,384]{1,0:T(8,128)(2,1)S(1)} %add_convert_fusion), channel_id=1, source_target_pairs={{0,3},{1,2},{2,1},{3,0},{4,7},{5,6},{6,5},{7,4},{8,11},{9,10},{10,... | collective-permute-start | bytes 589832 | tf_op jit(solution)/shard_map/ppermute | solution.py:438
  103.8 5.6 %collective-permute-start.25 = (bf16[128,384]{1,0:T(8,128)(2,1)S(1)}, bf16[128,384]{1,0:T(8,128)(2,1)S(1)}, u32[]{:S(2)}, u32[]{:S(2)}) collective-permute-start(bf16[128,384]{1,0:T(8,128)(2,1)S(1)} %get-tuple-element.96), channel_id=1, source_target_pairs={{0,64},{8,72},{16,80},{24,88},{32,96},{40,104},{48,112},{56,120},{... | collective-permute-start | bytes 294920 | tf_op jit(solution)/shard_map/ppermute | solution.py:442

commit v4 on v3

--- a/solution.py
+++ b/solution.py
@@ -23,6 +23,7 @@
 HEADS_HERE = 3
 SLOTS = 6
 WINDOW = 3 * PIECE
+HALF = N_HEAD // 2
 SCORE_SCALE = HEAD_DIM ** (-0.5) * 1.4426950408889634
 
 LOADS = 4
@@ -38,16 +39,19 @@
     return pltpu.CompilerParams(vmem_limit_bytes=mib * 1024 * 1024)
 
 
-def plan_kernel(ids, neighbours, tile_owner, starts, flags, tile_of, first, half):
+STARTS, FLAGS, TILE_OF, FIRST, SIDE, GROUP = 0, 8, 80, 112, 113, 114
+
+
+def plan_kernel(ids, neighbours, tile_owner, table):
     position = ids[0]
     tile_row = position // TILE
     odd = (position // PLANE) % 2
     for c in range(TILE_COLS):
         tile = tile_row * TILE_COLS + c
         start = jnp.minimum(neighbours[0, tile] % TILE_COLS, TILE_COLS - 3)
-        starts[c] = start
+        table[STARTS + c] = start
         for n in range(9):
-            flags[c, n] = 0
+            table[FLAGS + 9 * c + n] = 0
         for n in range(9):
             listed = neighbours[n, tile]
 
@@ -55,22 +59,22 @@
             def _():
                 step = listed // TILE_COLS - tile_row
                 kind = jnp.where(step == 0, 0, jnp.where((step > 0) == (odd == 1), 1, 2))
-                flags[c, kind * 3 + listed % TILE_COLS - start] = 1
+                table[FLAGS + 9 * c + kind * 3 + listed % TILE_COLS - start] = 1
 
     for t in range(TILES):
-        tile_of[tile_owner[t]] = t
-    first[0] = tile_of[position] // (2 * TILE_COLS)
-    half[0] = tile_row % 2
+        table[TILE_OF + tile_owner[t]] = t
+    table[FIRST] = table[TILE_OF + position] // (2 * TILE_COLS)
+    table[SIDE] = tile_row % 2
+    table[GROUP] = ids[1]
 
 
 def plan(ids, neighbours, tile_owner):
     scalars = pl.BlockSpec(memory_space=pltpu.SMEM)
-    shapes = [(TILE_COLS,), (TILE_COLS, 9), (TILES,), (1,), (1,)]
     return pl.pallas_call(
         plan_kernel,
         in_specs=[scalars] * 3,
-        out_specs=[scalars] * len(shapes),
-        out_shape=[jax.ShapeDtypeStruct(shape, jnp.int32) for shape in shapes],
+        out_specs=scalars,
+        out_shape=jax.ShapeDtypeStruct((128,), jnp.int32),
         compiler_params=params(8),
         cost_estimate=pl.CostEstimate(flops=0, bytes_accessed=8_000_000, transcendentals=0),
         name="plan",
@@ -86,9 +90,10 @@
     return jnp.concatenate(heads, axis=1)
 
 
-def gather_rows(ids, pieces, rows):
-    for k, piece in enumerate(pieces):
-        start = pl.multiple_of((ids[1] ^ k) * PIECE, PIECE)
+def gather_rows(ids, steps, pieces, rows):
+    count = len(pieces)
+    for k, piece in zip(steps, pieces):
+        start = pl.multiple_of(((ids[1] ^ k) % count) * PIECE, PIECE)
         rows[pl.ds(start, PIECE), :] = piece[...]
 
 
@@ -122,7 +127,7 @@
 
 def queries_kernel(ids, *refs):
     pieces, (w_ref, gain_ref, out_ref, rows_ref) = refs[:N_HEAD], refs[N_HEAD:]
-    gather_rows(ids, pieces, rows_ref)
+    gather_rows(ids, range(N_HEAD), pieces, rows_ref)
     result = jnp.dot(rows_ref[...], w_ref[0], preferred_element_type=jnp.float32)
     out_ref[...] = normed(result, gain_ref[...])
 
@@ -133,11 +138,9 @@
     return pl.pallas_call(
         queries_kernel,
         in_specs=[pl.BlockSpec(memory_space=pltpu.SMEM)] + [whole] * (N_HEAD + 2),
-        out_specs=[whole] * 2,
-        out_shape=[
-            jax.ShapeDtypeStruct((tokens, WIDTH), jnp.bfloat16),
-            jax.ShapeDtypeStruct((tokens, D), jnp.bfloat16),
-        ],
+        out_specs=whole,
+        out_shape=jax.ShapeDtypeStruct((tokens, WIDTH), jnp.bfloat16),
+        scratch_shapes=[pltpu.VMEM((tokens, D), jnp.bfloat16)],
         compiler_params=params(16),
         cost_estimate=pl.CostEstimate(
             flops=2 * tokens * D * WIDTH, bytes_accessed=4_000_000, transcendentals=0
@@ -146,7 +149,9 @@
     )(ids, *pieces, weight, gain)
 
 
-def keys_kernel(rows_ref, w_ref, gain_ref, out_ref):
+def keys_kernel(steps, ids, *refs):
+    pieces, (w_ref, gain_ref, out_ref, rows_ref) = refs[:HALF], refs[HALF:]
+    gather_rows(ids, steps, pieces, rows_ref)
     rows = rows_ref[...]
     keys = jnp.dot(rows, w_ref[1], preferred_element_type=jnp.float32)
     out_ref[:, :WIDTH] = normed(keys, gain_ref[...])
@@ -154,20 +159,21 @@
     out_ref[:, WIDTH:] = values.astype(jnp.bfloat16)
 
 
-def project_keys(rows, weight, gain):
-    tokens = N_HEAD * PIECE
-    whole = pl.BlockSpec(memory_space=pltpu.VMEM)
-    return pl.pallas_call(
-        keys_kernel,
-        in_specs=[whole] * 3,
+def project_keys(steps, ids, pieces, weight, gain):
+    tokens = HALF * PIECE
+    whole = pl.BlockSpec(memory_space=pltpu.VMEM)
+    return pl.pallas_call(
+        functools.partial(keys_kernel, steps),
+        in_specs=[pl.BlockSpec(memory_space=pltpu.SMEM)] + [whole] * (HALF + 2),
         out_specs=whole,
         out_shape=jax.ShapeDtypeStruct((tokens, 2 * WIDTH), jnp.bfloat16),
+        scratch_shapes=[pltpu.VMEM((tokens, D), jnp.bfloat16)],
         compiler_params=params(16),
         cost_estimate=pl.CostEstimate(
             flops=2 * tokens * D * 2 * WIDTH, bytes_accessed=6_000_000, transcendentals=0
         ),
         name="project_keys",
-    )(rows, weight, gain)
+    )(ids, *pieces, weight, gain)
 
 
 TAIL = slice(TILE_COLS * PIECE, (TILE_COLS + 1) * PIECE)
@@ -221,23 +227,30 @@
     )(first, second)
 
 
-def attend_kernel(kinds, last, starts, flags, *refs):
+def attend_kernel(kinds, last, table, *refs):
     count = len(kinds)
     refs = list(refs)
     take = lambda n: [refs.pop(0) for _ in range(n)]
-    queries, slots = take(PLANE), take(count)
+    queries, halves = take(PLANE), take(2 * count)
     before = take(PLANE + 1) if last else None
     outs = take(PLANE) if last else take(PLANE + 1)
     piece_of = lax.broadcasted_iota(jnp.int32, (1, count * WINDOW), 1) // PIECE
     ones = jnp.ones((count * WINDOW, HEAD_DIM), jnp.bfloat16)
+    slots_ref = refs.pop(0)
     level_ref = refs.pop(0) if last else outs[PLANE]
+    size = HALF * PIECE
+    for n in range(count):
+        for e in range(2):
+            start = pl.multiple_of((table[GROUP] // HALF ^ e) * size, size)
+            slots_ref[n, pl.ds(start, size), :] = halves[2 * n + e][...]
+    slots = [slots_ref.at[n] for n in range(count)]
     level_ref[...] = jnp.zeros_like(level_ref)
     for c in range(TILE_COLS):
         here = slice(c * PIECE, (c + 1) * PIECE)
-        window = pl.ds(pl.multiple_of(starts[c] * PIECE, PIECE), WINDOW)
+        window = pl.ds(pl.multiple_of(table[STARTS + c] * PIECE, PIECE), WINDOW)
         bias = jnp.full((1, count * WINDOW), -jnp.inf, jnp.float32)
         for n in range(3 * count):
-            bias = jnp.where((piece_of == n) & (flags[c, kinds[n // 3] * 3 + n % 3] > 0), 0.0, bias)
+            bias = jnp.where((piece_of == n) & (table[FLAGS + 9 * c + kinds[n // 3] * 3 + n % 3] > 0), 0.0, bias)
         for h in range(HEADS_HERE):
             head = slice(h * HEAD_DIM, (h + 1) * HEAD_DIM)
             value_head = slice(WIDTH + h * HEAD_DIM, WIDTH + (h + 1) * HEAD_DIM)
@@ -276,23 +289,25 @@
             store_level(outs[n], level_ref[n * PIECE : (n + 1) * PIECE])
 
 
-def attend(starts, flags, queries, slots, kinds, before=()):
+def attend(table, queries, slots, kinds, before=()):
     tokens = TILE_COLS * PIECE
     count = len(slots)
     last = bool(before)
     whole = pl.BlockSpec(memory_space=pltpu.VMEM)
     scalars = pl.BlockSpec(memory_space=pltpu.SMEM)
-    operands = [*queries, *slots, *before]
+    operands = [*queries, *(half for slot in slots for half in slot), *before]
     levels = (PLANE * PIECE, HEAD_DIM)
     if last:
         out_shape = [jax.ShapeDtypeStruct((tokens + PIECE, WIDTH), jnp.bfloat16)] * PLANE
     else:
         out_shape = [jax.ShapeDtypeStruct((tokens, WIDTH), jnp.bfloat16)] * PLANE
         out_shape.append(jax.ShapeDtypeStruct(levels, jnp.float32))
-    scratch = [pltpu.VMEM(levels, jnp.float32)] if last else []
+    scratch = [pltpu.VMEM((count, tokens, 2 * WIDTH), jnp.bfloat16)]
+    if last:
+        scratch.append(pltpu.VMEM(levels, jnp.float32))
     return pl.pallas_call(
         functools.partial(attend_kernel, kinds, last),
-        in_specs=[scalars] * 2 + [whole] * len(operands),
+        in_specs=[scalars] + [whole] * len(operands),
         out_specs=[whole] * len(out_shape),
         out_shape=out_shape,
         scratch_shapes=scratch,
@@ -303,7 +318,7 @@
             transcendentals=1_000_000,
         ),
         name="attend",
-    )(starts, flags, *operands)
+    )(table, *operands)
 
 
 def term(ids, k, attended, w_ref, out_ref):
@@ -356,7 +371,7 @@
     )(ids, joined, w_out)
 
 
-def add_kernel(side, *refs):
+def add_kernel(table, *refs):
     *terms, kept_ref, given_ref, rows = refs
     total = terms[0][...].astype(jnp.float32)
     for ref in terms[1:]:
@@ -364,12 +379,12 @@
     rows[...] = total.astype(jnp.bfloat16)
     for c in range(TILE_COLS):
         to = slice(c * PAIR, (c + 1) * PAIR)
-        for ref, which in ((kept_ref, side[0]), (given_ref, 1 - side[0])):
+        for ref, which in ((kept_ref, table[SIDE]), (given_ref, 1 - table[SIDE])):
             start = pl.multiple_of(c * PIECE + which * PAIR, PAIR)
             ref[to, :] = rows[pl.ds(start, PAIR), :]
 
 
-def add_terms(side, terms):
+def add_terms(table, terms):
     whole = pl.BlockSpec(memory_space=pltpu.VMEM)
     return pl.pallas_call(
         add_kernel,
@@ -380,35 +395,35 @@
         compiler_params=params(8),
         cost_estimate=pl.CostEstimate(flops=800_000, bytes_accessed=2_000_000, transcendentals=0),
         name="add_terms",
-    )(side, *terms)
-
-
-def order_kernel(side, tile_of, kept_ref, got_ref, out_ref, rows):
+    )(table, *terms)
+
+
+def order_kernel(table, kept_ref, got_ref, out_ref, rows):
     size = TILE_COLS * PAIR
-    for ref, which in ((kept_ref, side[0]), (got_ref, 1 - side[0])):
+    for ref, which in ((kept_ref, table[SIDE]), (got_ref, 1 - table[SIDE])):
         rows[pl.ds(pl.multiple_of(which * size, size), size), :] = ref[...]
     for d in range(TILES):
-        start = pl.multiple_of((tile_of[d] % (2 * TILE_COLS)) * PAIR, PAIR)
+        start = pl.multiple_of((table[TILE_OF + d] % (2 * TILE_COLS)) * PAIR, PAIR)
         out_ref[d * PAIR : (d + 1) * PAIR, :] = rows[pl.ds(start, PAIR), :]
 
 
-def order(side, tile_of, kept, got):
+def order(table, kept, got):
     whole = pl.BlockSpec(memory_space=pltpu.VMEM)
     scalars = pl.BlockSpec(memory_space=pltpu.SMEM)
     return pl.pallas_call(
         order_kernel,
-        in_specs=[scalars, scalars, whole, whole],
+        in_specs=[scalars, whole, whole],
         out_specs=whole,
         out_shape=jax.ShapeDtypeStruct((TILES * PAIR, WIDTH), jnp.bfloat16),
         scratch_shapes=[pltpu.VMEM((2 * TILE_COLS * PAIR, WIDTH), jnp.bfloat16)],
         compiler_params=params(8),
         cost_estimate=pl.CostEstimate(flops=100_000, bytes_accessed=800_000, transcendentals=0),
         name="order",
-    )(side, tile_of, kept, got)
-
-
-def tile_kernel(first, arrived, out_ref):
-    base = first[0] * (2 * TILE * PAIR)
+    )(table, kept, got)
+
+
+def tile_kernel(table, arrived, out_ref):
+    base = table[FIRST] * (2 * TILE * PAIR)
     pieces = [
         arrived[pl.ds(pl.multiple_of(base + n * PAIR, PAIR), PAIR), :].astype(jnp.float32)
         for n in range(2 * TILE)
@@ -421,7 +436,7 @@
     out_ref[...] = jnp.concatenate(parts, axis=0).astype(jnp.bfloat16)
 
 
-def to_tile(first, arrived):
+def to_tile(table, arrived):
     whole = pl.BlockSpec(memory_space=pltpu.VMEM)
     return pl.pallas_call(
         tile_kernel,
@@ -431,7 +446,7 @@
         compiler_params=params(8),
         cost_estimate=pl.CostEstimate(flops=100_000, bytes_accessed=800_000, transcendentals=0),
         name="to_tile",
-    )(first, arrived)
+    )(table, arrived)
 
 
 def head_swap(array, k):
@@ -458,25 +473,33 @@
     ids = jnp.stack([lax.axis_index("seq"), lax.axis_index("head")]).astype(jnp.int32)
     weight = load_weight(jnp.transpose(w_qkv, (1, 0, 2)))
     q_gain, k_gain = q_gain.reshape(1, HEAD_DIM), k_gain.reshape(1, HEAD_DIM)
-    starts, flags, tile_of, first, half = plan(ids, neighbours.T, tile_owner)
+    table = plan(ids, neighbours.T, tile_owner)
 
     pieces = [latent.reshape(PIECE, D)] * N_HEAD
     for k in (1, 2, 3, 6, 7):
         pieces[k] = head_swap(pieces[0], k)
     pieces[4], pieces[5] = head_swap(pieces[6], 2), head_swap(pieces[3], 6)
 
-    tables = (starts, flags, tile_of, first, half)
-    (starts, flags, tile_of, first, half), pieces = lax.optimization_barrier((tables, pieces))
-
-    queries, rows = project_queries(ids, pieces, weight, q_gain)
-    all_queries = [queries] + [plane_swap(queries, k) for k in range(1, PLANE)]
-    own = project_keys(rows, weight, k_gain)
-    mate, edge = mate_swap(own), edge_swap(own)
-    mate, edge, *all_queries = lax.optimization_barrier((mate, edge, *all_queries))
-    far_1, edge_2 = mate_swap(edge), edge_swap(mate)
-    far_2 = mate_swap(edge_2)
-    near = attend(starts, flags, all_queries, [own, mate, edge], (0, 0, 1))
-    shares = attend(starts, flags, all_queries, [edge_2, far_1, far_2], (1, 2, 2), near)
+    own_a = project_keys(range(HALF), ids, pieces[:HALF], weight, k_gain)
+    mate_a, edge_a = mate_swap(own_a), edge_swap(own_a)
+    pieces_b, _own = lax.optimization_barrier((pieces[HALF:], own_a))
+    own_b = project_keys(range(HALF, N_HEAD), ids, pieces_b, weight, k_gain)
+    mate_b, edge_b = mate_swap(own_b), edge_swap(own_b)
+    edge_2a, far_1a = edge_swap(mate_a), mate_swap(edge_a)
+
+    queries = project_queries(ids, [*pieces[:HALF], *pieces_b], weight, q_gain)
+    q_chip = plane_swap(queries, 2)
+    all_queries = [queries, plane_swap(queries, 1), q_chip, plane_swap(q_chip, 1)]
+
+    edge_b, edge_2a, all_queries = lax.optimization_barrier((edge_b, edge_2a, all_queries))
+    edge_2b = edge_swap(mate_b)
+    far_1b, far_2a = mate_swap(edge_b), mate_swap(edge_2a)
+    far_2b = mate_swap(edge_2b)
+    near_slots = [(_own, own_b), (mate_a, mate_b), (edge_a, edge_b)]
+    far_slots = [(edge_2a, edge_2b), (far_1a, far_1b), (far_2a, far_2b)]
+    near = attend(table, all_queries, near_slots, (0, 0, 1))
+    shares = attend(table, all_queries, far_slots, (1, 2, 2), near)
+
     from_core, for_chip = plane_swap(shares[1], 1), plane_swap(shares[3], 1)
     from_chip = plane_swap(merge_shares(shares[2], for_chip), 2)
 
@@ -487,12 +510,12 @@
         terms[k] = (terms[k].astype(jnp.float32) + passed[k].astype(jnp.float32)).astype(jnp.bfloat16)
     terms = [terms[0]] + [head_swap(terms[k], k) for k in DIRECT[1:]]
 
-    kept, given = add_terms(half, terms)
-    sent = order(half, tile_of, kept, plane_swap(given, TILE))
+    kept, given = add_terms(table, terms)
+    sent = order(table, kept, plane_swap(given, TILE))
     arrived = lax.all_to_all(
         sent.reshape(TILES, PAIR, WIDTH), "seq", split_axis=0, concat_axis=0, tiled=True
     )
-    return to_tile(first, arrived.reshape(TILES * PAIR, WIDTH)).reshape(1, TILE_TOKENS, WIDTH)
+    return to_tile(table, arrived.reshape(TILES * PAIR, WIDTH)).reshape(1, TILE_TOKENS, WIDTH)
 
 
 def solution(mesh):

time: 136 us -> 131 us (0.963)
  waiting for transfers between devices: 34.8 us -> 25.8 us
  starting transfers between devices: 51.7 us -> 53.8 us
  blocking collectives: 23.3 us -> 25.1 us
    ppermute x10 -> x13, waiting for transfers between devices: 24.8 us -> 18.9 us  [plane_swap(): lax.ppermute(array, 'seq', [(s, s ^ k) for s in range(PLANE * PLANES)])]
    ppermute x14, waiting for transfers between devices: 9.98 us -> 6.92 us  [head_swap(): return lax.ppermute(array, 'head', [(h, h ^ k) for h in range(N_HEAD)])]
    ppermute x14, starting transfers between devices: 23 us -> 25.8 us  [head_swap(): return lax.ppermute(array, 'head', [(h, h ^ k) for h in range(N_HEAD)])]
    ppermute x10 -> x13, starting transfers between devices: 27.3 us -> 25.3 us  [plane_swap(): lax.ppermute(array, 'seq', [(s, s ^ k) for s in range(PLANE * PLANES)])]
    all_to_all x1, blocking collectives: 23.3 us -> 25.1 us  [local(): lax.all_to_all(sent.reshape(TILES, PAIR, WIDTH), 'seq', split_axis=0, con...]
    pallas_call x3 -> x4, Pallas kernels: 5.42 us -> 6.06 us  [the longest x2 3.22 us: project_keys(): pl.pallas_call(functools.partial(keys_kernel, steps), in_specs=[pl.BlockS...]
  transfers between devices with their start and end apart: 26 -> 31, of which waited for: 10 -> 11; matrix products, arithmetic and copies ran while one was open for 0% -> 0% of each run, Pallas kernels for 6% -> 10%
where the time goes in v4:
time: 131 us
  starting transfers between devices  53.8 us (41%)
  waiting for transfers between devices  25.8 us (20%)
  blocking collectives  25.1 us (19%)
  Pallas kernels  22.5 us (17%)
  local copies, waits for them, and re-layouts  3.04 us (2%)
    ppermute x14, starting transfers between devices, head_swap(): return lax.ppermute(array, 'head', [(h, h ^ k) for h in range(N_HEAD)])  25.8 us
    ppermute x13, starting transfers between devices, plane_swap(): lax.ppermute(array, 'seq', [(s, s ^ k) for s in range(PLANE * PLANES)])  25.3 us
    all_to_all x1, blocking collectives, local(): lax.all_to_all(sent.reshape(TILES, PAIR, WIDTH), 'seq', split_axis=0, con...  25.1 us
    ppermute x13, waiting for transfers between devices, plane_swap(): lax.ppermute(array, 'seq', [(s, s ^ k) for s in range(PLANE * PLANES)])  18.9 us
    pallas_call x2, Pallas kernels, attend(): pl.pallas_call(functools.partial(attend_kernel, kinds, last), in_specs=[s...  7.95 us
    ppermute x14, waiting for transfers between devices, head_swap(): return lax.ppermute(array, 'head', [(h, h ^ k) for h in range(N_HEAD)])  6.92 us
    pallas_call x2, Pallas kernels, project_keys(): pl.pallas_call(functools.partial(keys_kernel, steps), in_specs=[pl.BlockS...  3.22 us
    unnamed x14, local copies, waits for them, and re-layouts  3.04 us
  transfers between devices with their start and end apart: 31, of which 11 were waited for; matrix products, arithmetic and copies ran while one was open for 0% of the time, Pallas kernels for 10%

profile of v4, /device:TPU:2, one launch (start us, length us, event | category | flops | bytes accessed | tf_op | source)
XLA Modules:
  0.0 130.7 jit_solution(12806129662066835715)
XLA Ops:
  0.0 3.1 %collective-permute-start.2 = (bf16[32,3072]{1,0:T(8,128)(2,1)}, bf16[32,3072]{1,0:T(8,128)(2,1)S(1)}, u32[]{:S(2)}, u32[]{:S(2)}) collective-permute-start(bf16[32,3072]{1,0:T(8,128)(2,1)} %bitcast.13), channel_id=1, source_target_pairs={{0,3},{1,2},{2,1},{3,0},{4,7},{5,6},{6,5},{7,4},{8,11},{9,10},{10,... | collective-permute-start | bytes 589832 | tf_op jit(solution)/shard_map/ppermute | solution.py:453
  3.1 2.2 %collective-permute-start = (bf16[32,3072]{1,0:T(8,128)(2,1)}, bf16[32,3072]{1,0:T(8,128)(2,1)S(1)}, u32[]{:S(2)}, u32[]{:S(2)}) collective-permute-start(bf16[32,3072]{1,0:T(8,128)(2,1)} %bitcast.14), channel_id=1, source_target_pairs={{0,6},{1,7},{2,4},{3,5},{4,2},{5,3},{6,0},{7,1},{8,14},{9,15},{10,... | collective-permute-start | bytes 589832 | tf_op jit(solution)/shard_map/ppermute | solution.py:453
  5.3 0.7 collective-permute-start.6
  6.0 1.4 %collective-permute-start.5 = (bf16[32,3072]{1,0:T(8,128)(2,1)}, bf16[32,3072]{1,0:T(8,128)(2,1)S(1)}, u32[]{:S(2)}, u32[]{:S(2)}) collective-permute-start(bf16[32,3072]{1,0:T(8,128)(2,1)} %bitcast.16), channel_id=1, source_target_pairs={{0,1},{1,0},{2,3},{3,2},{4,5},{5,4},{6,7},{7,6},{8,9},{9,8},{10,11... | collective-permute-start | bytes 589832 | tf_op jit(solution)/shard_map/ppermute | solution.py:453
  7.4 2.2 %collective-permute-start.4 = (bf16[32,3072]{1,0:T(8,128)(2,1)}, bf16[32,3072]{1,0:T(8,128)(2,1)S(1)}, u32[]{:S(2)}, u32[]{:S(2)}) collective-permute-start(bf16[32,3072]{1,0:T(8,128)(2,1)} %bitcast.17), channel_id=1, source_target_pairs={{0,7},{1,6},{2,5},{3,4},{4,3},{5,2},{6,1},{7,0},{8,15},{9,14},{10,... | collective-permute-start | bytes 589832 | tf_op jit(solution)/shard_map/ppermute | solution.py:453
  9.6 0.0 collective-permute-done.2.refs_3_
  9.6 3.8 %collective-permute-start.3 = (bf16[32,3072]{1,0:T(8,128)(2,1)S(1)}, bf16[32,3072]{1,0:T(8,128)(2,1)S(1)}, u32[]{:S(2)}, u32[]{:S(2)}) collective-permute-start(bf16[32,3072]{1,0:T(8,128)(2,1)S(1)} %collective-permute-done.2.refs_3_), channel_id=1, source_target_pairs={{0,6},{1,7},{2,4},{3,5},{4,2},{5,3},{6,0},{7,1},{8,14},{9,15},{10,... | collective-permute-start | bytes 589832 | tf_op jit(solution)/shard_map/ppermute | solution.py:453
  13.4 0.2 collective-permute-start.1
  13.6 3.0 %copy-done.1 = bf16[3072,3,384]{2,0,1:T(8,128)(2,1)S(1)} copy-done((bf16[3072,3,384]{2,0,1:T(8,128)(2,1)S(1)}, bf16[3072,3,384]{2,0,1:T(8,128)(2,1)}, u32[]{:S(2)}) %copy-start.1) | copy-done | bytes 7077912
  16.6 1.6 %load_weight.1.refs_4_.refs_8_ = bf16[3,3072,384]{2,1,0:T(8,128)(2,1)S(1)} custom-call(bf16[3,3072,384]{2,1,0:T(8,128)(2,1)S(1)} %bitcast.10), custom_call_target="tpu_custom_call" | custom-call | bytes 7100000 | tf_op jit(solution)/shard_map/load_weight/pallas_call | solution.py:116
  18.2 0.0 copy-start.5
  18.2 0.1 pad_add_fusion.ids
  18.3 1.6 %project_keys.2.refs_4_ = bf16[128,768]{1,0:T(8,128)(2,1)S(1)} custom-call(s32[2]{0:T(128)S(1)} %pad_add_fusion.ids, bf16[32,3072]{1,0:T(8,128)(2,1)S(1)} %bitcast.18, bf16[32,3072]{1,0:T(8,128)(2,1)S(1)} %collective-permute-done.5.refs_1_, bf16[32,3072]{1,0:T(8,128)(2,1)S(1)} %collective-permute-done.6.refs_2_, ...), custom_call_target="tpu_custom_call" | custom-call | flops 603979776 | bytes 6000000 | tf_op jit(solution)/shard_map/project_keys/pallas_call | solution.py:165
  19.9 0.7 collective-permute-start.15
  20.6 5.2 %collective-permute-start.8 = (bf16[128,768]{1,0:T(8,128)(2,1)S(1)}, bf16[128,768]{1,0:T(8,128)(2,1)S(1)}, u32[]{:S(2)}, u32[]{:S(2)}) collective-permute-start(bf16[128,768]{1,0:T(8,128)(2,1)S(1)} %project_keys.2.refs_4_), channel_id=1, source_target_pairs={{0,32},{8,40},{16,48},{24,56},{32,0},{40,8},{48,16},{56,24},{64,96... | collective-permute-start | bytes 589832 | tf_op jit(solution)/shard_map/ppermute | solution.py:457
  25.8 0.0 copy-start.3
  25.8 0.0 copy-start.6
  25.8 1.7 %project_queries.1.refs_0_ = bf16[256,384]{1,0:T(8,128)(2,1)S(1)} custom-call(s32[2]{0:T(128)S(1)} %pad_add_fusion.ids, bf16[32,3072]{1,0:T(8,128)(2,1)S(1)} %bitcast.19, bf16[32,3072]{1,0:T(8,128)(2,1)S(1)} %collective-permute-done.5.refs_1_, bf16[32,3072]{1,0:T(8,128)(2,1)S(1)} %collective-permute-done.6.refs_2_, ...), custom_call_target="tpu_custom_call" | custom-call | flops 603979776 | bytes 4000000 | tf_op jit(solution)/shard_map/project_queries/pallas_call | solution.py:138
  27.5 0.0 copy-start
  27.6 0.3 collective-permute-start.11
  27.8 1.6 %project_keys.3.refs_5_ = bf16[128,768]{1,0:T(8,128)(2,1)S(1)} custom-call(s32[2]{0:T(128)S(1)} %pad_add_fusion.ids, bf16[32,3072]{1,0:T(8,128)(2,1)S(1)} %collective-permute-done.1.refs_0_.refs_4_, bf16[32,3072]{1,0:T(8,128)(2,1)S(1)} %collective-permute-done.3.refs_1_.refs_5_, bf16[32,3072]{1,0:T(8,128)(2,1)S(1)} %collective-permute-done.refs_2_.refs_6_, ...), custom_call_target="tpu_custom_call" | custom-call | flops 603979776 | bytes 6000000 | tf_op jit(solution)/shard_map/project_keys/pallas_call | solution.py:165
  29.4 0.1 collective-permute-start.13
  29.6 0.7 collective-permute-start.7
  30.2 0.1 collective-permute-start.10
  30.3 0.4 collective-permute-done.8.refs_6_
  30.7 0.7 collective-permute-start.9
  31.4 1.9 %collective-permute-done.11.refs_2_ = bf16[256,384]{1,0:T(8,128)(2,1)S(1)} collective-permute-done((bf16[256,384]{1,0:T(8,128)(2,1)S(1)}, bf16[256,384]{1,0:T(8,128)(2,1)S(1)}, u32[]{:S(2)}, u32[]{:S(2)}) %collective-permute-start.11) | collective-permute-done | bytes 196640 | tf_op jit(solution)/shard_map/ppermute | solution.py:457
  33.3 1.9 %collective-permute-done.13.refs_7_ = bf16[128,768]{1,0:T(8,128)(2,1)S(1)} collective-permute-done((bf16[128,768]{1,0:T(8,128)(2,1)S(1)}, bf16[128,768]{1,0:T(8,128)(2,1)S(1)}, u32[]{:S(2)}, u32[]{:S(2)}) %collective-permute-start.13) | collective-permute-done | bytes 196640 | tf_op jit(solution)/shard_map/ppermute | solution.py:457
  35.2 0.7 collective-permute-start.14
  35.9 7.0 %collective-permute-start.16 = (bf16[128,768]{1,0:T(8,128)(2,1)S(1)}, bf16[128,768]{1,0:T(8,128)(2,1)S(1)}, u32[]{:S(2)}, u32[]{:S(2)}) collective-permute-start(bf16[128,768]{1,0:T(8,128)(2,1)S(1)} %collective-permute-done.15.refs_8_), channel_id=1, source_target_pairs={{0,32},{8,40},{16,48},{24,56},{32,0},{40,8},{48,16},{56,24},{64,96... | collective-permute-start | bytes 589832 | tf_op jit(solution)/shard_map/ppermute | solution.py:457
  42.9 3.3 %collective-permute-start.18 = (bf16[128,768]{1,0:T(8,128)(2,1)S(1)}, bf16[128,768]{1,0:T(8,128)(2,1)S(1)}, u32[]{:S(2)}, u32[]{:S(2)}) collective-permute-start(bf16[128,768]{1,0:T(8,128)(2,1)S(1)} %collective-permute-done.9.refs_4_), channel_id=1, source_target_pairs={{0,32},{8,40},{16,48},{24,56},{32,0},{40,8},{48,16},{56,24},{64,96... | collective-permute-start | bytes 589832 | tf_op jit(solution)/shard_map/ppermute | solution.py:457
  46.2 3.8 %collective-permute-start.19 = (bf16[128,768]{1,0:T(8,128)(2,1)S(1)}, bf16[128,768]{1,0:T(8,128)(2,1)S(1)}, u32[]{:S(2)}, u32[]{:S(2)}) collective-permute-start(bf16[128,768]{1,0:T(8,128)(2,1)S(1)} %collective-permute-done.14.refs_5_), channel_id=1, source_target_pairs={{0,32},{8,40},{16,48},{24,56},{32,0},{40,8},{48,16},{56,24},{64,96... | collective-permute-start | bytes 589832 | tf_op jit(solution)/shard_map/ppermute | solution.py:457
  50.0 0.0 collective-permute-start.17
  50.1 2.2 %plan.1.table = s32[128]{0:T(128)S(1)} custom-call(s32[2]{0:T(128)S(1)} %pad_add_fusion.ids, s32[9,32]{1,0:T(8,128)S(1)} %bitcast.20, s32[32]{0:T(128)S(1)} %copy-done.6), custom_call_target="tpu_custom_call" | custom-call | bytes 8000000 | tf_op jit(solution)/shard_map/plan/pallas_call | solution.py:73
  52.2 3.0 %attend.2 = (bf16[256,384]{1,0:T(8,128)(2,1)S(1)}, bf16[256,384]{1,0:T(8,128)(2,1)S(1)}, bf16[256,384]{1,0:T(8,128)(2,1)S(1)}, bf16[256,384]{1,0:T(8,128)(2,1)S(1)}, f32[128,128]{1,0:T(8,128)S(1)}) custom-call(s32[128]{0:T(128)S(1)} %plan.1.table, bf16[256,384]{1,0:T(8,128)(2,1)S(1)} %project_queries.1.refs_0_, ...), custom_call_target="tpu_custom_call" | custom-call | flops 452984832 | bytes 4000000 | tf_op jit(solution)/shard_map/attend/pallas_call | solution.py:308
  55.2 1.8 %collective-permute-done.19.refs_9_ = bf16[128,768]{1,0:T(8,128)(2,1)S(1)} collective-permute-done((bf16[128,768]{1,0:T(8,128)(2,1)S(1)}, bf16[128,768]{1,0:T(8,128)(2,1)S(1)}, u32[]{:S(2)}, u32[]{:S(2)}) %collective-permute-start.19) | collective-permute-done | bytes 196640 | tf_op jit(solution)/shard_map/ppermute | solution.py:457
  57.0 3.6 %collective-permute-done.17.refs_7_ = bf16[128,768]{1,0:T(8,128)(2,1)S(1)} collective-permute-done((bf16[128,768]{1,0:T(8,128)(2,1)S(1)}, bf16[128,768]{1,0:T(8,128)(2,1)S(1)}, u32[]{:S(2)}, u32[]{:S(2)}) %collective-permute-start.17) | collective-permute-done | bytes 196640 | tf_op jit(solution)/shard_map/ppermute | solution.py:457
  60.6 5.0 %attend.3 = (bf16[288,384]{1,0:T(8,128)(2,1)S(1)}, bf16[288,384]{1,0:T(8,128)(2,1)S(1)}, bf16[288,384]{1,0:T(8,128)(2,1)S(1)}, bf16[288,384]{1,0:T(8,128)(2,1)S(1)}) custom-call(s32[128]{0:T(128)S(1)} %plan.1.table, bf16[256,384]{1,0:T(8,128)(2,1)S(1)} %project_queries.1.refs_0_, bf16[256,384]{1,0:T(8,128)(2,1)S(1)} %collective-permute-done.10.refs_1_, ...), custom_call_target="tpu_custom_call" | custom-call | flops 452984832 | bytes 4000000 | tf_op jit(solution)/shard_map/attend/pallas_call | solution.py:308
  65.6 0.1 collective-permute-start.21
  65.7 0.5 collective-permute-start.20
  66.2 1.0 collective-permute-done.21.second_ref
  67.1 0.3 merge_shares.1
  67.5 1.9 %collective-permute-start.22 = (bf16[288,384]{1,0:T(8,128)(2,1)S(1)}, bf16[288,384]{1,0:T(8,128)(2,1)S(1)}, u32[]{:S(2)}, u32[]{:S(2)}) collective-permute-start(bf16[288,384]{1,0:T(8,128)(2,1)S(1)} %merge_shares.1), channel_id=1, source_target_pairs={{0,16},{8,24},{16,0},{24,8},{32,48},{40,56},{48,32},{56,40},{64,80... | collective-permute-start | bytes 663560 | tf_op jit(solution)/shard_map/ppermute | solution.py:457
  69.4 5.7 %collective-permute-done.22.refs_2_ = bf16[288,384]{1,0:T(8,128)(2,1)S(1)} collective-permute-done((bf16[288,384]{1,0:T(8,128)(2,1)S(1)}, bf16[288,384]{1,0:T(8,128)(2,1)S(1)}, u32[]{:S(2)}, u32[]{:S(2)}) %collective-permute-start.22) | collective-permute-done | bytes 221216 | tf_op jit(solution)/shard_map/ppermute | solution.py:457
  75.1 1.4 %join.1 = (bf16[256,384]{1,0:T(8,128)(2,1)S(1)}, bf16[256,384]{1,0:T(8,128)(2,1)S(1)}, bf16[256,384]{1,0:T(8,128)(2,1)S(1)}) custom-call(s32[2]{0:T(128)S(1)} %pad_add_fusion.ids, bf16[288,384]{1,0:T(8,128)(2,1)S(1)} %get-tuple-element.52.refs_0_, bf16[288,384]{1,0:T(8,128)(2,1)S(1)} %collective-permute-done.20.refs_1_, ...), custom_call_target="tpu_custom_call" | custom-call | flops 150994944 | bytes 3000000 | tf_op jit(solution)/shard_map/join/pallas_call | solution.py:341
  76.5 1.9 %collective-permute-start.26 = (bf16[256,384]{1,0:T(8,128)(2,1)S(1)}, bf16[256,384]{1,0:T(8,128)(2,1)S(1)}, u32[]{:S(2)}, u32[]{:S(2)}) collective-permute-start(bf16[256,384]{1,0:T(8,128)(2,1)S(1)} %get-tuple-element.62), channel_id=1, source_target_pairs={{0,2},{1,3},{2,0},{3,1},{4,6},{5,7},{6,4},{7,5},{8,10},{9,11},{10,... | collective-permute-start | bytes 589832 | tf_op jit(solution)/shard_map/ppermute | solution.py:453
  78.4 0.9 collective-permute-start.28
  79.3 1.4 %direct_terms.1 = (bf16[256,384]{1,0:T(8,128)(2,1)S(1)}, bf16[256,384]{1,0:T(8,128)(2,1)S(1)}, bf16[256,384]{1,0:T(8,128)(2,1)S(1)}, bf16[256,384]{1,0:T(8,128)(...) custom-call(s32[2]{0:T(128)S(1)} %pad_add_fusion.ids, ...), custom_call_target="tpu_custom_call" | custom-call | flops 452984832 | bytes 4000000 | tf_op jit(solution)/shard_map/direct_terms/pallas_call | solution.py:361
  80.7 2.2 %collective-permute-start.23 = (bf16[256,384]{1,0:T(8,128)(2,1)S(1)}, bf16[256,384]{1,0:T(8,128)(2,1)S(1)}, u32[]{:S(2)}, u32[]{:S(2)}) collective-permute-start(bf16[256,384]{1,0:T(8,128)(2,1)S(1)} %get-tuple-element.58), channel_id=1, source_target_pairs={{0,1},{1,0},{2,3},{3,2},{4,5},{5,4},{6,7},{7,6},{8,9},{9,8},{10,11... | collective-permute-start | bytes 589832 | tf_op jit(solution)/shard_map/ppermute | solution.py:453
  82.9 0.6 collective-permute-start.24
  83.5 2.8 %collective-permute-start.25 = (bf16[256,384]{1,0:T(8,128)(2,1)S(1)}, bf16[256,384]{1,0:T(8,128)(2,1)S(1)}, u32[]{:S(2)}, u32[]{:S(2)}) collective-permute-start(bf16[256,384]{1,0:T(8,128)(2,1)S(1)} %get-tuple-element.60), channel_id=1, source_target_pairs={{0,7},{1,6},{2,5},{3,4},{4,3},{5,2},{6,1},{7,0},{8,15},{9,14},{10,... | collective-permute-start | bytes 589832 | tf_op jit(solution)/shard_map/ppermute | solution.py:453
  86.3 0.1 add_convert_fusion.1
  86.4 1.0 collective-permute-start.27
  87.4 0.1 add_convert_fusion
  87.4 2.9 %collective-permute-start.29 = (bf16[256,384]{1,0:T(8,128)(2,1)S(1)}, bf16[256,384]{1,0:T(8,128)(2,1)S(1)}, u32[]{:S(2)}, u32[]{:S(2)}) collective-permute-start(bf16[256,384]{1,0:T(8,128)(2,1)S(1)} %add_convert_fusion), channel_id=1, source_target_pairs={{0,3},{1,2},{2,1},{3,0},{4,7},{5,6},{6,5},{7,4},{8,11},{9,10},{10,... | collective-permute-start | bytes 589832 | tf_op jit(solution)/shard_map/ppermute | solution.py:453
  90.3 5.9 %collective-permute-done.25.refs_3_ = bf16[256,384]{1,0:T(8,128)(2,1)S(1)} collective-permute-done((bf16[256,384]{1,0:T(8,128)(2,1)S(1)}, bf16[256,384]{1,0:T(8,128)(2,1)S(1)}, u32[]{:S(2)}, u32[]{:S(2)}) %collective-permute-start.25) | collective-permute-done | bytes 196640 | tf_op jit(solution)/shard_map/ppermute | solution.py:453
  96.2 0.5 collective-permute-done.27.refs_4_
  96.7 0.5 collective-permute-done.29.refs_5_
  97.2 0.8 add_terms.1
  98.0 3.0 %collective-permute-start.30 = (bf16[128,384]{1,0:T(8,128)(2,1)S(1)}, bf16[128,384]{1,0:T(8,128)(2,1)S(1)}, u32[]{:S(2)}, u32[]{:S(2)}) collective-permute-start(bf16[128,384]{1,0:T(8,128)(2,1)S(1)} %get-tuple-element.66), channel_id=1, source_target_pairs={{0,64},{8,72},{16,80},{24,88},{32,96},{40,104},{48,112},{56,120},{... | collective-permute-start | bytes 294920 | tf_op jit(solution)/shard_map/ppermute | solution.py:457
  101.0 2.6 %collective-permute-done.30.got_ref = bf16[128,384]{1,0:T(8,128)(2,1)S(1)} collective-permute-done((bf16[128,384]{1,0:T(8,128)(2,1)S(1)}, bf16[128,384]{1,0:T(8,128)(2,1)S(1)}, u32[]{:S(2)}, u32[]{:S(2)}) %collective-permute-start.30) | collective-permute-done | bytes 98336 | tf_op jit(solution)/shard_map/ppermute | solution.py:457
  103.6 0.7 order.1
  104.3 25.1 %all_to_all.5 = bf16[32,16,384]{2,1,0:T(8,128)(2,1)S(1)} all-to-all(bf16[32,16,384]{2,1,0:T(8,128)(2,1)S(1)} %bitcast.11), channel_id=1, replica_groups=mesh['seq'=32,'head'=8] {'seq'}, dimensions={0} | all-to-all | bytes 786432 | tf_op jit(solution)/shard_map/all_to_all | solution.py:515
  129.4 1.2 to_tile.1
  (29 shorter events, 0.1 us)
Async XLA Ops:
  0.0 9.6 %collective-permute-start.2 = (bf16[32,3072]{1,0:T(8,128)(2,1)}, bf16[32,3072]{1,0:T(8,128)(2,1)S(1)}, u32[]{:S(2)}, u32[]{:S(2)}) collective-permute-start(bf16[32,3072]{1,0:T(8,128)(2,1)} %bitcast.13), channel_id=1, source_target_pairs={{0,3},{1,2},{2,1},{3,0},{4,7},{5,6},{6,5},{7,4},{8,11},{9,10},{10,... | collective-permute-start | bytes 589832 | tf_op jit(solution)/shard_map/ppermute | solution.py:453
  3.1 10.2 %collective-permute-start = (bf16[32,3072]{1,0:T(8,128)(2,1)}, bf16[32,3072]{1,0:T(8,128)(2,1)S(1)}, u32[]{:S(2)}, u32[]{:S(2)}) collective-permute-start(bf16[32,3072]{1,0:T(8,128)(2,1)} %bitcast.14), channel_id=1, source_target_pairs={{0,6},{1,7},{2,4},{3,5},{4,2},{5,3},{6,0},{7,1},{8,14},{9,15},{10,... | collective-permute-start | bytes 589832 | tf_op jit(solution)/shard_map/ppermute | solution.py:453
  5.3 13.0 %collective-permute-start.6 = (bf16[32,3072]{1,0:T(8,128)(2,1)}, bf16[32,3072]{1,0:T(8,128)(2,1)S(1)}, u32[]{:S(2)}, u32[]{:S(2)}) collective-permute-start(bf16[32,3072]{1,0:T(8,128)(2,1)} %bitcast.15), channel_id=1, source_target_pairs={{0,2},{1,3},{2,0},{3,1},{4,6},{5,7},{6,4},{7,5},{8,10},{9,11},{10,... | collective-permute-start | bytes 589832 | tf_op jit(solution)/shard_map/ppermute | solution.py:453
  6.0 12.3 %collective-permute-start.5 = (bf16[32,3072]{1,0:T(8,128)(2,1)}, bf16[32,3072]{1,0:T(8,128)(2,1)S(1)}, u32[]{:S(2)}, u32[]{:S(2)}) collective-permute-start(bf16[32,3072]{1,0:T(8,128)(2,1)} %bitcast.16), channel_id=1, source_target_pairs={{0,1},{1,0},{2,3},{3,2},{4,5},{5,4},{6,7},{7,6},{8,9},{9,8},{10,11... | collective-permute-start | bytes 589832 | tf_op jit(solution)/shard_map/ppermute | solution.py:453
  7.4 18.3 %collective-permute-start.4 = (bf16[32,3072]{1,0:T(8,128)(2,1)}, bf16[32,3072]{1,0:T(8,128)(2,1)S(1)}, u32[]{:S(2)}, u32[]{:S(2)}) collective-permute-start(bf16[32,3072]{1,0:T(8,128)(2,1)} %bitcast.17), channel_id=1, source_target_pairs={{0,7},{1,6},{2,5},{3,4},{4,3},{5,2},{6,1},{7,0},{8,15},{9,14},{10,... | collective-permute-start | bytes 589832 | tf_op jit(solution)/shard_map/ppermute | solution.py:453
  9.6 16.2 %collective-permute-start.3 = (bf16[32,3072]{1,0:T(8,128)(2,1)S(1)}, bf16[32,3072]{1,0:T(8,128)(2,1)S(1)}, u32[]{:S(2)}, u32[]{:S(2)}) collective-permute-start(bf16[32,3072]{1,0:T(8,128)(2,1)S(1)} %collective-permute-done.2.refs_3_), channel_id=1, source_target_pairs={{0,6},{1,7},{2,4},{3,5},{4,2},{5,3},{6,0},{7,1},{8,14},{9,15},{10,... | collective-permute-start | bytes 589832 | tf_op jit(solution)/shard_map/ppermute | solution.py:453
  13.4 12.4 %collective-permute-start.1 = (bf16[32,3072]{1,0:T(8,128)(2,1)S(1)}, bf16[32,3072]{1,0:T(8,128)(2,1)S(1)}, u32[]{:S(2)}, u32[]{:S(2)}) collective-permute-start(bf16[32,3072]{1,0:T(8,128)(2,1)S(1)} %collective-permute-done.refs_2_.refs_6_), channel_id=1, source_target_pairs={{0,2},{1,3},{2,0},{3,1},{4,6},{5,7},{6,4},{7,5},{8,10},{9,11},{10,... | collective-permute-start | bytes 589832 | tf_op jit(solution)/shard_map/ppermute | solution.py:453
  13.6 3.0 %copy-start.1 = (bf16[3072,3,384]{2,0,1:T(8,128)(2,1)S(1)}, bf16[3072,3,384]{2,0,1:T(8,128)(2,1)}, u32[]{:S(2)}) copy-start(bf16[3072,3,384]{2,0,1:T(8,128)(2,1)} %param.8) | copy-start | bytes 21233668
  16.6 1.7 %copy-start.2 = (bf16[4,1,8,3072]{3,2,1,0:T(8,128)(2,1)S(1)}, bf16[4,1,8,3072]{3,2,1,0:T(8,128)(2,1)}, u32[]{:S(2)}) copy-start(bf16[4,1,8,3072]{3,2,1,0:T(8,128)(2,1)} %param.7) | copy-start | bytes 589828
  16.6 1.7 %copy-start.4 = (f32[128]{0:T(128)S(1)}, f32[128]{0:T(128)}, u32[]{:S(2)}) copy-start(f32[128]{0:T(128)} %param.10) | copy-start | bytes 1540
  18.2 7.6 %copy-start.5 = (f32[128]{0:T(128)S(1)}, f32[128]{0:T(128)}, u32[]{:S(2)}) copy-start(f32[128]{0:T(128)} %param.9) | copy-start | bytes 1540
  19.9 10.3 %collective-permute-start.15 = (bf16[128,768]{1,0:T(8,128)(2,1)S(1)}, bf16[128,768]{1,0:T(8,128)(2,1)S(1)}, u32[]{:S(2)}, u32[]{:S(2)}) collective-permute-start(bf16[128,768]{1,0:T(8,128)(2,1)S(1)} %project_keys.2.refs_4_), channel_id=1, source_target_pairs={{32,64},{64,32},{40,72},{72,40},{48,80},{80,48},{56,88},{88,56},{9... | collective-permute-start | bytes 589832 | tf_op jit(solution)/shard_map/ppermute | solution.py:469
  20.6 10.1 %collective-permute-start.8 = (bf16[128,768]{1,0:T(8,128)(2,1)S(1)}, bf16[128,768]{1,0:T(8,128)(2,1)S(1)}, u32[]{:S(2)}, u32[]{:S(2)}) collective-permute-start(bf16[128,768]{1,0:T(8,128)(2,1)S(1)} %project_keys.2.refs_4_), channel_id=1, source_target_pairs={{0,32},{8,40},{16,48},{24,56},{32,0},{40,8},{48,16},{56,24},{64,96... | collective-permute-start | bytes 589832 | tf_op jit(solution)/shard_map/ppermute | solution.py:457
  25.8 24.3 %copy-start.3 = (s32[32,9]{0,1:T(8,128)S(1)}, s32[32,9]{0,1:T(8,128)}, u32[]{:S(2)}) copy-start(s32[32,9]{0,1:T(8,128)} %param.12) | copy-start | bytes 3460
  25.8 24.3 %copy-start.6 = (s32[32]{0:T(128)S(1)}, s32[32]{0:T(128)}, u32[]{:S(2)}) copy-start(s32[32]{0:T(128)} %tile_owner.1) | copy-start | bytes 388
  27.5 47.6 %copy-start = (bf16[384,3072]{1,0:T(8,128)(2,1)S(1)}, bf16[384,3072]{1,0:T(8,128)(2,1)}, u32[]{:S(2)}) copy-start(bf16[384,3072]{1,0:T(8,128)(2,1)} %w_ref.1) | copy-start | bytes 7077892
  27.6 5.8 %collective-permute-start.11 = (bf16[256,384]{1,0:T(8,128)(2,1)S(1)}, bf16[256,384]{1,0:T(8,128)(2,1)S(1)}, u32[]{:S(2)}, u32[]{:S(2)}) collective-permute-start(bf16[256,384]{1,0:T(8,128)(2,1)S(1)} %project_queries.1.refs_0_), channel_id=1, source_target_pairs={{0,16},{8,24},{16,0},{24,8},{32,48},{40,56},{48,32},{56,40},{64,80... | collective-permute-start | bytes 589832 | tf_op jit(solution)/shard_map/ppermute | solution.py:457
  29.4 5.8 %collective-permute-start.13 = (bf16[128,768]{1,0:T(8,128)(2,1)S(1)}, bf16[128,768]{1,0:T(8,128)(2,1)S(1)}, u32[]{:S(2)}, u32[]{:S(2)}) collective-permute-start(bf16[128,768]{1,0:T(8,128)(2,1)S(1)} %project_keys.3.refs_5_), channel_id=1, source_target_pairs={{0,32},{8,40},{16,48},{24,56},{32,0},{40,8},{48,16},{56,24},{64,96... | collective-permute-start | bytes 589832 | tf_op jit(solution)/shard_map/ppermute | solution.py:457
  29.6 6.3 %collective-permute-start.7 = (bf16[128,768]{1,0:T(8,128)(2,1)S(1)}, bf16[128,768]{1,0:T(8,128)(2,1)S(1)}, u32[]{:S(2)}, u32[]{:S(2)}) collective-permute-start(bf16[128,768]{1,0:T(8,128)(2,1)S(1)} %project_keys.3.refs_5_), channel_id=1, source_target_pairs={{32,64},{64,32},{40,72},{72,40},{48,80},{80,48},{56,88},{88,56},{9... | collective-permute-start | bytes 589832 | tf_op jit(solution)/shard_map/ppermute | solution.py:469
  30.2 12.6 %collective-permute-start.10 = (bf16[256,384]{1,0:T(8,128)(2,1)S(1)}, bf16[256,384]{1,0:T(8,128)(2,1)S(1)}, u32[]{:S(2)}, u32[]{:S(2)}) collective-permute-start(bf16[256,384]{1,0:T(8,128)(2,1)S(1)} %project_queries.1.refs_0_), channel_id=1, source_target_pairs={{0,8},{8,0},{16,24},{24,16},{32,40},{40,32},{48,56},{56,48},{64,72... | collective-permute-start | bytes 589832 | tf_op jit(solution)/shard_map/ppermute | solution.py:457
  30.7 12.1 %collective-permute-start.9 = (bf16[128,768]{1,0:T(8,128)(2,1)S(1)}, bf16[128,768]{1,0:T(8,128)(2,1)S(1)}, u32[]{:S(2)}, u32[]{:S(2)}) collective-permute-start(bf16[128,768]{1,0:T(8,128)(2,1)S(1)} %collective-permute-done.8.refs_6_), channel_id=1, source_target_pairs={{32,64},{64,32},{40,72},{72,40},{48,80},{80,48},{56,88},{88,56},{9... | collective-permute-start | bytes 589832 | tf_op jit(solution)/shard_map/ppermute | solution.py:469
  33.3 9.6 %collective-permute-start.12 = (bf16[256,384]{1,0:T(8,128)(2,1)S(1)}, bf16[256,384]{1,0:T(8,128)(2,1)S(1)}, u32[]{:S(2)}, u32[]{:S(2)}) collective-permute-start(bf16[256,384]{1,0:T(8,128)(2,1)S(1)} %collective-permute-done.11.refs_2_), channel_id=1, source_target_pairs={{0,8},{8,0},{16,24},{24,16},{32,40},{40,32},{48,56},{56,48},{64,72... | collective-permute-start | bytes 589832 | tf_op jit(solution)/shard_map/ppermute | solution.py:457
  35.2 11.0 %collective-permute-start.14 = (bf16[128,768]{1,0:T(8,128)(2,1)S(1)}, bf16[128,768]{1,0:T(8,128)(2,1)S(1)}, u32[]{:S(2)}, u32[]{:S(2)}) collective-permute-start(bf16[128,768]{1,0:T(8,128)(2,1)S(1)} %collective-permute-done.13.refs_7_), channel_id=1, source_target_pairs={{32,64},{64,32},{40,72},{72,40},{48,80},{80,48},{56,88},{88,56},{9... | collective-permute-start | bytes 589832 | tf_op jit(solution)/shard_map/ppermute | solution.py:469
  35.9 19.3 %collective-permute-start.16 = (bf16[128,768]{1,0:T(8,128)(2,1)S(1)}, bf16[128,768]{1,0:T(8,128)(2,1)S(1)}, u32[]{:S(2)}, u32[]{:S(2)}) collective-permute-start(bf16[128,768]{1,0:T(8,128)(2,1)S(1)} %collective-permute-done.15.refs_8_), channel_id=1, source_target_pairs={{0,32},{8,40},{16,48},{24,56},{32,0},{40,8},{48,16},{56,24},{64,96... | collective-permute-start | bytes 589832 | tf_op jit(solution)/shard_map/ppermute | solution.py:457
  42.9 14.1 %collective-permute-start.18 = (bf16[128,768]{1,0:T(8,128)(2,1)S(1)}, bf16[128,768]{1,0:T(8,128)(2,1)S(1)}, u32[]{:S(2)}, u32[]{:S(2)}) collective-permute-start(bf16[128,768]{1,0:T(8,128)(2,1)S(1)} %collective-permute-done.9.refs_4_), channel_id=1, source_target_pairs={{0,32},{8,40},{16,48},{24,56},{32,0},{40,8},{48,16},{56,24},{64,96... | collective-permute-start | bytes 589832 | tf_op jit(solution)/shard_map/ppermute | solution.py:457
  46.2 10.8 %collective-permute-start.19 = (bf16[128,768]{1,0:T(8,128)(2,1)S(1)}, bf16[128,768]{1,0:T(8,128)(2,1)S(1)}, u32[]{:S(2)}, u32[]{:S(2)}) collective-permute-start(bf16[128,768]{1,0:T(8,128)(2,1)S(1)} %collective-permute-done.14.refs_5_), channel_id=1, source_target_pairs={{0,32},{8,40},{16,48},{24,56},{32,0},{40,8},{48,16},{56,24},{64,96... | collective-permute-start | bytes 589832 | tf_op jit(solution)/shard_map/ppermute | solution.py:457
  50.0 10.6 %collective-permute-start.17 = (bf16[128,768]{1,0:T(8,128)(2,1)S(1)}, bf16[128,768]{1,0:T(8,128)(2,1)S(1)}, u32[]{:S(2)}, u32[]{:S(2)}) collective-permute-start(bf16[128,768]{1,0:T(8,128)(2,1)S(1)} %collective-permute-done.7.refs_9_), channel_id=1, source_target_pairs={{0,32},{8,40},{16,48},{24,56},{32,0},{40,8},{48,16},{56,24},{64,96... | collective-permute-start | bytes 589832 | tf_op jit(solution)/shard_map/ppermute | solution.py:457
  65.6 1.6 %collective-permute-start.21 = (bf16[288,384]{1,0:T(8,128)(2,1)S(1)}, bf16[288,384]{1,0:T(8,128)(2,1)S(1)}, u32[]{:S(2)}, u32[]{:S(2)}) collective-permute-start(bf16[288,384]{1,0:T(8,128)(2,1)S(1)} %get-tuple-element.55), channel_id=1, source_target_pairs={{0,8},{8,0},{16,24},{24,16},{32,40},{40,32},{48,56},{56,48},{64,72... | collective-permute-start | bytes 663560 | tf_op jit(solution)/shard_map/ppermute | solution.py:457
  65.7 3.7 %collective-permute-start.20 = (bf16[288,384]{1,0:T(8,128)(2,1)S(1)}, bf16[288,384]{1,0:T(8,128)(2,1)S(1)}, u32[]{:S(2)}, u32[]{:S(2)}) collective-permute-start(bf16[288,384]{1,0:T(8,128)(2,1)S(1)} %get-tuple-element.53), channel_id=1, source_target_pairs={{0,8},{8,0},{16,24},{24,16},{32,40},{40,32},{48,56},{56,48},{64,72... | collective-permute-start | bytes 663560 | tf_op jit(solution)/shard_map/ppermute | solution.py:457
  67.5 7.7 %collective-permute-start.22 = (bf16[288,384]{1,0:T(8,128)(2,1)S(1)}, bf16[288,384]{1,0:T(8,128)(2,1)S(1)}, u32[]{:S(2)}, u32[]{:S(2)}) collective-permute-start(bf16[288,384]{1,0:T(8,128)(2,1)S(1)} %merge_shares.1), channel_id=1, source_target_pairs={{0,16},{8,24},{16,0},{24,8},{32,48},{40,56},{48,32},{56,40},{64,80... | collective-permute-start | bytes 663560 | tf_op jit(solution)/shard_map/ppermute | solution.py:457
  76.5 9.8 %collective-permute-start.26 = (bf16[256,384]{1,0:T(8,128)(2,1)S(1)}, bf16[256,384]{1,0:T(8,128)(2,1)S(1)}, u32[]{:S(2)}, u32[]{:S(2)}) collective-permute-start(bf16[256,384]{1,0:T(8,128)(2,1)S(1)} %get-tuple-element.62), channel_id=1, source_target_pairs={{0,2},{1,3},{2,0},{3,1},{4,6},{5,7},{6,4},{7,5},{8,10},{9,11},{10,... | collective-permute-start | bytes 589832 | tf_op jit(solution)/shard_map/ppermute | solution.py:453
  78.4 9.0 %collective-permute-start.28 = (bf16[256,384]{1,0:T(8,128)(2,1)S(1)}, bf16[256,384]{1,0:T(8,128)(2,1)S(1)}, u32[]{:S(2)}, u32[]{:S(2)}) collective-permute-start(bf16[256,384]{1,0:T(8,128)(2,1)S(1)} %get-tuple-element.64), channel_id=1, source_target_pairs={{0,6},{1,7},{2,4},{3,5},{4,2},{5,3},{6,0},{7,1},{8,14},{9,15},{10,... | collective-permute-start | bytes 589832 | tf_op jit(solution)/shard_map/ppermute | solution.py:453
  80.7 9.6 %collective-permute-start.23 = (bf16[256,384]{1,0:T(8,128)(2,1)S(1)}, bf16[256,384]{1,0:T(8,128)(2,1)S(1)}, u32[]{:S(2)}, u32[]{:S(2)}) collective-permute-start(bf16[256,384]{1,0:T(8,128)(2,1)S(1)} %get-tuple-element.58), channel_id=1, source_target_pairs={{0,1},{1,0},{2,3},{3,2},{4,5},{5,4},{6,7},{7,6},{8,9},{9,8},{10,11... | collective-permute-start | bytes 589832 | tf_op jit(solution)/shard_map/ppermute | solution.py:453
  82.9 7.4 %collective-permute-start.24 = (bf16[256,384]{1,0:T(8,128)(2,1)S(1)}, bf16[256,384]{1,0:T(8,128)(2,1)S(1)}, u32[]{:S(2)}, u32[]{:S(2)}) collective-permute-start(bf16[256,384]{1,0:T(8,128)(2,1)S(1)} %get-tuple-element.59), channel_id=1, source_target_pairs={{0,2},{1,3},{2,0},{3,1},{4,6},{5,7},{6,4},{7,5},{8,10},{9,11},{10,... | collective-permute-start | bytes 589832 | tf_op jit(solution)/shard_map/ppermute | solution.py:453
  83.5 12.7 %collective-permute-start.25 = (bf16[256,384]{1,0:T(8,128)(2,1)S(1)}, bf16[256,384]{1,0:T(8,128)(2,1)S(1)}, u32[]{:S(2)}, u32[]{:S(2)}) collective-permute-start(bf16[256,384]{1,0:T(8,128)(2,1)S(1)} %get-tuple-element.60), channel_id=1, source_target_pairs={{0,7},{1,6},{2,5},{3,4},{4,3},{5,2},{6,1},{7,0},{8,15},{9,14},{10,... | collective-permute-start | bytes 589832 | tf_op jit(solution)/shard_map/ppermute | solution.py:453
  86.4 10.3 %collective-permute-start.27 = (bf16[256,384]{1,0:T(8,128)(2,1)S(1)}, bf16[256,384]{1,0:T(8,128)(2,1)S(1)}, u32[]{:S(2)}, u32[]{:S(2)}) collective-permute-start(bf16[256,384]{1,0:T(8,128)(2,1)S(1)} %add_convert_fusion.1), channel_id=1, source_target_pairs={{0,6},{1,7},{2,4},{3,5},{4,2},{5,3},{6,0},{7,1},{8,14},{9,15},{10,... | collective-permute-start | bytes 589832 | tf_op jit(solution)/shard_map/ppermute | solution.py:453
  87.4 9.8 %collective-permute-start.29 = (bf16[256,384]{1,0:T(8,128)(2,1)S(1)}, bf16[256,384]{1,0:T(8,128)(2,1)S(1)}, u32[]{:S(2)}, u32[]{:S(2)}) collective-permute-start(bf16[256,384]{1,0:T(8,128)(2,1)S(1)} %add_convert_fusion), channel_id=1, source_target_pairs={{0,3},{1,2},{2,1},{3,0},{4,7},{5,6},{6,5},{7,4},{8,11},{9,10},{10,... | collective-permute-start | bytes 589832 | tf_op jit(solution)/shard_map/ppermute | solution.py:453
  98.0 5.6 %collective-permute-start.30 = (bf16[128,384]{1,0:T(8,128)(2,1)S(1)}, bf16[128,384]{1,0:T(8,128)(2,1)S(1)}, u32[]{:S(2)}, u32[]{:S(2)}) collective-permute-start(bf16[128,384]{1,0:T(8,128)(2,1)S(1)} %get-tuple-element.66), channel_id=1, source_target_pairs={{0,64},{8,72},{16,80},{24,88},{32,96},{40,104},{48,112},{56,120},{... | collective-permute-start | bytes 294920 | tf_op jit(solution)/shard_map/ppermute | solution.py:457

commit v5 on v4

--- a/solution.py
+++ b/solution.py
@@ -210,34 +210,34 @@
     return top + jnp.log2(total)
 
 
-def merge_kernel(first_ref, second_ref, out_ref):
-    store_level(out_ref, merge([first_ref, second_ref], out_ref))
-
-
-def merge_shares(first, second):
+def merge_kernel(*refs):
+    *shares, out_ref = refs
+    store_level(out_ref, merge(shares, out_ref))
+
+
+def merge_shares(*shares):
     whole = pl.BlockSpec(memory_space=pltpu.VMEM)
     return pl.pallas_call(
         merge_kernel,
-        in_specs=[whole] * 2,
+        in_specs=[whole] * len(shares),
         out_specs=whole,
-        out_shape=jax.ShapeDtypeStruct(first.shape, first.dtype),
+        out_shape=jax.ShapeDtypeStruct(shares[0].shape, shares[0].dtype),
         compiler_params=params(8),
         cost_estimate=pl.CostEstimate(flops=500_000, bytes_accessed=1_000_000, transcendentals=0),
         name="merge_shares",
-    )(first, second)
-
-
-def attend_kernel(kinds, last, table, *refs):
+    )(*shares)
+
+
+def attend_kernel(kinds, table, *refs):
     count = len(kinds)
     refs = list(refs)
     take = lambda n: [refs.pop(0) for _ in range(n)]
     queries, halves = take(PLANE), take(2 * count)
-    before = take(PLANE + 1) if last else None
-    outs = take(PLANE) if last else take(PLANE + 1)
+    outs = take(PLANE)
     piece_of = lax.broadcasted_iota(jnp.int32, (1, count * WINDOW), 1) // PIECE
     ones = jnp.ones((count * WINDOW, HEAD_DIM), jnp.bfloat16)
     slots_ref = refs.pop(0)
-    level_ref = refs.pop(0) if last else outs[PLANE]
+    level_ref = refs.pop(0)
     size = HALF * PIECE
     for n in range(count):
         for e in range(2):
@@ -268,45 +268,29 @@
                 weights, jnp.concatenate([v, ones], axis=1), preferred_element_type=jnp.float32
             )
             mixed, total = both[:, :HEAD_DIM], both[:, HEAD_DIM:]
-            if last:
-                other = before[PLANE][:, lane]
-                mixed_before = jnp.concatenate([ref[here, head] for ref in before[:PLANE]], axis=0)
-                high = jnp.maximum(top, other)
-                share = jnp.exp2(other - high)
-                mine = jnp.exp2(top - high)
-                whole = mine * total + share
-                mixed = (mixed * mine + mixed_before.astype(jnp.float32) * share) / whole
-                level = high + jnp.log2(whole)
-            else:
-                mixed = mixed / total
-                level = top + jnp.log2(total)
+            mixed = mixed / jnp.maximum(total, 0.5)
+            level = jnp.maximum(top + jnp.log2(total), LOWEST)
             mixed = mixed.astype(jnp.bfloat16)
             for n in range(PLANE):
                 outs[n][here, head] = mixed[n * PIECE : (n + 1) * PIECE]
             level_ref[:, lane] = level[:, lane]
-    if last:
-        for n in range(PLANE):
-            store_level(outs[n], level_ref[n * PIECE : (n + 1) * PIECE])
-
-
-def attend(table, queries, slots, kinds, before=()):
+    for n in range(PLANE):
+        store_level(outs[n], level_ref[n * PIECE : (n + 1) * PIECE])
+
+
+def attend(table, queries, slots, kinds):
     tokens = TILE_COLS * PIECE
     count = len(slots)
-    last = bool(before)
     whole = pl.BlockSpec(memory_space=pltpu.VMEM)
     scalars = pl.BlockSpec(memory_space=pltpu.SMEM)
-    operands = [*queries, *(half for slot in slots for half in slot), *before]
-    levels = (PLANE * PIECE, HEAD_DIM)
-    if last:
-        out_shape = [jax.ShapeDtypeStruct((tokens + PIECE, WIDTH), jnp.bfloat16)] * PLANE
-    else:
-        out_shape = [jax.ShapeDtypeStruct((tokens, WIDTH), jnp.bfloat16)] * PLANE
-        out_shape.append(jax.ShapeDtypeStruct(levels, jnp.float32))
-    scratch = [pltpu.VMEM((count, tokens, 2 * WIDTH), jnp.bfloat16)]
-    if last:
-        scratch.append(pltpu.VMEM(levels, jnp.float32))
-    return pl.pallas_call(
-        functools.partial(attend_kernel, kinds, last),
+    operands = [*queries, *(half for slot in slots for half in slot)]
+    out_shape = [jax.ShapeDtypeStruct((tokens + PIECE, WIDTH), jnp.bfloat16)] * PLANE
+    scratch = [
+        pltpu.VMEM((count, tokens, 2 * WIDTH), jnp.bfloat16),
+        pltpu.VMEM((PLANE * PIECE, HEAD_DIM), jnp.float32),
+    ]
+    return pl.pallas_call(
+        functools.partial(attend_kernel, kinds),
         in_specs=[scalars] + [whole] * len(operands),
         out_specs=[whole] * len(out_shape),
         out_shape=out_shape,
@@ -498,12 +482,13 @@
     near_slots = [(_own, own_b), (mate_a, mate_b), (edge_a, edge_b)]
     far_slots = [(edge_2a, edge_2b), (far_1a, far_1b), (far_2a, far_2b)]
     near = attend(table, all_queries, near_slots, (0, 0, 1))
-    shares = attend(table, all_queries, far_slots, (1, 2, 2), near)
-
-    from_core, for_chip = plane_swap(shares[1], 1), plane_swap(shares[3], 1)
-    from_chip = plane_swap(merge_shares(shares[2], for_chip), 2)
-
-    joined, *relayed = join(ids, [shares[0], from_core, from_chip], w_out)
+    near_own = merge_shares(near[0], plane_swap(near[1], 1))
+    near_chip = merge_shares(near[2], plane_swap(near[3], 1))
+    far = attend(table, all_queries, far_slots, (1, 2, 2))
+    from_core, for_chip = plane_swap(far[1], 1), plane_swap(far[3], 1)
+    from_chip = plane_swap(merge_shares(near_chip, far[2], for_chip), 2)
+
+    joined, *relayed = join(ids, [near_own, far[0], from_core, from_chip], w_out)
     passed = {6: head_swap(relayed[0], 2), 3: head_swap(relayed[1], 6)}
     terms = dict(zip(DIRECT, direct_terms(ids, joined, w_out)))
     for k in (6, 3):

time: 131 us -> 129 us (0.985)
    pallas_call x3 -> x5, Pallas kernels: 8.28 us -> 7.12 us  [the longest x2 6.03 us: attend(): pl.pallas_call(functools.partial(attend_kernel, kinds), in_specs=[scalars...]
    ppermute x13 -> x15, waiting for transfers between devices: 18.9 us -> 18 us  [plane_swap(): lax.ppermute(array, 'seq', [(s, s ^ k) for s in range(PLANE * PLANES)])]
    ppermute x13 -> x15, starting transfers between devices: 25.3 us -> 25.5 us  [plane_swap(): lax.ppermute(array, 'seq', [(s, s ^ k) for s in range(PLANE * PLANES)])]
  transfers between devices with their start and end apart: 31 -> 33, of which waited for: 11 -> 11; matrix products, arithmetic and copies ran while one was open for 0% -> 0% of each run, Pallas kernels for 10% -> 13%
where the time goes in v5:
time: 129 us
  starting transfers between devices  53.8 us (42%)
  blocking collectives  25.1 us (19%)
  waiting for transfers between devices  24.9 us (19%)
  Pallas kernels  21.4 us (17%)
  local copies, waits for them, and re-layouts  3.04 us (2%)
    ppermute x14, starting transfers between devices, head_swap(): return lax.ppermute(array, 'head', [(h, h ^ k) for h in range(N_HEAD)])  25.6 us
    ppermute x15, starting transfers between devices, plane_swap(): lax.ppermute(array, 'seq', [(s, s ^ k) for s in range(PLANE * PLANES)])  25.5 us
    all_to_all x1, blocking collectives, local(): lax.all_to_all(sent.reshape(TILES, PAIR, WIDTH), 'seq', split_axis=0, con...  25.1 us
    ppermute x15, waiting for transfers between devices, plane_swap(): lax.ppermute(array, 'seq', [(s, s ^ k) for s in range(PLANE * PLANES)])  18 us
    ppermute x14, waiting for transfers between devices, head_swap(): return lax.ppermute(array, 'head', [(h, h ^ k) for h in range(N_HEAD)])  6.92 us
    pallas_call x2, Pallas kernels, attend(): pl.pallas_call(functools.partial(attend_kernel, kinds), in_specs=[scalars...  6.03 us
    pallas_call x2, Pallas kernels, project_keys(): pl.pallas_call(functools.partial(keys_kernel, steps), in_specs=[pl.BlockS...  3.22 us
    unnamed x14, local copies, waits for them, and re-layouts  3.04 us
  transfers between devices with their start and end apart: 33, of which 11 were waited for; matrix products, arithmetic and copies ran while one was open for 0% of the time, Pallas kernels for 13%

profile of v5, /device:TPU:2, one launch (start us, length us, event | category | flops | bytes accessed | tf_op | source)
XLA Modules:
  0.0 128.7 jit_solution(3738796008060863590)
XLA Ops:
  0.0 3.1 %collective-permute-start.2 = (bf16[32,3072]{1,0:T(8,128)(2,1)}, bf16[32,3072]{1,0:T(8,128)(2,1)S(1)}, u32[]{:S(2)}, u32[]{:S(2)}) collective-permute-start(bf16[32,3072]{1,0:T(8,128)(2,1)} %bitcast.13), channel_id=1, source_target_pairs={{0,3},{1,2},{2,1},{3,0},{4,7},{5,6},{6,5},{7,4},{8,11},{9,10},{10,... | collective-permute-start | bytes 589832 | tf_op jit(solution)/shard_map/ppermute | solution.py:437
  3.1 2.2 %collective-permute-start = (bf16[32,3072]{1,0:T(8,128)(2,1)}, bf16[32,3072]{1,0:T(8,128)(2,1)S(1)}, u32[]{:S(2)}, u32[]{:S(2)}) collective-permute-start(bf16[32,3072]{1,0:T(8,128)(2,1)} %bitcast.14), channel_id=1, source_target_pairs={{0,6},{1,7},{2,4},{3,5},{4,2},{5,3},{6,0},{7,1},{8,14},{9,15},{10,... | collective-permute-start | bytes 589832 | tf_op jit(solution)/shard_map/ppermute | solution.py:437
  5.3 0.7 collective-permute-start.6
  6.0 1.4 %collective-permute-start.5 = (bf16[32,3072]{1,0:T(8,128)(2,1)}, bf16[32,3072]{1,0:T(8,128)(2,1)S(1)}, u32[]{:S(2)}, u32[]{:S(2)}) collective-permute-start(bf16[32,3072]{1,0:T(8,128)(2,1)} %bitcast.16), channel_id=1, source_target_pairs={{0,1},{1,0},{2,3},{3,2},{4,5},{5,4},{6,7},{7,6},{8,9},{9,8},{10,11... | collective-permute-start | bytes 589832 | tf_op jit(solution)/shard_map/ppermute | solution.py:437
  7.4 2.2 %collective-permute-start.4 = (bf16[32,3072]{1,0:T(8,128)(2,1)}, bf16[32,3072]{1,0:T(8,128)(2,1)S(1)}, u32[]{:S(2)}, u32[]{:S(2)}) collective-permute-start(bf16[32,3072]{1,0:T(8,128)(2,1)} %bitcast.17), channel_id=1, source_target_pairs={{0,7},{1,6},{2,5},{3,4},{4,3},{5,2},{6,1},{7,0},{8,15},{9,14},{10,... | collective-permute-start | bytes 589832 | tf_op jit(solution)/shard_map/ppermute | solution.py:437
  9.6 3.8 %collective-permute-start.3 = (bf16[32,3072]{1,0:T(8,128)(2,1)S(1)}, bf16[32,3072]{1,0:T(8,128)(2,1)S(1)}, u32[]{:S(2)}, u32[]{:S(2)}) collective-permute-start(bf16[32,3072]{1,0:T(8,128)(2,1)S(1)} %collective-permute-done.2.refs_3_), channel_id=1, source_target_pairs={{0,6},{1,7},{2,4},{3,5},{4,2},{5,3},{6,0},{7,1},{8,14},{9,15},{10,... | collective-permute-start | bytes 589832 | tf_op jit(solution)/shard_map/ppermute | solution.py:437
  13.4 0.2 collective-permute-start.1
  13.6 3.0 %copy-done.1 = bf16[3072,3,384]{2,0,1:T(8,128)(2,1)S(1)} copy-done((bf16[3072,3,384]{2,0,1:T(8,128)(2,1)S(1)}, bf16[3072,3,384]{2,0,1:T(8,128)(2,1)}, u32[]{:S(2)}) %copy-start.1) | copy-done | bytes 7077912
  16.6 1.6 %load_weight.1.refs_4_.refs_8_ = bf16[3,3072,384]{2,1,0:T(8,128)(2,1)S(1)} custom-call(bf16[3,3072,384]{2,1,0:T(8,128)(2,1)S(1)} %bitcast.10), custom_call_target="tpu_custom_call" | custom-call | bytes 7100000 | tf_op jit(solution)/shard_map/load_weight/pallas_call | solution.py:116
  18.2 0.1 pad_add_fusion.ids
  18.3 1.6 %project_keys.2.refs_4_ = bf16[128,768]{1,0:T(8,128)(2,1)S(1)} custom-call(s32[2]{0:T(128)S(1)} %pad_add_fusion.ids, bf16[32,3072]{1,0:T(8,128)(2,1)S(1)} %bitcast.18, bf16[32,3072]{1,0:T(8,128)(2,1)S(1)} %collective-permute-done.5.refs_1_, bf16[32,3072]{1,0:T(8,128)(2,1)S(1)} %collective-permute-done.6.refs_2_, ...), custom_call_target="tpu_custom_call" | custom-call | flops 603979776 | bytes 6000000 | tf_op jit(solution)/shard_map/project_keys/pallas_call | solution.py:165
  19.9 0.7 collective-permute-start.14
  20.6 5.2 %collective-permute-start.8 = (bf16[128,768]{1,0:T(8,128)(2,1)S(1)}, bf16[128,768]{1,0:T(8,128)(2,1)S(1)}, u32[]{:S(2)}, u32[]{:S(2)}) collective-permute-start(bf16[128,768]{1,0:T(8,128)(2,1)S(1)} %project_keys.2.refs_4_), channel_id=1, source_target_pairs={{0,32},{8,40},{16,48},{24,56},{32,0},{40,8},{48,16},{56,24},{64,96... | collective-permute-start | bytes 589832 | tf_op jit(solution)/shard_map/ppermute | solution.py:441
  25.8 0.0 copy-start.6
  25.8 1.7 %project_queries.1.refs_0_ = bf16[256,384]{1,0:T(8,128)(2,1)S(1)} custom-call(s32[2]{0:T(128)S(1)} %pad_add_fusion.ids, bf16[32,3072]{1,0:T(8,128)(2,1)S(1)} %bitcast.19, bf16[32,3072]{1,0:T(8,128)(2,1)S(1)} %collective-permute-done.5.refs_1_, bf16[32,3072]{1,0:T(8,128)(2,1)S(1)} %collective-permute-done.6.refs_2_, ...), custom_call_target="tpu_custom_call" | custom-call | flops 603979776 | bytes 4000000 | tf_op jit(solution)/shard_map/project_queries/pallas_call | solution.py:138
  27.6 0.3 collective-permute-start.11
  27.8 1.6 %project_keys.3.refs_5_ = bf16[128,768]{1,0:T(8,128)(2,1)S(1)} custom-call(s32[2]{0:T(128)S(1)} %pad_add_fusion.ids, bf16[32,3072]{1,0:T(8,128)(2,1)S(1)} %collective-permute-done.1.refs_0_.refs_4_, bf16[32,3072]{1,0:T(8,128)(2,1)S(1)} %collective-permute-done.3.refs_1_.refs_5_, bf16[32,3072]{1,0:T(8,128)(2,1)S(1)} %collective-permute-done.refs_2_.refs_6_, ...), custom_call_target="tpu_custom_call" | custom-call | flops 603979776 | bytes 6000000 | tf_op jit(solution)/shard_map/project_keys/pallas_call | solution.py:165
  29.4 0.1 collective-permute-start.13
  29.6 0.7 collective-permute-start.7
  30.2 0.1 collective-permute-start.10
  30.3 0.4 collective-permute-done.8.refs_6_
  30.7 0.7 collective-permute-start.9
  31.4 1.9 %collective-permute-done.11.refs_2_ = bf16[256,384]{1,0:T(8,128)(2,1)S(1)} collective-permute-done((bf16[256,384]{1,0:T(8,128)(2,1)S(1)}, bf16[256,384]{1,0:T(8,128)(2,1)S(1)}, u32[]{:S(2)}, u32[]{:S(2)}) %collective-permute-start.11) | collective-permute-done | bytes 196640 | tf_op jit(solution)/shard_map/ppermute | solution.py:441
  33.3 1.9 %collective-permute-done.13.refs_7_ = bf16[128,768]{1,0:T(8,128)(2,1)S(1)} collective-permute-done((bf16[128,768]{1,0:T(8,128)(2,1)S(1)}, bf16[128,768]{1,0:T(8,128)(2,1)S(1)}, u32[]{:S(2)}, u32[]{:S(2)}) %collective-permute-start.13) | collective-permute-done | bytes 196640 | tf_op jit(solution)/shard_map/ppermute | solution.py:441
  35.2 0.7 collective-permute-start.16
  35.9 7.0 %collective-permute-start.17 = (bf16[128,768]{1,0:T(8,128)(2,1)S(1)}, bf16[128,768]{1,0:T(8,128)(2,1)S(1)}, u32[]{:S(2)}, u32[]{:S(2)}) collective-permute-start(bf16[128,768]{1,0:T(8,128)(2,1)S(1)} %collective-permute-done.14.refs_8_), channel_id=1, source_target_pairs={{0,32},{8,40},{16,48},{24,56},{32,0},{40,8},{48,16},{56,24},{64,96... | collective-permute-start | bytes 589832 | tf_op jit(solution)/shard_map/ppermute | solution.py:441
  42.9 3.3 %collective-permute-start.18 = (bf16[128,768]{1,0:T(8,128)(2,1)S(1)}, bf16[128,768]{1,0:T(8,128)(2,1)S(1)}, u32[]{:S(2)}, u32[]{:S(2)}) collective-permute-start(bf16[128,768]{1,0:T(8,128)(2,1)S(1)} %collective-permute-done.7.refs_9_), channel_id=1, source_target_pairs={{0,32},{8,40},{16,48},{24,56},{32,0},{40,8},{48,16},{56,24},{64,96... | collective-permute-start | bytes 589832 | tf_op jit(solution)/shard_map/ppermute | solution.py:441
  46.2 3.8 %collective-permute-start.20 = (bf16[128,768]{1,0:T(8,128)(2,1)S(1)}, bf16[128,768]{1,0:T(8,128)(2,1)S(1)}, u32[]{:S(2)}, u32[]{:S(2)}) collective-permute-start(bf16[128,768]{1,0:T(8,128)(2,1)S(1)} %collective-permute-done.16.refs_5_), channel_id=1, source_target_pairs={{0,32},{8,40},{16,48},{24,56},{32,0},{40,8},{48,16},{56,24},{64,96... | collective-permute-start | bytes 589832 | tf_op jit(solution)/shard_map/ppermute | solution.py:441
  50.0 0.0 collective-permute-start.19
  50.1 2.2 %plan.1.table = s32[128]{0:T(128)S(1)} custom-call(s32[2]{0:T(128)S(1)} %pad_add_fusion.ids, s32[9,32]{1,0:T(8,128)S(1)} %bitcast.20, s32[32]{0:T(128)S(1)} %copy-done.6), custom_call_target="tpu_custom_call" | custom-call | bytes 8000000 | tf_op jit(solution)/shard_map/plan/pallas_call | solution.py:73
  52.2 3.0 %attend.2 = (bf16[288,384]{1,0:T(8,128)(2,1)S(1)}, bf16[288,384]{1,0:T(8,128)(2,1)S(1)}, bf16[288,384]{1,0:T(8,128)(2,1)S(1)}, bf16[288,384]{1,0:T(8,128)(2,1)S(1)}) custom-call(s32[128]{0:T(128)S(1)} %plan.1.table, bf16[256,384]{1,0:T(8,128)(2,1)S(1)} %project_queries.1.refs_0_, bf16[256,384]{1,0:T(8,128)(2,1)S(1)} %collective-permute-done.10.refs_1_, ...), custom_call_target="tpu_custom_call" | custom-call | flops 452984832 | bytes 4000000 | tf_op jit(solution)/shard_map/attend/pallas_call | solution.py:292
  55.2 0.1 collective-permute-start.22
  55.4 1.6 %collective-permute-done.20.refs_9_ = bf16[128,768]{1,0:T(8,128)(2,1)S(1)} collective-permute-done((bf16[128,768]{1,0:T(8,128)(2,1)S(1)}, bf16[128,768]{1,0:T(8,128)(2,1)S(1)}, u32[]{:S(2)}, u32[]{:S(2)}) %collective-permute-start.20) | collective-permute-done | bytes 196640 | tf_op jit(solution)/shard_map/ppermute | solution.py:441
  57.0 3.6 %collective-permute-done.19.refs_8_ = bf16[128,768]{1,0:T(8,128)(2,1)S(1)} collective-permute-done((bf16[128,768]{1,0:T(8,128)(2,1)S(1)}, bf16[128,768]{1,0:T(8,128)(2,1)S(1)}, u32[]{:S(2)}, u32[]{:S(2)}) %collective-permute-start.19) | collective-permute-done | bytes 196640 | tf_op jit(solution)/shard_map/ppermute | solution.py:441
  60.6 3.0 %attend.3 = (bf16[288,384]{1,0:T(8,128)(2,1)S(1)}, bf16[288,384]{1,0:T(8,128)(2,1)S(1)}, bf16[288,384]{1,0:T(8,128)(2,1)S(1)}, bf16[288,384]{1,0:T(8,128)(2,1)S(1)}) custom-call(s32[128]{0:T(128)S(1)} %plan.1.table, bf16[256,384]{1,0:T(8,128)(2,1)S(1)} %project_queries.1.refs_0_, bf16[256,384]{1,0:T(8,128)(2,1)S(1)} %collective-permute-done.10.refs_1_, ...), custom_call_target="tpu_custom_call" | custom-call | flops 452984832 | bytes 4000000 | tf_op jit(solution)/shard_map/attend/pallas_call | solution.py:292
  63.6 0.1 collective-permute-start.23
  63.7 0.5 collective-permute-start.15
  64.2 0.1 collective-permute-start.21
  64.3 0.3 merge_shares.4.refs_0_
  64.7 0.5 collective-permute-done.23.refs_2_
  65.2 0.4 merge_shares.5
  65.6 1.9 %collective-permute-start.24 = (bf16[288,384]{1,0:T(8,128)(2,1)S(1)}, bf16[288,384]{1,0:T(8,128)(2,1)S(1)}, u32[]{:S(2)}, u32[]{:S(2)}) collective-permute-start(bf16[288,384]{1,0:T(8,128)(2,1)S(1)} %merge_shares.5), channel_id=1, source_target_pairs={{0,16},{8,24},{16,0},{24,8},{32,48},{40,56},{48,32},{56,40},{64,80... | collective-permute-start | bytes 663560 | tf_op jit(solution)/shard_map/ppermute | solution.py:441
  67.6 0.3 merge_shares.3.refs_0_
  67.9 5.4 %collective-permute-done.24.refs_3_ = bf16[288,384]{1,0:T(8,128)(2,1)S(1)} collective-permute-done((bf16[288,384]{1,0:T(8,128)(2,1)S(1)}, bf16[288,384]{1,0:T(8,128)(2,1)S(1)}, u32[]{:S(2)}, u32[]{:S(2)}) %collective-permute-start.24) | collective-permute-done | bytes 221216 | tf_op jit(solution)/shard_map/ppermute | solution.py:441
  73.3 1.5 %join.1 = (bf16[256,384]{1,0:T(8,128)(2,1)S(1)}, bf16[256,384]{1,0:T(8,128)(2,1)S(1)}, bf16[256,384]{1,0:T(8,128)(2,1)S(1)}) custom-call(s32[2]{0:T(128)S(1)} %pad_add_fusion.ids, bf16[288,384]{1,0:T(8,128)(2,1)S(1)} %merge_shares.3.refs_0_, bf16[288,384]{1,0:T(8,128)(2,1)S(1)} %get-tuple-element.48.refs_1_, ...), custom_call_target="tpu_custom_call" | custom-call | flops 150994944 | bytes 3000000 | tf_op jit(solution)/shard_map/join/pallas_call | solution.py:325
  74.8 1.9 %collective-permute-start.28 = (bf16[256,384]{1,0:T(8,128)(2,1)S(1)}, bf16[256,384]{1,0:T(8,128)(2,1)S(1)}, u32[]{:S(2)}, u32[]{:S(2)}) collective-permute-start(bf16[256,384]{1,0:T(8,128)(2,1)S(1)} %get-tuple-element.60), channel_id=1, source_target_pairs={{0,2},{1,3},{2,0},{3,1},{4,6},{5,7},{6,4},{7,5},{8,10},{9,11},{10,... | collective-permute-start | bytes 589832 | tf_op jit(solution)/shard_map/ppermute | solution.py:437
  76.7 0.9 collective-permute-start.30
  77.6 1.4 %direct_terms.1 = (bf16[256,384]{1,0:T(8,128)(2,1)S(1)}, bf16[256,384]{1,0:T(8,128)(2,1)S(1)}, bf16[256,384]{1,0:T(8,128)(2,1)S(1)}, bf16[256,384]{1,0:T(8,128)(...) custom-call(s32[2]{0:T(128)S(1)} %pad_add_fusion.ids, ...), custom_call_target="tpu_custom_call" | custom-call | flops 452984832 | bytes 4000000 | tf_op jit(solution)/shard_map/direct_terms/pallas_call | solution.py:345
  79.0 2.0 %collective-permute-start.25 = (bf16[256,384]{1,0:T(8,128)(2,1)S(1)}, bf16[256,384]{1,0:T(8,128)(2,1)S(1)}, u32[]{:S(2)}, u32[]{:S(2)}) collective-permute-start(bf16[256,384]{1,0:T(8,128)(2,1)S(1)} %get-tuple-element.56), channel_id=1, source_target_pairs={{0,1},{1,0},{2,3},{3,2},{4,5},{5,4},{6,7},{7,6},{8,9},{9,8},{10,11... | collective-permute-start | bytes 589832 | tf_op jit(solution)/shard_map/ppermute | solution.py:437
  81.0 0.6 collective-permute-start.26
  81.6 2.8 %collective-permute-start.27 = (bf16[256,384]{1,0:T(8,128)(2,1)S(1)}, bf16[256,384]{1,0:T(8,128)(2,1)S(1)}, u32[]{:S(2)}, u32[]{:S(2)}) collective-permute-start(bf16[256,384]{1,0:T(8,128)(2,1)S(1)} %get-tuple-element.58), channel_id=1, source_target_pairs={{0,7},{1,6},{2,5},{3,4},{4,3},{5,2},{6,1},{7,0},{8,15},{9,14},{10,... | collective-permute-start | bytes 589832 | tf_op jit(solution)/shard_map/ppermute | solution.py:437
  84.4 0.1 add_convert_fusion.1
  84.5 1.0 collective-permute-start.29
  85.4 0.1 add_convert_fusion
  85.5 2.8 %collective-permute-start.31 = (bf16[256,384]{1,0:T(8,128)(2,1)S(1)}, bf16[256,384]{1,0:T(8,128)(2,1)S(1)}, u32[]{:S(2)}, u32[]{:S(2)}) collective-permute-start(bf16[256,384]{1,0:T(8,128)(2,1)S(1)} %add_convert_fusion), channel_id=1, source_target_pairs={{0,3},{1,2},{2,1},{3,0},{4,7},{5,6},{6,5},{7,4},{8,11},{9,10},{10,... | collective-permute-start | bytes 589832 | tf_op jit(solution)/shard_map/ppermute | solution.py:437
  88.3 5.7 %collective-permute-done.27.refs_3_ = bf16[256,384]{1,0:T(8,128)(2,1)S(1)} collective-permute-done((bf16[256,384]{1,0:T(8,128)(2,1)S(1)}, bf16[256,384]{1,0:T(8,128)(2,1)S(1)}, u32[]{:S(2)}, u32[]{:S(2)}) %collective-permute-start.27) | collective-permute-done | bytes 196640 | tf_op jit(solution)/shard_map/ppermute | solution.py:437
  94.0 0.8 collective-permute-done.29.refs_4_
  94.8 0.4 collective-permute-done.31.refs_5_
  95.2 0.8 add_terms.1
  96.1 3.0 %collective-permute-start.32 = (bf16[128,384]{1,0:T(8,128)(2,1)S(1)}, bf16[128,384]{1,0:T(8,128)(2,1)S(1)}, u32[]{:S(2)}, u32[]{:S(2)}) collective-permute-start(bf16[128,384]{1,0:T(8,128)(2,1)S(1)} %get-tuple-element.64), channel_id=1, source_target_pairs={{0,64},{8,72},{16,80},{24,88},{32,96},{40,104},{48,112},{56,120},{... | collective-permute-start | bytes 294920 | tf_op jit(solution)/shard_map/ppermute | solution.py:441
  99.1 2.6 %collective-permute-done.32.got_ref = bf16[128,384]{1,0:T(8,128)(2,1)S(1)} collective-permute-done((bf16[128,384]{1,0:T(8,128)(2,1)S(1)}, bf16[128,384]{1,0:T(8,128)(2,1)S(1)}, u32[]{:S(2)}, u32[]{:S(2)}) %collective-permute-start.32) | collective-permute-done | bytes 98336 | tf_op jit(solution)/shard_map/ppermute | solution.py:441
  101.7 0.7 order.1
  102.4 25.1 %all_to_all.5 = bf16[32,16,384]{2,1,0:T(8,128)(2,1)S(1)} all-to-all(bf16[32,16,384]{2,1,0:T(8,128)(2,1)S(1)} %bitcast.11), channel_id=1, replica_groups=mesh['seq'=32,'head'=8] {'seq'}, dimensions={0} | all-to-all | bytes 786432 | tf_op jit(solution)/shard_map/all_to_all | solution.py:500
  127.5 1.2 to_tile.1
  (35 shorter events, 0.1 us)
Async XLA Ops:
  0.0 9.6 %collective-permute-start.2 = (bf16[32,3072]{1,0:T(8,128)(2,1)}, bf16[32,3072]{1,0:T(8,128)(2,1)S(1)}, u32[]{:S(2)}, u32[]{:S(2)}) collective-permute-start(bf16[32,3072]{1,0:T(8,128)(2,1)} %bitcast.13), channel_id=1, source_target_pairs={{0,3},{1,2},{2,1},{3,0},{4,7},{5,6},{6,5},{7,4},{8,11},{9,10},{10,... | collective-permute-start | bytes 589832 | tf_op jit(solution)/shard_map/ppermute | solution.py:437
  3.1 10.2 %collective-permute-start = (bf16[32,3072]{1,0:T(8,128)(2,1)}, bf16[32,3072]{1,0:T(8,128)(2,1)S(1)}, u32[]{:S(2)}, u32[]{:S(2)}) collective-permute-start(bf16[32,3072]{1,0:T(8,128)(2,1)} %bitcast.14), channel_id=1, source_target_pairs={{0,6},{1,7},{2,4},{3,5},{4,2},{5,3},{6,0},{7,1},{8,14},{9,15},{10,... | collective-permute-start | bytes 589832 | tf_op jit(solution)/shard_map/ppermute | solution.py:437
  5.3 13.0 %collective-permute-start.6 = (bf16[32,3072]{1,0:T(8,128)(2,1)}, bf16[32,3072]{1,0:T(8,128)(2,1)S(1)}, u32[]{:S(2)}, u32[]{:S(2)}) collective-permute-start(bf16[32,3072]{1,0:T(8,128)(2,1)} %bitcast.15), channel_id=1, source_target_pairs={{0,2},{1,3},{2,0},{3,1},{4,6},{5,7},{6,4},{7,5},{8,10},{9,11},{10,... | collective-permute-start | bytes 589832 | tf_op jit(solution)/shard_map/ppermute | solution.py:437
  6.0 12.3 %collective-permute-start.5 = (bf16[32,3072]{1,0:T(8,128)(2,1)}, bf16[32,3072]{1,0:T(8,128)(2,1)S(1)}, u32[]{:S(2)}, u32[]{:S(2)}) collective-permute-start(bf16[32,3072]{1,0:T(8,128)(2,1)} %bitcast.16), channel_id=1, source_target_pairs={{0,1},{1,0},{2,3},{3,2},{4,5},{5,4},{6,7},{7,6},{8,9},{9,8},{10,11... | collective-permute-start | bytes 589832 | tf_op jit(solution)/shard_map/ppermute | solution.py:437
  7.4 18.3 %collective-permute-start.4 = (bf16[32,3072]{1,0:T(8,128)(2,1)}, bf16[32,3072]{1,0:T(8,128)(2,1)S(1)}, u32[]{:S(2)}, u32[]{:S(2)}) collective-permute-start(bf16[32,3072]{1,0:T(8,128)(2,1)} %bitcast.17), channel_id=1, source_target_pairs={{0,7},{1,6},{2,5},{3,4},{4,3},{5,2},{6,1},{7,0},{8,15},{9,14},{10,... | collective-permute-start | bytes 589832 | tf_op jit(solution)/shard_map/ppermute | solution.py:437
  9.6 16.2 %collective-permute-start.3 = (bf16[32,3072]{1,0:T(8,128)(2,1)S(1)}, bf16[32,3072]{1,0:T(8,128)(2,1)S(1)}, u32[]{:S(2)}, u32[]{:S(2)}) collective-permute-start(bf16[32,3072]{1,0:T(8,128)(2,1)S(1)} %collective-permute-done.2.refs_3_), channel_id=1, source_target_pairs={{0,6},{1,7},{2,4},{3,5},{4,2},{5,3},{6,0},{7,1},{8,14},{9,15},{10,... | collective-permute-start | bytes 589832 | tf_op jit(solution)/shard_map/ppermute | solution.py:437
  13.4 12.4 %collective-permute-start.1 = (bf16[32,3072]{1,0:T(8,128)(2,1)S(1)}, bf16[32,3072]{1,0:T(8,128)(2,1)S(1)}, u32[]{:S(2)}, u32[]{:S(2)}) collective-permute-start(bf16[32,3072]{1,0:T(8,128)(2,1)S(1)} %collective-permute-done.refs_2_.refs_6_), channel_id=1, source_target_pairs={{0,2},{1,3},{2,0},{3,1},{4,6},{5,7},{6,4},{7,5},{8,10},{9,11},{10,... | collective-permute-start | bytes 589832 | tf_op jit(solution)/shard_map/ppermute | solution.py:437
  13.6 3.0 %copy-start.1 = (bf16[3072,3,384]{2,0,1:T(8,128)(2,1)S(1)}, bf16[3072,3,384]{2,0,1:T(8,128)(2,1)}, u32[]{:S(2)}) copy-start(bf16[3072,3,384]{2,0,1:T(8,128)(2,1)} %param.8) | copy-start | bytes 21233668
  16.6 1.7 %copy-start.2 = (bf16[4,1,8,3072]{3,2,1,0:T(8,128)(2,1)S(1)}, bf16[4,1,8,3072]{3,2,1,0:T(8,128)(2,1)}, u32[]{:S(2)}) copy-start(bf16[4,1,8,3072]{3,2,1,0:T(8,128)(2,1)} %param.7) | copy-start | bytes 589828
  16.6 1.7 %copy-start.4 = (f32[128]{0:T(128)S(1)}, f32[128]{0:T(128)}, u32[]{:S(2)}) copy-start(f32[128]{0:T(128)} %param.10) | copy-start | bytes 1540
  18.2 7.6 %copy-start.5 = (f32[128]{0:T(128)S(1)}, f32[128]{0:T(128)}, u32[]{:S(2)}) copy-start(f32[128]{0:T(128)} %param.9) | copy-start | bytes 1540
  19.9 10.3 %collective-permute-start.14 = (bf16[128,768]{1,0:T(8,128)(2,1)S(1)}, bf16[128,768]{1,0:T(8,128)(2,1)S(1)}, u32[]{:S(2)}, u32[]{:S(2)}) collective-permute-start(bf16[128,768]{1,0:T(8,128)(2,1)S(1)} %project_keys.2.refs_4_), channel_id=1, source_target_pairs={{32,64},{64,32},{40,72},{72,40},{48,80},{80,48},{56,88},{88,56},{9... | collective-permute-start | bytes 589832 | tf_op jit(solution)/shard_map/ppermute | solution.py:453
  20.6 10.1 %collective-permute-start.8 = (bf16[128,768]{1,0:T(8,128)(2,1)S(1)}, bf16[128,768]{1,0:T(8,128)(2,1)S(1)}, u32[]{:S(2)}, u32[]{:S(2)}) collective-permute-start(bf16[128,768]{1,0:T(8,128)(2,1)S(1)} %project_keys.2.refs_4_), channel_id=1, source_target_pairs={{0,32},{8,40},{16,48},{24,56},{32,0},{40,8},{48,16},{56,24},{64,96... | collective-permute-start | bytes 589832 | tf_op jit(solution)/shard_map/ppermute | solution.py:441
  25.8 24.3 %copy-start.3 = (s32[32,9]{0,1:T(8,128)S(1)}, s32[32,9]{0,1:T(8,128)}, u32[]{:S(2)}) copy-start(s32[32,9]{0,1:T(8,128)} %param.12) | copy-start | bytes 3460
  25.8 24.3 %copy-start.6 = (s32[32]{0:T(128)S(1)}, s32[32]{0:T(128)}, u32[]{:S(2)}) copy-start(s32[32]{0:T(128)} %tile_owner.1) | copy-start | bytes 388
  27.5 45.7 %copy-start = (bf16[384,3072]{1,0:T(8,128)(2,1)S(1)}, bf16[384,3072]{1,0:T(8,128)(2,1)}, u32[]{:S(2)}) copy-start(bf16[384,3072]{1,0:T(8,128)(2,1)} %w_ref.1) | copy-start | bytes 7077892
  27.6 5.8 %collective-permute-start.11 = (bf16[256,384]{1,0:T(8,128)(2,1)S(1)}, bf16[256,384]{1,0:T(8,128)(2,1)S(1)}, u32[]{:S(2)}, u32[]{:S(2)}) collective-permute-start(bf16[256,384]{1,0:T(8,128)(2,1)S(1)} %project_queries.1.refs_0_), channel_id=1, source_target_pairs={{0,16},{8,24},{16,0},{24,8},{32,48},{40,56},{48,32},{56,40},{64,80... | collective-permute-start | bytes 589832 | tf_op jit(solution)/shard_map/ppermute | solution.py:441
  29.4 5.8 %collective-permute-start.13 = (bf16[128,768]{1,0:T(8,128)(2,1)S(1)}, bf16[128,768]{1,0:T(8,128)(2,1)S(1)}, u32[]{:S(2)}, u32[]{:S(2)}) collective-permute-start(bf16[128,768]{1,0:T(8,128)(2,1)S(1)} %project_keys.3.refs_5_), channel_id=1, source_target_pairs={{0,32},{8,40},{16,48},{24,56},{32,0},{40,8},{48,16},{56,24},{64,96... | collective-permute-start | bytes 589832 | tf_op jit(solution)/shard_map/ppermute | solution.py:441
  29.6 6.3 %collective-permute-start.7 = (bf16[128,768]{1,0:T(8,128)(2,1)S(1)}, bf16[128,768]{1,0:T(8,128)(2,1)S(1)}, u32[]{:S(2)}, u32[]{:S(2)}) collective-permute-start(bf16[128,768]{1,0:T(8,128)(2,1)S(1)} %project_keys.3.refs_5_), channel_id=1, source_target_pairs={{32,64},{64,32},{40,72},{72,40},{48,80},{80,48},{56,88},{88,56},{9... | collective-permute-start | bytes 589832 | tf_op jit(solution)/shard_map/ppermute | solution.py:453
  30.2 12.6 %collective-permute-start.10 = (bf16[256,384]{1,0:T(8,128)(2,1)S(1)}, bf16[256,384]{1,0:T(8,128)(2,1)S(1)}, u32[]{:S(2)}, u32[]{:S(2)}) collective-permute-start(bf16[256,384]{1,0:T(8,128)(2,1)S(1)} %project_queries.1.refs_0_), channel_id=1, source_target_pairs={{0,8},{8,0},{16,24},{24,16},{32,40},{40,32},{48,56},{56,48},{64,72... | collective-permute-start | bytes 589832 | tf_op jit(solution)/shard_map/ppermute | solution.py:441
  30.7 12.1 %collective-permute-start.9 = (bf16[128,768]{1,0:T(8,128)(2,1)S(1)}, bf16[128,768]{1,0:T(8,128)(2,1)S(1)}, u32[]{:S(2)}, u32[]{:S(2)}) collective-permute-start(bf16[128,768]{1,0:T(8,128)(2,1)S(1)} %collective-permute-done.8.refs_6_), channel_id=1, source_target_pairs={{32,64},{64,32},{40,72},{72,40},{48,80},{80,48},{56,88},{88,56},{9... | collective-permute-start | bytes 589832 | tf_op jit(solution)/shard_map/ppermute | solution.py:453
  33.3 9.6 %collective-permute-start.12 = (bf16[256,384]{1,0:T(8,128)(2,1)S(1)}, bf16[256,384]{1,0:T(8,128)(2,1)S(1)}, u32[]{:S(2)}, u32[]{:S(2)}) collective-permute-start(bf16[256,384]{1,0:T(8,128)(2,1)S(1)} %collective-permute-done.11.refs_2_), channel_id=1, source_target_pairs={{0,8},{8,0},{16,24},{24,16},{32,40},{40,32},{48,56},{56,48},{64,72... | collective-permute-start | bytes 589832 | tf_op jit(solution)/shard_map/ppermute | solution.py:441
  35.2 11.0 %collective-permute-start.16 = (bf16[128,768]{1,0:T(8,128)(2,1)S(1)}, bf16[128,768]{1,0:T(8,128)(2,1)S(1)}, u32[]{:S(2)}, u32[]{:S(2)}) collective-permute-start(bf16[128,768]{1,0:T(8,128)(2,1)S(1)} %collective-permute-done.13.refs_7_), channel_id=1, source_target_pairs={{32,64},{64,32},{40,72},{72,40},{48,80},{80,48},{56,88},{88,56},{9... | collective-permute-start | bytes 589832 | tf_op jit(solution)/shard_map/ppermute | solution.py:453
  35.9 19.5 %collective-permute-start.17 = (bf16[128,768]{1,0:T(8,128)(2,1)S(1)}, bf16[128,768]{1,0:T(8,128)(2,1)S(1)}, u32[]{:S(2)}, u32[]{:S(2)}) collective-permute-start(bf16[128,768]{1,0:T(8,128)(2,1)S(1)} %collective-permute-done.14.refs_8_), channel_id=1, source_target_pairs={{0,32},{8,40},{16,48},{24,56},{32,0},{40,8},{48,16},{56,24},{64,96... | collective-permute-start | bytes 589832 | tf_op jit(solution)/shard_map/ppermute | solution.py:441
  42.9 14.1 %collective-permute-start.18 = (bf16[128,768]{1,0:T(8,128)(2,1)S(1)}, bf16[128,768]{1,0:T(8,128)(2,1)S(1)}, u32[]{:S(2)}, u32[]{:S(2)}) collective-permute-start(bf16[128,768]{1,0:T(8,128)(2,1)S(1)} %collective-permute-done.7.refs_9_), channel_id=1, source_target_pairs={{0,32},{8,40},{16,48},{24,56},{32,0},{40,8},{48,16},{56,24},{64,96... | collective-permute-start | bytes 589832 | tf_op jit(solution)/shard_map/ppermute | solution.py:441
  46.2 10.8 %collective-permute-start.20 = (bf16[128,768]{1,0:T(8,128)(2,1)S(1)}, bf16[128,768]{1,0:T(8,128)(2,1)S(1)}, u32[]{:S(2)}, u32[]{:S(2)}) collective-permute-start(bf16[128,768]{1,0:T(8,128)(2,1)S(1)} %collective-permute-done.16.refs_5_), channel_id=1, source_target_pairs={{0,32},{8,40},{16,48},{24,56},{32,0},{40,8},{48,16},{56,24},{64,96... | collective-permute-start | bytes 589832 | tf_op jit(solution)/shard_map/ppermute | solution.py:441
  50.0 10.6 %collective-permute-start.19 = (bf16[128,768]{1,0:T(8,128)(2,1)S(1)}, bf16[128,768]{1,0:T(8,128)(2,1)S(1)}, u32[]{:S(2)}, u32[]{:S(2)}) collective-permute-start(bf16[128,768]{1,0:T(8,128)(2,1)S(1)} %collective-permute-done.9.refs_4_), channel_id=1, source_target_pairs={{0,32},{8,40},{16,48},{24,56},{32,0},{40,8},{48,16},{56,24},{64,96... | collective-permute-start | bytes 589832 | tf_op jit(solution)/shard_map/ppermute | solution.py:441
  55.2 9.1 %collective-permute-start.22 = (bf16[288,384]{1,0:T(8,128)(2,1)S(1)}, bf16[288,384]{1,0:T(8,128)(2,1)S(1)}, u32[]{:S(2)}, u32[]{:S(2)}) collective-permute-start(bf16[288,384]{1,0:T(8,128)(2,1)S(1)} %get-tuple-element.51), channel_id=1, source_target_pairs={{0,8},{8,0},{16,24},{24,16},{32,40},{40,32},{48,56},{56,48},{64,72... | collective-permute-start | bytes 663560 | tf_op jit(solution)/shard_map/ppermute | solution.py:441
  63.6 1.6 %collective-permute-start.23 = (bf16[288,384]{1,0:T(8,128)(2,1)S(1)}, bf16[288,384]{1,0:T(8,128)(2,1)S(1)}, u32[]{:S(2)}, u32[]{:S(2)}) collective-permute-start(bf16[288,384]{1,0:T(8,128)(2,1)S(1)} %get-tuple-element.53), channel_id=1, source_target_pairs={{0,8},{8,0},{16,24},{24,16},{32,40},{40,32},{48,56},{56,48},{64,72... | collective-permute-start | bytes 663560 | tf_op jit(solution)/shard_map/ppermute | solution.py:441
  63.7 3.8 %collective-permute-start.15 = (bf16[288,384]{1,0:T(8,128)(2,1)S(1)}, bf16[288,384]{1,0:T(8,128)(2,1)S(1)}, u32[]{:S(2)}, u32[]{:S(2)}) collective-permute-start(bf16[288,384]{1,0:T(8,128)(2,1)S(1)} %get-tuple-element.46), channel_id=1, source_target_pairs={{0,8},{8,0},{16,24},{24,16},{32,40},{40,32},{48,56},{56,48},{64,72... | collective-permute-start | bytes 663560 | tf_op jit(solution)/shard_map/ppermute | solution.py:441
  64.2 3.7 %collective-permute-start.21 = (bf16[288,384]{1,0:T(8,128)(2,1)S(1)}, bf16[288,384]{1,0:T(8,128)(2,1)S(1)}, u32[]{:S(2)}, u32[]{:S(2)}) collective-permute-start(bf16[288,384]{1,0:T(8,128)(2,1)S(1)} %get-tuple-element.49), channel_id=1, source_target_pairs={{0,8},{8,0},{16,24},{24,16},{32,40},{40,32},{48,56},{56,48},{64,72... | collective-permute-start | bytes 663560 | tf_op jit(solution)/shard_map/ppermute | solution.py:441
  65.6 7.7 %collective-permute-start.24 = (bf16[288,384]{1,0:T(8,128)(2,1)S(1)}, bf16[288,384]{1,0:T(8,128)(2,1)S(1)}, u32[]{:S(2)}, u32[]{:S(2)}) collective-permute-start(bf16[288,384]{1,0:T(8,128)(2,1)S(1)} %merge_shares.5), channel_id=1, source_target_pairs={{0,16},{8,24},{16,0},{24,8},{32,48},{40,56},{48,32},{56,40},{64,80... | collective-permute-start | bytes 663560 | tf_op jit(solution)/shard_map/ppermute | solution.py:441
  74.8 9.6 %collective-permute-start.28 = (bf16[256,384]{1,0:T(8,128)(2,1)S(1)}, bf16[256,384]{1,0:T(8,128)(2,1)S(1)}, u32[]{:S(2)}, u32[]{:S(2)}) collective-permute-start(bf16[256,384]{1,0:T(8,128)(2,1)S(1)} %get-tuple-element.60), channel_id=1, source_target_pairs={{0,2},{1,3},{2,0},{3,1},{4,6},{5,7},{6,4},{7,5},{8,10},{9,11},{10,... | collective-permute-start | bytes 589832 | tf_op jit(solution)/shard_map/ppermute | solution.py:437
  76.7 8.8 %collective-permute-start.30 = (bf16[256,384]{1,0:T(8,128)(2,1)S(1)}, bf16[256,384]{1,0:T(8,128)(2,1)S(1)}, u32[]{:S(2)}, u32[]{:S(2)}) collective-permute-start(bf16[256,384]{1,0:T(8,128)(2,1)S(1)} %get-tuple-element.62), channel_id=1, source_target_pairs={{0,6},{1,7},{2,4},{3,5},{4,2},{5,3},{6,0},{7,1},{8,14},{9,15},{10,... | collective-permute-start | bytes 589832 | tf_op jit(solution)/shard_map/ppermute | solution.py:437
  79.0 9.4 %collective-permute-start.25 = (bf16[256,384]{1,0:T(8,128)(2,1)S(1)}, bf16[256,384]{1,0:T(8,128)(2,1)S(1)}, u32[]{:S(2)}, u32[]{:S(2)}) collective-permute-start(bf16[256,384]{1,0:T(8,128)(2,1)S(1)} %get-tuple-element.56), channel_id=1, source_target_pairs={{0,1},{1,0},{2,3},{3,2},{4,5},{5,4},{6,7},{7,6},{8,9},{9,8},{10,11... | collective-permute-start | bytes 589832 | tf_op jit(solution)/shard_map/ppermute | solution.py:437
  81.0 7.4 %collective-permute-start.26 = (bf16[256,384]{1,0:T(8,128)(2,1)S(1)}, bf16[256,384]{1,0:T(8,128)(2,1)S(1)}, u32[]{:S(2)}, u32[]{:S(2)}) collective-permute-start(bf16[256,384]{1,0:T(8,128)(2,1)S(1)} %get-tuple-element.57), channel_id=1, source_target_pairs={{0,2},{1,3},{2,0},{3,1},{4,6},{5,7},{6,4},{7,5},{8,10},{9,11},{10,... | collective-permute-start | bytes 589832 | tf_op jit(solution)/shard_map/ppermute | solution.py:437
  81.6 12.5 %collective-permute-start.27 = (bf16[256,384]{1,0:T(8,128)(2,1)S(1)}, bf16[256,384]{1,0:T(8,128)(2,1)S(1)}, u32[]{:S(2)}, u32[]{:S(2)}) collective-permute-start(bf16[256,384]{1,0:T(8,128)(2,1)S(1)} %get-tuple-element.58), channel_id=1, source_target_pairs={{0,7},{1,6},{2,5},{3,4},{4,3},{5,2},{6,1},{7,0},{8,15},{9,14},{10,... | collective-permute-start | bytes 589832 | tf_op jit(solution)/shard_map/ppermute | solution.py:437
  84.5 10.4 %collective-permute-start.29 = (bf16[256,384]{1,0:T(8,128)(2,1)S(1)}, bf16[256,384]{1,0:T(8,128)(2,1)S(1)}, u32[]{:S(2)}, u32[]{:S(2)}) collective-permute-start(bf16[256,384]{1,0:T(8,128)(2,1)S(1)} %add_convert_fusion.1), channel_id=1, source_target_pairs={{0,6},{1,7},{2,4},{3,5},{4,2},{5,3},{6,0},{7,1},{8,14},{9,15},{10,... | collective-permute-start | bytes 589832 | tf_op jit(solution)/shard_map/ppermute | solution.py:437
  85.5 9.7 %collective-permute-start.31 = (bf16[256,384]{1,0:T(8,128)(2,1)S(1)}, bf16[256,384]{1,0:T(8,128)(2,1)S(1)}, u32[]{:S(2)}, u32[]{:S(2)}) collective-permute-start(bf16[256,384]{1,0:T(8,128)(2,1)S(1)} %add_convert_fusion), channel_id=1, source_target_pairs={{0,3},{1,2},{2,1},{3,0},{4,7},{5,6},{6,5},{7,4},{8,11},{9,10},{10,... | collective-permute-start | bytes 589832 | tf_op jit(solution)/shard_map/ppermute | solution.py:437
  96.1 5.6 %collective-permute-start.32 = (bf16[128,384]{1,0:T(8,128)(2,1)S(1)}, bf16[128,384]{1,0:T(8,128)(2,1)S(1)}, u32[]{:S(2)}, u32[]{:S(2)}) collective-permute-start(bf16[128,384]{1,0:T(8,128)(2,1)S(1)} %get-tuple-element.64), channel_id=1, source_target_pairs={{0,64},{8,72},{16,80},{24,88},{32,96},{40,104},{48,112},{56,120},{... | collective-permute-start | bytes 294920 | tf_op jit(solution)/shard_map/ppermute | solution.py:441

commit v6 on v5

--- a/solution.py
+++ b/solution.py
@@ -119,7 +119,7 @@
         out_specs=pl.BlockSpec(memory_space=pltpu.VMEM),
         out_shape=jax.ShapeDtypeStruct(weight.shape, weight.dtype),
         scratch_shapes=[pltpu.SemaphoreType.DMA((3, LOADS))],
-        compiler_params=params(8),
+        compiler_params=params(47),
         cost_estimate=pl.CostEstimate(flops=0, bytes_accessed=7_100_000, transcendentals=0),
         name="load_weight",
     )(weight)

time: 129 us -> 127 us (0.984)
  local copies, waits for them, and re-layouts: 3.04 us -> 0.03 us
  Pallas kernels: 21.4 us -> 23 us
    unnamed x14 -> x12, local copies, waits for them, and re-layouts: 3.04 us -> 0.03 us
    pallas_call x1, Pallas kernels: 1.56 us -> 3.14 us  [load_weight(): pl.pallas_call(load_kernel, in_specs=[pl.BlockSpec(memory_space=pltpu.HBM...]
  transfers between devices with their start and end apart: 33 -> 33, of which waited for: 11 -> 11; matrix products, arithmetic and copies ran while one was open for 0% -> 0% of each run, Pallas kernels for 13% -> 15%
where the time goes in v6:
time: 127 us
  starting transfers between devices  53.9 us (42%)
  blocking collectives  25 us (20%)
  waiting for transfers between devices  24.9 us (20%)
  Pallas kernels  23 us (18%)
    ppermute x15, starting transfers between devices, plane_swap(): lax.ppermute(array, 'seq', [(s, s ^ k) for s in range(PLANE * PLANES)])  25.6 us
    ppermute x14, starting transfers between devices, head_swap(): return lax.ppermute(array, 'head', [(h, h ^ k) for h in range(N_HEAD)])  25.6 us
    all_to_all x1, blocking collectives, local(): lax.all_to_all(sent.reshape(TILES, PAIR, WIDTH), 'seq', split_axis=0, con...  25 us
    ppermute x15, waiting for transfers between devices, plane_swap(): lax.ppermute(array, 'seq', [(s, s ^ k) for s in range(PLANE * PLANES)])  18 us
    ppermute x14, waiting for transfers between devices, head_swap(): return lax.ppermute(array, 'head', [(h, h ^ k) for h in range(N_HEAD)])  6.93 us
    pallas_call x2, Pallas kernels, attend(): pl.pallas_call(functools.partial(attend_kernel, kinds), in_specs=[scalars...  6.02 us
    pallas_call x2, Pallas kernels, project_keys(): pl.pallas_call(functools.partial(keys_kernel, steps), in_specs=[pl.BlockS...  3.16 us
    pallas_call x1, Pallas kernels, load_weight(): pl.pallas_call(load_kernel, in_specs=[pl.BlockSpec(memory_space=pltpu.HBM...  3.14 us
  transfers between devices with their start and end apart: 33, of which 11 were waited for; matrix products, arithmetic and copies ran while one was open for 0% of the time, Pallas kernels for 15%

profile of v6, /device:TPU:2, one launch (start us, length us, event | category | flops | bytes accessed | tf_op | source)
XLA Modules:
  0.0 127.2 jit_solution(14384409171470715367)
XLA Ops:
  0.0 3.1 %collective-permute-start.2 = (bf16[32,3072]{1,0:T(8,128)(2,1)}, bf16[32,3072]{1,0:T(8,128)(2,1)S(1)}, u32[]{:S(2)}, u32[]{:S(2)}) collective-permute-start(bf16[32,3072]{1,0:T(8,128)(2,1)} %bitcast.12), channel_id=1, source_target_pairs={{0,3},{1,2},{2,1},{3,0},{4,7},{5,6},{6,5},{7,4},{8,11},{9,10},{10,... | collective-permute-start | bytes 589832 | tf_op jit(solution)/shard_map/ppermute | solution.py:437
  3.1 2.2 %collective-permute-start = (bf16[32,3072]{1,0:T(8,128)(2,1)}, bf16[32,3072]{1,0:T(8,128)(2,1)S(1)}, u32[]{:S(2)}, u32[]{:S(2)}) collective-permute-start(bf16[32,3072]{1,0:T(8,128)(2,1)} %bitcast.13), channel_id=1, source_target_pairs={{0,6},{1,7},{2,4},{3,5},{4,2},{5,3},{6,0},{7,1},{8,14},{9,15},{10,... | collective-permute-start | bytes 589832 | tf_op jit(solution)/shard_map/ppermute | solution.py:437
  5.3 0.7 collective-permute-start.6
  6.0 1.4 %collective-permute-start.5 = (bf16[32,3072]{1,0:T(8,128)(2,1)}, bf16[32,3072]{1,0:T(8,128)(2,1)S(1)}, u32[]{:S(2)}, u32[]{:S(2)}) collective-permute-start(bf16[32,3072]{1,0:T(8,128)(2,1)} %bitcast.15), channel_id=1, source_target_pairs={{0,1},{1,0},{2,3},{3,2},{4,5},{5,4},{6,7},{7,6},{8,9},{9,8},{10,11... | collective-permute-start | bytes 589832 | tf_op jit(solution)/shard_map/ppermute | solution.py:437
  7.4 2.2 %collective-permute-start.4 = (bf16[32,3072]{1,0:T(8,128)(2,1)}, bf16[32,3072]{1,0:T(8,128)(2,1)S(1)}, u32[]{:S(2)}, u32[]{:S(2)}) collective-permute-start(bf16[32,3072]{1,0:T(8,128)(2,1)} %bitcast.16), channel_id=1, source_target_pairs={{0,7},{1,6},{2,5},{3,4},{4,3},{5,2},{6,1},{7,0},{8,15},{9,14},{10,... | collective-permute-start | bytes 589832 | tf_op jit(solution)/shard_map/ppermute | solution.py:437
  9.6 3.8 %collective-permute-start.3 = (bf16[32,3072]{1,0:T(8,128)(2,1)S(1)}, bf16[32,3072]{1,0:T(8,128)(2,1)S(1)}, u32[]{:S(2)}, u32[]{:S(2)}) collective-permute-start(bf16[32,3072]{1,0:T(8,128)(2,1)S(1)} %collective-permute-done.2.refs_3_), channel_id=1, source_target_pairs={{0,6},{1,7},{2,4},{3,5},{4,2},{5,3},{6,0},{7,1},{8,14},{9,15},{10,... | collective-permute-start | bytes 589832 | tf_op jit(solution)/shard_map/ppermute | solution.py:437
  13.4 0.2 collective-permute-start.1
  13.6 3.1 %load_weight.1.refs_4_.refs_8_ = bf16[3,3072,384]{2,1,0:T(8,128)(2,1)S(1)} custom-call(bf16[3,3072,384]{2,1,0:T(8,128)(2,1)} %bitcast.23), custom_call_target="tpu_custom_call" | custom-call | bytes 7100000 | tf_op jit(solution)/shard_map/load_weight/pallas_call | solution.py:116
  16.8 0.0 copy-start.4
  16.8 0.1 pad_add_fusion.ids
  16.9 1.6 %project_keys.2.refs_4_ = bf16[128,768]{1,0:T(8,128)(2,1)S(1)} custom-call(s32[2]{0:T(128)S(1)} %pad_add_fusion.ids, bf16[32,3072]{1,0:T(8,128)(2,1)S(1)} %bitcast.17, bf16[32,3072]{1,0:T(8,128)(2,1)S(1)} %collective-permute-done.5.refs_1_, bf16[32,3072]{1,0:T(8,128)(2,1)S(1)} %collective-permute-done.6.refs_2_, ...), custom_call_target="tpu_custom_call" | custom-call | flops 603979776 | bytes 6000000 | tf_op jit(solution)/shard_map/project_keys/pallas_call | solution.py:165
  18.5 0.7 collective-permute-start.14
  19.1 5.2 %collective-permute-start.8 = (bf16[128,768]{1,0:T(8,128)(2,1)S(1)}, bf16[128,768]{1,0:T(8,128)(2,1)S(1)}, u32[]{:S(2)}, u32[]{:S(2)}) collective-permute-start(bf16[128,768]{1,0:T(8,128)(2,1)S(1)} %project_keys.2.refs_4_), channel_id=1, source_target_pairs={{0,32},{8,40},{16,48},{24,56},{32,0},{40,8},{48,16},{56,24},{64,96... | collective-permute-start | bytes 589832 | tf_op jit(solution)/shard_map/ppermute | solution.py:441
  24.3 0.0 copy-start.5
  24.3 1.7 %project_queries.1.refs_0_ = bf16[256,384]{1,0:T(8,128)(2,1)S(1)} custom-call(s32[2]{0:T(128)S(1)} %pad_add_fusion.ids, bf16[32,3072]{1,0:T(8,128)(2,1)S(1)} %bitcast.18, bf16[32,3072]{1,0:T(8,128)(2,1)S(1)} %collective-permute-done.5.refs_1_, bf16[32,3072]{1,0:T(8,128)(2,1)S(1)} %collective-permute-done.6.refs_2_, ...), custom_call_target="tpu_custom_call" | custom-call | flops 603979776 | bytes 4000000 | tf_op jit(solution)/shard_map/project_queries/pallas_call | solution.py:138
  26.1 0.3 collective-permute-start.11
  26.4 1.6 %project_keys.3.refs_5_ = bf16[128,768]{1,0:T(8,128)(2,1)S(1)} custom-call(s32[2]{0:T(128)S(1)} %pad_add_fusion.ids, bf16[32,3072]{1,0:T(8,128)(2,1)S(1)} %collective-permute-done.1.refs_0_.refs_4_, bf16[32,3072]{1,0:T(8,128)(2,1)S(1)} %collective-permute-done.3.refs_1_.refs_5_, bf16[32,3072]{1,0:T(8,128)(2,1)S(1)} %collective-permute-done.refs_2_.refs_6_, ...), custom_call_target="tpu_custom_call" | custom-call | flops 603979776 | bytes 6000000 | tf_op jit(solution)/shard_map/project_keys/pallas_call | solution.py:165
  27.9 0.1 collective-permute-start.13
  28.1 0.7 collective-permute-start.7
  28.7 0.1 collective-permute-start.10
  28.8 0.4 collective-permute-done.8.refs_6_
  29.3 0.7 collective-permute-start.9
  29.9 1.9 %collective-permute-done.11.refs_2_ = bf16[256,384]{1,0:T(8,128)(2,1)S(1)} collective-permute-done((bf16[256,384]{1,0:T(8,128)(2,1)S(1)}, bf16[256,384]{1,0:T(8,128)(2,1)S(1)}, u32[]{:S(2)}, u32[]{:S(2)}) %collective-permute-start.11) | collective-permute-done | bytes 196640 | tf_op jit(solution)/shard_map/ppermute | solution.py:441
  31.9 1.8 %collective-permute-done.13.refs_7_ = bf16[128,768]{1,0:T(8,128)(2,1)S(1)} collective-permute-done((bf16[128,768]{1,0:T(8,128)(2,1)S(1)}, bf16[128,768]{1,0:T(8,128)(2,1)S(1)}, u32[]{:S(2)}, u32[]{:S(2)}) %collective-permute-start.13) | collective-permute-done | bytes 196640 | tf_op jit(solution)/shard_map/ppermute | solution.py:441
  33.7 0.7 collective-permute-start.16
  34.4 7.0 %collective-permute-start.17 = (bf16[128,768]{1,0:T(8,128)(2,1)S(1)}, bf16[128,768]{1,0:T(8,128)(2,1)S(1)}, u32[]{:S(2)}, u32[]{:S(2)}) collective-permute-start(bf16[128,768]{1,0:T(8,128)(2,1)S(1)} %collective-permute-done.14.refs_8_), channel_id=1, source_target_pairs={{0,32},{8,40},{16,48},{24,56},{32,0},{40,8},{48,16},{56,24},{64,96... | collective-permute-start | bytes 589832 | tf_op jit(solution)/shard_map/ppermute | solution.py:441
  41.4 3.3 %collective-permute-start.18 = (bf16[128,768]{1,0:T(8,128)(2,1)S(1)}, bf16[128,768]{1,0:T(8,128)(2,1)S(1)}, u32[]{:S(2)}, u32[]{:S(2)}) collective-permute-start(bf16[128,768]{1,0:T(8,128)(2,1)S(1)} %collective-permute-done.7.refs_9_), channel_id=1, source_target_pairs={{0,32},{8,40},{16,48},{24,56},{32,0},{40,8},{48,16},{56,24},{64,96... | collective-permute-start | bytes 589832 | tf_op jit(solution)/shard_map/ppermute | solution.py:441
  44.7 3.8 %collective-permute-start.20 = (bf16[128,768]{1,0:T(8,128)(2,1)S(1)}, bf16[128,768]{1,0:T(8,128)(2,1)S(1)}, u32[]{:S(2)}, u32[]{:S(2)}) collective-permute-start(bf16[128,768]{1,0:T(8,128)(2,1)S(1)} %collective-permute-done.16.refs_5_), channel_id=1, source_target_pairs={{0,32},{8,40},{16,48},{24,56},{32,0},{40,8},{48,16},{56,24},{64,96... | collective-permute-start | bytes 589832 | tf_op jit(solution)/shard_map/ppermute | solution.py:441
  48.5 0.0 collective-permute-start.19
  48.6 2.2 %plan.1.table = s32[128]{0:T(128)S(1)} custom-call(s32[2]{0:T(128)S(1)} %pad_add_fusion.ids, s32[9,32]{1,0:T(8,128)S(1)} %bitcast.19, s32[32]{0:T(128)S(1)} %copy-done.5), custom_call_target="tpu_custom_call" | custom-call | bytes 8000000 | tf_op jit(solution)/shard_map/plan/pallas_call | solution.py:73
  50.7 3.0 %attend.2 = (bf16[288,384]{1,0:T(8,128)(2,1)S(1)}, bf16[288,384]{1,0:T(8,128)(2,1)S(1)}, bf16[288,384]{1,0:T(8,128)(2,1)S(1)}, bf16[288,384]{1,0:T(8,128)(2,1)S(1)}) custom-call(s32[128]{0:T(128)S(1)} %plan.1.table, bf16[256,384]{1,0:T(8,128)(2,1)S(1)} %project_queries.1.refs_0_, bf16[256,384]{1,0:T(8,128)(2,1)S(1)} %collective-permute-done.10.refs_1_, ...), custom_call_target="tpu_custom_call" | custom-call | flops 452984832 | bytes 4000000 | tf_op jit(solution)/shard_map/attend/pallas_call | solution.py:292
  53.8 0.1 collective-permute-start.22
  53.9 1.6 %collective-permute-done.20.refs_9_ = bf16[128,768]{1,0:T(8,128)(2,1)S(1)} collective-permute-done((bf16[128,768]{1,0:T(8,128)(2,1)S(1)}, bf16[128,768]{1,0:T(8,128)(2,1)S(1)}, u32[]{:S(2)}, u32[]{:S(2)}) %collective-permute-start.20) | collective-permute-done | bytes 196640 | tf_op jit(solution)/shard_map/ppermute | solution.py:441
  55.5 3.6 %collective-permute-done.19.refs_8_ = bf16[128,768]{1,0:T(8,128)(2,1)S(1)} collective-permute-done((bf16[128,768]{1,0:T(8,128)(2,1)S(1)}, bf16[128,768]{1,0:T(8,128)(2,1)S(1)}, u32[]{:S(2)}, u32[]{:S(2)}) %collective-permute-start.19) | collective-permute-done | bytes 196640 | tf_op jit(solution)/shard_map/ppermute | solution.py:441
  59.1 3.0 %attend.3 = (bf16[288,384]{1,0:T(8,128)(2,1)S(1)}, bf16[288,384]{1,0:T(8,128)(2,1)S(1)}, bf16[288,384]{1,0:T(8,128)(2,1)S(1)}, bf16[288,384]{1,0:T(8,128)(2,1)S(1)}) custom-call(s32[128]{0:T(128)S(1)} %plan.1.table, bf16[256,384]{1,0:T(8,128)(2,1)S(1)} %project_queries.1.refs_0_, bf16[256,384]{1,0:T(8,128)(2,1)S(1)} %collective-permute-done.10.refs_1_, ...), custom_call_target="tpu_custom_call" | custom-call | flops 452984832 | bytes 4000000 | tf_op jit(solution)/shard_map/attend/pallas_call | solution.py:292
  62.1 0.1 collective-permute-start.23
  62.2 0.5 collective-permute-start.15
  62.7 0.1 collective-permute-start.21
  62.8 0.3 merge_shares.4.refs_0_
  63.2 0.5 collective-permute-done.23.refs_2_
  63.7 0.4 merge_shares.5
  64.1 1.9 %collective-permute-start.24 = (bf16[288,384]{1,0:T(8,128)(2,1)S(1)}, bf16[288,384]{1,0:T(8,128)(2,1)S(1)}, u32[]{:S(2)}, u32[]{:S(2)}) collective-permute-start(bf16[288,384]{1,0:T(8,128)(2,1)S(1)} %merge_shares.5), channel_id=1, source_target_pairs={{0,16},{8,24},{16,0},{24,8},{32,48},{40,56},{48,32},{56,40},{64,80... | collective-permute-start | bytes 663560 | tf_op jit(solution)/shard_map/ppermute | solution.py:441
  66.1 0.3 merge_shares.3.refs_0_
  66.4 5.4 %collective-permute-done.24.refs_3_ = bf16[288,384]{1,0:T(8,128)(2,1)S(1)} collective-permute-done((bf16[288,384]{1,0:T(8,128)(2,1)S(1)}, bf16[288,384]{1,0:T(8,128)(2,1)S(1)}, u32[]{:S(2)}, u32[]{:S(2)}) %collective-permute-start.24) | collective-permute-done | bytes 221216 | tf_op jit(solution)/shard_map/ppermute | solution.py:441
  71.8 1.5 %join.1 = (bf16[256,384]{1,0:T(8,128)(2,1)S(1)}, bf16[256,384]{1,0:T(8,128)(2,1)S(1)}, bf16[256,384]{1,0:T(8,128)(2,1)S(1)}) custom-call(s32[2]{0:T(128)S(1)} %pad_add_fusion.ids, bf16[288,384]{1,0:T(8,128)(2,1)S(1)} %merge_shares.3.refs_0_, bf16[288,384]{1,0:T(8,128)(2,1)S(1)} %get-tuple-element.48.refs_1_, ...), custom_call_target="tpu_custom_call" | custom-call | flops 150994944 | bytes 3000000 | tf_op jit(solution)/shard_map/join/pallas_call | solution.py:325
  73.3 1.9 %collective-permute-start.28 = (bf16[256,384]{1,0:T(8,128)(2,1)S(1)}, bf16[256,384]{1,0:T(8,128)(2,1)S(1)}, u32[]{:S(2)}, u32[]{:S(2)}) collective-permute-start(bf16[256,384]{1,0:T(8,128)(2,1)S(1)} %get-tuple-element.60), channel_id=1, source_target_pairs={{0,2},{1,3},{2,0},{3,1},{4,6},{5,7},{6,4},{7,5},{8,10},{9,11},{10,... | collective-permute-start | bytes 589832 | tf_op jit(solution)/shard_map/ppermute | solution.py:437
  75.2 0.9 collective-permute-start.30
  76.1 1.4 %direct_terms.1 = (bf16[256,384]{1,0:T(8,128)(2,1)S(1)}, bf16[256,384]{1,0:T(8,128)(2,1)S(1)}, bf16[256,384]{1,0:T(8,128)(2,1)S(1)}, bf16[256,384]{1,0:T(8,128)(...) custom-call(s32[2]{0:T(128)S(1)} %pad_add_fusion.ids, ...), custom_call_target="tpu_custom_call" | custom-call | flops 452984832 | bytes 4000000 | tf_op jit(solution)/shard_map/direct_terms/pallas_call | solution.py:345
  77.5 2.0 %collective-permute-start.25 = (bf16[256,384]{1,0:T(8,128)(2,1)S(1)}, bf16[256,384]{1,0:T(8,128)(2,1)S(1)}, u32[]{:S(2)}, u32[]{:S(2)}) collective-permute-start(bf16[256,384]{1,0:T(8,128)(2,1)S(1)} %get-tuple-element.56), channel_id=1, source_target_pairs={{0,1},{1,0},{2,3},{3,2},{4,5},{5,4},{6,7},{7,6},{8,9},{9,8},{10,11... | collective-permute-start | bytes 589832 | tf_op jit(solution)/shard_map/ppermute | solution.py:437
  79.5 0.6 collective-permute-start.26
  80.1 2.8 %collective-permute-start.27 = (bf16[256,384]{1,0:T(8,128)(2,1)S(1)}, bf16[256,384]{1,0:T(8,128)(2,1)S(1)}, u32[]{:S(2)}, u32[]{:S(2)}) collective-permute-start(bf16[256,384]{1,0:T(8,128)(2,1)S(1)} %get-tuple-element.58), channel_id=1, source_target_pairs={{0,7},{1,6},{2,5},{3,4},{4,3},{5,2},{6,1},{7,0},{8,15},{9,14},{10,... | collective-permute-start | bytes 589832 | tf_op jit(solution)/shard_map/ppermute | solution.py:437
  82.9 0.1 add_convert_fusion.1
  83.0 1.0 collective-permute-start.29
  83.9 0.1 add_convert_fusion
  84.0 2.9 %collective-permute-start.31 = (bf16[256,384]{1,0:T(8,128)(2,1)S(1)}, bf16[256,384]{1,0:T(8,128)(2,1)S(1)}, u32[]{:S(2)}, u32[]{:S(2)}) collective-permute-start(bf16[256,384]{1,0:T(8,128)(2,1)S(1)} %add_convert_fusion), channel_id=1, source_target_pairs={{0,3},{1,2},{2,1},{3,0},{4,7},{5,6},{6,5},{7,4},{8,11},{9,10},{10,... | collective-permute-start | bytes 589832 | tf_op jit(solution)/shard_map/ppermute | solution.py:437
  86.8 5.7 %collective-permute-done.27.refs_3_ = bf16[256,384]{1,0:T(8,128)(2,1)S(1)} collective-permute-done((bf16[256,384]{1,0:T(8,128)(2,1)S(1)}, bf16[256,384]{1,0:T(8,128)(2,1)S(1)}, u32[]{:S(2)}, u32[]{:S(2)}) %collective-permute-start.27) | collective-permute-done | bytes 196640 | tf_op jit(solution)/shard_map/ppermute | solution.py:437
  92.6 0.8 collective-permute-done.29.refs_4_
  93.3 0.4 collective-permute-done.31.refs_5_
  93.8 0.8 add_terms.1
  94.6 3.1 %collective-permute-start.32 = (bf16[128,384]{1,0:T(8,128)(2,1)S(1)}, bf16[128,384]{1,0:T(8,128)(2,1)S(1)}, u32[]{:S(2)}, u32[]{:S(2)}) collective-permute-start(bf16[128,384]{1,0:T(8,128)(2,1)S(1)} %get-tuple-element.64), channel_id=1, source_target_pairs={{0,64},{8,72},{16,80},{24,88},{32,96},{40,104},{48,112},{56,120},{... | collective-permute-start | bytes 294920 | tf_op jit(solution)/shard_map/ppermute | solution.py:441
  97.7 2.6 %collective-permute-done.32.got_ref = bf16[128,384]{1,0:T(8,128)(2,1)S(1)} collective-permute-done((bf16[128,384]{1,0:T(8,128)(2,1)S(1)}, bf16[128,384]{1,0:T(8,128)(2,1)S(1)}, u32[]{:S(2)}, u32[]{:S(2)}) %collective-permute-start.32) | collective-permute-done | bytes 98336 | tf_op jit(solution)/shard_map/ppermute | solution.py:441
  100.3 0.7 order.1
  101.0 25.0 %all_to_all.5 = bf16[32,16,384]{2,1,0:T(8,128)(2,1)S(1)} all-to-all(bf16[32,16,384]{2,1,0:T(8,128)(2,1)S(1)} %bitcast.10), channel_id=1, replica_groups=mesh['seq'=32,'head'=8] {'seq'}, dimensions={0} | all-to-all | bytes 786432 | tf_op jit(solution)/shard_map/all_to_all | solution.py:500
  126.0 1.2 to_tile.1
  (33 shorter events, 0.1 us)
Async XLA Ops:
  0.0 9.6 %collective-permute-start.2 = (bf16[32,3072]{1,0:T(8,128)(2,1)}, bf16[32,3072]{1,0:T(8,128)(2,1)S(1)}, u32[]{:S(2)}, u32[]{:S(2)}) collective-permute-start(bf16[32,3072]{1,0:T(8,128)(2,1)} %bitcast.12), channel_id=1, source_target_pairs={{0,3},{1,2},{2,1},{3,0},{4,7},{5,6},{6,5},{7,4},{8,11},{9,10},{10,... | collective-permute-start | bytes 589832 | tf_op jit(solution)/shard_map/ppermute | solution.py:437
  3.1 10.2 %collective-permute-start = (bf16[32,3072]{1,0:T(8,128)(2,1)}, bf16[32,3072]{1,0:T(8,128)(2,1)S(1)}, u32[]{:S(2)}, u32[]{:S(2)}) collective-permute-start(bf16[32,3072]{1,0:T(8,128)(2,1)} %bitcast.13), channel_id=1, source_target_pairs={{0,6},{1,7},{2,4},{3,5},{4,2},{5,3},{6,0},{7,1},{8,14},{9,15},{10,... | collective-permute-start | bytes 589832 | tf_op jit(solution)/shard_map/ppermute | solution.py:437
  5.3 11.5 %collective-permute-start.6 = (bf16[32,3072]{1,0:T(8,128)(2,1)}, bf16[32,3072]{1,0:T(8,128)(2,1)S(1)}, u32[]{:S(2)}, u32[]{:S(2)}) collective-permute-start(bf16[32,3072]{1,0:T(8,128)(2,1)} %bitcast.14), channel_id=1, source_target_pairs={{0,2},{1,3},{2,0},{3,1},{4,6},{5,7},{6,4},{7,5},{8,10},{9,11},{10,... | collective-permute-start | bytes 589832 | tf_op jit(solution)/shard_map/ppermute | solution.py:437
  6.0 10.9 %collective-permute-start.5 = (bf16[32,3072]{1,0:T(8,128)(2,1)}, bf16[32,3072]{1,0:T(8,128)(2,1)S(1)}, u32[]{:S(2)}, u32[]{:S(2)}) collective-permute-start(bf16[32,3072]{1,0:T(8,128)(2,1)} %bitcast.15), channel_id=1, source_target_pairs={{0,1},{1,0},{2,3},{3,2},{4,5},{5,4},{6,7},{7,6},{8,9},{9,8},{10,11... | collective-permute-start | bytes 589832 | tf_op jit(solution)/shard_map/ppermute | solution.py:437
  7.4 16.9 %collective-permute-start.4 = (bf16[32,3072]{1,0:T(8,128)(2,1)}, bf16[32,3072]{1,0:T(8,128)(2,1)S(1)}, u32[]{:S(2)}, u32[]{:S(2)}) collective-permute-start(bf16[32,3072]{1,0:T(8,128)(2,1)} %bitcast.16), channel_id=1, source_target_pairs={{0,7},{1,6},{2,5},{3,4},{4,3},{5,2},{6,1},{7,0},{8,15},{9,14},{10,... | collective-permute-start | bytes 589832 | tf_op jit(solution)/shard_map/ppermute | solution.py:437
  9.6 14.7 %collective-permute-start.3 = (bf16[32,3072]{1,0:T(8,128)(2,1)S(1)}, bf16[32,3072]{1,0:T(8,128)(2,1)S(1)}, u32[]{:S(2)}, u32[]{:S(2)}) collective-permute-start(bf16[32,3072]{1,0:T(8,128)(2,1)S(1)} %collective-permute-done.2.refs_3_), channel_id=1, source_target_pairs={{0,6},{1,7},{2,4},{3,5},{4,2},{5,3},{6,0},{7,1},{8,14},{9,15},{10,... | collective-permute-start | bytes 589832 | tf_op jit(solution)/shard_map/ppermute | solution.py:437
  13.4 10.9 %collective-permute-start.1 = (bf16[32,3072]{1,0:T(8,128)(2,1)S(1)}, bf16[32,3072]{1,0:T(8,128)(2,1)S(1)}, u32[]{:S(2)}, u32[]{:S(2)}) collective-permute-start(bf16[32,3072]{1,0:T(8,128)(2,1)S(1)} %collective-permute-done.refs_2_.refs_6_), channel_id=1, source_target_pairs={{0,2},{1,3},{2,0},{3,1},{4,6},{5,7},{6,4},{7,5},{8,10},{9,11},{10,... | collective-permute-start | bytes 589832 | tf_op jit(solution)/shard_map/ppermute | solution.py:437
  13.6 3.3 %copy-start.1 = (bf16[4,1,8,3072]{3,2,1,0:T(8,128)(2,1)S(1)}, bf16[4,1,8,3072]{3,2,1,0:T(8,128)(2,1)}, u32[]{:S(2)}) copy-start(bf16[4,1,8,3072]{3,2,1,0:T(8,128)(2,1)} %param.7) | copy-start | bytes 589828
  13.6 3.3 %copy-start.3 = (f32[128]{0:T(128)S(1)}, f32[128]{0:T(128)}, u32[]{:S(2)}) copy-start(f32[128]{0:T(128)} %param.10) | copy-start | bytes 1540
  16.8 7.5 %copy-start.4 = (f32[128]{0:T(128)S(1)}, f32[128]{0:T(128)}, u32[]{:S(2)}) copy-start(f32[128]{0:T(128)} %param.9) | copy-start | bytes 1540
  18.5 10.3 %collective-permute-start.14 = (bf16[128,768]{1,0:T(8,128)(2,1)S(1)}, bf16[128,768]{1,0:T(8,128)(2,1)S(1)}, u32[]{:S(2)}, u32[]{:S(2)}) collective-permute-start(bf16[128,768]{1,0:T(8,128)(2,1)S(1)} %project_keys.2.refs_4_), channel_id=1, source_target_pairs={{32,64},{64,32},{40,72},{72,40},{48,80},{80,48},{56,88},{88,56},{9... | collective-permute-start | bytes 589832 | tf_op jit(solution)/shard_map/ppermute | solution.py:453
  19.1 10.1 %collective-permute-start.8 = (bf16[128,768]{1,0:T(8,128)(2,1)S(1)}, bf16[128,768]{1,0:T(8,128)(2,1)S(1)}, u32[]{:S(2)}, u32[]{:S(2)}) collective-permute-start(bf16[128,768]{1,0:T(8,128)(2,1)S(1)} %project_keys.2.refs_4_), channel_id=1, source_target_pairs={{0,32},{8,40},{16,48},{24,56},{32,0},{40,8},{48,16},{56,24},{64,96... | collective-permute-start | bytes 589832 | tf_op jit(solution)/shard_map/ppermute | solution.py:441
  24.3 24.2 %copy-start.2 = (s32[32,9]{0,1:T(8,128)S(1)}, s32[32,9]{0,1:T(8,128)}, u32[]{:S(2)}) copy-start(s32[32,9]{0,1:T(8,128)} %param.12) | copy-start | bytes 3460
  24.3 24.2 %copy-start.5 = (s32[32]{0:T(128)S(1)}, s32[32]{0:T(128)}, u32[]{:S(2)}) copy-start(s32[32]{0:T(128)} %tile_owner.1) | copy-start | bytes 388
  26.1 45.7 %copy-start = (bf16[384,3072]{1,0:T(8,128)(2,1)S(1)}, bf16[384,3072]{1,0:T(8,128)(2,1)}, u32[]{:S(2)}) copy-start(bf16[384,3072]{1,0:T(8,128)(2,1)} %w_ref.1) | copy-start | bytes 7077892
  26.1 5.8 %collective-permute-start.11 = (bf16[256,384]{1,0:T(8,128)(2,1)S(1)}, bf16[256,384]{1,0:T(8,128)(2,1)S(1)}, u32[]{:S(2)}, u32[]{:S(2)}) collective-permute-start(bf16[256,384]{1,0:T(8,128)(2,1)S(1)} %project_queries.1.refs_0_), channel_id=1, source_target_pairs={{0,16},{8,24},{16,0},{24,8},{32,48},{40,56},{48,32},{56,40},{64,80... | collective-permute-start | bytes 589832 | tf_op jit(solution)/shard_map/ppermute | solution.py:441
  27.9 5.8 %collective-permute-start.13 = (bf16[128,768]{1,0:T(8,128)(2,1)S(1)}, bf16[128,768]{1,0:T(8,128)(2,1)S(1)}, u32[]{:S(2)}, u32[]{:S(2)}) collective-permute-start(bf16[128,768]{1,0:T(8,128)(2,1)S(1)} %project_keys.3.refs_5_), channel_id=1, source_target_pairs={{0,32},{8,40},{16,48},{24,56},{32,0},{40,8},{48,16},{56,24},{64,96... | collective-permute-start | bytes 589832 | tf_op jit(solution)/shard_map/ppermute | solution.py:441
  28.1 6.3 %collective-permute-start.7 = (bf16[128,768]{1,0:T(8,128)(2,1)S(1)}, bf16[128,768]{1,0:T(8,128)(2,1)S(1)}, u32[]{:S(2)}, u32[]{:S(2)}) collective-permute-start(bf16[128,768]{1,0:T(8,128)(2,1)S(1)} %project_keys.3.refs_5_), channel_id=1, source_target_pairs={{32,64},{64,32},{40,72},{72,40},{48,80},{80,48},{56,88},{88,56},{9... | collective-permute-start | bytes 589832 | tf_op jit(solution)/shard_map/ppermute | solution.py:453
  28.7 12.6 %collective-permute-start.10 = (bf16[256,384]{1,0:T(8,128)(2,1)S(1)}, bf16[256,384]{1,0:T(8,128)(2,1)S(1)}, u32[]{:S(2)}, u32[]{:S(2)}) collective-permute-start(bf16[256,384]{1,0:T(8,128)(2,1)S(1)} %project_queries.1.refs_0_), channel_id=1, source_target_pairs={{0,8},{8,0},{16,24},{24,16},{32,40},{40,32},{48,56},{56,48},{64,72... | collective-permute-start | bytes 589832 | tf_op jit(solution)/shard_map/ppermute | solution.py:441
  29.3 12.1 %collective-permute-start.9 = (bf16[128,768]{1,0:T(8,128)(2,1)S(1)}, bf16[128,768]{1,0:T(8,128)(2,1)S(1)}, u32[]{:S(2)}, u32[]{:S(2)}) collective-permute-start(bf16[128,768]{1,0:T(8,128)(2,1)S(1)} %collective-permute-done.8.refs_6_), channel_id=1, source_target_pairs={{32,64},{64,32},{40,72},{72,40},{48,80},{80,48},{56,88},{88,56},{9... | collective-permute-start | bytes 589832 | tf_op jit(solution)/shard_map/ppermute | solution.py:453
  31.9 9.5 %collective-permute-start.12 = (bf16[256,384]{1,0:T(8,128)(2,1)S(1)}, bf16[256,384]{1,0:T(8,128)(2,1)S(1)}, u32[]{:S(2)}, u32[]{:S(2)}) collective-permute-start(bf16[256,384]{1,0:T(8,128)(2,1)S(1)} %collective-permute-done.11.refs_2_), channel_id=1, source_target_pairs={{0,8},{8,0},{16,24},{24,16},{32,40},{40,32},{48,56},{56,48},{64,72... | collective-permute-start | bytes 589832 | tf_op jit(solution)/shard_map/ppermute | solution.py:441
  33.7 11.0 %collective-permute-start.16 = (bf16[128,768]{1,0:T(8,128)(2,1)S(1)}, bf16[128,768]{1,0:T(8,128)(2,1)S(1)}, u32[]{:S(2)}, u32[]{:S(2)}) collective-permute-start(bf16[128,768]{1,0:T(8,128)(2,1)S(1)} %collective-permute-done.13.refs_7_), channel_id=1, source_target_pairs={{32,64},{64,32},{40,72},{72,40},{48,80},{80,48},{56,88},{88,56},{9... | collective-permute-start | bytes 589832 | tf_op jit(solution)/shard_map/ppermute | solution.py:453
  34.4 19.5 %collective-permute-start.17 = (bf16[128,768]{1,0:T(8,128)(2,1)S(1)}, bf16[128,768]{1,0:T(8,128)(2,1)S(1)}, u32[]{:S(2)}, u32[]{:S(2)}) collective-permute-start(bf16[128,768]{1,0:T(8,128)(2,1)S(1)} %collective-permute-done.14.refs_8_), channel_id=1, source_target_pairs={{0,32},{8,40},{16,48},{24,56},{32,0},{40,8},{48,16},{56,24},{64,96... | collective-permute-start | bytes 589832 | tf_op jit(solution)/shard_map/ppermute | solution.py:441
  41.4 14.1 %collective-permute-start.18 = (bf16[128,768]{1,0:T(8,128)(2,1)S(1)}, bf16[128,768]{1,0:T(8,128)(2,1)S(1)}, u32[]{:S(2)}, u32[]{:S(2)}) collective-permute-start(bf16[128,768]{1,0:T(8,128)(2,1)S(1)} %collective-permute-done.7.refs_9_), channel_id=1, source_target_pairs={{0,32},{8,40},{16,48},{24,56},{32,0},{40,8},{48,16},{56,24},{64,96... | collective-permute-start | bytes 589832 | tf_op jit(solution)/shard_map/ppermute | solution.py:441
  44.7 10.8 %collective-permute-start.20 = (bf16[128,768]{1,0:T(8,128)(2,1)S(1)}, bf16[128,768]{1,0:T(8,128)(2,1)S(1)}, u32[]{:S(2)}, u32[]{:S(2)}) collective-permute-start(bf16[128,768]{1,0:T(8,128)(2,1)S(1)} %collective-permute-done.16.refs_5_), channel_id=1, source_target_pairs={{0,32},{8,40},{16,48},{24,56},{32,0},{40,8},{48,16},{56,24},{64,96... | collective-permute-start | bytes 589832 | tf_op jit(solution)/shard_map/ppermute | solution.py:441
  48.5 10.6 %collective-permute-start.19 = (bf16[128,768]{1,0:T(8,128)(2,1)S(1)}, bf16[128,768]{1,0:T(8,128)(2,1)S(1)}, u32[]{:S(2)}, u32[]{:S(2)}) collective-permute-start(bf16[128,768]{1,0:T(8,128)(2,1)S(1)} %collective-permute-done.9.refs_4_), channel_id=1, source_target_pairs={{0,32},{8,40},{16,48},{24,56},{32,0},{40,8},{48,16},{56,24},{64,96... | collective-permute-start | bytes 589832 | tf_op jit(solution)/shard_map/ppermute | solution.py:441
  53.8 9.1 %collective-permute-start.22 = (bf16[288,384]{1,0:T(8,128)(2,1)S(1)}, bf16[288,384]{1,0:T(8,128)(2,1)S(1)}, u32[]{:S(2)}, u32[]{:S(2)}) collective-permute-start(bf16[288,384]{1,0:T(8,128)(2,1)S(1)} %get-tuple-element.51), channel_id=1, source_target_pairs={{0,8},{8,0},{16,24},{24,16},{32,40},{40,32},{48,56},{56,48},{64,72... | collective-permute-start | bytes 663560 | tf_op jit(solution)/shard_map/ppermute | solution.py:441
  62.1 1.6 %collective-permute-start.23 = (bf16[288,384]{1,0:T(8,128)(2,1)S(1)}, bf16[288,384]{1,0:T(8,128)(2,1)S(1)}, u32[]{:S(2)}, u32[]{:S(2)}) collective-permute-start(bf16[288,384]{1,0:T(8,128)(2,1)S(1)} %get-tuple-element.53), channel_id=1, source_target_pairs={{0,8},{8,0},{16,24},{24,16},{32,40},{40,32},{48,56},{56,48},{64,72... | collective-permute-start | bytes 663560 | tf_op jit(solution)/shard_map/ppermute | solution.py:441
  62.2 3.8 %collective-permute-start.15 = (bf16[288,384]{1,0:T(8,128)(2,1)S(1)}, bf16[288,384]{1,0:T(8,128)(2,1)S(1)}, u32[]{:S(2)}, u32[]{:S(2)}) collective-permute-start(bf16[288,384]{1,0:T(8,128)(2,1)S(1)} %get-tuple-element.46), channel_id=1, source_target_pairs={{0,8},{8,0},{16,24},{24,16},{32,40},{40,32},{48,56},{56,48},{64,72... | collective-permute-start | bytes 663560 | tf_op jit(solution)/shard_map/ppermute | solution.py:441
  62.7 3.7 %collective-permute-start.21 = (bf16[288,384]{1,0:T(8,128)(2,1)S(1)}, bf16[288,384]{1,0:T(8,128)(2,1)S(1)}, u32[]{:S(2)}, u32[]{:S(2)}) collective-permute-start(bf16[288,384]{1,0:T(8,128)(2,1)S(1)} %get-tuple-element.49), channel_id=1, source_target_pairs={{0,8},{8,0},{16,24},{24,16},{32,40},{40,32},{48,56},{56,48},{64,72... | collective-permute-start | bytes 663560 | tf_op jit(solution)/shard_map/ppermute | solution.py:441
  64.1 7.7 %collective-permute-start.24 = (bf16[288,384]{1,0:T(8,128)(2,1)S(1)}, bf16[288,384]{1,0:T(8,128)(2,1)S(1)}, u32[]{:S(2)}, u32[]{:S(2)}) collective-permute-start(bf16[288,384]{1,0:T(8,128)(2,1)S(1)} %merge_shares.5), channel_id=1, source_target_pairs={{0,16},{8,24},{16,0},{24,8},{32,48},{40,56},{48,32},{56,40},{64,80... | collective-permute-start | bytes 663560 | tf_op jit(solution)/shard_map/ppermute | solution.py:441
  73.3 9.6 %collective-permute-start.28 = (bf16[256,384]{1,0:T(8,128)(2,1)S(1)}, bf16[256,384]{1,0:T(8,128)(2,1)S(1)}, u32[]{:S(2)}, u32[]{:S(2)}) collective-permute-start(bf16[256,384]{1,0:T(8,128)(2,1)S(1)} %get-tuple-element.60), channel_id=1, source_target_pairs={{0,2},{1,3},{2,0},{3,1},{4,6},{5,7},{6,4},{7,5},{8,10},{9,11},{10,... | collective-permute-start | bytes 589832 | tf_op jit(solution)/shard_map/ppermute | solution.py:437
  75.2 8.7 %collective-permute-start.30 = (bf16[256,384]{1,0:T(8,128)(2,1)S(1)}, bf16[256,384]{1,0:T(8,128)(2,1)S(1)}, u32[]{:S(2)}, u32[]{:S(2)}) collective-permute-start(bf16[256,384]{1,0:T(8,128)(2,1)S(1)} %get-tuple-element.62), channel_id=1, source_target_pairs={{0,6},{1,7},{2,4},{3,5},{4,2},{5,3},{6,0},{7,1},{8,14},{9,15},{10,... | collective-permute-start | bytes 589832 | tf_op jit(solution)/shard_map/ppermute | solution.py:437
  77.5 9.4 %collective-permute-start.25 = (bf16[256,384]{1,0:T(8,128)(2,1)S(1)}, bf16[256,384]{1,0:T(8,128)(2,1)S(1)}, u32[]{:S(2)}, u32[]{:S(2)}) collective-permute-start(bf16[256,384]{1,0:T(8,128)(2,1)S(1)} %get-tuple-element.56), channel_id=1, source_target_pairs={{0,1},{1,0},{2,3},{3,2},{4,5},{5,4},{6,7},{7,6},{8,9},{9,8},{10,11... | collective-permute-start | bytes 589832 | tf_op jit(solution)/shard_map/ppermute | solution.py:437
  79.5 7.4 %collective-permute-start.26 = (bf16[256,384]{1,0:T(8,128)(2,1)S(1)}, bf16[256,384]{1,0:T(8,128)(2,1)S(1)}, u32[]{:S(2)}, u32[]{:S(2)}) collective-permute-start(bf16[256,384]{1,0:T(8,128)(2,1)S(1)} %get-tuple-element.57), channel_id=1, source_target_pairs={{0,2},{1,3},{2,0},{3,1},{4,6},{5,7},{6,4},{7,5},{8,10},{9,11},{10,... | collective-permute-start | bytes 589832 | tf_op jit(solution)/shard_map/ppermute | solution.py:437
  80.1 12.5 %collective-permute-start.27 = (bf16[256,384]{1,0:T(8,128)(2,1)S(1)}, bf16[256,384]{1,0:T(8,128)(2,1)S(1)}, u32[]{:S(2)}, u32[]{:S(2)}) collective-permute-start(bf16[256,384]{1,0:T(8,128)(2,1)S(1)} %get-tuple-element.58), channel_id=1, source_target_pairs={{0,7},{1,6},{2,5},{3,4},{4,3},{5,2},{6,1},{7,0},{8,15},{9,14},{10,... | collective-permute-start | bytes 589832 | tf_op jit(solution)/shard_map/ppermute | solution.py:437
  83.0 10.4 %collective-permute-start.29 = (bf16[256,384]{1,0:T(8,128)(2,1)S(1)}, bf16[256,384]{1,0:T(8,128)(2,1)S(1)}, u32[]{:S(2)}, u32[]{:S(2)}) collective-permute-start(bf16[256,384]{1,0:T(8,128)(2,1)S(1)} %add_convert_fusion.1), channel_id=1, source_target_pairs={{0,6},{1,7},{2,4},{3,5},{4,2},{5,3},{6,0},{7,1},{8,14},{9,15},{10,... | collective-permute-start | bytes 589832 | tf_op jit(solution)/shard_map/ppermute | solution.py:437
  84.0 9.8 %collective-permute-start.31 = (bf16[256,384]{1,0:T(8,128)(2,1)S(1)}, bf16[256,384]{1,0:T(8,128)(2,1)S(1)}, u32[]{:S(2)}, u32[]{:S(2)}) collective-permute-start(bf16[256,384]{1,0:T(8,128)(2,1)S(1)} %add_convert_fusion), channel_id=1, source_target_pairs={{0,3},{1,2},{2,1},{3,0},{4,7},{5,6},{6,5},{7,4},{8,11},{9,10},{10,... | collective-permute-start | bytes 589832 | tf_op jit(solution)/shard_map/ppermute | solution.py:437
  94.6 5.7 %collective-permute-start.32 = (bf16[128,384]{1,0:T(8,128)(2,1)S(1)}, bf16[128,384]{1,0:T(8,128)(2,1)S(1)}, u32[]{:S(2)}, u32[]{:S(2)}) collective-permute-start(bf16[128,384]{1,0:T(8,128)(2,1)S(1)} %get-tuple-element.64), channel_id=1, source_target_pairs={{0,64},{8,72},{16,80},{24,88},{32,96},{40,104},{48,112},{56,120},{... | collective-permute-start | bytes 294920 | tf_op jit(solution)/shard_map/ppermute | solution.py:441

commit v7 on v6

--- a/solution.py
+++ b/solution.py
@@ -97,14 +97,14 @@
         rows[pl.ds(start, PIECE), :] = piece[...]
 
 
-def load_kernel(w_ref, out_ref, sems):
+def load_kernel(parts, w_ref, out_ref, sems):
     rows = D // LOADS
     copies = []
-    for n in range(3):
+    for n, part in enumerate(parts):
         for e in range(LOADS):
-            part = pl.ds(e * rows, rows)
+            some = pl.ds(e * rows, rows)
             copies.append(
-                pltpu.make_async_copy(w_ref.at[n, part], out_ref.at[n, part], sems.at[n, e])
+                pltpu.make_async_copy(w_ref.at[part, some], out_ref.at[n, some], sems.at[n, e])
             )
     for copy in copies:
         copy.start()
@@ -112,15 +112,17 @@
         copy.wait()
 
 
-def load_weight(weight):
-    return pl.pallas_call(
-        load_kernel,
+def load_weight(weight, parts, mib):
+    return pl.pallas_call(
+        functools.partial(load_kernel, parts),
         in_specs=[pl.BlockSpec(memory_space=pltpu.HBM)],
         out_specs=pl.BlockSpec(memory_space=pltpu.VMEM),
-        out_shape=jax.ShapeDtypeStruct(weight.shape, weight.dtype),
-        scratch_shapes=[pltpu.SemaphoreType.DMA((3, LOADS))],
-        compiler_params=params(47),
-        cost_estimate=pl.CostEstimate(flops=0, bytes_accessed=7_100_000, transcendentals=0),
+        out_shape=jax.ShapeDtypeStruct((len(parts),) + weight.shape[1:], weight.dtype),
+        scratch_shapes=[pltpu.SemaphoreType.DMA((len(parts), LOADS))],
+        compiler_params=params(mib),
+        cost_estimate=pl.CostEstimate(
+            flops=0, bytes_accessed=2_400_000 * len(parts), transcendentals=0
+        ),
         name="load_weight",
     )(weight)
 
@@ -153,9 +155,9 @@
     pieces, (w_ref, gain_ref, out_ref, rows_ref) = refs[:HALF], refs[HALF:]
     gather_rows(ids, steps, pieces, rows_ref)
     rows = rows_ref[...]
-    keys = jnp.dot(rows, w_ref[1], preferred_element_type=jnp.float32)
+    keys = jnp.dot(rows, w_ref[0], preferred_element_type=jnp.float32)
     out_ref[:, :WIDTH] = normed(keys, gain_ref[...])
-    values = jnp.dot(rows, w_ref[2], preferred_element_type=jnp.float32)
+    values = jnp.dot(rows, w_ref[1], preferred_element_type=jnp.float32)
     out_ref[:, WIDTH:] = values.astype(jnp.bfloat16)
 
 
@@ -455,7 +457,8 @@
 
 def local(latent, w_qkv, q_gain, k_gain, w_out, neighbours, tile_owner):
     ids = jnp.stack([lax.axis_index("seq"), lax.axis_index("head")]).astype(jnp.int32)
-    weight = load_weight(jnp.transpose(w_qkv, (1, 0, 2)))
+    weight = jnp.transpose(w_qkv, (1, 0, 2))
+    kv_weight = load_weight(weight, (1, 2), 50)
     q_gain, k_gain = q_gain.reshape(1, HEAD_DIM), k_gain.reshape(1, HEAD_DIM)
     table = plan(ids, neighbours.T, tile_owner)
 
@@ -464,14 +467,14 @@
         pieces[k] = head_swap(pieces[0], k)
     pieces[4], pieces[5] = head_swap(pieces[6], 2), head_swap(pieces[3], 6)
 
-    own_a = project_keys(range(HALF), ids, pieces[:HALF], weight, k_gain)
+    own_a = project_keys(range(HALF), ids, pieces[:HALF], kv_weight, k_gain)
     mate_a, edge_a = mate_swap(own_a), edge_swap(own_a)
     pieces_b, _own = lax.optimization_barrier((pieces[HALF:], own_a))
-    own_b = project_keys(range(HALF, N_HEAD), ids, pieces_b, weight, k_gain)
+    own_b = project_keys(range(HALF, N_HEAD), ids, pieces_b, kv_weight, k_gain)
     mate_b, edge_b = mate_swap(own_b), edge_swap(own_b)
     edge_2a, far_1a = edge_swap(mate_a), mate_swap(edge_a)
 
-    queries = project_queries(ids, [*pieces[:HALF], *pieces_b], weight, q_gain)
+    queries = project_queries(ids, [*pieces[:HALF], *pieces_b], load_weight(weight, (0,), 49), q_gain)
     q_chip = plane_swap(queries, 2)
     all_queries = [queries, plane_swap(queries, 1), q_chip, plane_swap(q_chip, 1)]
 

time: 127 us -> 143 us (1.13)
  waiting for transfers between devices: 24.9 us -> 33 us
  Pallas kernels: 23 us -> 28 us
  local copies, waits for them, and re-layouts: 0.03 us -> 2.38 us
  blocking collectives: 25 us -> 23.1 us
    ppermute x14, waiting for transfers between devices: 6.93 us -> 17 us  [head_swap(): return lax.ppermute(array, 'head', [(h, h ^ k) for h in range(N_HEAD)])]
    ppermute x15, starting transfers between devices: 25.6 us -> 28.8 us  [plane_swap(): lax.ppermute(array, 'seq', [(s, s ^ k) for s in range(PLANE * PLANES)])]
    pallas_call x1 -> x2, Pallas kernels: 3.14 us -> 6.22 us  [load_weight(): pl.pallas_call(functools.partial(load_kernel, parts), in_specs=[pl.BlockS...]
    unnamed x12 -> x18, local copies, waits for them, and re-layouts: 0.03 us -> 2.38 us
    all_to_all x1, blocking collectives: 25 us -> 23.1 us  [local(): lax.all_to_all(sent.reshape(TILES, PAIR, WIDTH), 'seq', split_axis=0, con...]
    ppermute x15, waiting for transfers between devices: 18 us -> 16 us  [plane_swap(): lax.ppermute(array, 'seq', [(s, s ^ k) for s in range(PLANE * PLANES)])]
    ppermute x14, starting transfers between devices: 25.6 us -> 23.9 us  [head_swap(): return lax.ppermute(array, 'head', [(h, h ^ k) for h in range(N_HEAD)])]
  transfers between devices with their start and end apart: 33 -> 33, of which waited for: 11 -> 10; matrix products, arithmetic and copies ran while one was open for 0% -> 0% of each run, Pallas kernels for 15% -> 17%
where the time goes in v7:
time: 143 us; the launch traced here: 142 us
  starting transfers between devices  55.3 us (39%)
  waiting for transfers between devices  33 us (23%)
  Pallas kernels  28 us (20%)
  blocking collectives  23.1 us (16%)
  local copies, waits for them, and re-layouts  2.38 us (2%)
    ppermute x15, starting transfers between devices, plane_swap(): lax.ppermute(array, 'seq', [(s, s ^ k) for s in range(PLANE * PLANES)])  28.8 us
    ppermute x14, starting transfers between devices, head_swap(): return lax.ppermute(array, 'head', [(h, h ^ k) for h in range(N_HEAD)])  23.9 us
    all_to_all x1, blocking collectives, local(): lax.all_to_all(sent.reshape(TILES, PAIR, WIDTH), 'seq', split_axis=0, con...  23.1 us
    ppermute x14, waiting for transfers between devices, head_swap(): return lax.ppermute(array, 'head', [(h, h ^ k) for h in range(N_HEAD)])  17 us
    ppermute x15, waiting for transfers between devices, plane_swap(): lax.ppermute(array, 'seq', [(s, s ^ k) for s in range(PLANE * PLANES)])  16 us
    pallas_call x2, Pallas kernels, load_weight(): pl.pallas_call(functools.partial(load_kernel, parts), in_specs=[pl.BlockS...  6.22 us
    pallas_call x2, Pallas kernels, attend(): pl.pallas_call(functools.partial(attend_kernel, kinds), in_specs=[scalars...  6.02 us
    pallas_call x2, Pallas kernels, project_keys(): pl.pallas_call(functools.partial(keys_kernel, steps), in_specs=[pl.BlockS...  4.42 us
  transfers between devices with their start and end apart: 33, of which 10 were waited for; matrix products, arithmetic and copies ran while one was open for 0% of the time, Pallas kernels for 17%

profile of v7, /device:TPU:2, one launch (start us, length us, event | category | flops | bytes accessed | tf_op | source)
XLA Modules:
  0.0 142.3 jit_solution(5933132427276447316)
XLA Ops:
  0.0 3.0 %collective-permute-start = (bf16[32,3072]{1,0:T(8,128)(2,1)}, bf16[32,3072]{1,0:T(8,128)(2,1)S(1)}, u32[]{:S(2)}, u32[]{:S(2)}) collective-permute-start(bf16[32,3072]{1,0:T(8,128)(2,1)} %bitcast.14), channel_id=1, source_target_pairs={{0,6},{1,7},{2,4},{3,5},{4,2},{5,3},{6,0},{7,1},{8,14},{9,15},{10,... | collective-permute-start | bytes 589832 | tf_op jit(solution)/shard_map/ppermute | solution.py:439
  3.0 1.7 %collective-permute-start.2 = (bf16[32,3072]{1,0:T(8,128)(2,1)}, bf16[32,3072]{1,0:T(8,128)(2,1)S(1)}, u32[]{:S(2)}, u32[]{:S(2)}) collective-permute-start(bf16[32,3072]{1,0:T(8,128)(2,1)} %bitcast.15), channel_id=1, source_target_pairs={{0,3},{1,2},{2,1},{3,0},{4,7},{5,6},{6,5},{7,4},{8,11},{9,10},{10,... | collective-permute-start | bytes 589832 | tf_op jit(solution)/shard_map/ppermute | solution.py:439
  4.7 1.4 collective-permute-start.5
  6.1 1.9 %collective-permute-start.6 = (bf16[32,3072]{1,0:T(8,128)(2,1)}, bf16[32,3072]{1,0:T(8,128)(2,1)}, u32[]{:S(2)}, u32[]{:S(2)}) collective-permute-start(bf16[32,3072]{1,0:T(8,128)(2,1)} %bitcast.17), channel_id=1, source_target_pairs={{0,2},{1,3},{2,0},{3,1},{4,6},{5,7},{6,4},{7,5},{8,10},{9,11},{10,... | collective-permute-start | bytes 589832 | tf_op jit(solution)/shard_map/ppermute | solution.py:439
  8.0 1.8 %collective-permute-start.4 = (bf16[32,3072]{1,0:T(8,128)(2,1)}, bf16[32,3072]{1,0:T(8,128)(2,1)}, u32[]{:S(2)}, u32[]{:S(2)}) collective-permute-start(bf16[32,3072]{1,0:T(8,128)(2,1)} %bitcast.18), channel_id=1, source_target_pairs={{0,7},{1,6},{2,5},{3,4},{4,3},{5,2},{6,1},{7,0},{8,15},{9,14},{10,... | collective-permute-start | bytes 589832 | tf_op jit(solution)/shard_map/ppermute | solution.py:439
  9.8 0.4 collective-permute-start.1
  10.2 3.3 %collective-permute-done.2.refs_3_ = bf16[32,3072]{1,0:T(8,128)(2,1)S(1)} collective-permute-done((bf16[32,3072]{1,0:T(8,128)(2,1)}, bf16[32,3072]{1,0:T(8,128)(2,1)S(1)}, u32[]{:S(2)}, u32[]{:S(2)}) %collective-permute-start.2) | collective-permute-done | bytes 196640 | tf_op jit(solution)/shard_map/ppermute | solution.py:439
  13.5 0.2 collective-permute-start.3
  13.7 4.5 %load_weight.2.refs_4_ = bf16[2,3072,384]{2,1,0:T(8,128)(2,1)} custom-call(bf16[3,3072,384]{2,1,0:T(8,128)(2,1)} %bitcast.25), custom_call_target="tpu_custom_call" | custom-call | bytes 4800000 | tf_op jit(solution)/shard_map/load_weight/pallas_call | solution.py:116
  18.3 1.7 %load_weight.3.refs_8_ = bf16[1,3072,384]{2,1,0:T(8,128)(2,1)S(1)} custom-call(bf16[3,3072,384]{2,1,0:T(8,128)(2,1)} %bitcast.26), custom_call_target="tpu_custom_call" | custom-call | bytes 2400000 | tf_op jit(solution)/shard_map/load_weight/pallas_call | solution.py:116
  20.0 0.1 pad_add_fusion.ids
  20.1 2.3 %copy-done = bf16[2,3072,384]{2,1,0:T(8,128)(2,1)S(1)} copy-done((bf16[2,3072,384]{2,1,0:T(8,128)(2,1)S(1)}, bf16[2,3072,384]{2,1,0:T(8,128)(2,1)}, u32[]{:S(2)}) %copy-start) | copy-done | bytes 4718616
  22.4 2.3 %project_keys.2.refs_4_ = bf16[128,768]{1,0:T(8,128)(2,1)S(1)} custom-call(s32[2]{0:T(128)S(1)} %pad_add_fusion.ids, bf16[32,3072]{1,0:T(8,128)(2,1)S(1)} %bitcast.19, bf16[32,3072]{1,0:T(8,128)(2,1)} %collective-permute-done.5.refs_1_, bf16[32,3072]{1,0:T(8,128)(2,1)} %collective-permute-done.6.refs_2_, ...), custom_call_target="tpu_custom_call" | custom-call | flops 603979776 | bytes 6000000 | tf_op jit(solution)/shard_map/project_keys/pallas_call | solution.py:167
  24.7 2.0 %collective-permute-start.8 = (bf16[128,768]{1,0:T(8,128)(2,1)S(1)}, bf16[128,768]{1,0:T(8,128)(2,1)S(1)}, u32[]{:S(2)}, u32[]{:S(2)}) collective-permute-start(bf16[128,768]{1,0:T(8,128)(2,1)S(1)} %project_keys.2.refs_4_), channel_id=1, source_target_pairs={{0,32},{8,40},{16,48},{24,56},{32,0},{40,8},{48,16},{56,24},{64,96... | collective-permute-start | bytes 589832 | tf_op jit(solution)/shard_map/ppermute | solution.py:443
  26.7 0.7 collective-permute-start.14
  27.4 2.5 %project_queries.1.refs_0_ = bf16[256,384]{1,0:T(8,128)(2,1)S(1)} custom-call(s32[2]{0:T(128)S(1)} %pad_add_fusion.ids, bf16[32,3072]{1,0:T(8,128)(2,1)S(1)} %bitcast.20, bf16[32,3072]{1,0:T(8,128)(2,1)} %collective-permute-done.5.refs_1_, bf16[32,3072]{1,0:T(8,128)(2,1)} %collective-permute-done.6.refs_2_, ...), custom_call_target="tpu_custom_call" | custom-call | flops 603979776 | bytes 4000000 | tf_op jit(solution)/shard_map/project_queries/pallas_call | solution.py:140
  29.9 0.7 collective-permute-start.11
  30.7 2.2 %project_keys.3.refs_5_ = bf16[128,768]{1,0:T(8,128)(2,1)S(1)} custom-call(s32[2]{0:T(128)S(1)} %pad_add_fusion.ids, bf16[32,3072]{1,0:T(8,128)(2,1)} %collective-permute-done.1.refs_0_.refs_4_, bf16[32,3072]{1,0:T(8,128)(2,1)} %collective-permute-done.3.refs_1_.refs_5_, bf16[32,3072]{1,0:T(8,128)(2,1)S(1)} %collective-permute-done.refs_2_.refs_6_, ...), custom_call_target="tpu_custom_call" | custom-call | flops 603979776 | bytes 6000000 | tf_op jit(solution)/shard_map/project_keys/pallas_call | solution.py:167
  32.8 5.2 %collective-permute-start.13 = (bf16[128,768]{1,0:T(8,128)(2,1)S(1)}, bf16[128,768]{1,0:T(8,128)(2,1)S(1)}, u32[]{:S(2)}, u32[]{:S(2)}) collective-permute-start(bf16[128,768]{1,0:T(8,128)(2,1)S(1)} %project_keys.3.refs_5_), channel_id=1, source_target_pairs={{0,32},{8,40},{16,48},{24,56},{32,0},{40,8},{48,16},{56,24},{64,96... | collective-permute-start | bytes 589832 | tf_op jit(solution)/shard_map/ppermute | solution.py:443
  38.0 0.7 collective-permute-start.7
  38.7 0.1 collective-permute-start.10
  38.8 0.7 collective-permute-start.9
  39.5 0.6 collective-permute-start.12
  40.0 1.6 %collective-permute-done.13.refs_7_ = bf16[128,768]{1,0:T(8,128)(2,1)S(1)} collective-permute-done((bf16[128,768]{1,0:T(8,128)(2,1)S(1)}, bf16[128,768]{1,0:T(8,128)(2,1)S(1)}, u32[]{:S(2)}, u32[]{:S(2)}) %collective-permute-start.13) | collective-permute-done | bytes 196640 | tf_op jit(solution)/shard_map/ppermute | solution.py:443
  41.6 0.7 collective-permute-start.16
  42.3 8.1 %collective-permute-start.17 = (bf16[128,768]{1,0:T(8,128)(2,1)S(1)}, bf16[128,768]{1,0:T(8,128)(2,1)S(1)}, u32[]{:S(2)}, u32[]{:S(2)}) collective-permute-start(bf16[128,768]{1,0:T(8,128)(2,1)S(1)} %collective-permute-done.14.refs_8_), channel_id=1, source_target_pairs={{0,32},{8,40},{16,48},{24,56},{32,0},{40,8},{48,16},{56,24},{64,96... | collective-permute-start | bytes 589832 | tf_op jit(solution)/shard_map/ppermute | solution.py:443
  50.4 3.3 %collective-permute-start.18 = (bf16[128,768]{1,0:T(8,128)(2,1)S(1)}, bf16[128,768]{1,0:T(8,128)(2,1)S(1)}, u32[]{:S(2)}, u32[]{:S(2)}) collective-permute-start(bf16[128,768]{1,0:T(8,128)(2,1)S(1)} %collective-permute-done.7.refs_9_), channel_id=1, source_target_pairs={{0,32},{8,40},{16,48},{24,56},{32,0},{40,8},{48,16},{56,24},{64,96... | collective-permute-start | bytes 589832 | tf_op jit(solution)/shard_map/ppermute | solution.py:443
  53.8 0.1 collective-permute-start.19
  53.9 3.7 %collective-permute-start.20 = (bf16[128,768]{1,0:T(8,128)(2,1)S(1)}, bf16[128,768]{1,0:T(8,128)(2,1)S(1)}, u32[]{:S(2)}, u32[]{:S(2)}) collective-permute-start(bf16[128,768]{1,0:T(8,128)(2,1)S(1)} %collective-permute-done.16.refs_5_), channel_id=1, source_target_pairs={{0,32},{8,40},{16,48},{24,56},{32,0},{40,8},{48,16},{56,24},{64,96... | collective-permute-start | bytes 589832 | tf_op jit(solution)/shard_map/ppermute | solution.py:443
  57.6 2.2 %plan.1.table = s32[128]{0:T(128)S(1)} custom-call(s32[2]{0:T(128)S(1)} %pad_add_fusion.ids, s32[9,32]{1,0:T(8,128)S(1)} %bitcast.21, s32[32]{0:T(128)S(1)} %copy-done.6), custom_call_target="tpu_custom_call" | custom-call | bytes 8000000 | tf_op jit(solution)/shard_map/plan/pallas_call | solution.py:73
  59.7 3.0 %attend.2 = (bf16[288,384]{1,0:T(8,128)(2,1)S(1)}, bf16[288,384]{1,0:T(8,128)(2,1)S(1)}, bf16[288,384]{1,0:T(8,128)(2,1)S(1)}, bf16[288,384]{1,0:T(8,128)(2,1)S(1)}) custom-call(s32[128]{0:T(128)S(1)} %plan.1.table, bf16[256,384]{1,0:T(8,128)(2,1)S(1)} %project_queries.1.refs_0_, bf16[256,384]{1,0:T(8,128)(2,1)S(1)} %collective-permute-done.10.refs_1_, ...), custom_call_target="tpu_custom_call" | custom-call | flops 452984832 | bytes 4000000 | tf_op jit(solution)/shard_map/attend/pallas_call | solution.py:294
  62.7 0.1 collective-permute-start.22
  62.9 1.7 %collective-permute-done.19.refs_8_ = bf16[128,768]{1,0:T(8,128)(2,1)S(1)} collective-permute-done((bf16[128,768]{1,0:T(8,128)(2,1)S(1)}, bf16[128,768]{1,0:T(8,128)(2,1)S(1)}, u32[]{:S(2)}, u32[]{:S(2)}) %collective-permute-start.19) | collective-permute-done | bytes 196640 | tf_op jit(solution)/shard_map/ppermute | solution.py:443
  64.5 3.6 %collective-permute-done.20.refs_9_ = bf16[128,768]{1,0:T(8,128)(2,1)S(1)} collective-permute-done((bf16[128,768]{1,0:T(8,128)(2,1)S(1)}, bf16[128,768]{1,0:T(8,128)(2,1)S(1)}, u32[]{:S(2)}, u32[]{:S(2)}) %collective-permute-start.20) | collective-permute-done | bytes 196640 | tf_op jit(solution)/shard_map/ppermute | solution.py:443
  68.1 3.0 %attend.3 = (bf16[288,384]{1,0:T(8,128)(2,1)S(1)}, bf16[288,384]{1,0:T(8,128)(2,1)S(1)}, bf16[288,384]{1,0:T(8,128)(2,1)S(1)}, bf16[288,384]{1,0:T(8,128)(2,1)S(1)}) custom-call(s32[128]{0:T(128)S(1)} %plan.1.table, bf16[256,384]{1,0:T(8,128)(2,1)S(1)} %project_queries.1.refs_0_, bf16[256,384]{1,0:T(8,128)(2,1)S(1)} %collective-permute-done.10.refs_1_, ...), custom_call_target="tpu_custom_call" | custom-call | flops 452984832 | bytes 4000000 | tf_op jit(solution)/shard_map/attend/pallas_call | solution.py:294
  71.2 0.1 collective-permute-start.23
  71.3 0.5 collective-permute-start.15
  71.8 0.1 collective-permute-start.21
  71.9 0.3 merge_shares.4.refs_0_
  72.2 0.5 collective-permute-done.23.refs_2_
  72.7 0.4 merge_shares.5
  73.2 1.5 %collective-permute-start.24 = (bf16[288,384]{1,0:T(8,128)(2,1)S(1)}, bf16[288,384]{1,0:T(8,128)(2,1)S(1)}, u32[]{:S(2)}, u32[]{:S(2)}) collective-permute-start(bf16[288,384]{1,0:T(8,128)(2,1)S(1)} %merge_shares.5), channel_id=1, source_target_pairs={{0,16},{8,24},{16,0},{24,8},{32,48},{40,56},{48,32},{56,40},{64,80... | collective-permute-start | bytes 663560 | tf_op jit(solution)/shard_map/ppermute | solution.py:443
  74.7 0.3 merge_shares.3.refs_0_
  75.0 5.7 %collective-permute-done.24.refs_3_ = bf16[288,384]{1,0:T(8,128)(2,1)S(1)} collective-permute-done((bf16[288,384]{1,0:T(8,128)(2,1)S(1)}, bf16[288,384]{1,0:T(8,128)(2,1)S(1)}, u32[]{:S(2)}, u32[]{:S(2)}) %collective-permute-start.24) | collective-permute-done | bytes 221216 | tf_op jit(solution)/shard_map/ppermute | solution.py:443
  80.7 1.5 %join.1 = (bf16[256,384]{1,0:T(8,128)(2,1)S(1)}, bf16[256,384]{1,0:T(8,128)(2,1)S(1)}, bf16[256,384]{1,0:T(8,128)(2,1)S(1)}) custom-call(s32[2]{0:T(128)S(1)} %pad_add_fusion.ids, bf16[288,384]{1,0:T(8,128)(2,1)S(1)} %merge_shares.3.refs_0_, bf16[288,384]{1,0:T(8,128)(2,1)S(1)} %get-tuple-element.48.refs_1_, ...), custom_call_target="tpu_custom_call" | custom-call | flops 150994944 | bytes 3000000 | tf_op jit(solution)/shard_map/join/pallas_call | solution.py:327
  82.2 1.4 collective-permute-start.28
  83.6 1.4 %direct_terms.1 = (bf16[256,384]{1,0:T(8,128)(2,1)S(1)}, bf16[256,384]{1,0:T(8,128)(2,1)S(1)}, bf16[256,384]{1,0:T(8,128)(2,1)S(1)}, bf16[256,384]{1,0:T(8,128)(...) custom-call(s32[2]{0:T(128)S(1)} %pad_add_fusion.ids, ...), custom_call_target="tpu_custom_call" | custom-call | flops 452984832 | bytes 4000000 | tf_op jit(solution)/shard_map/direct_terms/pallas_call | solution.py:347
  85.1 1.7 %collective-permute-start.25 = (bf16[256,384]{1,0:T(8,128)(2,1)S(1)}, bf16[256,384]{1,0:T(8,128)(2,1)S(1)}, u32[]{:S(2)}, u32[]{:S(2)}) collective-permute-start(bf16[256,384]{1,0:T(8,128)(2,1)S(1)} %get-tuple-element.56), channel_id=1, source_target_pairs={{0,1},{1,0},{2,3},{3,2},{4,5},{5,4},{6,7},{7,6},{8,9},{9,8},{10,11... | collective-permute-start | bytes 589832 | tf_op jit(solution)/shard_map/ppermute | solution.py:439
  86.7 1.7 %collective-permute-start.26 = (bf16[256,384]{1,0:T(8,128)(2,1)S(1)}, bf16[256,384]{1,0:T(8,128)(2,1)S(1)}, u32[]{:S(2)}, u32[]{:S(2)}) collective-permute-start(bf16[256,384]{1,0:T(8,128)(2,1)S(1)} %get-tuple-element.57), channel_id=1, source_target_pairs={{0,2},{1,3},{2,0},{3,1},{4,6},{5,7},{6,4},{7,5},{8,10},{9,11},{10,... | collective-permute-start | bytes 589832 | tf_op jit(solution)/shard_map/ppermute | solution.py:439
  88.4 3.6 %collective-permute-start.27 = (bf16[256,384]{1,0:T(8,128)(2,1)S(1)}, bf16[256,384]{1,0:T(8,128)(2,1)S(1)}, u32[]{:S(2)}, u32[]{:S(2)}) collective-permute-start(bf16[256,384]{1,0:T(8,128)(2,1)S(1)} %get-tuple-element.58), channel_id=1, source_target_pairs={{0,7},{1,6},{2,5},{3,4},{4,3},{5,2},{6,1},{7,0},{8,15},{9,14},{10,... | collective-permute-start | bytes 589832 | tf_op jit(solution)/shard_map/ppermute | solution.py:439
  92.0 0.2 collective-permute-start.30
  92.3 0.1 add_convert_fusion.1
  92.3 3.1 %collective-permute-start.29 = (bf16[256,384]{1,0:T(8,128)(2,1)S(1)}, bf16[256,384]{1,0:T(8,128)(2,1)S(1)}, u32[]{:S(2)}, u32[]{:S(2)}) collective-permute-start(bf16[256,384]{1,0:T(8,128)(2,1)S(1)} %add_convert_fusion.1), channel_id=1, source_target_pairs={{0,6},{1,7},{2,4},{3,5},{4,2},{5,3},{6,0},{7,1},{8,14},{9,15},{10,... | collective-permute-start | bytes 589832 | tf_op jit(solution)/shard_map/ppermute | solution.py:439
  95.4 7.3 %collective-permute-done.30 = bf16[256,384]{1,0:T(8,128)(2,1)S(1)} collective-permute-done((bf16[256,384]{1,0:T(8,128)(2,1)S(1)}, bf16[256,384]{1,0:T(8,128)(2,1)S(1)}, u32[]{:S(2)}, u32[]{:S(2)}) %collective-permute-start.30) | collective-permute-done | bytes 196640 | tf_op jit(solution)/shard_map/ppermute | solution.py:439
  102.7 0.1 add_convert_fusion
  102.8 1.8 %collective-permute-start.31 = (bf16[256,384]{1,0:T(8,128)(2,1)S(1)}, bf16[256,384]{1,0:T(8,128)(2,1)S(1)}, u32[]{:S(2)}, u32[]{:S(2)}) collective-permute-start(bf16[256,384]{1,0:T(8,128)(2,1)S(1)} %add_convert_fusion), channel_id=1, source_target_pairs={{0,3},{1,2},{2,1},{3,0},{4,7},{5,6},{6,5},{7,4},{8,11},{9,10},{10,... | collective-permute-start | bytes 589832 | tf_op jit(solution)/shard_map/ppermute | solution.py:439
  104.6 1.7 %collective-permute-done.29.refs_4_ = bf16[256,384]{1,0:T(8,128)(2,1)S(1)} collective-permute-done((bf16[256,384]{1,0:T(8,128)(2,1)S(1)}, bf16[256,384]{1,0:T(8,128)(2,1)S(1)}, u32[]{:S(2)}, u32[]{:S(2)}) %collective-permute-start.29) | collective-permute-done | bytes 196640 | tf_op jit(solution)/shard_map/ppermute | solution.py:439
  106.2 4.7 %collective-permute-done.31.refs_5_ = bf16[256,384]{1,0:T(8,128)(2,1)S(1)} collective-permute-done((bf16[256,384]{1,0:T(8,128)(2,1)S(1)}, bf16[256,384]{1,0:T(8,128)(2,1)S(1)}, u32[]{:S(2)}, u32[]{:S(2)}) %collective-permute-start.31) | collective-permute-done | bytes 196640 | tf_op jit(solution)/shard_map/ppermute | solution.py:439
  110.9 0.8 add_terms.1
  111.7 2.8 %collective-permute-start.32 = (bf16[128,384]{1,0:T(8,128)(2,1)S(1)}, bf16[128,384]{1,0:T(8,128)(2,1)S(1)}, u32[]{:S(2)}, u32[]{:S(2)}) collective-permute-start(bf16[128,384]{1,0:T(8,128)(2,1)S(1)} %get-tuple-element.64), channel_id=1, source_target_pairs={{0,64},{8,72},{16,80},{24,88},{32,96},{40,104},{48,112},{56,120},{... | collective-permute-start | bytes 294920 | tf_op jit(solution)/shard_map/ppermute | solution.py:443
  114.5 2.8 %collective-permute-done.32.got_ref = bf16[128,384]{1,0:T(8,128)(2,1)S(1)} collective-permute-done((bf16[128,384]{1,0:T(8,128)(2,1)S(1)}, bf16[128,384]{1,0:T(8,128)(2,1)S(1)}, u32[]{:S(2)}, u32[]{:S(2)}) %collective-permute-start.32) | collective-permute-done | bytes 98336 | tf_op jit(solution)/shard_map/ppermute | solution.py:443
  117.3 0.7 order.1
  118.0 23.1 %all_to_all.5 = bf16[32,16,384]{2,1,0:T(8,128)(2,1)S(1)} all-to-all(bf16[32,16,384]{2,1,0:T(8,128)(2,1)S(1)} %bitcast.12), channel_id=1, replica_groups=mesh['seq'=32,'head'=8] {'seq'}, dimensions={0} | all-to-all | bytes 786432 | tf_op jit(solution)/shard_map/all_to_all | solution.py:503
  141.1 1.2 to_tile.1
  (41 shorter events, 0.1 us)
Async XLA Ops:
  0.0 9.8 %collective-permute-start = (bf16[32,3072]{1,0:T(8,128)(2,1)}, bf16[32,3072]{1,0:T(8,128)(2,1)S(1)}, u32[]{:S(2)}, u32[]{:S(2)}) collective-permute-start(bf16[32,3072]{1,0:T(8,128)(2,1)} %bitcast.14), channel_id=1, source_target_pairs={{0,6},{1,7},{2,4},{3,5},{4,2},{5,3},{6,0},{7,1},{8,14},{9,15},{10,... | collective-permute-start | bytes 589832 | tf_op jit(solution)/shard_map/ppermute | solution.py:439
  3.0 10.5 %collective-permute-start.2 = (bf16[32,3072]{1,0:T(8,128)(2,1)}, bf16[32,3072]{1,0:T(8,128)(2,1)S(1)}, u32[]{:S(2)}, u32[]{:S(2)}) collective-permute-start(bf16[32,3072]{1,0:T(8,128)(2,1)} %bitcast.15), channel_id=1, source_target_pairs={{0,3},{1,2},{2,1},{3,0},{4,7},{5,6},{6,5},{7,4},{8,11},{9,10},{10,... | collective-permute-start | bytes 589832 | tf_op jit(solution)/shard_map/ppermute | solution.py:439
  4.7 15.4 %collective-permute-start.5 = (bf16[32,3072]{1,0:T(8,128)(2,1)}, bf16[32,3072]{1,0:T(8,128)(2,1)}, u32[]{:S(2)}, u32[]{:S(2)}) collective-permute-start(bf16[32,3072]{1,0:T(8,128)(2,1)} %bitcast.16), channel_id=1, source_target_pairs={{0,1},{1,0},{2,3},{3,2},{4,5},{5,4},{6,7},{7,6},{8,9},{9,8},{10,11... | collective-permute-start | bytes 589832 | tf_op jit(solution)/shard_map/ppermute | solution.py:439
  6.1 14.0 %collective-permute-start.6 = (bf16[32,3072]{1,0:T(8,128)(2,1)}, bf16[32,3072]{1,0:T(8,128)(2,1)}, u32[]{:S(2)}, u32[]{:S(2)}) collective-permute-start(bf16[32,3072]{1,0:T(8,128)(2,1)} %bitcast.17), channel_id=1, source_target_pairs={{0,2},{1,3},{2,0},{3,1},{4,6},{5,7},{6,4},{7,5},{8,10},{9,11},{10,... | collective-permute-start | bytes 589832 | tf_op jit(solution)/shard_map/ppermute | solution.py:439
  8.0 19.4 %collective-permute-start.4 = (bf16[32,3072]{1,0:T(8,128)(2,1)}, bf16[32,3072]{1,0:T(8,128)(2,1)}, u32[]{:S(2)}, u32[]{:S(2)}) collective-permute-start(bf16[32,3072]{1,0:T(8,128)(2,1)} %bitcast.18), channel_id=1, source_target_pairs={{0,7},{1,6},{2,5},{3,4},{4,3},{5,2},{6,1},{7,0},{8,15},{9,14},{10,... | collective-permute-start | bytes 589832 | tf_op jit(solution)/shard_map/ppermute | solution.py:439
  9.8 17.6 %collective-permute-start.1 = (bf16[32,3072]{1,0:T(8,128)(2,1)S(1)}, bf16[32,3072]{1,0:T(8,128)(2,1)}, u32[]{:S(2)}, u32[]{:S(2)}) collective-permute-start(bf16[32,3072]{1,0:T(8,128)(2,1)S(1)} %collective-permute-done.refs_2_.refs_6_), channel_id=1, source_target_pairs={{0,2},{1,3},{2,0},{3,1},{4,6},{5,7},{6,4},{7,5},{8,10},{9,11},{10,... | collective-permute-start | bytes 589832 | tf_op jit(solution)/shard_map/ppermute | solution.py:439
  13.5 13.9 %collective-permute-start.3 = (bf16[32,3072]{1,0:T(8,128)(2,1)S(1)}, bf16[32,3072]{1,0:T(8,128)(2,1)}, u32[]{:S(2)}, u32[]{:S(2)}) collective-permute-start(bf16[32,3072]{1,0:T(8,128)(2,1)S(1)} %collective-permute-done.2.refs_3_), channel_id=1, source_target_pairs={{0,6},{1,7},{2,4},{3,5},{4,2},{5,3},{6,0},{7,1},{8,14},{9,15},{10,... | collective-permute-start | bytes 589832 | tf_op jit(solution)/shard_map/ppermute | solution.py:439
  18.2 1.8 %copy-start.2 = (bf16[4,1,8,3072]{3,2,1,0:T(8,128)(2,1)S(1)}, bf16[4,1,8,3072]{3,2,1,0:T(8,128)(2,1)}, u32[]{:S(2)}) copy-start(bf16[4,1,8,3072]{3,2,1,0:T(8,128)(2,1)} %param.7) | copy-start | bytes 589828
  18.3 1.8 %copy-start.4 = (f32[128]{0:T(128)S(1)}, f32[128]{0:T(128)}, u32[]{:S(2)}) copy-start(f32[128]{0:T(128)} %param.10) | copy-start | bytes 1540
  18.3 12.4 %slice-start = ((s8[4718592]{0:T(1024)(128)(4,1)}), s8[524288]{0:T(1024)(128)(4,1)S(1)}, s32[]{:S(2)}) async-start(s8[4718592]{0:T(1024)(128)(4,1)} %bitcast.10), calls=%async_computation.1 | async-start | bytes 1048576
  20.0 7.4 %copy-start.5 = (f32[128]{0:T(128)S(1)}, f32[128]{0:T(128)}, u32[]{:S(2)}) copy-start(f32[128]{0:T(128)} %param.9) | copy-start | bytes 1540
  20.1 2.3 %copy-start = (bf16[2,3072,384]{2,1,0:T(8,128)(2,1)S(1)}, bf16[2,3072,384]{2,1,0:T(8,128)(2,1)}, u32[]{:S(2)}) copy-start(bf16[2,3072,384]{2,1,0:T(8,128)(2,1)} %load_weight.2.refs_4_) | copy-start | bytes 14155780
  22.4 8.2 %slice-start.1 = ((s8[4718592]{0:T(1024)(128)(4,1)}), s8[4194304]{0:T(1024)(128)(4,1)S(1)}, s32[]{:S(2)}) async-start(s8[4718592]{0:T(1024)(128)(4,1)} %bitcast.10), calls=%async_computation.2 | async-start | bytes 8388608
  24.7 14.0 %collective-permute-start.8 = (bf16[128,768]{1,0:T(8,128)(2,1)S(1)}, bf16[128,768]{1,0:T(8,128)(2,1)S(1)}, u32[]{:S(2)}, u32[]{:S(2)}) collective-permute-start(bf16[128,768]{1,0:T(8,128)(2,1)S(1)} %project_keys.2.refs_4_), channel_id=1, source_target_pairs={{0,32},{8,40},{16,48},{24,56},{32,0},{40,8},{48,16},{56,24},{64,96... | collective-permute-start | bytes 589832 | tf_op jit(solution)/shard_map/ppermute | solution.py:443
  26.7 12.1 %collective-permute-start.14 = (bf16[128,768]{1,0:T(8,128)(2,1)S(1)}, bf16[128,768]{1,0:T(8,128)(2,1)S(1)}, u32[]{:S(2)}, u32[]{:S(2)}) collective-permute-start(bf16[128,768]{1,0:T(8,128)(2,1)S(1)} %project_keys.2.refs_4_), channel_id=1, source_target_pairs={{32,64},{64,32},{40,72},{72,40},{48,80},{80,48},{56,88},{88,56},{9... | collective-permute-start | bytes 589832 | tf_op jit(solution)/shard_map/ppermute | solution.py:455
  27.4 30.1 %copy-start.3 = (s32[32,9]{0,1:T(8,128)S(1)}, s32[32,9]{0,1:T(8,128)}, u32[]{:S(2)}) copy-start(s32[32,9]{0,1:T(8,128)} %param.12) | copy-start | bytes 3460
  27.4 30.1 %copy-start.6 = (s32[32]{0:T(128)S(1)}, s32[32]{0:T(128)}, u32[]{:S(2)}) copy-start(s32[32]{0:T(128)} %tile_owner.1) | copy-start | bytes 388
  29.9 50.8 %copy-start.1 = (bf16[384,3072]{1,0:T(8,128)(2,1)S(1)}, bf16[384,3072]{1,0:T(8,128)(2,1)}, u32[]{:S(2)}) copy-start(bf16[384,3072]{1,0:T(8,128)(2,1)} %w_ref.1) | copy-start | bytes 7077892
  29.9 9.5 %collective-permute-start.11 = (bf16[256,384]{1,0:T(8,128)(2,1)S(1)}, bf16[256,384]{1,0:T(8,128)(2,1)S(1)}, u32[]{:S(2)}, u32[]{:S(2)}) collective-permute-start(bf16[256,384]{1,0:T(8,128)(2,1)S(1)} %project_queries.1.refs_0_), channel_id=1, source_target_pairs={{0,16},{8,24},{16,0},{24,8},{32,48},{40,56},{48,32},{56,40},{64,80... | collective-permute-start | bytes 589832 | tf_op jit(solution)/shard_map/ppermute | solution.py:443
  32.8 8.8 %collective-permute-start.13 = (bf16[128,768]{1,0:T(8,128)(2,1)S(1)}, bf16[128,768]{1,0:T(8,128)(2,1)S(1)}, u32[]{:S(2)}, u32[]{:S(2)}) collective-permute-start(bf16[128,768]{1,0:T(8,128)(2,1)S(1)} %project_keys.3.refs_5_), channel_id=1, source_target_pairs={{0,32},{8,40},{16,48},{24,56},{32,0},{40,8},{48,16},{56,24},{64,96... | collective-permute-start | bytes 589832 | tf_op jit(solution)/shard_map/ppermute | solution.py:443
  38.0 4.3 %collective-permute-start.7 = (bf16[128,768]{1,0:T(8,128)(2,1)S(1)}, bf16[128,768]{1,0:T(8,128)(2,1)S(1)}, u32[]{:S(2)}, u32[]{:S(2)}) collective-permute-start(bf16[128,768]{1,0:T(8,128)(2,1)S(1)} %project_keys.3.refs_5_), channel_id=1, source_target_pairs={{32,64},{64,32},{40,72},{72,40},{48,80},{80,48},{56,88},{88,56},{9... | collective-permute-start | bytes 589832 | tf_op jit(solution)/shard_map/ppermute | solution.py:455
  38.7 11.7 %collective-permute-start.10 = (bf16[256,384]{1,0:T(8,128)(2,1)S(1)}, bf16[256,384]{1,0:T(8,128)(2,1)S(1)}, u32[]{:S(2)}, u32[]{:S(2)}) collective-permute-start(bf16[256,384]{1,0:T(8,128)(2,1)S(1)} %project_queries.1.refs_0_), channel_id=1, source_target_pairs={{0,8},{8,0},{16,24},{24,16},{32,40},{40,32},{48,56},{56,48},{64,72... | collective-permute-start | bytes 589832 | tf_op jit(solution)/shard_map/ppermute | solution.py:443
  38.8 11.6 %collective-permute-start.9 = (bf16[128,768]{1,0:T(8,128)(2,1)S(1)}, bf16[128,768]{1,0:T(8,128)(2,1)S(1)}, u32[]{:S(2)}, u32[]{:S(2)}) collective-permute-start(bf16[128,768]{1,0:T(8,128)(2,1)S(1)} %collective-permute-done.8.refs_6_), channel_id=1, source_target_pairs={{32,64},{64,32},{40,72},{72,40},{48,80},{80,48},{56,88},{88,56},{9... | collective-permute-start | bytes 589832 | tf_op jit(solution)/shard_map/ppermute | solution.py:455
  39.5 10.9 %collective-permute-start.12 = (bf16[256,384]{1,0:T(8,128)(2,1)S(1)}, bf16[256,384]{1,0:T(8,128)(2,1)S(1)}, u32[]{:S(2)}, u32[]{:S(2)}) collective-permute-start(bf16[256,384]{1,0:T(8,128)(2,1)S(1)} %collective-permute-done.11.refs_2_), channel_id=1, source_target_pairs={{0,8},{8,0},{16,24},{24,16},{32,40},{40,32},{48,56},{56,48},{64,72... | collective-permute-start | bytes 589832 | tf_op jit(solution)/shard_map/ppermute | solution.py:443
  41.6 12.2 %collective-permute-start.16 = (bf16[128,768]{1,0:T(8,128)(2,1)S(1)}, bf16[128,768]{1,0:T(8,128)(2,1)S(1)}, u32[]{:S(2)}, u32[]{:S(2)}) collective-permute-start(bf16[128,768]{1,0:T(8,128)(2,1)S(1)} %collective-permute-done.13.refs_7_), channel_id=1, source_target_pairs={{32,64},{64,32},{40,72},{72,40},{48,80},{80,48},{56,88},{88,56},{9... | collective-permute-start | bytes 589832 | tf_op jit(solution)/shard_map/ppermute | solution.py:455
  42.3 20.5 %collective-permute-start.17 = (bf16[128,768]{1,0:T(8,128)(2,1)S(1)}, bf16[128,768]{1,0:T(8,128)(2,1)S(1)}, u32[]{:S(2)}, u32[]{:S(2)}) collective-permute-start(bf16[128,768]{1,0:T(8,128)(2,1)S(1)} %collective-permute-done.14.refs_8_), channel_id=1, source_target_pairs={{0,32},{8,40},{16,48},{24,56},{32,0},{40,8},{48,16},{56,24},{64,96... | collective-permute-start | bytes 589832 | tf_op jit(solution)/shard_map/ppermute | solution.py:443
  50.4 12.4 %collective-permute-start.18 = (bf16[128,768]{1,0:T(8,128)(2,1)S(1)}, bf16[128,768]{1,0:T(8,128)(2,1)S(1)}, u32[]{:S(2)}, u32[]{:S(2)}) collective-permute-start(bf16[128,768]{1,0:T(8,128)(2,1)S(1)} %collective-permute-done.7.refs_9_), channel_id=1, source_target_pairs={{0,32},{8,40},{16,48},{24,56},{32,0},{40,8},{48,16},{56,24},{64,96... | collective-permute-start | bytes 589832 | tf_op jit(solution)/shard_map/ppermute | solution.py:443
  53.8 10.8 %collective-permute-start.19 = (bf16[128,768]{1,0:T(8,128)(2,1)S(1)}, bf16[128,768]{1,0:T(8,128)(2,1)S(1)}, u32[]{:S(2)}, u32[]{:S(2)}) collective-permute-start(bf16[128,768]{1,0:T(8,128)(2,1)S(1)} %collective-permute-done.9.refs_4_), channel_id=1, source_target_pairs={{0,32},{8,40},{16,48},{24,56},{32,0},{40,8},{48,16},{56,24},{64,96... | collective-permute-start | bytes 589832 | tf_op jit(solution)/shard_map/ppermute | solution.py:443
  53.9 14.3 %collective-permute-start.20 = (bf16[128,768]{1,0:T(8,128)(2,1)S(1)}, bf16[128,768]{1,0:T(8,128)(2,1)S(1)}, u32[]{:S(2)}, u32[]{:S(2)}) collective-permute-start(bf16[128,768]{1,0:T(8,128)(2,1)S(1)} %collective-permute-done.16.refs_5_), channel_id=1, source_target_pairs={{0,32},{8,40},{16,48},{24,56},{32,0},{40,8},{48,16},{56,24},{64,96... | collective-permute-start | bytes 589832 | tf_op jit(solution)/shard_map/ppermute | solution.py:443
  62.7 9.1 %collective-permute-start.22 = (bf16[288,384]{1,0:T(8,128)(2,1)S(1)}, bf16[288,384]{1,0:T(8,128)(2,1)S(1)}, u32[]{:S(2)}, u32[]{:S(2)}) collective-permute-start(bf16[288,384]{1,0:T(8,128)(2,1)S(1)} %get-tuple-element.51), channel_id=1, source_target_pairs={{0,8},{8,0},{16,24},{24,16},{32,40},{40,32},{48,56},{56,48},{64,72... | collective-permute-start | bytes 663560 | tf_op jit(solution)/shard_map/ppermute | solution.py:443
  71.2 1.6 %collective-permute-start.23 = (bf16[288,384]{1,0:T(8,128)(2,1)S(1)}, bf16[288,384]{1,0:T(8,128)(2,1)S(1)}, u32[]{:S(2)}, u32[]{:S(2)}) collective-permute-start(bf16[288,384]{1,0:T(8,128)(2,1)S(1)} %get-tuple-element.53), channel_id=1, source_target_pairs={{0,8},{8,0},{16,24},{24,16},{32,40},{40,32},{48,56},{56,48},{64,72... | collective-permute-start | bytes 663560 | tf_op jit(solution)/shard_map/ppermute | solution.py:443
  71.3 3.4 %collective-permute-start.15 = (bf16[288,384]{1,0:T(8,128)(2,1)S(1)}, bf16[288,384]{1,0:T(8,128)(2,1)S(1)}, u32[]{:S(2)}, u32[]{:S(2)}) collective-permute-start(bf16[288,384]{1,0:T(8,128)(2,1)S(1)} %get-tuple-element.46), channel_id=1, source_target_pairs={{0,8},{8,0},{16,24},{24,16},{32,40},{40,32},{48,56},{56,48},{64,72... | collective-permute-start | bytes 663560 | tf_op jit(solution)/shard_map/ppermute | solution.py:443
  71.8 3.2 %collective-permute-start.21 = (bf16[288,384]{1,0:T(8,128)(2,1)S(1)}, bf16[288,384]{1,0:T(8,128)(2,1)S(1)}, u32[]{:S(2)}, u32[]{:S(2)}) collective-permute-start(bf16[288,384]{1,0:T(8,128)(2,1)S(1)} %get-tuple-element.49), channel_id=1, source_target_pairs={{0,8},{8,0},{16,24},{24,16},{32,40},{40,32},{48,56},{56,48},{64,72... | collective-permute-start | bytes 663560 | tf_op jit(solution)/shard_map/ppermute | solution.py:443
  73.2 7.6 %collective-permute-start.24 = (bf16[288,384]{1,0:T(8,128)(2,1)S(1)}, bf16[288,384]{1,0:T(8,128)(2,1)S(1)}, u32[]{:S(2)}, u32[]{:S(2)}) collective-permute-start(bf16[288,384]{1,0:T(8,128)(2,1)S(1)} %merge_shares.5), channel_id=1, source_target_pairs={{0,16},{8,24},{16,0},{24,8},{32,48},{40,56},{48,32},{56,40},{64,80... | collective-permute-start | bytes 663560 | tf_op jit(solution)/shard_map/ppermute | solution.py:443
  82.2 10.1 %collective-permute-start.28 = (bf16[256,384]{1,0:T(8,128)(2,1)S(1)}, bf16[256,384]{1,0:T(8,128)(2,1)S(1)}, u32[]{:S(2)}, u32[]{:S(2)}) collective-permute-start(bf16[256,384]{1,0:T(8,128)(2,1)S(1)} %get-tuple-element.60), channel_id=1, source_target_pairs={{0,2},{1,3},{2,0},{3,1},{4,6},{5,7},{6,4},{7,5},{8,10},{9,11},{10,... | collective-permute-start | bytes 589832 | tf_op jit(solution)/shard_map/ppermute | solution.py:439
  85.1 19.5 %collective-permute-start.25 = (bf16[256,384]{1,0:T(8,128)(2,1)S(1)}, bf16[256,384]{1,0:T(8,128)(2,1)S(1)}, u32[]{:S(2)}, u32[]{:S(2)}) collective-permute-start(bf16[256,384]{1,0:T(8,128)(2,1)S(1)} %get-tuple-element.56), channel_id=1, source_target_pairs={{0,1},{1,0},{2,3},{3,2},{4,5},{5,4},{6,7},{7,6},{8,9},{9,8},{10,11... | collective-permute-start | bytes 589832 | tf_op jit(solution)/shard_map/ppermute | solution.py:439
  86.7 17.8 %collective-permute-start.26 = (bf16[256,384]{1,0:T(8,128)(2,1)S(1)}, bf16[256,384]{1,0:T(8,128)(2,1)S(1)}, u32[]{:S(2)}, u32[]{:S(2)}) collective-permute-start(bf16[256,384]{1,0:T(8,128)(2,1)S(1)} %get-tuple-element.57), channel_id=1, source_target_pairs={{0,2},{1,3},{2,0},{3,1},{4,6},{5,7},{6,4},{7,5},{8,10},{9,11},{10,... | collective-permute-start | bytes 589832 | tf_op jit(solution)/shard_map/ppermute | solution.py:439
  88.4 16.1 %collective-permute-start.27 = (bf16[256,384]{1,0:T(8,128)(2,1)S(1)}, bf16[256,384]{1,0:T(8,128)(2,1)S(1)}, u32[]{:S(2)}, u32[]{:S(2)}) collective-permute-start(bf16[256,384]{1,0:T(8,128)(2,1)S(1)} %get-tuple-element.58), channel_id=1, source_target_pairs={{0,7},{1,6},{2,5},{3,4},{4,3},{5,2},{6,1},{7,0},{8,15},{9,14},{10,... | collective-permute-start | bytes 589832 | tf_op jit(solution)/shard_map/ppermute | solution.py:439
  92.0 10.7 %collective-permute-start.30 = (bf16[256,384]{1,0:T(8,128)(2,1)S(1)}, bf16[256,384]{1,0:T(8,128)(2,1)S(1)}, u32[]{:S(2)}, u32[]{:S(2)}) collective-permute-start(bf16[256,384]{1,0:T(8,128)(2,1)S(1)} %get-tuple-element.62), channel_id=1, source_target_pairs={{0,6},{1,7},{2,4},{3,5},{4,2},{5,3},{6,0},{7,1},{8,14},{9,15},{10,... | collective-permute-start | bytes 589832 | tf_op jit(solution)/shard_map/ppermute | solution.py:439
  92.3 13.9 %collective-permute-start.29 = (bf16[256,384]{1,0:T(8,128)(2,1)S(1)}, bf16[256,384]{1,0:T(8,128)(2,1)S(1)}, u32[]{:S(2)}, u32[]{:S(2)}) collective-permute-start(bf16[256,384]{1,0:T(8,128)(2,1)S(1)} %add_convert_fusion.1), channel_id=1, source_target_pairs={{0,6},{1,7},{2,4},{3,5},{4,2},{5,3},{6,0},{7,1},{8,14},{9,15},{10,... | collective-permute-start | bytes 589832 | tf_op jit(solution)/shard_map/ppermute | solution.py:439
  102.8 8.2 %collective-permute-start.31 = (bf16[256,384]{1,0:T(8,128)(2,1)S(1)}, bf16[256,384]{1,0:T(8,128)(2,1)S(1)}, u32[]{:S(2)}, u32[]{:S(2)}) collective-permute-start(bf16[256,384]{1,0:T(8,128)(2,1)S(1)} %add_convert_fusion), channel_id=1, source_target_pairs={{0,3},{1,2},{2,1},{3,0},{4,7},{5,6},{6,5},{7,4},{8,11},{9,10},{10,... | collective-permute-start | bytes 589832 | tf_op jit(solution)/shard_map/ppermute | solution.py:439
  111.7 5.6 %collective-permute-start.32 = (bf16[128,384]{1,0:T(8,128)(2,1)S(1)}, bf16[128,384]{1,0:T(8,128)(2,1)S(1)}, u32[]{:S(2)}, u32[]{:S(2)}) collective-permute-start(bf16[128,384]{1,0:T(8,128)(2,1)S(1)} %get-tuple-element.64), channel_id=1, source_target_pairs={{0,64},{8,72},{16,80},{24,88},{32,96},{40,104},{48,112},{56,120},{... | collective-permute-start | bytes 294920 | tf_op jit(solution)/shard_map/ppermute | solution.py:443
